TPU v7x, 256 devices: a whole 4x4x8 slice. The times are simulated.
256 devices in a mesh: rep: 32 (over x_hi, z, core), head: 8 (over x_lo, y).
Axes of the slice: x: 4 (x_hi: 2, x_lo: 2; x = x_hi * 2 + x_lo), y: 4, z: 8, core: 2. Of those that a mesh axis runs over, the one named last changes fastest.
Arguments:
- queries: bfloat16 [4096, 32, 128], P('rep', 'head'), may hold values from -6 to 6
- tree_keys: bfloat16 [4096, 8, 128], P('rep', 'head'), may hold values from -160 to 160
- tree_values: bfloat16 [4096, 8, 128], P('rep', 'head'), may hold values from -6 to 6
- prefix_keys: bfloat16 [128, 8, 128, 128], P('rep', 'head'), may hold values from -6 to 6
- prefix_values: bfloat16 [128, 8, 128, 128], P('rep', 'head'), may hold values from -6 to 6
- tree_parent: int32 [4096], P('rep'), may hold values from 0 to 62, as said below
- page_table: int32 [64, 16], P('rep'), may hold values from 0 to 127, all different within a row
- out_weight: bfloat16 [4096, 5120], P('head'), may hold values from -1.5 to 1.5
Outputs:
- mixed: bfloat16 [4096, 5120], P(('rep', 'head'))
Inputs may be any that keep to these rules, and one draw needn't show every extreme that they name: `tree_parent`: within each session a row's parent is an earlier row, the first row being its own parent. `page_table`: each session names 16 different pages; every page is named by some session.
All inputs are finite; a program needn't handle non-finite values.
Results may differ from a plain program's by a relative error of at most 0.019.
Values may be sent and summed in bfloat16 or wider, within the bound.
No kernel may reach another device: no remote copies, remote signals or barrier semaphores. Data moves between devices by JAX's collectives and lax.ppermute only.
A program may use at most 64 MiB of HBM per device.

v0:
```python
import functools
import math

import jax
import jax.numpy as jnp
from jax import lax
from jax.experimental import pallas as pl
from jax.experimental.pallas import tpu as pltpu
from jax.sharding import PartitionSpec as P

NEG = -1e30
Z = 8
GROUP = 4
LOCAL_PAGES = 4
TK_AT = 528
TV_AT = 656
TREE = 64
QROWS = 256
HD = 128
SESS = 8
C2 = (HD ** -0.5) * math.log2(math.e)
BF = jnp.bfloat16
F32 = jnp.float32

STREAMS = 4
GROUPS = ((0,), (-1, 1, -2, 2), (-3, 3), (4,))


def rep_of(xh, z, c):
    return xh * 16 + (z % Z) * 2 + c


def z_perm(k):
    return [(rep_of(a, z, c), rep_of(a, z + k, c)) for a in range(2) for z in range(Z) for c in range(2)]


def group_perm(r):
    return [(rep_of(a, z, c), rep_of(a ^ (r >> 1), z, c ^ (r & 1))) for a in range(2) for z in range(Z) for c in range(2)]


def pair_steps(entries, q_ref, kv, streams):
    at = [(e >> 8, e & 255) for e in entries]
    scores = [
        lax.dot_general(kv[k], q_ref[pl.ds(pl.multiple_of((s & (SESS - 1)) * QROWS, QROWS), QROWS), :], (((1,), (1,)), ((), ())), preferred_element_type=F32)
        for s, k in at
    ]
    olds = [m[s] for (s, _), (m, _, _) in zip(at, streams)]
    news = [jnp.maximum(o, jnp.max(x, axis=0, keepdims=True)) for o, x in zip(olds, scores)]
    probs = [jnp.exp2(x * C2 - n * C2) for x, n in zip(scores, news)]
    fixes = [jnp.exp2((o - n) * C2) for o, n in zip(olds, news)]
    parts = [
        lax.dot_general(
            kv[k + LOCAL_PAGES], p.astype(BF), (((0,), (0,)), ((), ())), preferred_element_type=F32
        )
        for (_, k), p in zip(at, probs)
    ]
    for (s, _), n, p, fix, part, (m_ref, l_ref, a_ref) in zip(at, news, probs, fixes, parts, streams):
        m_ref[s] = n
        l_ref[s] = l_ref[s] * fix + jnp.sum(p, axis=0, keepdims=True)
        a_ref[s] = a_ref[s] * fix + part


def all_pairs(entries, q_ref, kv, streams):
    ns = len(streams)

    @pl.loop(0, (entries[0] + ns - 1) >> (ns.bit_length() - 1))
    def _(i):
        pair_steps([entries[ns * i + r + 1] for r in range(ns)], q_ref, kv, streams)


def streams_of(refs):
    return [tuple(refs[3 * r:3 * r + 3]) for r in range(STREAMS)]


def clear(streams):
    for m_ref, l_ref, a_ref in streams:
        m_ref[...] = jnp.full(m_ref.shape, NEG, F32)
        l_ref[...] = jnp.zeros(l_ref.shape, F32)
        a_ref[...] = jnp.zeros(a_ref.shape, F32)


def merge(states):
    top = functools.reduce(jnp.maximum, [m for m, _, _ in states])
    ws = [jnp.exp2((m - top) * C2) for m, _, _ in states]
    total = sum(w * l for w, (_, l, _) in zip(ws, states))
    acc = sum(w * a for w, (_, _, a) in zip(ws, states))
    return top, total, acc


def pack_kernel(pk, pv, q, tk, tv, table, parent, kv, sent, local, tail, sems):
    copies = [
        pltpu.make_async_copy(pk, kv.at[pl.ds(0, LOCAL_PAGES)], sems.at[0]),
        pltpu.make_async_copy(pv, kv.at[pl.ds(LOCAL_PAGES, LOCAL_PAGES)], sems.at[1]),
        pltpu.make_async_copy(q, sent.at[pl.ds(0, 2 * QROWS)], sems.at[2]),
        pltpu.make_async_copy(q, local.at[pl.ds(0, 2 * QROWS)], sems.at[3]),
        pltpu.make_async_copy(tk, local.at[pl.ds(TK_AT, 128)], sems.at[4]),
        pltpu.make_async_copy(tv, local.at[pl.ds(TV_AT, 128)], sems.at[5]),
    ]
    for cp in copies:
        cp.start()
    ids = table[...].astype(F32)
    row = lax.broadcasted_iota(jnp.int32, (16, 128), 0)
    tail[...] = jnp.where(row == 2, parent[...].astype(F32), 0.0).astype(BF)
    row = row[:, :16]
    tail[:, :16] = jnp.where(
        row == 0, ids[0:1, :], jnp.where(row == 1, ids[1:2, :], jnp.where(row == 2, parent[:, :16].astype(F32), 0.0))
    ).astype(BF)
    last = [
        pltpu.make_async_copy(tail, sent.at[pl.ds(2 * QROWS, 16)], sems.at[6]),
        pltpu.make_async_copy(tail, local.at[pl.ds(2 * QROWS, 16)], sems.at[7]),
    ]
    for cp in last:
        cp.start()
    for cp in copies + last:
        cp.wait()


def own_kernel(maps, local, s1, s2, s3, kv, q_out, *refs):
    lists = refs[:3]
    m_out, l_out, a_out, tails, ids, tbl, list_own, found = refs[3:11]
    lists = (list_own,) + lists
    streams = streams_of(refs[11:-1])
    sems = refs[-1]
    sents = (local, s1, s2, s3)
    for r, x in enumerate(sents):
        tails[pl.ds(r * 16, 16), :] = x[pl.ds(2 * QROWS, 16), :]
    ids[...] = tails[...].astype(F32).astype(jnp.int32)
    to_scalar = pltpu.make_async_copy(ids, tbl, sems.at[0])
    to_scalar.start()
    for r, x in enumerate(sents):
        q_out[pl.ds(r * 2 * QROWS, 2 * QROWS), :] = x[pl.ds(0, 2 * QROWS), :]
    clear(streams)
    both = 2 * TREE
    row = lax.broadcasted_iota(jnp.int32, (both, both), 0)
    lane = lax.broadcasted_iota(jnp.int32, (both, both), 1)
    above = ids[2:3, :] + jnp.where(lax.broadcasted_iota(jnp.int32, (1, both), 1) >= TREE, TREE, 0)
    reach = jnp.minimum((row == lane).astype(F32) + (row == above).astype(F32), 1.0)
    for _ in range(7):
        half = reach.astype(BF)
        reach = jnp.minimum(jnp.dot(half, half, preferred_element_type=F32), 1.0)
    half = reach.astype(BF)
    tree_row = lax.broadcasted_iota(jnp.int32, (both, QROWS), 0)
    of_query = lax.shift_right_logical(lax.broadcasted_iota(jnp.int32, (both, QROWS), 1), 2)
    m0, l0, a0 = streams[0]
    for s in range(2):
        widen = (tree_row == of_query + s * TREE).astype(BF)
        seen = jnp.dot(half[s * TREE:(s + 1) * TREE, :], widen, preferred_element_type=F32)
        scores = lax.dot_general(
            local[pl.ds(TK_AT + s * TREE, TREE), :],
            local[pl.ds(s * QROWS, QROWS), :],
            (((1,), (1,)), ((), ())),
            preferred_element_type=F32,
        )
        scores = jnp.where(seen > 0.5, scores, NEG)
        top = jnp.max(scores, axis=0, keepdims=True)
        probs = jnp.exp2(scores * C2 - top * C2)
        m0[s] = top
        l0[s] = jnp.sum(probs, axis=0, keepdims=True)
        a0[s] = lax.dot_general(
            local[pl.ds(TV_AT + s * TREE, TREE), :],
            probs.astype(BF),
            (((0,), (0,)), ((), ())),
            preferred_element_type=F32,
        )
    to_scalar.wait()

    def scan(r, n):
        for half in range(2):
            pages = [tbl[r * 16 + half, j] for j in range(16)]
            at = [maps[p >> 2] for p in pages]
            for p, where in zip(pages, at):
                found[n] = (r * 2 + half) * 256 + (p & 3) + where
                n = n + (where >= 0).astype(jnp.int32)
        return n

    total = lax.fori_loop(0, GROUP, scan, jnp.int32(0))

    def sort(i, counts):
        entry = found[i]
        kind = entry >> 16
        out = []
        for k in range(4):
            lists[k][counts[k] + 1] = entry & 65535
            out.append(counts[k] + (kind == k).astype(jnp.int32))
        return tuple(out)

    counts = lax.fori_loop(0, total, sort, (jnp.int32(0),) * 4)
    for k in range(4):
        lists[k][0] = counts[k]
        for r in range(STREAMS - 1):
            lists[k][counts[k] + 1 + r] = jnp.int32(SESS * 256)
    all_pairs(list_own, q_out, kv, streams)
    for s in range(SESS):
        top, total, acc = merge([(m[s], l[s], a[s]) for m, l, a in streams])
        m_out[s] = top
        l_out[s] = total
        a_out[s] = acc


def load_blocks(blocks, kv, sems):
    copies = [pltpu.make_async_copy(b, kv.at[pl.ds(i * 8, 8)], sems.at[i]) for i, b in enumerate(blocks)]
    for cp in copies:
        cp.start()
    return copies


def near_kernel(nb, *refs):
    list_near, q_ref = refs[:2]
    blocks = refs[2:2 + nb]
    before = refs[2 + nb:5 + nb]
    m_out, l_out, a_out, kv = refs[5 + nb:9 + nb]
    streams = streams_of(refs[9 + nb:-1])
    copies = load_blocks(blocks, kv, refs[-1])
    clear(streams)
    for cp in copies:
        cp.wait()
    all_pairs(list_near, q_ref, kv, streams)
    for s in range(SESS):
        top, total, acc = merge([(m[s], l[s], a[s]) for m, l, a in [before] + streams])
        m_out[s] = top
        l_out[s] = total
        a_out[s] = acc


def far_kernel(nb, *refs):
    list_far, q_ref = refs[:2]
    blocks = refs[2:2 + nb]
    before = refs[2 + nb:5 + nb]
    own = refs[5 + nb]
    outs = refs[6 + nb:9 + nb]
    kv = refs[9 + nb]
    streams = streams_of(refs[10 + nb:-1])
    copies = load_blocks(blocks, kv, refs[-1])
    clear(streams)
    for cp in copies:
        cp.wait()
    all_pairs(list_far, q_ref, kv, streams)
    for s in range(SESS):
        top, total, acc = merge([(m[s], l[s], a[s]) for m, l, a in [before] + streams])
        some = total > 0.0
        safe = jnp.where(some, total, 1.0)
        acc = acc * (1.0 / safe)
        lse = jnp.where(some, top * C2 + jnp.log2(safe), NEG)
        lanes = pl.ds((s % 2) * QROWS, QROWS)
        if s < 2:
            own[pl.ds(0, HD), lanes] = acc
            own[pl.ds(HD, 8), lanes] = jnp.broadcast_to(lse, (8, QROWS))
        else:
            out = outs[s // 2 - 1]
            out[pl.ds(0, HD), lanes] = acc.astype(BF)
            hi = lse.astype(BF).astype(F32)
            mid = (lse - hi).astype(BF).astype(F32)
            low = lse - hi - mid
            row = lax.broadcasted_iota(jnp.int32, (16, QROWS), 0)
            parts = jnp.where(row == 0, hi, jnp.where(row == 1, mid, jnp.where(row == 2, low, 0.0)))
            out[pl.ds(HD, 16), lanes] = parts.astype(BF)


def combine_kernel(head_ref, own, p1, p2, p3, attn, rows_f32):
    lses = [own[HD:HD + 1, :]]
    vals = [own[:HD, :]]
    for p in (p1, p2, p3):
        tail = p[HD:HD + 16, :].astype(F32)
        lses.append(tail[0:1] + tail[1:2] + tail[2:3])
        vals.append(p[:HD, :].astype(F32))
    top = functools.reduce(jnp.maximum, lses)
    ws = [jnp.exp2(x - top) for x in lses]
    inv = 1.0 / sum(ws)
    mixed = sum(v * (w * inv) for v, w in zip(vals, ws))
    rows_f32[...] = mixed.T
    for k in range(8):
        first = (head_ref[0] ^ k) * 64
        for h in range(4):
            block = rows_f32[pl.ds(first + h, 16, stride=4), :]
            attn[pl.ds(k * 16, 16), pl.ds(h * HD, HD)] = block.astype(BF)


def sum_kernel(*refs):
    out = refs[-1]
    out[...] = functools.reduce(jnp.add, [r[...].astype(F32) for r in refs[:-1]]).astype(BF)


VMEM = pl.BlockSpec(memory_space=pltpu.VMEM)
SMEM = pl.BlockSpec(memory_space=pltpu.SMEM)
ANY = pl.BlockSpec(memory_space=pl.ANY)


def stream_scratch():
    return [
        pltpu.VMEM((SESS + 1, 1, QROWS), F32),
        pltpu.VMEM((SESS + 1, 1, QROWS), F32),
        pltpu.VMEM((SESS + 1, HD, QROWS), F32),
    ]


def state_shapes(n):
    return [
        jax.ShapeDtypeStruct((n, 1, QROWS), F32),
        jax.ShapeDtypeStruct((n, 1, QROWS), F32),
        jax.ShapeDtypeStruct((n, HD, QROWS), F32),
    ]


def lists(n):
    return [jax.ShapeDtypeStruct((160,), jnp.int32)] * n


def own_call(*args):
    return pl.pallas_call(
        own_kernel,
        out_shape=[jax.ShapeDtypeStruct((SESS * QROWS, HD), BF)] + lists(3) + state_shapes(SESS),
        in_specs=[SMEM] + [VMEM] * 5,
        out_specs=[VMEM] + [SMEM] * 3 + [VMEM] * 3,
        scratch_shapes=[
            pltpu.VMEM((64, 128), BF),
            pltpu.VMEM((64, 128), jnp.int32),
            pltpu.SMEM((64, 128), jnp.int32),
            pltpu.SMEM((160,), jnp.int32),
            pltpu.SMEM((160,), jnp.int32),
        ]
        + stream_scratch() * STREAMS
        + [pltpu.SemaphoreType.DMA((1,))],
        compiler_params=pltpu.CompilerParams(vmem_limit_bytes=24 << 20),
        cost_estimate=pl.CostEstimate(flops=2 * 10**9, bytes_accessed=4 << 20, transcendentals=1 << 20),
        name="own_pages",
    )(*args)


def block_scratch(nb):
    return (
        [pltpu.VMEM((8 * nb, 128, HD), BF)]
        + stream_scratch() * STREAMS
        + [pltpu.SemaphoreType.DMA((nb,))]
    )


def near_call(pages, q_all, blocks, state, name):
    nb = len(blocks)
    return pl.pallas_call(
        functools.partial(near_kernel, nb),
        out_shape=state_shapes(SESS),
        in_specs=[SMEM, VMEM] + [ANY] * nb + [VMEM] * 3,
        out_specs=[VMEM] * 3,
        scratch_shapes=block_scratch(nb),
        compiler_params=pltpu.CompilerParams(vmem_limit_bytes=24 << 20),
        cost_estimate=pl.CostEstimate(flops=10**9 * nb, bytes_accessed=4 << 20, transcendentals=1 << 20),
        name=name,
    )(pages, q_all, *blocks, *state)


def far_call(pages, q_all, blocks, state):
    nb = len(blocks)
    return pl.pallas_call(
        functools.partial(far_kernel, nb),
        out_shape=[jax.ShapeDtypeStruct((HD + 8, 2 * QROWS), F32)]
        + [jax.ShapeDtypeStruct((HD + 16, 2 * QROWS), BF)] * 3,
        in_specs=[SMEM, VMEM] + [ANY] * nb + [VMEM] * 3,
        out_specs=[VMEM] * 4,
        scratch_shapes=block_scratch(nb),
        compiler_params=pltpu.CompilerParams(vmem_limit_bytes=24 << 20),
        cost_estimate=pl.CostEstimate(flops=10**9, bytes_accessed=4 << 20, transcendentals=1 << 20),
        name="last_pages",
    )(pages, q_all, *blocks, *state)


def on_device(
    queries, tree_keys, tree_values, prefix_keys, prefix_values, tree_parent, page_table, out_weight
):
    rep = lax.axis_index("rep")
    head = lax.axis_index("head")
    q_own = queries.reshape(2 * QROWS, HD)
    kv, sent, local = pl.pallas_call(
        pack_kernel,
        out_shape=[
            jax.ShapeDtypeStruct((2 * LOCAL_PAGES, 128, HD), BF),
            jax.ShapeDtypeStruct((2 * QROWS + 16, HD), BF),
            jax.ShapeDtypeStruct((TV_AT + 128, HD), BF),
        ],
        in_specs=[ANY] * 5 + [VMEM] * 2,
        out_specs=[ANY] * 3,
        scratch_shapes=[pltpu.VMEM((16, 128), BF), pltpu.SemaphoreType.DMA((8,))],
        compiler_params=pltpu.CompilerParams(vmem_limit_bytes=59 << 20),
        name="pack",
    )(
        prefix_keys.reshape(LOCAL_PAGES, 128, HD), prefix_values.reshape(LOCAL_PAGES, 128, HD), q_own,
        tree_keys.reshape(-1, HD), tree_values.reshape(-1, HD), page_table, tree_parent.reshape(1, -1),
    )
    up1 = lax.ppermute(kv, "rep", z_perm(1))
    dn1 = lax.ppermute(kv, "rep", z_perm(-1))
    sents = [lax.ppermute(sent, "rep", group_perm(r)) for r in (1, 2, 3)]
    up2 = lax.ppermute(up1, "rep", z_perm(1))
    dn2 = lax.ppermute(dn1, "rep", z_perm(-1))
    up3 = lax.ppermute(up2, "rep", z_perm(1))
    dn3 = lax.ppermute(dn2, "rep", z_perm(-1))
    up4 = lax.ppermute(up3, "rep", z_perm(1))

    reps = jnp.arange(32, dtype=jnp.int32)
    same = ((reps ^ rep) & 17) == 0
    step = ((reps >> 1) - (rep >> 1)) & 7
    maps = jnp.full((32,), -(1 << 20), jnp.int32)
    for k, offsets in enumerate(GROUPS):
        for i, o in enumerate(offsets):
            maps = jnp.where(same & (step == o % Z), k * 65536 + i * 8, maps)
    q_all, list_1, list_2, list_3, *state = own_call(maps, local, *sents, kv)
    state = near_call(list_1, q_all, (up1, dn1, up2, dn2), state, "near_pages")
    state = near_call(list_2, q_all, (up3, dn3), state, "far_pages")
    own, p1, p2, p3 = far_call(list_3, q_all, (up4,), state)
    back = [lax.ppermute(p, "rep", group_perm(r)) for r, p in ((1, p1), (2, p2), (3, p3))]
    width = out_weight.shape[1]
    attn = pl.pallas_call(
        combine_kernel,
        out_shape=jax.ShapeDtypeStruct((128, 512), BF),
        in_specs=[SMEM] + [VMEM] * 4,
        out_specs=VMEM,
        scratch_shapes=[pltpu.VMEM((2 * QROWS, HD), F32)],
        compiler_params=pltpu.CompilerParams(vmem_limit_bytes=24 << 20),
        cost_estimate=pl.CostEstimate(flops=10**6, bytes_accessed=1 << 20, transcendentals=4096),
        name="combine",
    )(head.reshape(1).astype(jnp.int32), own, *back)
    rows = jnp.dot(attn, out_weight, preferred_element_type=F32).astype(BF)
    parts = [rows[k * 16:(k + 1) * 16] for k in range(8)]
    terms = [lax.ppermute(parts[k], "head", [(i, i ^ k) for i in range(8)]) for k in (1, 3, 4, 2, 5, 7, 6)]
    return pl.pallas_call(
        sum_kernel,
        out_shape=jax.ShapeDtypeStruct((16, width), BF),
        in_specs=[VMEM] * 8,
        out_specs=VMEM,
        compiler_params=pltpu.CompilerParams(vmem_limit_bytes=24 << 20),
        name="sum_heads",
    )(parts[0], *terms)


def solution(mesh):
    in_specs = (
        P("rep", "head", None),
        P("rep", "head", None),
        P("rep", "head", None),
        P("rep", "head", None, None),
        P("rep", "head", None, None),
        P("rep"),
        P("rep", None),
        P("head", None),
    )
    out_specs = P(("rep", "head"), None)
    return jax.shard_map(
        on_device, mesh=mesh, in_specs=in_specs, out_specs=out_specs, check_vma=False
    )
```

profile of v0, /device:TPU:2, one launch (start us, length us, event | category | flops | bytes accessed | tf_op | source)
XLA Modules:
  0.0 102.0 jit_solution(17671167496100018286)
XLA Ops:
  0.0 19.7 %pack.1 = (bf16[8,128,128]{2,1,0:T(8,128)(2,1)}, bf16[528,128]{1,0:T(8,128)(2,1)}, bf16[784,128]{1,0:T(8,128)(2,1)}) custom-call(bf16[4,128,128]{2,1,0:T(8,128)(2,1)} %bitcast.9, bf16[4,128,128]{2,1,0:T(8,128)(2,1)} %bitcast.10, bf16[512,128]{1,0:T(8,128)(2,1)} %bitcast.11, bf16[128,128]{1,0:T(8,128)(2,1)} %bitcast.12, bf16[128,128]{1,0:T(8,128)(2,1)} %bitcast.13, ...), custom_call_target="tpu_custom_call" | custom-call | tf_op jit(solution)/shard_map/pack/pallas_call | solution.py:372
  19.7 2.0 %collective-permute-start.3 = (bf16[8,128,128]{2,1,0:T(8,128)(2,1)}, bf16[8,128,128]{2,1,0:T(8,128)(2,1)S(1)}, u32[]{:S(2)}, u32[]{:S(2)}) collective-permute-start(bf16[8,128,128]{2,1,0:T(8,128)(2,1)} %get-tuple-element.27.kv), channel_id=1, source_target_pairs={{0,16},{8,24},{16,32},{24,40},{32,48},{40,56},{48,64},{56,72},{64,... | collective-permute-start | bytes 786440 | tf_op jit(solution)/shard_map/ppermute | solution.py:388
  21.7 4.0 %collective-permute-start.7 = (bf16[8,128,128]{2,1,0:T(8,128)(2,1)}, bf16[8,128,128]{2,1,0:T(8,128)(2,1)S(1)}, u32[]{:S(2)}, u32[]{:S(2)}) collective-permute-start(bf16[8,128,128]{2,1,0:T(8,128)(2,1)} %get-tuple-element.27.kv), channel_id=1, source_target_pairs={{0,112},{8,120},{16,0},{24,8},{32,16},{40,24},{48,32},{56,40},{64,... | collective-permute-start | bytes 786440 | tf_op jit(solution)/shard_map/ppermute | solution.py:389
  25.8 6.4 %collective-permute-done.3.refs_2_ = bf16[8,128,128]{2,1,0:T(8,128)(2,1)S(1)} collective-permute-done((bf16[8,128,128]{2,1,0:T(8,128)(2,1)}, bf16[8,128,128]{2,1,0:T(8,128)(2,1)S(1)}, u32[]{:S(2)}, u32[]{:S(2)}) %collective-permute-start.3) | collective-permute-done | bytes 262176 | tf_op jit(solution)/shard_map/ppermute | solution.py:388
  32.2 2.1 %collective-permute-start.1 = (bf16[528,128]{1,0:T(8,128)(2,1)}, bf16[528,128]{1,0:T(8,128)(2,1)S(1)}, u32[]{:S(2)}, u32[]{:S(2)}) collective-permute-start(bf16[528,128]{1,0:T(8,128)(2,1)} %get-tuple-element.26), channel_id=1, source_target_pairs={{0,128},{8,136},{16,144},{24,152},{32,160},{40,168},{48,176},{56,1... | collective-permute-start | bytes 405512 | tf_op jit(solution)/shard_map/ppermute | solution.py:390
  35.6 3.2 %collective-permute-start.8 = (bf16[8,128,128]{2,1,0:T(8,128)(2,1)S(1)}, bf16[8,128,128]{2,1,0:T(8,128)(2,1)S(1)}, u32[]{:S(2)}, u32[]{:S(2)}) collective-permute-start(bf16[8,128,128]{2,1,0:T(8,128)(2,1)S(1)} %collective-permute-done.7.refs_3_), channel_id=1, source_target_pairs={{0,112},{8,120},{16,0},{24,8},{32,16},{40,24},{48,32},{56,40},{64,... | collective-permute-start | bytes 786440 | tf_op jit(solution)/shard_map/ppermute | solution.py:392
  38.8 2.1 %collective-permute-done.4.refs_4_ = bf16[8,128,128]{2,1,0:T(8,128)(2,1)S(1)} collective-permute-done((bf16[8,128,128]{2,1,0:T(8,128)(2,1)S(1)}, bf16[8,128,128]{2,1,0:T(8,128)(2,1)S(1)}, u32[]{:S(2)}, u32[]{:S(2)}) %collective-permute-start.4) | collective-permute-done | bytes 262176 | tf_op jit(solution)/shard_map/ppermute | solution.py:391
  40.9 1.5 %collective-permute-done.2.s3 = bf16[528,128]{1,0:T(8,128)(2,1)S(1)} collective-permute-done((bf16[528,128]{1,0:T(8,128)(2,1)}, bf16[528,128]{1,0:T(8,128)(2,1)S(1)}, u32[]{:S(2)}, u32[]{:S(2)}) %collective-permute-start.2) | collective-permute-done | bytes 135200 | tf_op jit(solution)/shard_map/ppermute | solution.py:390
  44.3 5.5 %own_pages.1 = (bf16[2048,128]{1,0:T(8,128)(2,1)S(1)}, s32[160]{0:T(256)S(1)}, s32[160]{0:T(256)S(1)}, s32[160]{0:T(256)S(1)}, f32[8,1,256]{2,1,0:T(1,128)S(1)},...) custom-call(s32[32]{0:T(128)S(1)} %and_select_fusion.7.maps, bf16[784,128]{1,0:T(8,128)(2,1)S(1)} %copy-done.1, ...), custom_call_target="tpu_custom_call" | custom-call | flops 2000000000 | bytes 4194304 | tf_op jit(solution)/shard_map/own_pages/pallas_call | solution.py:309
  49.8 3.2 %collective-permute-start.9 = (bf16[8,128,128]{2,1,0:T(8,128)(2,1)S(1)}, bf16[8,128,128]{2,1,0:T(8,128)(2,1)S(1)}, u32[]{:S(2)}, u32[]{:S(2)}) collective-permute-start(bf16[8,128,128]{2,1,0:T(8,128)(2,1)S(1)} %collective-permute-done.8.refs_5_), channel_id=1, source_target_pairs={{0,112},{8,120},{16,0},{24,8},{32,16},{40,24},{48,32},{56,40},{64,... | collective-permute-start | bytes 786440 | tf_op jit(solution)/shard_map/ppermute | solution.py:394
  53.0 3.4 %near_pages.1 = (f32[8,1,256]{2,1,0:T(1,128)S(1)}, f32[8,1,256]{2,1,0:T(1,128)S(1)}, f32[8,128,256]{2,1,0:T(8,128)S(1)}) custom-call(s32[160]{0:T(256)S(1)} %get-tuple-element.31.refs_0_, bf16[2048,128]{1,0:T(8,128)(2,1)S(1)} %get-tuple-element.29.refs_1_, bf16[8,128,128]{2,1,0:T(8,128)(2,1)S(1)} %collective-permute-done.3.refs_2_, ...), custom_call_target="tpu_custom_call" | custom-call | flops 4000000000 | bytes 4194304 | tf_op jit(solution)/shard_map/near_pages/pallas_call | solution.py:339
  56.4 3.0 %collective-permute-done.9.refs_3_ = bf16[8,128,128]{2,1,0:T(8,128)(2,1)S(1)} collective-permute-done((bf16[8,128,128]{2,1,0:T(8,128)(2,1)S(1)}, bf16[8,128,128]{2,1,0:T(8,128)(2,1)S(1)}, u32[]{:S(2)}, u32[]{:S(2)}) %collective-permute-start.9) | collective-permute-done | bytes 262176 | tf_op jit(solution)/shard_map/ppermute | solution.py:394
  59.5 3.8 %far_pages.1 = (f32[8,1,256]{2,1,0:T(1,128)S(1)}, f32[8,1,256]{2,1,0:T(1,128)S(1)}, f32[8,128,256]{2,1,0:T(8,128)S(1)}) custom-call(s32[160]{0:T(256)S(1)} %get-tuple-element.30.refs_0_, bf16[2048,128]{1,0:T(8,128)(2,1)S(1)} %get-tuple-element.29.refs_1_, bf16[8,128,128]{2,1,0:T(8,128)(2,1)S(1)} %collective-permute-done.5.refs_2_, ...), custom_call_target="tpu_custom_call" | custom-call | flops 2000000000 | bytes 4194304 | tf_op jit(solution)/shard_map/far_pages/pallas_call | solution.py:339
  63.4 1.6 %last_pages.1 = (f32[136,512]{1,0:T(8,128)S(1)}, bf16[144,512]{1,0:T(8,128)(2,1)S(1)}, bf16[144,512]{1,0:T(8,128)(2,1)S(1)}, bf16[144,512]{1,0:T(8,128)(2,1)S(1)}) custom-call(s32[160]{0:T(256)S(1)} %get-tuple-element.28.refs_0_, bf16[2048,128]{1,0:T(8,128)(2,1)S(1)} %get-tuple-element.29.refs_1_, bf16[8,128,128]{2,1,0:T(8,128)(2,1)S(1)} %collective-permute-done.6.refs_2_, ...), custom_call_target="tpu_custom_call" | custom-call | flops 1000000000 | bytes 4194304 | tf_op jit(solution)/shard_map/last_pages/pallas_call | solution.py:353
  66.8 1.8 %collective-permute-start.12 = (bf16[144,512]{1,0:T(8,128)(2,1)S(1)}, bf16[144,512]{1,0:T(8,128)(2,1)S(1)}, u32[]{:S(2)}, u32[]{:S(2)}) collective-permute-start(bf16[144,512]{1,0:T(8,128)(2,1)S(1)} %get-tuple-element.44), channel_id=1, source_target_pairs={{0,136},{8,128},{16,152},{24,144},{32,168},{40,160},{48,184},{56,1... | collective-permute-start | bytes 442376 | tf_op jit(solution)/shard_map/ppermute | solution.py:408
  68.6 5.2 %collective-permute-done.11.p2 = bf16[144,512]{1,0:T(8,128)(2,1)S(1)} collective-permute-done((bf16[144,512]{1,0:T(8,128)(2,1)S(1)}, bf16[144,512]{1,0:T(8,128)(2,1)S(1)}, u32[]{:S(2)}, u32[]{:S(2)}) %collective-permute-start.11) | collective-permute-done | bytes 147488 | tf_op jit(solution)/shard_map/ppermute | solution.py:408
  73.9 1.5 %collective-permute-done.12.p3 = bf16[144,512]{1,0:T(8,128)(2,1)S(1)} collective-permute-done((bf16[144,512]{1,0:T(8,128)(2,1)S(1)}, bf16[144,512]{1,0:T(8,128)(2,1)S(1)}, u32[]{:S(2)}, u32[]{:S(2)}) %collective-permute-start.12) | collective-permute-done | bytes 147488 | tf_op jit(solution)/shard_map/ppermute | solution.py:408
  75.6 3.3 %convolution_convert_fusion = bf16[128,5120]{1,0:T(8,128)(2,1)S(1)} fusion(bf16[128,512]{1,0:T(8,128)(2,1)S(1)} %combine.1, bf16[512,5120]{1,0:T(8,128)(2,1)} %param.15), kind=kOutput, calls=%fused_computation | convolution fusion | flops 671744000 | bytes 6684672 | tf_op jit(solution)/shard_map/dot_general | solution.py:420
  79.0 1.6 %collective-permute-start.13 = (bf16[16,5120]{1,0:T(8,128)(2,1)S(1)}, bf16[16,5120]{1,0:T(8,128)(2,1)S(1)}, u32[]{:S(2)}, u32[]{:S(2)}) collective-permute-start(bf16[16,5120]{1,0:T(8,128)(2,1)S(1)} %get-tuple-element.51), channel_id=1, source_target_pairs={{0,1},{1,0},{2,3},{3,2},{4,5},{5,4},{6,7},{7,6},{8,9},{9,8},{10,11... | collective-permute-start | bytes 491528 | tf_op jit(solution)/shard_map/ppermute | solution.py:422
  80.6 2.2 %collective-permute-start.14 = (bf16[16,5120]{1,0:T(8,128)(2,1)S(1)}, bf16[16,5120]{1,0:T(8,128)(2,1)S(1)}, u32[]{:S(2)}, u32[]{:S(2)}) collective-permute-start(bf16[16,5120]{1,0:T(8,128)(2,1)S(1)} %get-tuple-element.50), channel_id=1, source_target_pairs={{0,3},{1,2},{2,1},{3,0},{4,7},{5,6},{6,5},{7,4},{8,11},{9,10},{10,... | collective-permute-start | bytes 491528 | tf_op jit(solution)/shard_map/ppermute | solution.py:422
  84.5 1.7 %collective-permute-start.17 = (bf16[16,5120]{1,0:T(8,128)(2,1)S(1)}, bf16[16,5120]{1,0:T(8,128)(2,1)S(1)}, u32[]{:S(2)}, u32[]{:S(2)}) collective-permute-start(bf16[16,5120]{1,0:T(8,128)(2,1)S(1)} %get-tuple-element.47), channel_id=1, source_target_pairs={{0,5},{1,4},{2,7},{3,6},{4,1},{5,0},{6,3},{7,2},{8,13},{9,12},{10,... | collective-permute-start | bytes 491528 | tf_op jit(solution)/shard_map/ppermute | solution.py:422
  86.2 2.6 %collective-permute-start.18 = (bf16[16,5120]{1,0:T(8,128)(2,1)S(1)}, bf16[16,5120]{1,0:T(8,128)(2,1)S(1)}, u32[]{:S(2)}, u32[]{:S(2)}) collective-permute-start(bf16[16,5120]{1,0:T(8,128)(2,1)S(1)} %get-tuple-element.46), channel_id=1, source_target_pairs={{0,7},{1,6},{2,5},{3,4},{4,3},{5,2},{6,1},{7,0},{8,15},{9,14},{10,... | collective-permute-start | bytes 491528 | tf_op jit(solution)/shard_map/ppermute | solution.py:422
  90.2 2.1 %collective-permute-start.19 = (bf16[16,5120]{1,0:T(8,128)(2,1)S(1)}, bf16[16,5120]{1,0:T(8,128)(2,1)S(1)}, u32[]{:S(2)}, u32[]{:S(2)}) collective-permute-start(bf16[16,5120]{1,0:T(8,128)(2,1)S(1)} %get-tuple-element.45), channel_id=1, source_target_pairs={{0,6},{1,7},{2,4},{3,5},{4,2},{5,3},{6,0},{7,1},{8,14},{9,15},{10,... | collective-permute-start | bytes 491528 | tf_op jit(solution)/shard_map/ppermute | solution.py:422
  92.3 8.9 %collective-permute-done.16.refs_4_ = bf16[16,5120]{1,0:T(8,128)(2,1)S(1)} collective-permute-done((bf16[16,5120]{1,0:T(8,128)(2,1)S(1)}, bf16[16,5120]{1,0:T(8,128)(2,1)S(1)}, u32[]{:S(2)}, u32[]{:S(2)}) %collective-permute-start.16) | collective-permute-done | bytes 163872 | tf_op jit(solution)/shard_map/ppermute | solution.py:422
  (30 shorter events, 9.2 us)
Async XLA Ops:
  19.7 12.4 %collective-permute-start.3 = (bf16[8,128,128]{2,1,0:T(8,128)(2,1)}, bf16[8,128,128]{2,1,0:T(8,128)(2,1)S(1)}, u32[]{:S(2)}, u32[]{:S(2)}) collective-permute-start(bf16[8,128,128]{2,1,0:T(8,128)(2,1)} %get-tuple-element.27.kv), channel_id=1, source_target_pairs={{0,16},{8,24},{16,32},{24,40},{32,48},{40,56},{48,64},{56,72},{64,... | collective-permute-start | bytes 786440 | tf_op jit(solution)/shard_map/ppermute | solution.py:388
  21.7 13.8 %collective-permute-start.7 = (bf16[8,128,128]{2,1,0:T(8,128)(2,1)}, bf16[8,128,128]{2,1,0:T(8,128)(2,1)S(1)}, u32[]{:S(2)}, u32[]{:S(2)}) collective-permute-start(bf16[8,128,128]{2,1,0:T(8,128)(2,1)} %get-tuple-element.27.kv), channel_id=1, source_target_pairs={{0,112},{8,120},{16,0},{24,8},{32,16},{40,24},{48,32},{56,40},{64,... | collective-permute-start | bytes 786440 | tf_op jit(solution)/shard_map/ppermute | solution.py:389
  32.2 8.7 %collective-permute-start.4 = (bf16[8,128,128]{2,1,0:T(8,128)(2,1)S(1)}, bf16[8,128,128]{2,1,0:T(8,128)(2,1)S(1)}, u32[]{:S(2)}, u32[]{:S(2)}) collective-permute-start(bf16[8,128,128]{2,1,0:T(8,128)(2,1)S(1)} %collective-permute-done.3.refs_2_), channel_id=1, source_target_pairs={{0,16},{8,24},{16,32},{24,40},{32,48},{40,56},{48,64},{56,72},{64,... | collective-permute-start | bytes 786440 | tf_op jit(solution)/shard_map/ppermute | solution.py:391
  32.2 8.7 %collective-permute-start = (bf16[528,128]{1,0:T(8,128)(2,1)}, bf16[528,128]{1,0:T(8,128)(2,1)S(1)}, u32[]{:S(2)}, u32[]{:S(2)}) collective-permute-start(bf16[528,128]{1,0:T(8,128)(2,1)} %get-tuple-element.26), channel_id=1, source_target_pairs={{0,8},{8,0},{16,24},{24,16},{32,40},{40,32},{48,56},{56,48},{64,72... | collective-permute-start | bytes 405512 | tf_op jit(solution)/shard_map/ppermute | solution.py:390
  32.2 8.7 %collective-permute-start.1 = (bf16[528,128]{1,0:T(8,128)(2,1)}, bf16[528,128]{1,0:T(8,128)(2,1)S(1)}, u32[]{:S(2)}, u32[]{:S(2)}) collective-permute-start(bf16[528,128]{1,0:T(8,128)(2,1)} %get-tuple-element.26), channel_id=1, source_target_pairs={{0,128},{8,136},{16,144},{24,152},{32,160},{40,168},{48,176},{56,1... | collective-permute-start | bytes 405512 | tf_op jit(solution)/shard_map/ppermute | solution.py:390
  34.3 8.1 %collective-permute-start.2 = (bf16[528,128]{1,0:T(8,128)(2,1)}, bf16[528,128]{1,0:T(8,128)(2,1)S(1)}, u32[]{:S(2)}, u32[]{:S(2)}) collective-permute-start(bf16[528,128]{1,0:T(8,128)(2,1)} %get-tuple-element.26), channel_id=1, source_target_pairs={{0,136},{8,128},{16,152},{24,144},{32,168},{40,160},{48,184},{56,1... | collective-permute-start | bytes 405512 | tf_op jit(solution)/shard_map/ppermute | solution.py:390
  35.6 14.2 %collective-permute-start.8 = (bf16[8,128,128]{2,1,0:T(8,128)(2,1)S(1)}, bf16[8,128,128]{2,1,0:T(8,128)(2,1)S(1)}, u32[]{:S(2)}, u32[]{:S(2)}) collective-permute-start(bf16[8,128,128]{2,1,0:T(8,128)(2,1)S(1)} %collective-permute-done.7.refs_3_), channel_id=1, source_target_pairs={{0,112},{8,120},{16,0},{24,8},{32,16},{40,24},{48,32},{56,40},{64,... | collective-permute-start | bytes 786440 | tf_op jit(solution)/shard_map/ppermute | solution.py:392
  40.9 12.1 %collective-permute-start.5 = (bf16[8,128,128]{2,1,0:T(8,128)(2,1)S(1)}, bf16[8,128,128]{2,1,0:T(8,128)(2,1)S(1)}, u32[]{:S(2)}, u32[]{:S(2)}) collective-permute-start(bf16[8,128,128]{2,1,0:T(8,128)(2,1)S(1)} %collective-permute-done.4.refs_4_), channel_id=1, source_target_pairs={{0,16},{8,24},{16,32},{24,40},{32,48},{40,56},{48,64},{56,72},{64,... | collective-permute-start | bytes 786440 | tf_op jit(solution)/shard_map/ppermute | solution.py:393
  42.4 1.0 copy-start
  43.4 0.9 copy-start.1
  49.8 9.7 %collective-permute-start.9 = (bf16[8,128,128]{2,1,0:T(8,128)(2,1)S(1)}, bf16[8,128,128]{2,1,0:T(8,128)(2,1)S(1)}, u32[]{:S(2)}, u32[]{:S(2)}) collective-permute-start(bf16[8,128,128]{2,1,0:T(8,128)(2,1)S(1)} %collective-permute-done.8.refs_5_), channel_id=1, source_target_pairs={{0,112},{8,120},{16,0},{24,8},{32,16},{40,24},{48,32},{56,40},{64,... | collective-permute-start | bytes 786440 | tf_op jit(solution)/shard_map/ppermute | solution.py:394
  53.0 10.4 %collective-permute-start.6 = (bf16[8,128,128]{2,1,0:T(8,128)(2,1)S(1)}, bf16[8,128,128]{2,1,0:T(8,128)(2,1)S(1)}, u32[]{:S(2)}, u32[]{:S(2)}) collective-permute-start(bf16[8,128,128]{2,1,0:T(8,128)(2,1)S(1)} %collective-permute-done.5.refs_2_), channel_id=1, source_target_pairs={{0,16},{8,24},{16,32},{24,40},{32,48},{40,56},{48,64},{56,72},{64,... | collective-permute-start | bytes 786440 | tf_op jit(solution)/shard_map/ppermute | solution.py:395
  65.0 3.6 %collective-permute-start.10 = (bf16[144,512]{1,0:T(8,128)(2,1)S(1)}, bf16[144,512]{1,0:T(8,128)(2,1)S(1)}, u32[]{:S(2)}, u32[]{:S(2)}) collective-permute-start(bf16[144,512]{1,0:T(8,128)(2,1)S(1)} %get-tuple-element.42), channel_id=1, source_target_pairs={{0,8},{8,0},{16,24},{24,16},{32,40},{40,32},{48,56},{56,48},{64,72... | collective-permute-start | bytes 442376 | tf_op jit(solution)/shard_map/ppermute | solution.py:408
  65.7 8.2 %collective-permute-start.11 = (bf16[144,512]{1,0:T(8,128)(2,1)S(1)}, bf16[144,512]{1,0:T(8,128)(2,1)S(1)}, u32[]{:S(2)}, u32[]{:S(2)}) collective-permute-start(bf16[144,512]{1,0:T(8,128)(2,1)S(1)} %get-tuple-element.43), channel_id=1, source_target_pairs={{0,128},{8,136},{16,144},{24,152},{32,160},{40,168},{48,176},{56,1... | collective-permute-start | bytes 442376 | tf_op jit(solution)/shard_map/ppermute | solution.py:408
  66.8 8.5 %collective-permute-start.12 = (bf16[144,512]{1,0:T(8,128)(2,1)S(1)}, bf16[144,512]{1,0:T(8,128)(2,1)S(1)}, u32[]{:S(2)}, u32[]{:S(2)}) collective-permute-start(bf16[144,512]{1,0:T(8,128)(2,1)S(1)} %get-tuple-element.44), channel_id=1, source_target_pairs={{0,136},{8,128},{16,152},{24,144},{32,168},{40,160},{48,184},{56,1... | collective-permute-start | bytes 442376 | tf_op jit(solution)/shard_map/ppermute | solution.py:408
  79.0 7.2 %collective-permute-start.13 = (bf16[16,5120]{1,0:T(8,128)(2,1)S(1)}, bf16[16,5120]{1,0:T(8,128)(2,1)S(1)}, u32[]{:S(2)}, u32[]{:S(2)}) collective-permute-start(bf16[16,5120]{1,0:T(8,128)(2,1)S(1)} %get-tuple-element.51), channel_id=1, source_target_pairs={{0,1},{1,0},{2,3},{3,2},{4,5},{5,4},{6,7},{7,6},{8,9},{9,8},{10,11... | collective-permute-start | bytes 491528 | tf_op jit(solution)/shard_map/ppermute | solution.py:422
  80.6 9.6 %collective-permute-start.14 = (bf16[16,5120]{1,0:T(8,128)(2,1)S(1)}, bf16[16,5120]{1,0:T(8,128)(2,1)S(1)}, u32[]{:S(2)}, u32[]{:S(2)}) collective-permute-start(bf16[16,5120]{1,0:T(8,128)(2,1)S(1)} %get-tuple-element.50), channel_id=1, source_target_pairs={{0,3},{1,2},{2,1},{3,0},{4,7},{5,6},{6,5},{7,4},{8,11},{9,10},{10,... | collective-permute-start | bytes 491528 | tf_op jit(solution)/shard_map/ppermute | solution.py:422
  82.8 9.4 %collective-permute-start.15 = (bf16[16,5120]{1,0:T(8,128)(2,1)S(1)}, bf16[16,5120]{1,0:T(8,128)(2,1)S(1)}, u32[]{:S(2)}, u32[]{:S(2)}) collective-permute-start(bf16[16,5120]{1,0:T(8,128)(2,1)S(1)} %get-tuple-element.49), channel_id=1, source_target_pairs={{0,4},{1,5},{2,6},{3,7},{4,0},{5,1},{6,2},{7,3},{8,12},{9,13},{10,... | collective-permute-start | bytes 491528 | tf_op jit(solution)/shard_map/ppermute | solution.py:422
  83.8 17.4 %collective-permute-start.16 = (bf16[16,5120]{1,0:T(8,128)(2,1)S(1)}, bf16[16,5120]{1,0:T(8,128)(2,1)S(1)}, u32[]{:S(2)}, u32[]{:S(2)}) collective-permute-start(bf16[16,5120]{1,0:T(8,128)(2,1)S(1)} %get-tuple-element.48), channel_id=1, source_target_pairs={{0,2},{1,3},{2,0},{3,1},{4,6},{5,7},{6,4},{7,5},{8,10},{9,11},{10,... | collective-permute-start | bytes 491528 | tf_op jit(solution)/shard_map/ppermute | solution.py:422
  84.5 16.7 %collective-permute-start.17 = (bf16[16,5120]{1,0:T(8,128)(2,1)S(1)}, bf16[16,5120]{1,0:T(8,128)(2,1)S(1)}, u32[]{:S(2)}, u32[]{:S(2)}) collective-permute-start(bf16[16,5120]{1,0:T(8,128)(2,1)S(1)} %get-tuple-element.47), channel_id=1, source_target_pairs={{0,5},{1,4},{2,7},{3,6},{4,1},{5,0},{6,3},{7,2},{8,13},{9,12},{10,... | collective-permute-start | bytes 491528 | tf_op jit(solution)/shard_map/ppermute | solution.py:422
  86.2 14.9 %collective-permute-start.18 = (bf16[16,5120]{1,0:T(8,128)(2,1)S(1)}, bf16[16,5120]{1,0:T(8,128)(2,1)S(1)}, u32[]{:S(2)}, u32[]{:S(2)}) collective-permute-start(bf16[16,5120]{1,0:T(8,128)(2,1)S(1)} %get-tuple-element.46), channel_id=1, source_target_pairs={{0,7},{1,6},{2,5},{3,4},{4,3},{5,2},{6,1},{7,0},{8,15},{9,14},{10,... | collective-permute-start | bytes 491528 | tf_op jit(solution)/shard_map/ppermute | solution.py:422
  90.2 10.9 %collective-permute-start.19 = (bf16[16,5120]{1,0:T(8,128)(2,1)S(1)}, bf16[16,5120]{1,0:T(8,128)(2,1)S(1)}, u32[]{:S(2)}, u32[]{:S(2)}) collective-permute-start(bf16[16,5120]{1,0:T(8,128)(2,1)S(1)} %get-tuple-element.45), channel_id=1, source_target_pairs={{0,6},{1,7},{2,4},{3,5},{4,2},{5,3},{6,0},{7,1},{8,14},{9,15},{10,... | collective-permute-start | bytes 491528 | tf_op jit(solution)/shard_map/ppermute | solution.py:422
where the time goes:
time: 102 us
  Pallas kernels  35.1 us (34%)
  starting transfers between devices  31.4 us (31%)
  waiting for transfers between devices  30.1 us (30%)
  matrix products  3.34 us (3%)
  local copies, waits for them, and re-layouts  1.97 us (2%)
    pallas_call x1, Pallas kernels, on_device(): pl.pallas_call(pack_kernel, out_shape=[jax.ShapeDtypeStruct((2 * LOCAL_PA...  19.7 us
    ppermute x7, starting transfers between devices, on_device(): lax.ppermute(parts[k], 'head', [(i, i ^ k) for i in range(8)])  11.9 us
    ppermute x7, waiting for transfers between devices, on_device(): lax.ppermute(parts[k], 'head', [(i, i ^ k) for i in range(8)])  10.3 us
    pallas_call x2, Pallas kernels, near_call(): pl.pallas_call(functools.partial(near_kernel, nb), out_shape=state_shapes...  7.25 us
    ppermute x3, waiting for transfers between devices, on_device(): lax.ppermute(p, 'rep', group_perm(r))  6.71 us
    ppermute x1, waiting for transfers between devices, on_device(): up1 = lax.ppermute(kv, 'rep', z_perm(1))  6.43 us
    pallas_call x1, Pallas kernels, own_call(): pl.pallas_call(own_kernel, out_shape=[jax.ShapeDtypeStruct((SESS * QROWS,...  5.47 us
    ppermute x1, starting transfers between devices, on_device(): dn1 = lax.ppermute(kv, 'rep', z_perm(-1))  4.03 us
  transfers between devices with their start and end apart: 20, of which 9 were waited for; matrix products, arithmetic and copies ran while one was open for 0% of the time, Pallas kernels for 12%

commit v1 on v0

--- a/solution.py
+++ b/solution.py
@@ -87,35 +87,32 @@
     return top, total, acc
 
 
-def pack_kernel(pk, pv, q, tk, tv, table, parent, kv, sent, local, tail, sems):
+def pack_kernel(q, tk, tv, table, parent, up1, dn1, sent, local, sems):
+    del up1, dn1
     copies = [
-        pltpu.make_async_copy(pk, kv.at[pl.ds(0, LOCAL_PAGES)], sems.at[0]),
-        pltpu.make_async_copy(pv, kv.at[pl.ds(LOCAL_PAGES, LOCAL_PAGES)], sems.at[1]),
-        pltpu.make_async_copy(q, sent.at[pl.ds(0, 2 * QROWS)], sems.at[2]),
-        pltpu.make_async_copy(q, local.at[pl.ds(0, 2 * QROWS)], sems.at[3]),
-        pltpu.make_async_copy(tk, local.at[pl.ds(TK_AT, 128)], sems.at[4]),
-        pltpu.make_async_copy(tv, local.at[pl.ds(TV_AT, 128)], sems.at[5]),
+        pltpu.make_async_copy(q, sent.at[pl.ds(0, 2 * QROWS)], sems.at[0]),
+        pltpu.make_async_copy(q, local.at[pl.ds(0, 2 * QROWS)], sems.at[1]),
+        pltpu.make_async_copy(tk, local.at[pl.ds(TK_AT, 128)], sems.at[2]),
+        pltpu.make_async_copy(tv, local.at[pl.ds(TV_AT, 128)], sems.at[3]),
     ]
     for cp in copies:
         cp.start()
     ids = table[...].astype(F32)
     row = lax.broadcasted_iota(jnp.int32, (16, 128), 0)
-    tail[...] = jnp.where(row == 2, parent[...].astype(F32), 0.0).astype(BF)
+    above = parent[...].astype(F32)
+    tail = pl.ds(2 * QROWS, 16)
+    sent[tail, :] = jnp.zeros((16, 128), BF)
+    local[tail, :] = jnp.where(row == 2, above, 0.0).astype(BF)
     row = row[:, :16]
-    tail[:, :16] = jnp.where(
-        row == 0, ids[0:1, :], jnp.where(row == 1, ids[1:2, :], jnp.where(row == 2, parent[:, :16].astype(F32), 0.0))
-    ).astype(BF)
-    last = [
-        pltpu.make_async_copy(tail, sent.at[pl.ds(2 * QROWS, 16)], sems.at[6]),
-        pltpu.make_async_copy(tail, local.at[pl.ds(2 * QROWS, 16)], sems.at[7]),
-    ]
-    for cp in last:
-        cp.start()
-    for cp in copies + last:
+    pages = jnp.where(row == 0, ids[0:1, :], jnp.where(row == 1, ids[1:2, :], 0.0))
+    sent[tail, :16] = pages.astype(BF)
+    local[tail, :16] = jnp.where(row == 2, above[:, :16], pages).astype(BF)
+    for cp in copies:
         cp.wait()
 
 
-def own_kernel(maps, local, s1, s2, s3, kv, q_out, *refs):
+def own_kernel(maps, local, s1, s2, s3, kv, up2, dn2, q_out, *refs):
+    del up2, dn2
     lists = refs[:3]
     m_out, l_out, a_out, tails, ids, tbl, list_own, found = refs[3:11]
     lists = (list_own,) + lists
@@ -309,7 +306,7 @@
     return pl.pallas_call(
         own_kernel,
         out_shape=[jax.ShapeDtypeStruct((SESS * QROWS, HD), BF)] + lists(3) + state_shapes(SESS),
-        in_specs=[SMEM] + [VMEM] * 5,
+        in_specs=[SMEM] + [VMEM] * 5 + [ANY] * 2,
         out_specs=[VMEM] + [SMEM] * 3 + [VMEM] * 3,
         scratch_shapes=[
             pltpu.VMEM((64, 128), BF),
@@ -369,27 +366,27 @@
     rep = lax.axis_index("rep")
     head = lax.axis_index("head")
     q_own = queries.reshape(2 * QROWS, HD)
-    kv, sent, local = pl.pallas_call(
+    kv = jnp.concatenate([prefix_keys, prefix_values], axis=0).reshape(2 * LOCAL_PAGES, 128, HD)
+    up1 = lax.ppermute(kv, "rep", z_perm(1))
+    dn1 = lax.ppermute(kv, "rep", z_perm(-1))
+    up2 = lax.ppermute(up1, "rep", z_perm(1))
+    dn2 = lax.ppermute(dn1, "rep", z_perm(-1))
+    sent, local = pl.pallas_call(
         pack_kernel,
         out_shape=[
-            jax.ShapeDtypeStruct((2 * LOCAL_PAGES, 128, HD), BF),
             jax.ShapeDtypeStruct((2 * QROWS + 16, HD), BF),
             jax.ShapeDtypeStruct((TV_AT + 128, HD), BF),
         ],
-        in_specs=[ANY] * 5 + [VMEM] * 2,
-        out_specs=[ANY] * 3,
-        scratch_shapes=[pltpu.VMEM((16, 128), BF), pltpu.SemaphoreType.DMA((8,))],
+        in_specs=[ANY] * 3 + [VMEM] * 2 + [ANY] * 2,
+        out_specs=[VMEM] * 2,
+        scratch_shapes=[pltpu.SemaphoreType.DMA((4,))],
         compiler_params=pltpu.CompilerParams(vmem_limit_bytes=59 << 20),
         name="pack",
     )(
-        prefix_keys.reshape(LOCAL_PAGES, 128, HD), prefix_values.reshape(LOCAL_PAGES, 128, HD), q_own,
-        tree_keys.reshape(-1, HD), tree_values.reshape(-1, HD), page_table, tree_parent.reshape(1, -1),
+        q_own, tree_keys.reshape(-1, HD), tree_values.reshape(-1, HD), page_table, tree_parent.reshape(1, -1),
+        up1, dn1,
     )
-    up1 = lax.ppermute(kv, "rep", z_perm(1))
-    dn1 = lax.ppermute(kv, "rep", z_perm(-1))
     sents = [lax.ppermute(sent, "rep", group_perm(r)) for r in (1, 2, 3)]
-    up2 = lax.ppermute(up1, "rep", z_perm(1))
-    dn2 = lax.ppermute(dn1, "rep", z_perm(-1))
     up3 = lax.ppermute(up2, "rep", z_perm(1))
     dn3 = lax.ppermute(dn2, "rep", z_perm(-1))
     up4 = lax.ppermute(up3, "rep", z_perm(1))
@@ -401,7 +398,7 @@
     for k, offsets in enumerate(GROUPS):
         for i, o in enumerate(offsets):
             maps = jnp.where(same & (step == o % Z), k * 65536 + i * 8, maps)
-    q_all, list_1, list_2, list_3, *state = own_call(maps, local, *sents, kv)
+    q_all, list_1, list_2, list_3, *state = own_call(maps, local, *sents, kv, up2, dn2)
     state = near_call(list_1, q_all, (up1, dn1, up2, dn2), state, "near_pages")
     state = near_call(list_2, q_all, (up3, dn3), state, "far_pages")
     own, p1, p2, p3 = far_call(list_3, q_all, (up4,), state)

time: 102 us -> 85.3 us (0.84); the launches traced: 102 us -> 84.1 us
  Pallas kernels: 35.1 us -> 17.9 us
  waiting for transfers between devices: 30.1 us -> 26.8 us
  starting transfers between devices: 31.4 us -> 33.9 us
    pallas_call x1, Pallas kernels: 19.7 us -> 2.42 us  [on_device(): pl.pallas_call(pack_kernel, out_shape=[jax.ShapeDtypeStruct((2 * QROWS +...]
    ppermute x7, waiting for transfers between devices: 10.3 us -> 7.09 us  [on_device(): lax.ppermute(parts[k], 'head', [(i, i ^ k) for i in range(8)])]
    ppermute x1, waiting for transfers between devices: 3.02 us -> 0.01 us  [on_device(): dn3 = lax.ppermute(dn2, 'rep', z_perm(-1))]
    ppermute x1, waiting for transfers between devices: 0.07 us -> 2.64 us  [on_device(): up4 = lax.ppermute(up3, 'rep', z_perm(1))]
    ppermute x7, starting transfers between devices: 11.9 us -> 14 us  [on_device(): lax.ppermute(parts[k], 'head', [(i, i ^ k) for i in range(8)])]
    ppermute x1, waiting for transfers between devices: 2.1 us -> 0.01 us  [on_device(): up2 = lax.ppermute(up1, 'rep', z_perm(1))]
    ppermute x3, waiting for transfers between devices: 1.49 us -> 3.41 us  [on_device(): sents = [lax.ppermute(sent, 'rep', group_perm(r)) for r in (1, 2, 3)]]
  transfers between devices with their start and end apart: 20 -> 20, of which waited for: 9 -> 9; matrix products, arithmetic and copies ran while one was open for 0% -> 0% of each run, Pallas kernels for 12% -> 18%
where the time goes in v1:
time: 85.3 us; the launch traced here: 84.1 us
  starting transfers between devices  33.9 us (40%)
  waiting for transfers between devices  26.8 us (31%)
  Pallas kernels  17.9 us (21%)
  matrix products  3.34 us (4%)
  local copies, waits for them, and re-layouts  1.02 us (1%)
  other arithmetic  1.01 us (1%)
    ppermute x7, starting transfers between devices, on_device(): lax.ppermute(parts[k], 'head', [(i, i ^ k) for i in range(8)])  14 us
    pallas_call x2, Pallas kernels, near_call(): pl.pallas_call(functools.partial(near_kernel, nb), out_shape=state_shapes...  7.38 us
    ppermute x3, waiting for transfers between devices, on_device(): lax.ppermute(p, 'rep', group_perm(r))  7.34 us
    ppermute x7, waiting for transfers between devices, on_device(): lax.ppermute(parts[k], 'head', [(i, i ^ k) for i in range(8)])  7.09 us
    ppermute x1, waiting for transfers between devices, on_device(): up1 = lax.ppermute(kv, 'rep', z_perm(1))  6.32 us
    pallas_call x1, Pallas kernels, own_call(): pl.pallas_call(own_kernel, out_shape=[jax.ShapeDtypeStruct((SESS * QROWS,...  5.41 us
    ppermute x1, starting transfers between devices, on_device(): dn1 = lax.ppermute(kv, 'rep', z_perm(-1))  4.03 us
    ppermute x3, starting transfers between devices, on_device(): lax.ppermute(p, 'rep', group_perm(r))  3.81 us
  transfers between devices with their start and end apart: 20, of which 9 were waited for; matrix products, arithmetic and copies ran while one was open for 0% of the time, Pallas kernels for 18%

profile of v1, /device:TPU:2, one launch (start us, length us, event | category | flops | bytes accessed | tf_op | source)
XLA Modules:
  0.0 84.1 jit_solution(792792420651633286)
XLA Ops:
  1.0 2.0 %collective-permute-start = (bf16[8,128,128]{2,1,0:T(8,128)(2,1)S(1)}, bf16[8,128,128]{2,1,0:T(8,128)(2,1)}, u32[]{:S(2)}, u32[]{:S(2)}) collective-permute-start(bf16[8,128,128]{2,1,0:T(8,128)(2,1)S(1)} %maximum_bitcast_fusion.kv), channel_id=1, source_target_pairs={{0,16},{8,24},{16,32},{24,40},{32,48},{40,56},{48,64},{56,72},{64,... | collective-permute-start | bytes 786440 | tf_op jit(solution)/shard_map/ppermute | solution.py:370
  3.0 4.0 %collective-permute-start.1 = (bf16[8,128,128]{2,1,0:T(8,128)(2,1)S(1)}, bf16[8,128,128]{2,1,0:T(8,128)(2,1)}, u32[]{:S(2)}, u32[]{:S(2)}) collective-permute-start(bf16[8,128,128]{2,1,0:T(8,128)(2,1)S(1)} %maximum_bitcast_fusion.kv), channel_id=1, source_target_pairs={{0,112},{8,120},{16,0},{24,8},{32,16},{40,24},{48,32},{56,40},{64,... | collective-permute-start | bytes 786440 | tf_op jit(solution)/shard_map/ppermute | solution.py:371
  7.0 6.3 %collective-permute-done.up1.refs_2_ = bf16[8,128,128]{2,1,0:T(8,128)(2,1)} collective-permute-done((bf16[8,128,128]{2,1,0:T(8,128)(2,1)S(1)}, bf16[8,128,128]{2,1,0:T(8,128)(2,1)}, u32[]{:S(2)}, u32[]{:S(2)}) %collective-permute-start) | collective-permute-done | bytes 262176 | tf_op jit(solution)/shard_map/ppermute | solution.py:370
  13.3 3.2 %collective-permute-start.6 = (bf16[8,128,128]{2,1,0:T(8,128)(2,1)}, bf16[8,128,128]{2,1,0:T(8,128)(2,1)S(1)}, u32[]{:S(2)}, u32[]{:S(2)}) collective-permute-start(bf16[8,128,128]{2,1,0:T(8,128)(2,1)} %collective-permute-done.1.dn1.refs_3_), channel_id=1, source_target_pairs={{0,112},{8,120},{16,0},{24,8},{32,16},{40,24},{48,32},{56,40},{64,... | collective-permute-start | bytes 786440 | tf_op jit(solution)/shard_map/ppermute | solution.py:373
  16.6 2.4 %pack.1 = (bf16[528,128]{1,0:T(8,128)(2,1)}, bf16[784,128]{1,0:T(8,128)(2,1)}) custom-call(bf16[512,128]{1,0:T(8,128)(2,1)} %bitcast.11, bf16[128,128]{1,0:T(8,128)(2,1)} %bitcast.14, bf16[128,128]{1,0:T(8,128)(2,1)} %bitcast.15, s32[2,16]{1,0:T(2,128)} %table.1, s32[1,128]{1,0:T(1,128)} %bitcast.16, bf16[8,128,128]{2,1,0:T(8,128)(2,1)} %collective-permute-done.up1.refs_2_, ...), custom_call_target="tpu_custom_call" | custom-call | tf_op jit(solution)/shard_map/pack/pallas_call | solution.py:374
  19.1 2.2 %collective-permute-start.3 = (bf16[528,128]{1,0:T(8,128)(2,1)}, bf16[528,128]{1,0:T(8,128)(2,1)S(1)}, u32[]{:S(2)}, u32[]{:S(2)}) collective-permute-start(bf16[528,128]{1,0:T(8,128)(2,1)} %get-tuple-element.25), channel_id=1, source_target_pairs={{0,128},{8,136},{16,144},{24,152},{32,160},{40,168},{48,176},{56,1... | collective-permute-start | bytes 405512 | tf_op jit(solution)/shard_map/ppermute | solution.py:389
  22.5 3.3 %collective-permute-start.9 = (bf16[8,128,128]{2,1,0:T(8,128)(2,1)S(1)}, bf16[8,128,128]{2,1,0:T(8,128)(2,1)S(1)}, u32[]{:S(2)}, u32[]{:S(2)}) collective-permute-start(bf16[8,128,128]{2,1,0:T(8,128)(2,1)S(1)} %collective-permute-done.6.dn2.refs_5_), channel_id=1, source_target_pairs={{0,112},{8,120},{16,0},{24,8},{32,16},{40,24},{48,32},{56,40},{64,... | collective-permute-start | bytes 786440 | tf_op jit(solution)/shard_map/ppermute | solution.py:391
  27.3 1.9 %collective-permute-done.4.s3 = bf16[528,128]{1,0:T(8,128)(2,1)S(1)} collective-permute-done((bf16[528,128]{1,0:T(8,128)(2,1)}, bf16[528,128]{1,0:T(8,128)(2,1)S(1)}, u32[]{:S(2)}, u32[]{:S(2)}) %collective-permute-start.4) | collective-permute-done | bytes 135200 | tf_op jit(solution)/shard_map/ppermute | solution.py:389
  30.2 5.4 %own_pages.1 = (bf16[2048,128]{1,0:T(8,128)(2,1)S(1)}, s32[160]{0:T(256)S(1)}, s32[160]{0:T(256)S(1)}, s32[160]{0:T(256)S(1)}, f32[8,1,256]{2,1,0:T(1,128)S(1)},...) custom-call(s32[32]{0:T(128)S(1)} %and_select_fusion.7.maps, bf16[784,128]{1,0:T(8,128)(2,1)S(1)} %copy-done, ...), custom_call_target="tpu_custom_call" | custom-call | flops 2000000000 | bytes 4194304 | tf_op jit(solution)/shard_map/own_pages/pallas_call | solution.py:306
  35.7 4.5 %near_pages.1 = (f32[8,1,256]{2,1,0:T(1,128)S(1)}, f32[8,1,256]{2,1,0:T(1,128)S(1)}, f32[8,128,256]{2,1,0:T(8,128)S(1)}) custom-call(s32[160]{0:T(256)S(1)} %get-tuple-element.29.refs_0_, bf16[2048,128]{1,0:T(8,128)(2,1)S(1)} %get-tuple-element.27.refs_1_, bf16[8,128,128]{2,1,0:T(8,128)(2,1)} %collective-permute-done.up1.refs_2_, ...), custom_call_target="tpu_custom_call" | custom-call | flops 4000000000 | bytes 4194304 | tf_op jit(solution)/shard_map/near_pages/pallas_call | solution.py:336
  40.3 2.8 %far_pages.1 = (f32[8,1,256]{2,1,0:T(1,128)S(1)}, f32[8,1,256]{2,1,0:T(1,128)S(1)}, f32[8,128,256]{2,1,0:T(8,128)S(1)}) custom-call(s32[160]{0:T(256)S(1)} %get-tuple-element.28.refs_0_, bf16[2048,128]{1,0:T(8,128)(2,1)S(1)} %get-tuple-element.27.refs_1_, bf16[8,128,128]{2,1,0:T(8,128)(2,1)S(1)} %collective-permute-done.7.refs_2_, ...), custom_call_target="tpu_custom_call" | custom-call | flops 2000000000 | bytes 4194304 | tf_op jit(solution)/shard_map/far_pages/pallas_call | solution.py:336
  43.1 2.6 %collective-permute-done.8.refs_2_ = bf16[8,128,128]{2,1,0:T(8,128)(2,1)S(1)} collective-permute-done((bf16[8,128,128]{2,1,0:T(8,128)(2,1)S(1)}, bf16[8,128,128]{2,1,0:T(8,128)(2,1)S(1)}, u32[]{:S(2)}, u32[]{:S(2)}) %collective-permute-start.8) | collective-permute-done | bytes 262176 | tf_op jit(solution)/shard_map/ppermute | solution.py:392
  45.7 1.6 %last_pages.1 = (f32[136,512]{1,0:T(8,128)S(1)}, bf16[144,512]{1,0:T(8,128)(2,1)S(1)}, bf16[144,512]{1,0:T(8,128)(2,1)S(1)}, bf16[144,512]{1,0:T(8,128)(2,1)S(1)}) custom-call(s32[160]{0:T(256)S(1)} %get-tuple-element.26.refs_0_, bf16[2048,128]{1,0:T(8,128)(2,1)S(1)} %get-tuple-element.27.refs_1_, bf16[8,128,128]{2,1,0:T(8,128)(2,1)S(1)} %collective-permute-done.8.refs_2_, ...), custom_call_target="tpu_custom_call" | custom-call | flops 1000000000 | bytes 4194304 | tf_op jit(solution)/shard_map/last_pages/pallas_call | solution.py:350
  48.2 2.6 %collective-permute-start.11 = (bf16[144,512]{1,0:T(8,128)(2,1)S(1)}, bf16[144,512]{1,0:T(8,128)(2,1)S(1)}, u32[]{:S(2)}, u32[]{:S(2)}) collective-permute-start(bf16[144,512]{1,0:T(8,128)(2,1)S(1)} %get-tuple-element.41), channel_id=1, source_target_pairs={{0,128},{8,136},{16,144},{24,152},{32,160},{40,168},{48,176},{56,1... | collective-permute-start | bytes 442376 | tf_op jit(solution)/shard_map/ppermute | solution.py:405
  51.2 4.6 %collective-permute-done.11.p2 = bf16[144,512]{1,0:T(8,128)(2,1)S(1)} collective-permute-done((bf16[144,512]{1,0:T(8,128)(2,1)S(1)}, bf16[144,512]{1,0:T(8,128)(2,1)S(1)}, u32[]{:S(2)}, u32[]{:S(2)}) %collective-permute-start.11) | collective-permute-done | bytes 147488 | tf_op jit(solution)/shard_map/ppermute | solution.py:405
  55.8 2.7 %collective-permute-done.12.p3 = bf16[144,512]{1,0:T(8,128)(2,1)S(1)} collective-permute-done((bf16[144,512]{1,0:T(8,128)(2,1)S(1)}, bf16[144,512]{1,0:T(8,128)(2,1)S(1)}, u32[]{:S(2)}, u32[]{:S(2)}) %collective-permute-start.12) | collective-permute-done | bytes 147488 | tf_op jit(solution)/shard_map/ppermute | solution.py:405
  58.7 3.3 %convolution_convert_fusion = bf16[128,5120]{1,0:T(8,128)(2,1)S(1)} fusion(bf16[128,512]{1,0:T(8,128)(2,1)S(1)} %combine.1, bf16[512,5120]{1,0:T(8,128)(2,1)} %param.15), kind=kOutput, calls=%fused_computation | convolution fusion | flops 671744000 | bytes 6684672 | tf_op jit(solution)/shard_map/dot_general | solution.py:417
  62.2 1.7 %collective-permute-start.13 = (bf16[16,5120]{1,0:T(8,128)(2,1)S(1)}, bf16[16,5120]{1,0:T(8,128)(2,1)S(1)}, u32[]{:S(2)}, u32[]{:S(2)}) collective-permute-start(bf16[16,5120]{1,0:T(8,128)(2,1)S(1)} %get-tuple-element.49), channel_id=1, source_target_pairs={{0,1},{1,0},{2,3},{3,2},{4,5},{5,4},{6,7},{7,6},{8,9},{9,8},{10,11... | collective-permute-start | bytes 491528 | tf_op jit(solution)/shard_map/ppermute | solution.py:419
  63.9 2.2 %collective-permute-start.14 = (bf16[16,5120]{1,0:T(8,128)(2,1)S(1)}, bf16[16,5120]{1,0:T(8,128)(2,1)S(1)}, u32[]{:S(2)}, u32[]{:S(2)}) collective-permute-start(bf16[16,5120]{1,0:T(8,128)(2,1)S(1)} %get-tuple-element.48), channel_id=1, source_target_pairs={{0,3},{1,2},{2,1},{3,0},{4,7},{5,6},{6,5},{7,4},{8,11},{9,10},{10,... | collective-permute-start | bytes 491528 | tf_op jit(solution)/shard_map/ppermute | solution.py:419
  69.4 3.7 %collective-permute-start.18 = (bf16[16,5120]{1,0:T(8,128)(2,1)S(1)}, bf16[16,5120]{1,0:T(8,128)(2,1)S(1)}, u32[]{:S(2)}, u32[]{:S(2)}) collective-permute-start(bf16[16,5120]{1,0:T(8,128)(2,1)S(1)} %get-tuple-element.44), channel_id=1, source_target_pairs={{0,7},{1,6},{2,5},{3,4},{4,3},{5,2},{6,1},{7,0},{8,15},{9,14},{10,... | collective-permute-start | bytes 491528 | tf_op jit(solution)/shard_map/ppermute | solution.py:419
  73.1 3.1 %collective-permute-start.19 = (bf16[16,5120]{1,0:T(8,128)(2,1)S(1)}, bf16[16,5120]{1,0:T(8,128)(2,1)S(1)}, u32[]{:S(2)}, u32[]{:S(2)}) collective-permute-start(bf16[16,5120]{1,0:T(8,128)(2,1)S(1)} %get-tuple-element.43), channel_id=1, source_target_pairs={{0,6},{1,7},{2,4},{3,5},{4,2},{5,3},{6,0},{7,1},{8,14},{9,15},{10,... | collective-permute-start | bytes 491528 | tf_op jit(solution)/shard_map/ppermute | solution.py:419
  76.2 1.6 %collective-permute-done.16.refs_4_ = bf16[16,5120]{1,0:T(8,128)(2,1)S(1)} collective-permute-done((bf16[16,5120]{1,0:T(8,128)(2,1)S(1)}, bf16[16,5120]{1,0:T(8,128)(2,1)S(1)}, u32[]{:S(2)}, u32[]{:S(2)}) %collective-permute-start.16) | collective-permute-done | bytes 163872 | tf_op jit(solution)/shard_map/ppermute | solution.py:419
  77.8 3.2 %collective-permute-done.18.refs_6_ = bf16[16,5120]{1,0:T(8,128)(2,1)S(1)} collective-permute-done((bf16[16,5120]{1,0:T(8,128)(2,1)S(1)}, bf16[16,5120]{1,0:T(8,128)(2,1)S(1)}, u32[]{:S(2)}, u32[]{:S(2)}) %collective-permute-start.18) | collective-permute-done | bytes 163872 | tf_op jit(solution)/shard_map/ppermute | solution.py:419
  81.1 2.2 %collective-permute-done.19.refs_7_ = bf16[16,5120]{1,0:T(8,128)(2,1)S(1)} collective-permute-done((bf16[16,5120]{1,0:T(8,128)(2,1)S(1)}, bf16[16,5120]{1,0:T(8,128)(2,1)S(1)}, u32[]{:S(2)}, u32[]{:S(2)}) %collective-permute-start.19) | collective-permute-done | bytes 163872 | tf_op jit(solution)/shard_map/ppermute | solution.py:419
  (29 shorter events, 10.5 us)
Async XLA Ops:
  1.0 12.3 %collective-permute-start = (bf16[8,128,128]{2,1,0:T(8,128)(2,1)S(1)}, bf16[8,128,128]{2,1,0:T(8,128)(2,1)}, u32[]{:S(2)}, u32[]{:S(2)}) collective-permute-start(bf16[8,128,128]{2,1,0:T(8,128)(2,1)S(1)} %maximum_bitcast_fusion.kv), channel_id=1, source_target_pairs={{0,16},{8,24},{16,32},{24,40},{32,48},{40,56},{48,64},{56,72},{64,... | collective-permute-start | bytes 786440 | tf_op jit(solution)/shard_map/ppermute | solution.py:370
  3.0 10.4 %collective-permute-start.1 = (bf16[8,128,128]{2,1,0:T(8,128)(2,1)S(1)}, bf16[8,128,128]{2,1,0:T(8,128)(2,1)}, u32[]{:S(2)}, u32[]{:S(2)}) collective-permute-start(bf16[8,128,128]{2,1,0:T(8,128)(2,1)S(1)} %maximum_bitcast_fusion.kv), channel_id=1, source_target_pairs={{0,112},{8,120},{16,0},{24,8},{32,16},{40,24},{48,32},{56,40},{64,... | collective-permute-start | bytes 786440 | tf_op jit(solution)/shard_map/ppermute | solution.py:371
  13.3 9.1 %collective-permute-start.5 = (bf16[8,128,128]{2,1,0:T(8,128)(2,1)}, bf16[8,128,128]{2,1,0:T(8,128)(2,1)S(1)}, u32[]{:S(2)}, u32[]{:S(2)}) collective-permute-start(bf16[8,128,128]{2,1,0:T(8,128)(2,1)} %collective-permute-done.up1.refs_2_), channel_id=1, source_target_pairs={{0,16},{8,24},{16,32},{24,40},{32,48},{40,56},{48,64},{56,72},{64,... | collective-permute-start | bytes 786440 | tf_op jit(solution)/shard_map/ppermute | solution.py:372
  13.3 9.2 %collective-permute-start.6 = (bf16[8,128,128]{2,1,0:T(8,128)(2,1)}, bf16[8,128,128]{2,1,0:T(8,128)(2,1)S(1)}, u32[]{:S(2)}, u32[]{:S(2)}) collective-permute-start(bf16[8,128,128]{2,1,0:T(8,128)(2,1)} %collective-permute-done.1.dn1.refs_3_), channel_id=1, source_target_pairs={{0,112},{8,120},{16,0},{24,8},{32,16},{40,24},{48,32},{56,40},{64,... | collective-permute-start | bytes 786440 | tf_op jit(solution)/shard_map/ppermute | solution.py:373
  19.0 6.8 %collective-permute-start.2 = (bf16[528,128]{1,0:T(8,128)(2,1)}, bf16[528,128]{1,0:T(8,128)(2,1)S(1)}, u32[]{:S(2)}, u32[]{:S(2)}) collective-permute-start(bf16[528,128]{1,0:T(8,128)(2,1)} %get-tuple-element.25), channel_id=1, source_target_pairs={{0,8},{8,0},{16,24},{24,16},{32,40},{40,32},{48,56},{56,48},{64,72... | collective-permute-start | bytes 405512 | tf_op jit(solution)/shard_map/ppermute | solution.py:389
  19.1 8.2 %collective-permute-start.3 = (bf16[528,128]{1,0:T(8,128)(2,1)}, bf16[528,128]{1,0:T(8,128)(2,1)S(1)}, u32[]{:S(2)}, u32[]{:S(2)}) collective-permute-start(bf16[528,128]{1,0:T(8,128)(2,1)} %get-tuple-element.25), channel_id=1, source_target_pairs={{0,128},{8,136},{16,144},{24,152},{32,160},{40,168},{48,176},{56,1... | collective-permute-start | bytes 405512 | tf_op jit(solution)/shard_map/ppermute | solution.py:389
  21.3 7.9 %collective-permute-start.4 = (bf16[528,128]{1,0:T(8,128)(2,1)}, bf16[528,128]{1,0:T(8,128)(2,1)S(1)}, u32[]{:S(2)}, u32[]{:S(2)}) collective-permute-start(bf16[528,128]{1,0:T(8,128)(2,1)} %get-tuple-element.25), channel_id=1, source_target_pairs={{0,136},{8,128},{16,152},{24,144},{32,168},{40,160},{48,184},{56,1... | collective-permute-start | bytes 405512 | tf_op jit(solution)/shard_map/ppermute | solution.py:389
  22.5 13.1 %collective-permute-start.7 = (bf16[8,128,128]{2,1,0:T(8,128)(2,1)S(1)}, bf16[8,128,128]{2,1,0:T(8,128)(2,1)S(1)}, u32[]{:S(2)}, u32[]{:S(2)}) collective-permute-start(bf16[8,128,128]{2,1,0:T(8,128)(2,1)S(1)} %collective-permute-done.5.up2.refs_4_), channel_id=1, source_target_pairs={{0,16},{8,24},{16,32},{24,40},{32,48},{40,56},{48,64},{56,72},{64,... | collective-permute-start | bytes 786440 | tf_op jit(solution)/shard_map/ppermute | solution.py:390
  22.5 17.7 %collective-permute-start.9 = (bf16[8,128,128]{2,1,0:T(8,128)(2,1)S(1)}, bf16[8,128,128]{2,1,0:T(8,128)(2,1)S(1)}, u32[]{:S(2)}, u32[]{:S(2)}) collective-permute-start(bf16[8,128,128]{2,1,0:T(8,128)(2,1)S(1)} %collective-permute-done.6.dn2.refs_5_), channel_id=1, source_target_pairs={{0,112},{8,120},{16,0},{24,8},{32,16},{40,24},{48,32},{56,40},{64,... | collective-permute-start | bytes 786440 | tf_op jit(solution)/shard_map/ppermute | solution.py:391
  29.3 0.9 %copy-start = (bf16[784,128]{1,0:T(8,128)(2,1)S(1)}, bf16[784,128]{1,0:T(8,128)(2,1)}, u32[]{:S(2)}) copy-start(bf16[784,128]{1,0:T(8,128)(2,1)} %get-tuple-element.24.local) | copy-start | bytes 602116
  35.6 10.1 %collective-permute-start.8 = (bf16[8,128,128]{2,1,0:T(8,128)(2,1)S(1)}, bf16[8,128,128]{2,1,0:T(8,128)(2,1)S(1)}, u32[]{:S(2)}, u32[]{:S(2)}) collective-permute-start(bf16[8,128,128]{2,1,0:T(8,128)(2,1)S(1)} %collective-permute-done.7.refs_2_), channel_id=1, source_target_pairs={{0,16},{8,24},{16,32},{24,40},{32,48},{40,56},{48,64},{56,72},{64,... | collective-permute-start | bytes 786440 | tf_op jit(solution)/shard_map/ppermute | solution.py:392
  47.4 3.8 %collective-permute-start.10 = (bf16[144,512]{1,0:T(8,128)(2,1)S(1)}, bf16[144,512]{1,0:T(8,128)(2,1)S(1)}, u32[]{:S(2)}, u32[]{:S(2)}) collective-permute-start(bf16[144,512]{1,0:T(8,128)(2,1)S(1)} %get-tuple-element.40), channel_id=1, source_target_pairs={{0,8},{8,0},{16,24},{24,16},{32,40},{40,32},{48,56},{56,48},{64,72... | collective-permute-start | bytes 442376 | tf_op jit(solution)/shard_map/ppermute | solution.py:405
  48.2 7.6 %collective-permute-start.11 = (bf16[144,512]{1,0:T(8,128)(2,1)S(1)}, bf16[144,512]{1,0:T(8,128)(2,1)S(1)}, u32[]{:S(2)}, u32[]{:S(2)}) collective-permute-start(bf16[144,512]{1,0:T(8,128)(2,1)S(1)} %get-tuple-element.41), channel_id=1, source_target_pairs={{0,128},{8,136},{16,144},{24,152},{32,160},{40,168},{48,176},{56,1... | collective-permute-start | bytes 442376 | tf_op jit(solution)/shard_map/ppermute | solution.py:405
  50.8 7.7 %collective-permute-start.12 = (bf16[144,512]{1,0:T(8,128)(2,1)S(1)}, bf16[144,512]{1,0:T(8,128)(2,1)S(1)}, u32[]{:S(2)}, u32[]{:S(2)}) collective-permute-start(bf16[144,512]{1,0:T(8,128)(2,1)S(1)} %get-tuple-element.42), channel_id=1, source_target_pairs={{0,136},{8,128},{16,152},{24,144},{32,168},{40,160},{48,184},{56,1... | collective-permute-start | bytes 442376 | tf_op jit(solution)/shard_map/ppermute | solution.py:405
  62.2 7.2 %collective-permute-start.13 = (bf16[16,5120]{1,0:T(8,128)(2,1)S(1)}, bf16[16,5120]{1,0:T(8,128)(2,1)S(1)}, u32[]{:S(2)}, u32[]{:S(2)}) collective-permute-start(bf16[16,5120]{1,0:T(8,128)(2,1)S(1)} %get-tuple-element.49), channel_id=1, source_target_pairs={{0,1},{1,0},{2,3},{3,2},{4,5},{5,4},{6,7},{7,6},{8,9},{9,8},{10,11... | collective-permute-start | bytes 491528 | tf_op jit(solution)/shard_map/ppermute | solution.py:419
  63.9 9.3 %collective-permute-start.14 = (bf16[16,5120]{1,0:T(8,128)(2,1)S(1)}, bf16[16,5120]{1,0:T(8,128)(2,1)S(1)}, u32[]{:S(2)}, u32[]{:S(2)}) collective-permute-start(bf16[16,5120]{1,0:T(8,128)(2,1)S(1)} %get-tuple-element.48), channel_id=1, source_target_pairs={{0,3},{1,2},{2,1},{3,0},{4,7},{5,6},{6,5},{7,4},{8,11},{9,10},{10,... | collective-permute-start | bytes 491528 | tf_op jit(solution)/shard_map/ppermute | solution.py:419
  66.0 10.1 %collective-permute-start.15 = (bf16[16,5120]{1,0:T(8,128)(2,1)S(1)}, bf16[16,5120]{1,0:T(8,128)(2,1)S(1)}, u32[]{:S(2)}, u32[]{:S(2)}) collective-permute-start(bf16[16,5120]{1,0:T(8,128)(2,1)S(1)} %get-tuple-element.47), channel_id=1, source_target_pairs={{0,4},{1,5},{2,6},{3,7},{4,0},{5,1},{6,2},{7,3},{8,12},{9,13},{10,... | collective-permute-start | bytes 491528 | tf_op jit(solution)/shard_map/ppermute | solution.py:419
  67.4 10.4 %collective-permute-start.16 = (bf16[16,5120]{1,0:T(8,128)(2,1)S(1)}, bf16[16,5120]{1,0:T(8,128)(2,1)S(1)}, u32[]{:S(2)}, u32[]{:S(2)}) collective-permute-start(bf16[16,5120]{1,0:T(8,128)(2,1)S(1)} %get-tuple-element.46), channel_id=1, source_target_pairs={{0,2},{1,3},{2,0},{3,1},{4,6},{5,7},{6,4},{7,5},{8,10},{9,11},{10,... | collective-permute-start | bytes 491528 | tf_op jit(solution)/shard_map/ppermute | solution.py:419
  68.1 9.7 %collective-permute-start.17 = (bf16[16,5120]{1,0:T(8,128)(2,1)S(1)}, bf16[16,5120]{1,0:T(8,128)(2,1)S(1)}, u32[]{:S(2)}, u32[]{:S(2)}) collective-permute-start(bf16[16,5120]{1,0:T(8,128)(2,1)S(1)} %get-tuple-element.45), channel_id=1, source_target_pairs={{0,5},{1,4},{2,7},{3,6},{4,1},{5,0},{6,3},{7,2},{8,13},{9,12},{10,... | collective-permute-start | bytes 491528 | tf_op jit(solution)/shard_map/ppermute | solution.py:419
  69.4 11.6 %collective-permute-start.18 = (bf16[16,5120]{1,0:T(8,128)(2,1)S(1)}, bf16[16,5120]{1,0:T(8,128)(2,1)S(1)}, u32[]{:S(2)}, u32[]{:S(2)}) collective-permute-start(bf16[16,5120]{1,0:T(8,128)(2,1)S(1)} %get-tuple-element.44), channel_id=1, source_target_pairs={{0,7},{1,6},{2,5},{3,4},{4,3},{5,2},{6,1},{7,0},{8,15},{9,14},{10,... | collective-permute-start | bytes 491528 | tf_op jit(solution)/shard_map/ppermute | solution.py:419
  73.1 10.2 %collective-permute-start.19 = (bf16[16,5120]{1,0:T(8,128)(2,1)S(1)}, bf16[16,5120]{1,0:T(8,128)(2,1)S(1)}, u32[]{:S(2)}, u32[]{:S(2)}) collective-permute-start(bf16[16,5120]{1,0:T(8,128)(2,1)S(1)} %get-tuple-element.43), channel_id=1, source_target_pairs={{0,6},{1,7},{2,4},{3,5},{4,2},{5,3},{6,0},{7,1},{8,14},{9,15},{10,... | collective-permute-start | bytes 491528 | tf_op jit(solution)/shard_map/ppermute | solution.py:419

commit v2 on v1

--- a/solution.py
+++ b/solution.py
@@ -14,6 +14,7 @@
 LOCAL_PAGES = 4
 TK_AT = 528
 TV_AT = 656
+PAGES_AT = 784
 TREE = 64
 QROWS = 256
 HD = 128
@@ -38,10 +39,10 @@
     return [(rep_of(a, z, c), rep_of(a ^ (r >> 1), z, c ^ (r & 1))) for a in range(2) for z in range(Z) for c in range(2)]
 
 
-def pair_steps(entries, q_ref, kv, streams):
+def pair_steps(entries, q_ref, page, streams):
     at = [(e >> 8, e & 255) for e in entries]
     scores = [
-        lax.dot_general(kv[k], q_ref[pl.ds(pl.multiple_of((s & (SESS - 1)) * QROWS, QROWS), QROWS), :], (((1,), (1,)), ((), ())), preferred_element_type=F32)
+        lax.dot_general(page(k), q_ref[pl.ds(pl.multiple_of((s & (SESS - 1)) * QROWS, QROWS), QROWS), :], (((1,), (1,)), ((), ())), preferred_element_type=F32)
         for s, k in at
     ]
     olds = [m[s] for (s, _), (m, _, _) in zip(at, streams)]
@@ -50,7 +51,7 @@
     fixes = [jnp.exp2((o - n) * C2) for o, n in zip(olds, news)]
     parts = [
         lax.dot_general(
-            kv[k + LOCAL_PAGES], p.astype(BF), (((0,), (0,)), ((), ())), preferred_element_type=F32
+            page(k + LOCAL_PAGES), p.astype(BF), (((0,), (0,)), ((), ())), preferred_element_type=F32
         )
         for (_, k), p in zip(at, probs)
     ]
@@ -60,12 +61,12 @@
         a_ref[s] = a_ref[s] * fix + part
 
 
-def all_pairs(entries, q_ref, kv, streams):
+def all_pairs(entries, q_ref, page, streams):
     ns = len(streams)
 
     @pl.loop(0, (entries[0] + ns - 1) >> (ns.bit_length() - 1))
     def _(i):
-        pair_steps([entries[ns * i + r + 1] for r in range(ns)], q_ref, kv, streams)
+        pair_steps([entries[ns * i + r + 1] for r in range(ns)], q_ref, page, streams)
 
 
 def streams_of(refs):
@@ -87,13 +88,15 @@
     return top, total, acc
 
 
-def pack_kernel(q, tk, tv, table, parent, up1, dn1, sent, local, sems):
-    del up1, dn1
+def pack_kernel(q, tk, tv, pk, pv, table, parent, kv, sent, local, sems):
+    del kv
     copies = [
         pltpu.make_async_copy(q, sent.at[pl.ds(0, 2 * QROWS)], sems.at[0]),
         pltpu.make_async_copy(q, local.at[pl.ds(0, 2 * QROWS)], sems.at[1]),
         pltpu.make_async_copy(tk, local.at[pl.ds(TK_AT, 128)], sems.at[2]),
         pltpu.make_async_copy(tv, local.at[pl.ds(TV_AT, 128)], sems.at[3]),
+        pltpu.make_async_copy(pk, local.at[pl.ds(PAGES_AT, LOCAL_PAGES * 128)], sems.at[4]),
+        pltpu.make_async_copy(pv, local.at[pl.ds(PAGES_AT + LOCAL_PAGES * 128, LOCAL_PAGES * 128)], sems.at[5]),
     ]
     for cp in copies:
         cp.start()
@@ -111,8 +114,8 @@
         cp.wait()
 
 
-def own_kernel(maps, local, s1, s2, s3, kv, up2, dn2, q_out, *refs):
-    del up2, dn2
+def own_kernel(maps, local, s1, s2, s3, up1, dn1, q_out, *refs):
+    del up1, dn1
     lists = refs[:3]
     m_out, l_out, a_out, tails, ids, tbl, list_own, found = refs[3:11]
     lists = (list_own,) + lists
@@ -186,7 +189,9 @@
         lists[k][0] = counts[k]
         for r in range(STREAMS - 1):
             lists[k][counts[k] + 1 + r] = jnp.int32(SESS * 256)
-    all_pairs(list_own, q_out, kv, streams)
+    all_pairs(
+        list_own, q_out, lambda i: local[pl.ds(pl.multiple_of(PAGES_AT + i * 128, 16), 128), :], streams
+    )
     for s in range(SESS):
         top, total, acc = merge([(m[s], l[s], a[s]) for m, l, a in streams])
         m_out[s] = top
@@ -211,7 +216,7 @@
     clear(streams)
     for cp in copies:
         cp.wait()
-    all_pairs(list_near, q_ref, kv, streams)
+    all_pairs(list_near, q_ref, lambda i: kv[i], streams)
     for s in range(SESS):
         top, total, acc = merge([(m[s], l[s], a[s]) for m, l, a in [before] + streams])
         m_out[s] = top
@@ -231,7 +236,7 @@
     clear(streams)
     for cp in copies:
         cp.wait()
-    all_pairs(list_far, q_ref, kv, streams)
+    all_pairs(list_far, q_ref, lambda i: kv[i], streams)
     for s in range(SESS):
         top, total, acc = merge([(m[s], l[s], a[s]) for m, l, a in [before] + streams])
         some = total > 0.0
@@ -306,7 +311,7 @@
     return pl.pallas_call(
         own_kernel,
         out_shape=[jax.ShapeDtypeStruct((SESS * QROWS, HD), BF)] + lists(3) + state_shapes(SESS),
-        in_specs=[SMEM] + [VMEM] * 5 + [ANY] * 2,
+        in_specs=[SMEM] + [VMEM] * 4 + [ANY] * 2,
         out_specs=[VMEM] + [SMEM] * 3 + [VMEM] * 3,
         scratch_shapes=[
             pltpu.VMEM((64, 128), BF),
@@ -375,21 +380,25 @@
         pack_kernel,
         out_shape=[
             jax.ShapeDtypeStruct((2 * QROWS + 16, HD), BF),
-            jax.ShapeDtypeStruct((TV_AT + 128, HD), BF),
+            jax.ShapeDtypeStruct((PAGES_AT + 2 * LOCAL_PAGES * 128, HD), BF),
         ],
-        in_specs=[ANY] * 3 + [VMEM] * 2 + [ANY] * 2,
+        in_specs=[ANY] * 5 + [VMEM] * 2 + [ANY],
         out_specs=[VMEM] * 2,
-        scratch_shapes=[pltpu.SemaphoreType.DMA((4,))],
+        scratch_shapes=[pltpu.SemaphoreType.DMA((6,))],
         compiler_params=pltpu.CompilerParams(vmem_limit_bytes=59 << 20),
         name="pack",
     )(
-        q_own, tree_keys.reshape(-1, HD), tree_values.reshape(-1, HD), page_table, tree_parent.reshape(1, -1),
-        up1, dn1,
+        q_own, tree_keys.reshape(-1, HD), tree_values.reshape(-1, HD),
+        prefix_keys.reshape(-1, HD), prefix_values.reshape(-1, HD), page_table, tree_parent.reshape(1, -1),
+        kv,
     )
     sents = [lax.ppermute(sent, "rep", group_perm(r)) for r in (1, 2, 3)]
     up3 = lax.ppermute(up2, "rep", z_perm(1))
     dn3 = lax.ppermute(dn2, "rep", z_perm(-1))
-    up4 = lax.ppermute(up3, "rep", z_perm(1))
+    held = jnp.where((rep & 1) == 0, up2, dn2)
+    opposite = lax.ppermute(
+        held, "rep", [(rep_of(a, z, c), rep_of(a, z + 2 - 4 * c, c)) for a in range(2) for z in range(Z) for c in range(2)]
+    )
 
     reps = jnp.arange(32, dtype=jnp.int32)
     same = ((reps ^ rep) & 17) == 0
@@ -398,11 +407,11 @@
     for k, offsets in enumerate(GROUPS):
         for i, o in enumerate(offsets):
             maps = jnp.where(same & (step == o % Z), k * 65536 + i * 8, maps)
-    q_all, list_1, list_2, list_3, *state = own_call(maps, local, *sents, kv, up2, dn2)
+    q_all, list_1, list_2, list_3, *state = own_call(maps, local, *sents, up1, dn1)
     state = near_call(list_1, q_all, (up1, dn1, up2, dn2), state, "near_pages")
     state = near_call(list_2, q_all, (up3, dn3), state, "far_pages")
-    own, p1, p2, p3 = far_call(list_3, q_all, (up4,), state)
-    back = [lax.ppermute(p, "rep", group_perm(r)) for r, p in ((1, p1), (2, p2), (3, p3))]
+    own, p1, p2, p3 = far_call(list_3, q_all, (opposite,), state)
+    back = [lax.ppermute(p, "rep", group_perm(r)) for r, p in ((3, p3), (2, p2), (1, p1))]
     width = out_weight.shape[1]
     attn = pl.pallas_call(
         combine_kernel,

time: 85.3 us -> 83.5 us (0.979); the launches traced: 84.1 us -> 83.2 us
  waiting for transfers between devices: 26.8 us -> 25.4 us
  starting transfers between devices: 33.9 us -> 35.2 us
  Pallas kernels: 17.9 us -> 17 us
    ppermute x1, waiting for transfers between devices: 0.01 us -> 8.52 us  [on_device(): up3 = lax.ppermute(up2, 'rep', z_perm(1))]
    ppermute x1, waiting for transfers between devices: 6.32 us -> 0.04 us  [on_device(): up1 = lax.ppermute(kv, 'rep', z_perm(1))]
    ppermute x1, starting transfers between devices: 3.32 us -> 0.43 us  [on_device(): dn3 = lax.ppermute(dn2, 'rep', z_perm(-1))]
    ppermute x1, starting transfers between devices: 0.01 us -> 2.89 us  [on_device(): up3 = lax.ppermute(up2, 'rep', z_perm(1))]
    ppermute x1, waiting for transfers between devices: 2.64 us -> 0.01 us  [on_device(): lax.ppermute(held, 'rep', [(rep_of(a, z, c), rep_of(a, z + 2 - 4 * c, c))...]
    pallas_call x2, Pallas kernels: 7.38 us -> 5.76 us  [near_call(): pl.pallas_call(functools.partial(near_kernel, nb), out_shape=state_shapes...]
    ppermute x3, waiting for transfers between devices: 7.34 us -> 6.31 us  [on_device(): lax.ppermute(p, 'rep', group_perm(r))]
  transfers between devices with their start and end apart: 20 -> 20, of which waited for: 9 -> 8; matrix products, arithmetic and copies ran while one was open for 0% -> 0% of each run, Pallas kernels for 18% -> 17%
where the time goes in v2:
time: 83.5 us; the launch traced here: 83.2 us
  starting transfers between devices  35.2 us (42%)
  waiting for transfers between devices  25.4 us (30%)
  Pallas kernels  17 us (20%)
  matrix products  3.34 us (4%)
  local copies, waits for them, and re-layouts  1.11 us (1%)
  other arithmetic  1.04 us (1%)
    ppermute x7, starting transfers between devices, on_device(): lax.ppermute(parts[k], 'head', [(i, i ^ k) for i in range(8)])  14.5 us
    ppermute x1, waiting for transfers between devices, on_device(): up3 = lax.ppermute(up2, 'rep', z_perm(1))  8.52 us
    ppermute x7, waiting for transfers between devices, on_device(): lax.ppermute(parts[k], 'head', [(i, i ^ k) for i in range(8)])  7.05 us
    ppermute x3, waiting for transfers between devices, on_device(): lax.ppermute(p, 'rep', group_perm(r))  6.31 us
    pallas_call x2, Pallas kernels, near_call(): pl.pallas_call(functools.partial(near_kernel, nb), out_shape=state_shapes...  5.76 us
    pallas_call x1, Pallas kernels, own_call(): pl.pallas_call(own_kernel, out_shape=[jax.ShapeDtypeStruct((SESS * QROWS,...  5.39 us
    ppermute x3, starting transfers between devices, on_device(): lax.ppermute(p, 'rep', group_perm(r))  4.56 us
    ppermute x1, starting transfers between devices, on_device(): dn1 = lax.ppermute(kv, 'rep', z_perm(-1))  4.03 us
  transfers between devices with their start and end apart: 20, of which 8 were waited for; matrix products, arithmetic and copies ran while one was open for 0% of the time, Pallas kernels for 17%

profile of v2, /device:TPU:2, one launch (start us, length us, event | category | flops | bytes accessed | tf_op | source)
XLA Modules:
  0.0 83.2 jit_solution(15303037516411227278)
XLA Ops:
  1.0 2.0 %collective-permute-start.3 = (bf16[8,128,128]{2,1,0:T(8,128)(2,1)S(1)}, bf16[8,128,128]{2,1,0:T(8,128)(2,1)S(1)}, u32[]{:S(2)}, u32[]{:S(2)}) collective-permute-start(bf16[8,128,128]{2,1,0:T(8,128)(2,1)S(1)} %maximum_bitcast_fusion.kv), channel_id=1, source_target_pairs={{0,16},{8,24},{16,32},{24,40},{32,48},{40,56},{48,64},{56,72},{64,... | collective-permute-start | bytes 786440 | tf_op jit(solution)/shard_map/ppermute | solution.py:375
  3.0 4.0 %collective-permute-start.4 = (bf16[8,128,128]{2,1,0:T(8,128)(2,1)S(1)}, bf16[8,128,128]{2,1,0:T(8,128)(2,1)S(1)}, u32[]{:S(2)}, u32[]{:S(2)}) collective-permute-start(bf16[8,128,128]{2,1,0:T(8,128)(2,1)S(1)} %maximum_bitcast_fusion.kv), channel_id=1, source_target_pairs={{0,112},{8,120},{16,0},{24,8},{32,16},{40,24},{48,32},{56,40},{64,... | collective-permute-start | bytes 786440 | tf_op jit(solution)/shard_map/ppermute | solution.py:376
  7.0 2.7 %pack.1 = (bf16[528,128]{1,0:T(8,128)(2,1)}, bf16[1808,128]{1,0:T(8,128)(2,1)}) custom-call(bf16[512,128]{1,0:T(8,128)(2,1)} %bitcast.17, bf16[128,128]{1,0:T(8,128)(2,1)} %bitcast.18, bf16[128,128]{1,0:T(8,128)(2,1)} %bitcast.19, bf16[512,128]{1,0:T(8,128)(2,1)} %bitcast.14, bf16[512,128]{1,0:T(8,128)(2,1)} %bitcast.16, s32[2,16]{1,0:T(2,128)} %table.1, ...), custom_call_target="tpu_custom_call" | custom-call | tf_op jit(solution)/shard_map/pack/pallas_call | solution.py:379
  9.8 2.2 %collective-permute-start.1 = (bf16[528,128]{1,0:T(8,128)(2,1)}, bf16[528,128]{1,0:T(8,128)(2,1)S(1)}, u32[]{:S(2)}, u32[]{:S(2)}) collective-permute-start(bf16[528,128]{1,0:T(8,128)(2,1)} %get-tuple-element.25), channel_id=1, source_target_pairs={{0,128},{8,136},{16,144},{24,152},{32,160},{40,168},{48,176},{56,1... | collective-permute-start | bytes 405512 | tf_op jit(solution)/shard_map/ppermute | solution.py:395
  13.3 3.2 %collective-permute-start.6 = (bf16[8,128,128]{2,1,0:T(8,128)(2,1)S(1)}, bf16[8,128,128]{2,1,0:T(8,128)(2,1)S(1)}, u32[]{:S(2)}, u32[]{:S(2)}) collective-permute-start(bf16[8,128,128]{2,1,0:T(8,128)(2,1)S(1)} %collective-permute-done.4.dn1.refs_3_), channel_id=1, source_target_pairs={{0,112},{8,120},{16,0},{24,8},{32,16},{40,24},{48,32},{56,40},{64,... | collective-permute-start | bytes 786440 | tf_op jit(solution)/shard_map/ppermute | solution.py:378
  18.0 1.9 %collective-permute-done.2.s3 = bf16[528,128]{1,0:T(8,128)(2,1)S(1)} collective-permute-done((bf16[528,128]{1,0:T(8,128)(2,1)}, bf16[528,128]{1,0:T(8,128)(2,1)S(1)}, u32[]{:S(2)}, u32[]{:S(2)}) %collective-permute-start.2) | collective-permute-done | bytes 135200 | tf_op jit(solution)/shard_map/ppermute | solution.py:395
  21.0 5.4 %own_pages.1 = (bf16[2048,128]{1,0:T(8,128)(2,1)S(1)}, s32[160]{0:T(256)S(1)}, s32[160]{0:T(256)S(1)}, s32[160]{0:T(256)S(1)}, f32[8,1,256]{2,1,0:T(1,128)S(1)},...) custom-call(s32[32]{0:T(128)S(1)} %and_select_fusion.7.maps, bf16[1808,128]{1,0:T(8,128)(2,1)S(1)} %copy-done, ...), custom_call_target="tpu_custom_call" | custom-call | flops 2000000000 | bytes 4194304 | tf_op jit(solution)/shard_map/own_pages/pallas_call | solution.py:311
  26.6 2.9 %collective-permute-start.8 = (bf16[8,128,128]{2,1,0:T(8,128)(2,1)S(1)}, bf16[8,128,128]{2,1,0:T(8,128)(2,1)S(1)}, u32[]{:S(2)}, u32[]{:S(2)}) collective-permute-start(bf16[8,128,128]{2,1,0:T(8,128)(2,1)S(1)} %collective-permute-done.5.refs_4_), channel_id=1, source_target_pairs={{0,16},{8,24},{16,32},{24,40},{32,48},{40,56},{48,64},{56,72},{64,... | collective-permute-start | bytes 786440 | tf_op jit(solution)/shard_map/ppermute | solution.py:396
  29.9 3.4 %near_pages.1 = (f32[8,1,256]{2,1,0:T(1,128)S(1)}, f32[8,1,256]{2,1,0:T(1,128)S(1)}, f32[8,128,256]{2,1,0:T(8,128)S(1)}) custom-call(s32[160]{0:T(256)S(1)} %get-tuple-element.29.refs_0_, bf16[2048,128]{1,0:T(8,128)(2,1)S(1)} %get-tuple-element.27.refs_1_, bf16[8,128,128]{2,1,0:T(8,128)(2,1)S(1)} %collective-permute-done.3.up1.refs_2_, ...), custom_call_target="tpu_custom_call" | custom-call | flops 4000000000 | bytes 4194304 | tf_op jit(solution)/shard_map/near_pages/pallas_call | solution.py:341
  33.3 8.5 %collective-permute-done.8.refs_2_ = bf16[8,128,128]{2,1,0:T(8,128)(2,1)S(1)} collective-permute-done((bf16[8,128,128]{2,1,0:T(8,128)(2,1)S(1)}, bf16[8,128,128]{2,1,0:T(8,128)(2,1)S(1)}, u32[]{:S(2)}, u32[]{:S(2)}) %collective-permute-start.8) | collective-permute-done | bytes 262176 | tf_op jit(solution)/shard_map/ppermute | solution.py:396
  41.8 2.3 %far_pages.1 = (f32[8,1,256]{2,1,0:T(1,128)S(1)}, f32[8,1,256]{2,1,0:T(1,128)S(1)}, f32[8,128,256]{2,1,0:T(8,128)S(1)}) custom-call(s32[160]{0:T(256)S(1)} %get-tuple-element.28.refs_0_, bf16[2048,128]{1,0:T(8,128)(2,1)S(1)} %get-tuple-element.27.refs_1_, bf16[8,128,128]{2,1,0:T(8,128)(2,1)S(1)} %collective-permute-done.8.refs_2_, ...), custom_call_target="tpu_custom_call" | custom-call | flops 2000000000 | bytes 4194304 | tf_op jit(solution)/shard_map/far_pages/pallas_call | solution.py:341
  44.2 2.1 %last_pages.1 = (f32[136,512]{1,0:T(8,128)S(1)}, bf16[144,512]{1,0:T(8,128)(2,1)S(1)}, bf16[144,512]{1,0:T(8,128)(2,1)S(1)}, bf16[144,512]{1,0:T(8,128)(2,1)S(1)}) custom-call(s32[160]{0:T(256)S(1)} %get-tuple-element.26.refs_0_, bf16[2048,128]{1,0:T(8,128)(2,1)S(1)} %get-tuple-element.27.refs_1_, bf16[8,128,128]{2,1,0:T(8,128)(2,1)S(1)} %collective-permute-done.7.refs_2_, ...), custom_call_target="tpu_custom_call" | custom-call | flops 1000000000 | bytes 4194304 | tf_op jit(solution)/shard_map/last_pages/pallas_call | solution.py:355
  46.3 2.8 %collective-permute-start.10 = (bf16[144,512]{1,0:T(8,128)(2,1)S(1)}, bf16[144,512]{1,0:T(8,128)(2,1)S(1)}, u32[]{:S(2)}, u32[]{:S(2)}) collective-permute-start(bf16[144,512]{1,0:T(8,128)(2,1)S(1)} %get-tuple-element.40), channel_id=1, source_target_pairs={{0,136},{8,128},{16,152},{24,144},{32,168},{40,160},{48,184},{56,1... | collective-permute-start | bytes 442376 | tf_op jit(solution)/shard_map/ppermute | solution.py:414
  49.1 1.7 %collective-permute-start.11 = (bf16[144,512]{1,0:T(8,128)(2,1)S(1)}, bf16[144,512]{1,0:T(8,128)(2,1)S(1)}, u32[]{:S(2)}, u32[]{:S(2)}) collective-permute-start(bf16[144,512]{1,0:T(8,128)(2,1)S(1)} %get-tuple-element.41), channel_id=1, source_target_pairs={{0,128},{8,136},{16,144},{24,152},{32,160},{40,168},{48,176},{56,1... | collective-permute-start | bytes 442376 | tf_op jit(solution)/shard_map/ppermute | solution.py:414
  50.8 2.1 %collective-permute-done.10.p1 = bf16[144,512]{1,0:T(8,128)(2,1)S(1)} collective-permute-done((bf16[144,512]{1,0:T(8,128)(2,1)S(1)}, bf16[144,512]{1,0:T(8,128)(2,1)S(1)}, u32[]{:S(2)}, u32[]{:S(2)}) %collective-permute-start.10) | collective-permute-done | bytes 147488 | tf_op jit(solution)/shard_map/ppermute | solution.py:414
  53.0 4.2 %collective-permute-done.11.p2 = bf16[144,512]{1,0:T(8,128)(2,1)S(1)} collective-permute-done((bf16[144,512]{1,0:T(8,128)(2,1)S(1)}, bf16[144,512]{1,0:T(8,128)(2,1)S(1)}, u32[]{:S(2)}, u32[]{:S(2)}) %collective-permute-start.11) | collective-permute-done | bytes 147488 | tf_op jit(solution)/shard_map/ppermute | solution.py:414
  57.4 3.3 %convolution_convert_fusion = bf16[128,5120]{1,0:T(8,128)(2,1)S(1)} fusion(bf16[128,512]{1,0:T(8,128)(2,1)S(1)} %combine.1, bf16[512,5120]{1,0:T(8,128)(2,1)} %param.15), kind=kOutput, calls=%fused_computation | convolution fusion | flops 671744000 | bytes 6684672 | tf_op jit(solution)/shard_map/dot_general | solution.py:426
  60.8 1.6 %collective-permute-start.13 = (bf16[16,5120]{1,0:T(8,128)(2,1)S(1)}, bf16[16,5120]{1,0:T(8,128)(2,1)S(1)}, u32[]{:S(2)}, u32[]{:S(2)}) collective-permute-start(bf16[16,5120]{1,0:T(8,128)(2,1)S(1)} %get-tuple-element.49), channel_id=1, source_target_pairs={{0,1},{1,0},{2,3},{3,2},{4,5},{5,4},{6,7},{7,6},{8,9},{9,8},{10,11... | collective-permute-start | bytes 491528 | tf_op jit(solution)/shard_map/ppermute | solution.py:428
  62.5 2.2 %collective-permute-start.14 = (bf16[16,5120]{1,0:T(8,128)(2,1)S(1)}, bf16[16,5120]{1,0:T(8,128)(2,1)S(1)}, u32[]{:S(2)}, u32[]{:S(2)}) collective-permute-start(bf16[16,5120]{1,0:T(8,128)(2,1)S(1)} %get-tuple-element.48), channel_id=1, source_target_pairs={{0,3},{1,2},{2,1},{3,0},{4,7},{5,6},{6,5},{7,4},{8,11},{9,10},{10,... | collective-permute-start | bytes 491528 | tf_op jit(solution)/shard_map/ppermute | solution.py:428
  64.6 1.9 %collective-permute-start.15 = (bf16[16,5120]{1,0:T(8,128)(2,1)S(1)}, bf16[16,5120]{1,0:T(8,128)(2,1)S(1)}, u32[]{:S(2)}, u32[]{:S(2)}) collective-permute-start(bf16[16,5120]{1,0:T(8,128)(2,1)S(1)} %get-tuple-element.47), channel_id=1, source_target_pairs={{0,4},{1,5},{2,6},{3,7},{4,0},{5,1},{6,2},{7,3},{8,12},{9,13},{10,... | collective-permute-start | bytes 491528 | tf_op jit(solution)/shard_map/ppermute | solution.py:428
  68.0 4.4 %collective-permute-start.18 = (bf16[16,5120]{1,0:T(8,128)(2,1)S(1)}, bf16[16,5120]{1,0:T(8,128)(2,1)S(1)}, u32[]{:S(2)}, u32[]{:S(2)}) collective-permute-start(bf16[16,5120]{1,0:T(8,128)(2,1)S(1)} %get-tuple-element.44), channel_id=1, source_target_pairs={{0,7},{1,6},{2,5},{3,4},{4,3},{5,2},{6,1},{7,0},{8,15},{9,14},{10,... | collective-permute-start | bytes 491528 | tf_op jit(solution)/shard_map/ppermute | solution.py:428
  72.4 3.0 %collective-permute-start.19 = (bf16[16,5120]{1,0:T(8,128)(2,1)S(1)}, bf16[16,5120]{1,0:T(8,128)(2,1)S(1)}, u32[]{:S(2)}, u32[]{:S(2)}) collective-permute-start(bf16[16,5120]{1,0:T(8,128)(2,1)S(1)} %get-tuple-element.43), channel_id=1, source_target_pairs={{0,6},{1,7},{2,4},{3,5},{4,2},{5,3},{6,0},{7,1},{8,14},{9,15},{10,... | collective-permute-start | bytes 491528 | tf_op jit(solution)/shard_map/ppermute | solution.py:428
  76.5 3.5 %collective-permute-done.18.refs_6_ = bf16[16,5120]{1,0:T(8,128)(2,1)S(1)} collective-permute-done((bf16[16,5120]{1,0:T(8,128)(2,1)S(1)}, bf16[16,5120]{1,0:T(8,128)(2,1)S(1)}, u32[]{:S(2)}, u32[]{:S(2)}) %collective-permute-start.18) | collective-permute-done | bytes 163872 | tf_op jit(solution)/shard_map/ppermute | solution.py:428
  80.0 2.4 %collective-permute-done.19.refs_7_ = bf16[16,5120]{1,0:T(8,128)(2,1)S(1)} collective-permute-done((bf16[16,5120]{1,0:T(8,128)(2,1)S(1)}, bf16[16,5120]{1,0:T(8,128)(2,1)S(1)}, u32[]{:S(2)}, u32[]{:S(2)}) %collective-permute-start.19) | collective-permute-done | bytes 163872 | tf_op jit(solution)/shard_map/ppermute | solution.py:428
  (32 shorter events, 9.2 us)
Async XLA Ops:
  1.0 6.0 %copy-start.1 = (bf16[8,128,128]{2,1,0:T(8,128)(2,1)}, bf16[8,128,128]{2,1,0:T(8,128)(2,1)S(1)}, u32[]{:S(2)}) copy-start(bf16[8,128,128]{2,1,0:T(8,128)(2,1)S(1)} %maximum_bitcast_fusion.kv) | copy-start | bytes 786436
  1.0 12.2 %collective-permute-start.3 = (bf16[8,128,128]{2,1,0:T(8,128)(2,1)S(1)}, bf16[8,128,128]{2,1,0:T(8,128)(2,1)S(1)}, u32[]{:S(2)}, u32[]{:S(2)}) collective-permute-start(bf16[8,128,128]{2,1,0:T(8,128)(2,1)S(1)} %maximum_bitcast_fusion.kv), channel_id=1, source_target_pairs={{0,16},{8,24},{16,32},{24,40},{32,48},{40,56},{48,64},{56,72},{64,... | collective-permute-start | bytes 786440 | tf_op jit(solution)/shard_map/ppermute | solution.py:375
  3.0 10.2 %collective-permute-start.4 = (bf16[8,128,128]{2,1,0:T(8,128)(2,1)S(1)}, bf16[8,128,128]{2,1,0:T(8,128)(2,1)S(1)}, u32[]{:S(2)}, u32[]{:S(2)}) collective-permute-start(bf16[8,128,128]{2,1,0:T(8,128)(2,1)S(1)} %maximum_bitcast_fusion.kv), channel_id=1, source_target_pairs={{0,112},{8,120},{16,0},{24,8},{32,16},{40,24},{48,32},{56,40},{64,... | collective-permute-start | bytes 786440 | tf_op jit(solution)/shard_map/ppermute | solution.py:376
  9.7 6.8 %collective-permute-start = (bf16[528,128]{1,0:T(8,128)(2,1)}, bf16[528,128]{1,0:T(8,128)(2,1)S(1)}, u32[]{:S(2)}, u32[]{:S(2)}) collective-permute-start(bf16[528,128]{1,0:T(8,128)(2,1)} %get-tuple-element.25), channel_id=1, source_target_pairs={{0,8},{8,0},{16,24},{24,16},{32,40},{40,32},{48,56},{56,48},{64,72... | collective-permute-start | bytes 405512 | tf_op jit(solution)/shard_map/ppermute | solution.py:395
  9.8 8.2 %collective-permute-start.1 = (bf16[528,128]{1,0:T(8,128)(2,1)}, bf16[528,128]{1,0:T(8,128)(2,1)S(1)}, u32[]{:S(2)}, u32[]{:S(2)}) collective-permute-start(bf16[528,128]{1,0:T(8,128)(2,1)} %get-tuple-element.25), channel_id=1, source_target_pairs={{0,128},{8,136},{16,144},{24,152},{32,160},{40,168},{48,176},{56,1... | collective-permute-start | bytes 405512 | tf_op jit(solution)/shard_map/ppermute | solution.py:395
  12.0 7.9 %collective-permute-start.2 = (bf16[528,128]{1,0:T(8,128)(2,1)}, bf16[528,128]{1,0:T(8,128)(2,1)S(1)}, u32[]{:S(2)}, u32[]{:S(2)}) collective-permute-start(bf16[528,128]{1,0:T(8,128)(2,1)} %get-tuple-element.25), channel_id=1, source_target_pairs={{0,136},{8,128},{16,152},{24,144},{32,168},{40,160},{48,184},{56,1... | collective-permute-start | bytes 405512 | tf_op jit(solution)/shard_map/ppermute | solution.py:395
  13.2 13.2 %collective-permute-start.5 = (bf16[8,128,128]{2,1,0:T(8,128)(2,1)S(1)}, bf16[8,128,128]{2,1,0:T(8,128)(2,1)S(1)}, u32[]{:S(2)}, u32[]{:S(2)}) collective-permute-start(bf16[8,128,128]{2,1,0:T(8,128)(2,1)S(1)} %collective-permute-done.3.up1.refs_2_), channel_id=1, source_target_pairs={{0,16},{8,24},{16,32},{24,40},{32,48},{40,56},{48,64},{56,72},{64,... | collective-permute-start | bytes 786440 | tf_op jit(solution)/shard_map/ppermute | solution.py:377
  13.3 13.2 %collective-permute-start.6 = (bf16[8,128,128]{2,1,0:T(8,128)(2,1)S(1)}, bf16[8,128,128]{2,1,0:T(8,128)(2,1)S(1)}, u32[]{:S(2)}, u32[]{:S(2)}) collective-permute-start(bf16[8,128,128]{2,1,0:T(8,128)(2,1)S(1)} %collective-permute-done.4.dn1.refs_3_), channel_id=1, source_target_pairs={{0,112},{8,120},{16,0},{24,8},{32,16},{40,24},{48,32},{56,40},{64,... | collective-permute-start | bytes 786440 | tf_op jit(solution)/shard_map/ppermute | solution.py:378
  20.0 1.0 %copy-start = (bf16[1808,128]{1,0:T(8,128)(2,1)S(1)}, bf16[1808,128]{1,0:T(8,128)(2,1)}, u32[]{:S(2)}) copy-start(bf16[1808,128]{1,0:T(8,128)(2,1)} %get-tuple-element.24.local) | copy-start | bytes 1388548
  26.5 17.7 %collective-permute-start.7 = (bf16[8,128,128]{2,1,0:T(8,128)(2,1)S(1)}, bf16[8,128,128]{2,1,0:T(8,128)(2,1)S(1)}, u32[]{:S(2)}, u32[]{:S(2)}) collective-permute-start(bf16[8,128,128]{2,1,0:T(8,128)(2,1)S(1)} %broadcast_select_fusion), channel_id=1, source_target_pairs={{0,32},{8,104},{16,48},{24,120},{32,64},{40,8},{48,80},{56,24},{64... | collective-permute-start | bytes 786440 | tf_op jit(solution)/shard_map/ppermute | solution.py:399
  26.6 15.3 %collective-permute-start.8 = (bf16[8,128,128]{2,1,0:T(8,128)(2,1)S(1)}, bf16[8,128,128]{2,1,0:T(8,128)(2,1)S(1)}, u32[]{:S(2)}, u32[]{:S(2)}) collective-permute-start(bf16[8,128,128]{2,1,0:T(8,128)(2,1)S(1)} %collective-permute-done.5.refs_4_), channel_id=1, source_target_pairs={{0,16},{8,24},{16,32},{24,40},{32,48},{40,56},{48,64},{56,72},{64,... | collective-permute-start | bytes 786440 | tf_op jit(solution)/shard_map/ppermute | solution.py:396
  29.4 12.4 %collective-permute-start.9 = (bf16[8,128,128]{2,1,0:T(8,128)(2,1)S(1)}, bf16[8,128,128]{2,1,0:T(8,128)(2,1)S(1)}, u32[]{:S(2)}, u32[]{:S(2)}) collective-permute-start(bf16[8,128,128]{2,1,0:T(8,128)(2,1)S(1)} %collective-permute-done.6.refs_5_), channel_id=1, source_target_pairs={{0,112},{8,120},{16,0},{24,8},{32,16},{40,24},{48,32},{56,40},{64,... | collective-permute-start | bytes 786440 | tf_op jit(solution)/shard_map/ppermute | solution.py:397
  46.3 6.7 %collective-permute-start.10 = (bf16[144,512]{1,0:T(8,128)(2,1)S(1)}, bf16[144,512]{1,0:T(8,128)(2,1)S(1)}, u32[]{:S(2)}, u32[]{:S(2)}) collective-permute-start(bf16[144,512]{1,0:T(8,128)(2,1)S(1)} %get-tuple-element.40), channel_id=1, source_target_pairs={{0,136},{8,128},{16,152},{24,144},{32,168},{40,160},{48,184},{56,1... | collective-permute-start | bytes 442376 | tf_op jit(solution)/shard_map/ppermute | solution.py:414
  49.1 8.0 %collective-permute-start.11 = (bf16[144,512]{1,0:T(8,128)(2,1)S(1)}, bf16[144,512]{1,0:T(8,128)(2,1)S(1)}, u32[]{:S(2)}, u32[]{:S(2)}) collective-permute-start(bf16[144,512]{1,0:T(8,128)(2,1)S(1)} %get-tuple-element.41), channel_id=1, source_target_pairs={{0,128},{8,136},{16,144},{24,152},{32,160},{40,168},{48,176},{56,1... | collective-permute-start | bytes 442376 | tf_op jit(solution)/shard_map/ppermute | solution.py:414
  50.8 6.3 %collective-permute-start.12 = (bf16[144,512]{1,0:T(8,128)(2,1)S(1)}, bf16[144,512]{1,0:T(8,128)(2,1)S(1)}, u32[]{:S(2)}, u32[]{:S(2)}) collective-permute-start(bf16[144,512]{1,0:T(8,128)(2,1)S(1)} %get-tuple-element.42), channel_id=1, source_target_pairs={{0,8},{8,0},{16,24},{24,16},{32,40},{40,32},{48,56},{56,48},{64,72... | collective-permute-start | bytes 442376 | tf_op jit(solution)/shard_map/ppermute | solution.py:414
  60.8 7.2 %collective-permute-start.13 = (bf16[16,5120]{1,0:T(8,128)(2,1)S(1)}, bf16[16,5120]{1,0:T(8,128)(2,1)S(1)}, u32[]{:S(2)}, u32[]{:S(2)}) collective-permute-start(bf16[16,5120]{1,0:T(8,128)(2,1)S(1)} %get-tuple-element.49), channel_id=1, source_target_pairs={{0,1},{1,0},{2,3},{3,2},{4,5},{5,4},{6,7},{7,6},{8,9},{9,8},{10,11... | collective-permute-start | bytes 491528 | tf_op jit(solution)/shard_map/ppermute | solution.py:428
  62.5 9.9 %collective-permute-start.14 = (bf16[16,5120]{1,0:T(8,128)(2,1)S(1)}, bf16[16,5120]{1,0:T(8,128)(2,1)S(1)}, u32[]{:S(2)}, u32[]{:S(2)}) collective-permute-start(bf16[16,5120]{1,0:T(8,128)(2,1)S(1)} %get-tuple-element.48), channel_id=1, source_target_pairs={{0,3},{1,2},{2,1},{3,0},{4,7},{5,6},{6,5},{7,4},{8,11},{9,10},{10,... | collective-permute-start | bytes 491528 | tf_op jit(solution)/shard_map/ppermute | solution.py:428
  64.6 10.7 %collective-permute-start.15 = (bf16[16,5120]{1,0:T(8,128)(2,1)S(1)}, bf16[16,5120]{1,0:T(8,128)(2,1)S(1)}, u32[]{:S(2)}, u32[]{:S(2)}) collective-permute-start(bf16[16,5120]{1,0:T(8,128)(2,1)S(1)} %get-tuple-element.47), channel_id=1, source_target_pairs={{0,4},{1,5},{2,6},{3,7},{4,0},{5,1},{6,2},{7,3},{8,12},{9,13},{10,... | collective-permute-start | bytes 491528 | tf_op jit(solution)/shard_map/ppermute | solution.py:428
  66.5 10.0 %collective-permute-start.16 = (bf16[16,5120]{1,0:T(8,128)(2,1)S(1)}, bf16[16,5120]{1,0:T(8,128)(2,1)S(1)}, u32[]{:S(2)}, u32[]{:S(2)}) collective-permute-start(bf16[16,5120]{1,0:T(8,128)(2,1)S(1)} %get-tuple-element.46), channel_id=1, source_target_pairs={{0,2},{1,3},{2,0},{3,1},{4,6},{5,7},{6,4},{7,5},{8,10},{9,11},{10,... | collective-permute-start | bytes 491528 | tf_op jit(solution)/shard_map/ppermute | solution.py:428
  67.3 9.2 %collective-permute-start.17 = (bf16[16,5120]{1,0:T(8,128)(2,1)S(1)}, bf16[16,5120]{1,0:T(8,128)(2,1)S(1)}, u32[]{:S(2)}, u32[]{:S(2)}) collective-permute-start(bf16[16,5120]{1,0:T(8,128)(2,1)S(1)} %get-tuple-element.45), channel_id=1, source_target_pairs={{0,5},{1,4},{2,7},{3,6},{4,1},{5,0},{6,3},{7,2},{8,13},{9,12},{10,... | collective-permute-start | bytes 491528 | tf_op jit(solution)/shard_map/ppermute | solution.py:428
  68.0 12.0 %collective-permute-start.18 = (bf16[16,5120]{1,0:T(8,128)(2,1)S(1)}, bf16[16,5120]{1,0:T(8,128)(2,1)S(1)}, u32[]{:S(2)}, u32[]{:S(2)}) collective-permute-start(bf16[16,5120]{1,0:T(8,128)(2,1)S(1)} %get-tuple-element.44), channel_id=1, source_target_pairs={{0,7},{1,6},{2,5},{3,4},{4,3},{5,2},{6,1},{7,0},{8,15},{9,14},{10,... | collective-permute-start | bytes 491528 | tf_op jit(solution)/shard_map/ppermute | solution.py:428
  72.4 10.0 %collective-permute-start.19 = (bf16[16,5120]{1,0:T(8,128)(2,1)S(1)}, bf16[16,5120]{1,0:T(8,128)(2,1)S(1)}, u32[]{:S(2)}, u32[]{:S(2)}) collective-permute-start(bf16[16,5120]{1,0:T(8,128)(2,1)S(1)} %get-tuple-element.43), channel_id=1, source_target_pairs={{0,6},{1,7},{2,4},{3,5},{4,2},{5,3},{6,0},{7,1},{8,14},{9,15},{10,... | collective-permute-start | bytes 491528 | tf_op jit(solution)/shard_map/ppermute | solution.py:428

commit v3 on v2

--- a/solution.py
+++ b/solution.py
@@ -14,6 +14,7 @@
 LOCAL_PAGES = 4
 TK_AT = 528
 TV_AT = 656
+BLOCK = 1024
 PAGES_AT = 784
 TREE = 64
 QROWS = 256
@@ -24,7 +25,7 @@
 F32 = jnp.float32
 
 STREAMS = 4
-GROUPS = ((0,), (-1, 1, -2, 2), (-3, 3), (4,))
+GROUPS = ((0, -1, 1, -2, 2), (-3, 3, 4))
 
 
 def rep_of(xh, z, c):
@@ -39,10 +40,14 @@
     return [(rep_of(a, z, c), rep_of(a ^ (r >> 1), z, c ^ (r & 1))) for a in range(2) for z in range(Z) for c in range(2)]
 
 
-def pair_steps(entries, q_ref, page, streams):
+def page(kv, i):
+    return kv[pl.ds(pl.multiple_of(i * 128, 128), 128), :]
+
+
+def pair_steps(entries, q_ref, kv, streams):
     at = [(e >> 8, e & 255) for e in entries]
     scores = [
-        lax.dot_general(page(k), q_ref[pl.ds(pl.multiple_of((s & (SESS - 1)) * QROWS, QROWS), QROWS), :], (((1,), (1,)), ((), ())), preferred_element_type=F32)
+        lax.dot_general(page(kv, k), q_ref[pl.ds(pl.multiple_of((s & (SESS - 1)) * QROWS, QROWS), QROWS), :], (((1,), (1,)), ((), ())), preferred_element_type=F32)
         for s, k in at
     ]
     olds = [m[s] for (s, _), (m, _, _) in zip(at, streams)]
@@ -51,7 +56,7 @@
     fixes = [jnp.exp2((o - n) * C2) for o, n in zip(olds, news)]
     parts = [
         lax.dot_general(
-            page(k + LOCAL_PAGES), p.astype(BF), (((0,), (0,)), ((), ())), preferred_element_type=F32
+            page(kv, k + LOCAL_PAGES), p.astype(BF), (((0,), (0,)), ((), ())), preferred_element_type=F32
         )
         for (_, k), p in zip(at, probs)
     ]
@@ -61,12 +66,12 @@
         a_ref[s] = a_ref[s] * fix + part
 
 
-def all_pairs(entries, q_ref, page, streams):
+def all_pairs(entries, q_ref, kv, streams):
     ns = len(streams)
 
     @pl.loop(0, (entries[0] + ns - 1) >> (ns.bit_length() - 1))
     def _(i):
-        pair_steps([entries[ns * i + r + 1] for r in range(ns)], q_ref, page, streams)
+        pair_steps([entries[ns * i + r + 1] for r in range(ns)], q_ref, kv, streams)
 
 
 def streams_of(refs):
@@ -114,12 +119,10 @@
         cp.wait()
 
 
-def own_kernel(maps, local, s1, s2, s3, up1, dn1, q_out, *refs):
-    del up1, dn1
-    lists = refs[:3]
-    m_out, l_out, a_out, tails, ids, tbl, list_own, found = refs[3:11]
-    lists = (list_own,) + lists
-    streams = streams_of(refs[11:-1])
+def near_kernel(maps, local, s1, s2, s3, up1, dn1, up2, dn2, q_out, list_far, *refs):
+    m_out, l_out, a_out, tails, ids, tbl, list_near, found, kv = refs[:9]
+    lists = (list_near, list_far)
+    streams = streams_of(refs[9:-1])
     sems = refs[-1]
     sents = (local, s1, s2, s3)
     for r, x in enumerate(sents):
@@ -127,6 +130,9 @@
     ids[...] = tails[...].astype(F32).astype(jnp.int32)
     to_scalar = pltpu.make_async_copy(ids, tbl, sems.at[0])
     to_scalar.start()
+    copies = load_blocks(
+        [local.at[pl.ds(PAGES_AT, BLOCK)], up1, dn1, up2, dn2], kv, [sems.at[i + 1] for i in range(5)]
+    )
     for r, x in enumerate(sents):
         q_out[pl.ds(r * 2 * QROWS, 2 * QROWS), :] = x[pl.ds(0, 2 * QROWS), :]
     clear(streams)
@@ -179,19 +185,19 @@
         entry = found[i]
         kind = entry >> 16
         out = []
-        for k in range(4):
+        for k in range(2):
             lists[k][counts[k] + 1] = entry & 65535
             out.append(counts[k] + (kind == k).astype(jnp.int32))
         return tuple(out)
 
-    counts = lax.fori_loop(0, total, sort, (jnp.int32(0),) * 4)
-    for k in range(4):
+    counts = lax.fori_loop(0, total, sort, (jnp.int32(0),) * 2)
+    for k in range(2):
         lists[k][0] = counts[k]
         for r in range(STREAMS - 1):
             lists[k][counts[k] + 1 + r] = jnp.int32(SESS * 256)
-    all_pairs(
-        list_own, q_out, lambda i: local[pl.ds(pl.multiple_of(PAGES_AT + i * 128, 16), 128), :], streams
-    )
+    for cp in copies:
+        cp.wait()
+    all_pairs(list_near, q_out, kv, streams)
     for s in range(SESS):
         top, total, acc = merge([(m[s], l[s], a[s]) for m, l, a in streams])
         m_out[s] = top
@@ -200,28 +206,10 @@
 
 
 def load_blocks(blocks, kv, sems):
-    copies = [pltpu.make_async_copy(b, kv.at[pl.ds(i * 8, 8)], sems.at[i]) for i, b in enumerate(blocks)]
+    copies = [pltpu.make_async_copy(b, kv.at[pl.ds(i * BLOCK, BLOCK)], sem) for i, (b, sem) in enumerate(zip(blocks, sems))]
     for cp in copies:
         cp.start()
     return copies
-
-
-def near_kernel(nb, *refs):
-    list_near, q_ref = refs[:2]
-    blocks = refs[2:2 + nb]
-    before = refs[2 + nb:5 + nb]
-    m_out, l_out, a_out, kv = refs[5 + nb:9 + nb]
-    streams = streams_of(refs[9 + nb:-1])
-    copies = load_blocks(blocks, kv, refs[-1])
-    clear(streams)
-    for cp in copies:
-        cp.wait()
-    all_pairs(list_near, q_ref, lambda i: kv[i], streams)
-    for s in range(SESS):
-        top, total, acc = merge([(m[s], l[s], a[s]) for m, l, a in [before] + streams])
-        m_out[s] = top
-        l_out[s] = total
-        a_out[s] = acc
 
 
 def far_kernel(nb, *refs):
@@ -232,11 +220,11 @@
     outs = refs[6 + nb:9 + nb]
     kv = refs[9 + nb]
     streams = streams_of(refs[10 + nb:-1])
-    copies = load_blocks(blocks, kv, refs[-1])
+    copies = load_blocks(blocks, kv, [refs[-1].at[i] for i in range(nb)])
     clear(streams)
     for cp in copies:
         cp.wait()
-    all_pairs(list_far, q_ref, lambda i: kv[i], streams)
+    all_pairs(list_far, q_ref, kv, streams)
     for s in range(SESS):
         top, total, acc = merge([(m[s], l[s], a[s]) for m, l, a in [before] + streams])
         some = total > 0.0
@@ -303,51 +291,27 @@
     ]
 
 
-def lists(n):
-    return [jax.ShapeDtypeStruct((160,), jnp.int32)] * n
-
-
-def own_call(*args):
+def near_call(*args):
     return pl.pallas_call(
-        own_kernel,
-        out_shape=[jax.ShapeDtypeStruct((SESS * QROWS, HD), BF)] + lists(3) + state_shapes(SESS),
-        in_specs=[SMEM] + [VMEM] * 4 + [ANY] * 2,
-        out_specs=[VMEM] + [SMEM] * 3 + [VMEM] * 3,
+        near_kernel,
+        out_shape=[jax.ShapeDtypeStruct((SESS * QROWS, HD), BF), jax.ShapeDtypeStruct((160,), jnp.int32)]
+        + state_shapes(SESS),
+        in_specs=[SMEM] + [VMEM] * 4 + [ANY] * 4,
+        out_specs=[VMEM, SMEM] + [VMEM] * 3,
         scratch_shapes=[
             pltpu.VMEM((64, 128), BF),
             pltpu.VMEM((64, 128), jnp.int32),
             pltpu.SMEM((64, 128), jnp.int32),
             pltpu.SMEM((160,), jnp.int32),
             pltpu.SMEM((160,), jnp.int32),
+            pltpu.VMEM((5 * BLOCK, HD), BF),
         ]
         + stream_scratch() * STREAMS
-        + [pltpu.SemaphoreType.DMA((1,))],
+        + [pltpu.SemaphoreType.DMA((6,))],
         compiler_params=pltpu.CompilerParams(vmem_limit_bytes=24 << 20),
-        cost_estimate=pl.CostEstimate(flops=2 * 10**9, bytes_accessed=4 << 20, transcendentals=1 << 20),
-        name="own_pages",
+        cost_estimate=pl.CostEstimate(flops=4 * 10**9, bytes_accessed=4 << 20, transcendentals=1 << 20),
+        name="near_pages",
     )(*args)
-
-
-def block_scratch(nb):
-    return (
-        [pltpu.VMEM((8 * nb, 128, HD), BF)]
-        + stream_scratch() * STREAMS
-        + [pltpu.SemaphoreType.DMA((nb,))]
-    )
-
-
-def near_call(pages, q_all, blocks, state, name):
-    nb = len(blocks)
-    return pl.pallas_call(
-        functools.partial(near_kernel, nb),
-        out_shape=state_shapes(SESS),
-        in_specs=[SMEM, VMEM] + [ANY] * nb + [VMEM] * 3,
-        out_specs=[VMEM] * 3,
-        scratch_shapes=block_scratch(nb),
-        compiler_params=pltpu.CompilerParams(vmem_limit_bytes=24 << 20),
-        cost_estimate=pl.CostEstimate(flops=10**9 * nb, bytes_accessed=4 << 20, transcendentals=1 << 20),
-        name=name,
-    )(pages, q_all, *blocks, *state)
 
 
 def far_call(pages, q_all, blocks, state):
@@ -358,10 +322,12 @@
         + [jax.ShapeDtypeStruct((HD + 16, 2 * QROWS), BF)] * 3,
         in_specs=[SMEM, VMEM] + [ANY] * nb + [VMEM] * 3,
         out_specs=[VMEM] * 4,
-        scratch_shapes=block_scratch(nb),
+        scratch_shapes=[pltpu.VMEM((nb * BLOCK, HD), BF)]
+        + stream_scratch() * STREAMS
+        + [pltpu.SemaphoreType.DMA((nb,))],
         compiler_params=pltpu.CompilerParams(vmem_limit_bytes=24 << 20),
         cost_estimate=pl.CostEstimate(flops=10**9, bytes_accessed=4 << 20, transcendentals=1 << 20),
-        name="last_pages",
+        name="far_pages",
     )(pages, q_all, *blocks, *state)
 
 
@@ -371,7 +337,7 @@
     rep = lax.axis_index("rep")
     head = lax.axis_index("head")
     q_own = queries.reshape(2 * QROWS, HD)
-    kv = jnp.concatenate([prefix_keys, prefix_values], axis=0).reshape(2 * LOCAL_PAGES, 128, HD)
+    kv = jnp.concatenate([prefix_keys, prefix_values], axis=0).reshape(BLOCK, HD)
     up1 = lax.ppermute(kv, "rep", z_perm(1))
     dn1 = lax.ppermute(kv, "rep", z_perm(-1))
     up2 = lax.ppermute(up1, "rep", z_perm(1))
@@ -407,10 +373,8 @@
     for k, offsets in enumerate(GROUPS):
         for i, o in enumerate(offsets):
             maps = jnp.where(same & (step == o % Z), k * 65536 + i * 8, maps)
-    q_all, list_1, list_2, list_3, *state = own_call(maps, local, *sents, up1, dn1)
-    state = near_call(list_1, q_all, (up1, dn1, up2, dn2), state, "near_pages")
-    state = near_call(list_2, q_all, (up3, dn3), state, "far_pages")
-    own, p1, p2, p3 = far_call(list_3, q_all, (opposite,), state)
+    q_all, list_far, *state = near_call(maps, local, *sents, up1, dn1, up2, dn2)
+    own, p1, p2, p3 = far_call(list_far, q_all, (up3, dn3, opposite), state)
     back = [lax.ppermute(p, "rep", group_perm(r)) for r, p in ((3, p3), (2, p2), (1, p1))]
     width = out_weight.shape[1]
     attn = pl.pallas_call(

time: 83.5 us -> 78.1 us (0.935)
  the two profiles are of different devices: /device:TPU:2 before, /device:TPU:6 now
where the time goes in v3:
time: 78.1 us; the launch traced here: 77.8 us
  starting transfers between devices  33.1 us (42%)
  waiting for transfers between devices  24.8 us (32%)
  Pallas kernels  14.2 us (18%)
  matrix products  3.34 us (4%)
  local copies, waits for them, and re-layouts  1.11 us (1%)
  other arithmetic  1.04 us (1%)
    ppermute x7, starting transfers between devices, on_device(): lax.ppermute(parts[k], 'head', [(i, i ^ k) for i in range(8)])  12.5 us
    ppermute x7, waiting for transfers between devices, on_device(): lax.ppermute(parts[k], 'head', [(i, i ^ k) for i in range(8)])  8.66 us
    ppermute x3, waiting for transfers between devices, on_device(): lax.ppermute(p, 'rep', group_perm(r))  7.36 us
    pallas_call x1, Pallas kernels, near_call(): pl.pallas_call(near_kernel, out_shape=[jax.ShapeDtypeStruct((SESS * QROWS...  7.01 us
    ppermute x1, waiting for transfers between devices, on_device(): up1 = lax.ppermute(kv, 'rep', z_perm(1))  6.22 us
    ppermute x1, starting transfers between devices, on_device(): dn1 = lax.ppermute(kv, 'rep', z_perm(-1))  4.03 us
    pallas_call x1, Pallas kernels, far_call(): pl.pallas_call(functools.partial(far_kernel, nb), out_shape=[jax.ShapeDty...  3.47 us
    ppermute x3, starting transfers between devices, on_device(): sents = [lax.ppermute(sent, 'rep', group_perm(r)) for r in (1, 2, 3)]  3.46 us
  transfers between devices with their start and end apart: 20, of which 9 were waited for; matrix products, arithmetic and copies ran while one was open for 0% of the time, Pallas kernels for 12%

profile of v3, /device:TPU:6, one launch (start us, length us, event | category | flops | bytes accessed | tf_op | source)
XLA Modules:
  0.0 77.8 jit_solution(1738406911758084959)
XLA Ops:
  1.0 2.0 %collective-permute-start.3 = (bf16[1024,128]{1,0:T(8,128)(2,1)S(1)}, bf16[1024,128]{1,0:T(8,128)(2,1)S(1)}, u32[]{:S(2)}, u32[]{:S(2)}) collective-permute-start(bf16[1024,128]{1,0:T(8,128)(2,1)S(1)} %bitcast.10), channel_id=1, source_target_pairs={{0,16},{8,24},{16,32},{24,40},{32,48},{40,56},{48,64},{56,72},{64,... | collective-permute-start | bytes 786440 | tf_op jit(solution)/shard_map/ppermute | solution.py:341
  3.0 4.0 %collective-permute-start.4 = (bf16[1024,128]{1,0:T(8,128)(2,1)S(1)}, bf16[1024,128]{1,0:T(8,128)(2,1)S(1)}, u32[]{:S(2)}, u32[]{:S(2)}) collective-permute-start(bf16[1024,128]{1,0:T(8,128)(2,1)S(1)} %bitcast.11), channel_id=1, source_target_pairs={{0,112},{8,120},{16,0},{24,8},{32,16},{40,24},{48,32},{56,40},{64,... | collective-permute-start | bytes 786440 | tf_op jit(solution)/shard_map/ppermute | solution.py:342
  7.0 6.2 %collective-permute-done.3.up1 = bf16[1024,128]{1,0:T(8,128)(2,1)S(1)} collective-permute-done((bf16[1024,128]{1,0:T(8,128)(2,1)S(1)}, bf16[1024,128]{1,0:T(8,128)(2,1)S(1)}, u32[]{:S(2)}, u32[]{:S(2)}) %collective-permute-start.3) | collective-permute-done | bytes 262176 | tf_op jit(solution)/shard_map/ppermute | solution.py:341
  13.3 3.2 %collective-permute-start.6 = (bf16[1024,128]{1,0:T(8,128)(2,1)S(1)}, bf16[1024,128]{1,0:T(8,128)(2,1)S(1)}, u32[]{:S(2)}, u32[]{:S(2)}) collective-permute-start(bf16[1024,128]{1,0:T(8,128)(2,1)S(1)} %collective-permute-done.4.dn1), channel_id=1, source_target_pairs={{0,112},{8,120},{16,0},{24,8},{32,16},{40,24},{48,32},{56,40},{64,... | collective-permute-start | bytes 786440 | tf_op jit(solution)/shard_map/ppermute | solution.py:344
  16.5 2.7 %pack.1 = (bf16[528,128]{1,0:T(8,128)(2,1)}, bf16[1808,128]{1,0:T(8,128)(2,1)}) custom-call(bf16[512,128]{1,0:T(8,128)(2,1)} %bitcast.15, bf16[128,128]{1,0:T(8,128)(2,1)} %bitcast.16, bf16[128,128]{1,0:T(8,128)(2,1)} %bitcast.17, bf16[512,128]{1,0:T(8,128)(2,1)} %bitcast.13, bf16[512,128]{1,0:T(8,128)(2,1)} %bitcast.14, s32[2,16]{1,0:T(2,128)} %table.1, ...), custom_call_target="tpu_custom_call" | custom-call | tf_op jit(solution)/shard_map/pack/pallas_call | solution.py:345
  19.3 1.5 %collective-permute-start.1 = (bf16[528,128]{1,0:T(8,128)(2,1)}, bf16[528,128]{1,0:T(8,128)(2,1)S(1)}, u32[]{:S(2)}, u32[]{:S(2)}) collective-permute-start(bf16[528,128]{1,0:T(8,128)(2,1)} %get-tuple-element.17), channel_id=1, source_target_pairs={{0,128},{8,136},{16,144},{24,152},{32,160},{40,168},{48,176},{56,1... | collective-permute-start | bytes 405512 | tf_op jit(solution)/shard_map/ppermute | solution.py:361
  20.8 1.9 %collective-permute-start.2 = (bf16[528,128]{1,0:T(8,128)(2,1)}, bf16[528,128]{1,0:T(8,128)(2,1)S(1)}, u32[]{:S(2)}, u32[]{:S(2)}) collective-permute-start(bf16[528,128]{1,0:T(8,128)(2,1)} %get-tuple-element.17), channel_id=1, source_target_pairs={{0,136},{8,128},{16,152},{24,144},{32,168},{40,160},{48,184},{56,1... | collective-permute-start | bytes 405512 | tf_op jit(solution)/shard_map/ppermute | solution.py:361
  22.7 1.2 %collective-permute-start.9 = (bf16[1024,128]{1,0:T(8,128)(2,1)S(1)}, bf16[1024,128]{1,0:T(8,128)(2,1)S(1)}, u32[]{:S(2)}, u32[]{:S(2)}) collective-permute-start(bf16[1024,128]{1,0:T(8,128)(2,1)S(1)} %broadcast_select_fusion), channel_id=1, source_target_pairs={{0,32},{8,104},{16,48},{24,120},{32,64},{40,8},{48,80},{56,24},{64... | collective-permute-start | bytes 786440 | tf_op jit(solution)/shard_map/ppermute | solution.py:365
  23.9 3.0 %collective-permute-start.7 = (bf16[1024,128]{1,0:T(8,128)(2,1)S(1)}, bf16[1024,128]{1,0:T(8,128)(2,1)S(1)}, u32[]{:S(2)}, u32[]{:S(2)}) collective-permute-start(bf16[1024,128]{1,0:T(8,128)(2,1)S(1)} %collective-permute-done.5.up2), channel_id=1, source_target_pairs={{0,16},{8,24},{16,32},{24,40},{32,48},{40,56},{48,64},{56,72},{64,... | collective-permute-start | bytes 786440 | tf_op jit(solution)/shard_map/ppermute | solution.py:362
  27.5 1.9 %collective-permute-done.2.s3 = bf16[528,128]{1,0:T(8,128)(2,1)S(1)} collective-permute-done((bf16[528,128]{1,0:T(8,128)(2,1)}, bf16[528,128]{1,0:T(8,128)(2,1)S(1)}, u32[]{:S(2)}, u32[]{:S(2)}) %collective-permute-start.2) | collective-permute-done | bytes 135200 | tf_op jit(solution)/shard_map/ppermute | solution.py:361
  29.4 1.0 %copy-done = bf16[1808,128]{1,0:T(8,128)(2,1)S(1)} copy-done((bf16[1808,128]{1,0:T(8,128)(2,1)S(1)}, bf16[1808,128]{1,0:T(8,128)(2,1)}, u32[]{:S(2)}) %copy-start) | copy-done | bytes 462872
  30.5 7.0 %near_pages.1 = (bf16[2048,128]{1,0:T(8,128)(2,1)S(1)}, s32[160]{0:T(256)S(1)}, f32[8,1,256]{2,1,0:T(1,128)S(1)}, f32[8,1,256]{2,1,0:T(1,128)S(1)}, f32[8,128,256]{2,1,0:T(8,128)S(1)}) custom-call(s32[32]{0:T(128)S(1)} %and_select_fusion.7.maps, bf16[1808,128]{1,0:T(8,128)(2,1)S(1)} %copy-done, bf16[528,128]{1,0:T(8,128)(2,1)S(1)} %collective-permute-done.s1, ...), custom_call_target="tpu_custom_call" | custom-call | flops 4000000000 | bytes 4194304 | tf_op jit(solution)/shard_map/near_pages/pallas_call | solution.py:295
  37.8 3.5 %far_pages.1 = (f32[136,512]{1,0:T(8,128)S(1)}, bf16[144,512]{1,0:T(8,128)(2,1)S(1)}, bf16[144,512]{1,0:T(8,128)(2,1)S(1)}, bf16[144,512]{1,0:T(8,128)(2,1)S(1)}) custom-call(s32[160]{0:T(256)S(1)} %get-tuple-element.18.refs_0_, bf16[2048,128]{1,0:T(8,128)(2,1)S(1)} %get-tuple-element.19.refs_1_, bf16[1024,128]{1,0:T(8,128)(2,1)S(1)} %collective-permute-done.7.refs_2_, ...), custom_call_target="tpu_custom_call" | custom-call | flops 1000000000 | bytes 4194304 | tf_op jit(solution)/shard_map/far_pages/pallas_call | solution.py:319
  42.2 2.1 %collective-permute-start.11 = (bf16[144,512]{1,0:T(8,128)(2,1)S(1)}, bf16[144,512]{1,0:T(8,128)(2,1)S(1)}, u32[]{:S(2)}, u32[]{:S(2)}) collective-permute-start(bf16[144,512]{1,0:T(8,128)(2,1)S(1)} %get-tuple-element.25), channel_id=1, source_target_pairs={{0,128},{8,136},{16,144},{24,152},{32,160},{40,168},{48,176},{56,1... | collective-permute-start | bytes 442376 | tf_op jit(solution)/shard_map/ppermute | solution.py:378
  44.7 4.3 %collective-permute-done.10.p1 = bf16[144,512]{1,0:T(8,128)(2,1)S(1)} collective-permute-done((bf16[144,512]{1,0:T(8,128)(2,1)S(1)}, bf16[144,512]{1,0:T(8,128)(2,1)S(1)}, u32[]{:S(2)}, u32[]{:S(2)}) %collective-permute-start.10) | collective-permute-done | bytes 147488 | tf_op jit(solution)/shard_map/ppermute | solution.py:378
  49.0 3.1 %collective-permute-done.11.p2 = bf16[144,512]{1,0:T(8,128)(2,1)S(1)} collective-permute-done((bf16[144,512]{1,0:T(8,128)(2,1)S(1)}, bf16[144,512]{1,0:T(8,128)(2,1)S(1)}, u32[]{:S(2)}, u32[]{:S(2)}) %collective-permute-start.11) | collective-permute-done | bytes 147488 | tf_op jit(solution)/shard_map/ppermute | solution.py:378
  52.3 3.3 %convolution_convert_fusion = bf16[128,5120]{1,0:T(8,128)(2,1)S(1)} fusion(bf16[128,512]{1,0:T(8,128)(2,1)S(1)} %combine.1, bf16[512,5120]{1,0:T(8,128)(2,1)} %param.15), kind=kOutput, calls=%fused_computation | convolution fusion | flops 671744000 | bytes 6684672 | tf_op jit(solution)/shard_map/dot_general | solution.py:390
  55.8 1.7 %collective-permute-start.13 = (bf16[16,5120]{1,0:T(8,128)(2,1)S(1)}, bf16[16,5120]{1,0:T(8,128)(2,1)S(1)}, u32[]{:S(2)}, u32[]{:S(2)}) collective-permute-start(bf16[16,5120]{1,0:T(8,128)(2,1)S(1)} %get-tuple-element.33), channel_id=1, source_target_pairs={{0,1},{1,0},{2,3},{3,2},{4,5},{5,4},{6,7},{7,6},{8,9},{9,8},{10,11... | collective-permute-start | bytes 491528 | tf_op jit(solution)/shard_map/ppermute | solution.py:392
  57.4 2.2 %collective-permute-start.14 = (bf16[16,5120]{1,0:T(8,128)(2,1)S(1)}, bf16[16,5120]{1,0:T(8,128)(2,1)S(1)}, u32[]{:S(2)}, u32[]{:S(2)}) collective-permute-start(bf16[16,5120]{1,0:T(8,128)(2,1)S(1)} %get-tuple-element.32), channel_id=1, source_target_pairs={{0,3},{1,2},{2,1},{3,0},{4,7},{5,6},{6,5},{7,4},{8,11},{9,10},{10,... | collective-permute-start | bytes 491528 | tf_op jit(solution)/shard_map/ppermute | solution.py:392
  61.2 1.8 %collective-permute-start.17 = (bf16[16,5120]{1,0:T(8,128)(2,1)S(1)}, bf16[16,5120]{1,0:T(8,128)(2,1)S(1)}, u32[]{:S(2)}, u32[]{:S(2)}) collective-permute-start(bf16[16,5120]{1,0:T(8,128)(2,1)S(1)} %get-tuple-element.29), channel_id=1, source_target_pairs={{0,5},{1,4},{2,7},{3,6},{4,1},{5,0},{6,3},{7,2},{8,13},{9,12},{10,... | collective-permute-start | bytes 491528 | tf_op jit(solution)/shard_map/ppermute | solution.py:392
  63.0 2.6 %collective-permute-start.18 = (bf16[16,5120]{1,0:T(8,128)(2,1)S(1)}, bf16[16,5120]{1,0:T(8,128)(2,1)S(1)}, u32[]{:S(2)}, u32[]{:S(2)}) collective-permute-start(bf16[16,5120]{1,0:T(8,128)(2,1)S(1)} %get-tuple-element.28), channel_id=1, source_target_pairs={{0,7},{1,6},{2,5},{3,4},{4,3},{5,2},{6,1},{7,0},{8,15},{9,14},{10,... | collective-permute-start | bytes 491528 | tf_op jit(solution)/shard_map/ppermute | solution.py:392
  66.4 2.7 %collective-permute-start.19 = (bf16[16,5120]{1,0:T(8,128)(2,1)S(1)}, bf16[16,5120]{1,0:T(8,128)(2,1)S(1)}, u32[]{:S(2)}, u32[]{:S(2)}) collective-permute-start(bf16[16,5120]{1,0:T(8,128)(2,1)S(1)} %get-tuple-element.27), channel_id=1, source_target_pairs={{0,6},{1,7},{2,4},{3,5},{4,2},{5,3},{6,0},{7,1},{8,14},{9,15},{10,... | collective-permute-start | bytes 491528 | tf_op jit(solution)/shard_map/ppermute | solution.py:392
  69.1 6.1 %collective-permute-done.16.refs_4_ = bf16[16,5120]{1,0:T(8,128)(2,1)S(1)} collective-permute-done((bf16[16,5120]{1,0:T(8,128)(2,1)S(1)}, bf16[16,5120]{1,0:T(8,128)(2,1)S(1)}, u32[]{:S(2)}, u32[]{:S(2)}) %collective-permute-start.16) | collective-permute-done | bytes 163872 | tf_op jit(solution)/shard_map/ppermute | solution.py:392
  75.2 1.7 %collective-permute-done.19.refs_7_ = bf16[16,5120]{1,0:T(8,128)(2,1)S(1)} collective-permute-done((bf16[16,5120]{1,0:T(8,128)(2,1)S(1)}, bf16[16,5120]{1,0:T(8,128)(2,1)S(1)}, u32[]{:S(2)}, u32[]{:S(2)}) %collective-permute-start.19) | collective-permute-done | bytes 163872 | tf_op jit(solution)/shard_map/ppermute | solution.py:392
  (30 shorter events, 6.9 us)
Async XLA Ops:
  1.0 15.5 %copy-start.1 = (bf16[8,1,128,128]{3,2,1,0:T(8,128)(2,1)}, bf16[8,1,128,128]{3,2,1,0:T(8,128)(2,1)S(1)}, u32[]{:S(2)}) copy-start(bf16[8,1,128,128]{3,2,1,0:T(8,128)(2,1)S(1)} %pad_maximum_fusion) | copy-start | bytes 786436
  1.0 12.2 %collective-permute-start.3 = (bf16[1024,128]{1,0:T(8,128)(2,1)S(1)}, bf16[1024,128]{1,0:T(8,128)(2,1)S(1)}, u32[]{:S(2)}, u32[]{:S(2)}) collective-permute-start(bf16[1024,128]{1,0:T(8,128)(2,1)S(1)} %bitcast.10), channel_id=1, source_target_pairs={{0,16},{8,24},{16,32},{24,40},{32,48},{40,56},{48,64},{56,72},{64,... | collective-permute-start | bytes 786440 | tf_op jit(solution)/shard_map/ppermute | solution.py:341
  3.0 10.2 %collective-permute-start.4 = (bf16[1024,128]{1,0:T(8,128)(2,1)S(1)}, bf16[1024,128]{1,0:T(8,128)(2,1)S(1)}, u32[]{:S(2)}, u32[]{:S(2)}) collective-permute-start(bf16[1024,128]{1,0:T(8,128)(2,1)S(1)} %bitcast.11), channel_id=1, source_target_pairs={{0,112},{8,120},{16,0},{24,8},{32,16},{40,24},{48,32},{56,40},{64,... | collective-permute-start | bytes 786440 | tf_op jit(solution)/shard_map/ppermute | solution.py:342
  13.2 9.4 %collective-permute-start.5 = (bf16[1024,128]{1,0:T(8,128)(2,1)S(1)}, bf16[1024,128]{1,0:T(8,128)(2,1)S(1)}, u32[]{:S(2)}, u32[]{:S(2)}) collective-permute-start(bf16[1024,128]{1,0:T(8,128)(2,1)S(1)} %collective-permute-done.3.up1), channel_id=1, source_target_pairs={{0,16},{8,24},{16,32},{24,40},{32,48},{40,56},{48,64},{56,72},{64,... | collective-permute-start | bytes 786440 | tf_op jit(solution)/shard_map/ppermute | solution.py:343
  13.3 9.4 %collective-permute-start.6 = (bf16[1024,128]{1,0:T(8,128)(2,1)S(1)}, bf16[1024,128]{1,0:T(8,128)(2,1)S(1)}, u32[]{:S(2)}, u32[]{:S(2)}) collective-permute-start(bf16[1024,128]{1,0:T(8,128)(2,1)S(1)} %collective-permute-done.4.dn1), channel_id=1, source_target_pairs={{0,112},{8,120},{16,0},{24,8},{32,16},{40,24},{48,32},{56,40},{64,... | collective-permute-start | bytes 786440 | tf_op jit(solution)/shard_map/ppermute | solution.py:344
  19.2 7.7 %collective-permute-start = (bf16[528,128]{1,0:T(8,128)(2,1)}, bf16[528,128]{1,0:T(8,128)(2,1)S(1)}, u32[]{:S(2)}, u32[]{:S(2)}) collective-permute-start(bf16[528,128]{1,0:T(8,128)(2,1)} %get-tuple-element.17), channel_id=1, source_target_pairs={{0,8},{8,0},{16,24},{24,16},{32,40},{40,32},{48,56},{56,48},{64,72... | collective-permute-start | bytes 405512 | tf_op jit(solution)/shard_map/ppermute | solution.py:361
  19.3 8.2 %collective-permute-start.1 = (bf16[528,128]{1,0:T(8,128)(2,1)}, bf16[528,128]{1,0:T(8,128)(2,1)S(1)}, u32[]{:S(2)}, u32[]{:S(2)}) collective-permute-start(bf16[528,128]{1,0:T(8,128)(2,1)} %get-tuple-element.17), channel_id=1, source_target_pairs={{0,128},{8,136},{16,144},{24,152},{32,160},{40,168},{48,176},{56,1... | collective-permute-start | bytes 405512 | tf_op jit(solution)/shard_map/ppermute | solution.py:361
  20.8 8.6 %collective-permute-start.2 = (bf16[528,128]{1,0:T(8,128)(2,1)}, bf16[528,128]{1,0:T(8,128)(2,1)S(1)}, u32[]{:S(2)}, u32[]{:S(2)}) collective-permute-start(bf16[528,128]{1,0:T(8,128)(2,1)} %get-tuple-element.17), channel_id=1, source_target_pairs={{0,136},{8,128},{16,152},{24,144},{32,168},{40,160},{48,184},{56,1... | collective-permute-start | bytes 405512 | tf_op jit(solution)/shard_map/ppermute | solution.py:361
  22.7 14.7 %collective-permute-start.9 = (bf16[1024,128]{1,0:T(8,128)(2,1)S(1)}, bf16[1024,128]{1,0:T(8,128)(2,1)S(1)}, u32[]{:S(2)}, u32[]{:S(2)}) collective-permute-start(bf16[1024,128]{1,0:T(8,128)(2,1)S(1)} %broadcast_select_fusion), channel_id=1, source_target_pairs={{0,32},{8,104},{16,48},{24,120},{32,64},{40,8},{48,80},{56,24},{64... | collective-permute-start | bytes 786440 | tf_op jit(solution)/shard_map/ppermute | solution.py:365
  23.9 13.9 %collective-permute-start.7 = (bf16[1024,128]{1,0:T(8,128)(2,1)S(1)}, bf16[1024,128]{1,0:T(8,128)(2,1)S(1)}, u32[]{:S(2)}, u32[]{:S(2)}) collective-permute-start(bf16[1024,128]{1,0:T(8,128)(2,1)S(1)} %collective-permute-done.5.up2), channel_id=1, source_target_pairs={{0,16},{8,24},{16,32},{24,40},{32,48},{40,56},{48,64},{56,72},{64,... | collective-permute-start | bytes 786440 | tf_op jit(solution)/shard_map/ppermute | solution.py:362
  26.9 10.9 %collective-permute-start.8 = (bf16[1024,128]{1,0:T(8,128)(2,1)S(1)}, bf16[1024,128]{1,0:T(8,128)(2,1)S(1)}, u32[]{:S(2)}, u32[]{:S(2)}) collective-permute-start(bf16[1024,128]{1,0:T(8,128)(2,1)S(1)} %collective-permute-done.6.dn2), channel_id=1, source_target_pairs={{0,112},{8,120},{16,0},{24,8},{32,16},{40,24},{48,32},{56,40},{64,... | collective-permute-start | bytes 786440 | tf_op jit(solution)/shard_map/ppermute | solution.py:363
  29.4 1.0 %copy-start = (bf16[1808,128]{1,0:T(8,128)(2,1)S(1)}, bf16[1808,128]{1,0:T(8,128)(2,1)}, u32[]{:S(2)}) copy-start(bf16[1808,128]{1,0:T(8,128)(2,1)} %get-tuple-element.16.local) | copy-start | bytes 1388548
  41.3 7.7 %collective-permute-start.10 = (bf16[144,512]{1,0:T(8,128)(2,1)S(1)}, bf16[144,512]{1,0:T(8,128)(2,1)S(1)}, u32[]{:S(2)}, u32[]{:S(2)}) collective-permute-start(bf16[144,512]{1,0:T(8,128)(2,1)S(1)} %get-tuple-element.24), channel_id=1, source_target_pairs={{0,136},{8,128},{16,152},{24,144},{32,168},{40,160},{48,184},{56,1... | collective-permute-start | bytes 442376 | tf_op jit(solution)/shard_map/ppermute | solution.py:378
  42.2 9.9 %collective-permute-start.11 = (bf16[144,512]{1,0:T(8,128)(2,1)S(1)}, bf16[144,512]{1,0:T(8,128)(2,1)S(1)}, u32[]{:S(2)}, u32[]{:S(2)}) collective-permute-start(bf16[144,512]{1,0:T(8,128)(2,1)S(1)} %get-tuple-element.25), channel_id=1, source_target_pairs={{0,128},{8,136},{16,144},{24,152},{32,160},{40,168},{48,176},{56,1... | collective-permute-start | bytes 442376 | tf_op jit(solution)/shard_map/ppermute | solution.py:378
  44.3 7.8 %collective-permute-start.12 = (bf16[144,512]{1,0:T(8,128)(2,1)S(1)}, bf16[144,512]{1,0:T(8,128)(2,1)S(1)}, u32[]{:S(2)}, u32[]{:S(2)}) collective-permute-start(bf16[144,512]{1,0:T(8,128)(2,1)S(1)} %get-tuple-element.26), channel_id=1, source_target_pairs={{0,8},{8,0},{16,24},{24,16},{32,40},{40,32},{48,56},{56,48},{64,72... | collective-permute-start | bytes 442376 | tf_op jit(solution)/shard_map/ppermute | solution.py:378
  55.8 7.2 %collective-permute-start.13 = (bf16[16,5120]{1,0:T(8,128)(2,1)S(1)}, bf16[16,5120]{1,0:T(8,128)(2,1)S(1)}, u32[]{:S(2)}, u32[]{:S(2)}) collective-permute-start(bf16[16,5120]{1,0:T(8,128)(2,1)S(1)} %get-tuple-element.33), channel_id=1, source_target_pairs={{0,1},{1,0},{2,3},{3,2},{4,5},{5,4},{6,7},{7,6},{8,9},{9,8},{10,11... | collective-permute-start | bytes 491528 | tf_op jit(solution)/shard_map/ppermute | solution.py:392
  57.4 8.9 %collective-permute-start.14 = (bf16[16,5120]{1,0:T(8,128)(2,1)S(1)}, bf16[16,5120]{1,0:T(8,128)(2,1)S(1)}, u32[]{:S(2)}, u32[]{:S(2)}) collective-permute-start(bf16[16,5120]{1,0:T(8,128)(2,1)S(1)} %get-tuple-element.32), channel_id=1, source_target_pairs={{0,3},{1,2},{2,1},{3,0},{4,7},{5,6},{6,5},{7,4},{8,11},{9,10},{10,... | collective-permute-start | bytes 491528 | tf_op jit(solution)/shard_map/ppermute | solution.py:392
  59.6 9.5 %collective-permute-start.15 = (bf16[16,5120]{1,0:T(8,128)(2,1)S(1)}, bf16[16,5120]{1,0:T(8,128)(2,1)S(1)}, u32[]{:S(2)}, u32[]{:S(2)}) collective-permute-start(bf16[16,5120]{1,0:T(8,128)(2,1)S(1)} %get-tuple-element.31), channel_id=1, source_target_pairs={{0,4},{1,5},{2,6},{3,7},{4,0},{5,1},{6,2},{7,3},{8,12},{9,13},{10,... | collective-permute-start | bytes 491528 | tf_op jit(solution)/shard_map/ppermute | solution.py:392
  60.4 14.8 %collective-permute-start.16 = (bf16[16,5120]{1,0:T(8,128)(2,1)S(1)}, bf16[16,5120]{1,0:T(8,128)(2,1)S(1)}, u32[]{:S(2)}, u32[]{:S(2)}) collective-permute-start(bf16[16,5120]{1,0:T(8,128)(2,1)S(1)} %get-tuple-element.30), channel_id=1, source_target_pairs={{0,2},{1,3},{2,0},{3,1},{4,6},{5,7},{6,4},{7,5},{8,10},{9,11},{10,... | collective-permute-start | bytes 491528 | tf_op jit(solution)/shard_map/ppermute | solution.py:392
  61.2 14.1 %collective-permute-start.17 = (bf16[16,5120]{1,0:T(8,128)(2,1)S(1)}, bf16[16,5120]{1,0:T(8,128)(2,1)S(1)}, u32[]{:S(2)}, u32[]{:S(2)}) collective-permute-start(bf16[16,5120]{1,0:T(8,128)(2,1)S(1)} %get-tuple-element.29), channel_id=1, source_target_pairs={{0,5},{1,4},{2,7},{3,6},{4,1},{5,0},{6,3},{7,2},{8,13},{9,12},{10,... | collective-permute-start | bytes 491528 | tf_op jit(solution)/shard_map/ppermute | solution.py:392
  63.0 12.2 %collective-permute-start.18 = (bf16[16,5120]{1,0:T(8,128)(2,1)S(1)}, bf16[16,5120]{1,0:T(8,128)(2,1)S(1)}, u32[]{:S(2)}, u32[]{:S(2)}) collective-permute-start(bf16[16,5120]{1,0:T(8,128)(2,1)S(1)} %get-tuple-element.28), channel_id=1, source_target_pairs={{0,7},{1,6},{2,5},{3,4},{4,3},{5,2},{6,1},{7,0},{8,15},{9,14},{10,... | collective-permute-start | bytes 491528 | tf_op jit(solution)/shard_map/ppermute | solution.py:392
  66.4 10.6 %collective-permute-start.19 = (bf16[16,5120]{1,0:T(8,128)(2,1)S(1)}, bf16[16,5120]{1,0:T(8,128)(2,1)S(1)}, u32[]{:S(2)}, u32[]{:S(2)}) collective-permute-start(bf16[16,5120]{1,0:T(8,128)(2,1)S(1)} %get-tuple-element.27), channel_id=1, source_target_pairs={{0,6},{1,7},{2,4},{3,5},{4,2},{5,3},{6,0},{7,1},{8,14},{9,15},{10,... | collective-permute-start | bytes 491528 | tf_op jit(solution)/shard_map/ppermute | solution.py:392

commit v4 on v3

--- a/solution.py
+++ b/solution.py
@@ -26,6 +26,9 @@
 
 STREAMS = 4
 GROUPS = ((0, -1, 1, -2, 2), (-3, 3, 4))
+
+
+HEADS = ((0, 0), (0, 1), (0, 3), (0, 2), (1, 0), (1, 1), (1, 3), (1, 2))
 
 
 def rep_of(xh, z, c):
@@ -258,8 +261,8 @@
     inv = 1.0 / sum(ws)
     mixed = sum(v * (w * inv) for v, w in zip(vals, ws))
     rows_f32[...] = mixed.T
-    for k in range(8):
-        first = (head_ref[0] ^ k) * 64
+    for k, (dx, dy) in enumerate(HEADS):
+        first = ((head_ref[0] & 4) ^ (dx * 4)) * 64 + ((head_ref[0] + dy) & 3) * 64
         for h in range(4):
             block = rows_f32[pl.ds(first + h, 16, stride=4), :]
             attn[pl.ds(k * 16, 16), pl.ds(h * HD, HD)] = block.astype(BF)
@@ -389,7 +392,10 @@
     )(head.reshape(1).astype(jnp.int32), own, *back)
     rows = jnp.dot(attn, out_weight, preferred_element_type=F32).astype(BF)
     parts = [rows[k * 16:(k + 1) * 16] for k in range(8)]
-    terms = [lax.ppermute(parts[k], "head", [(i, i ^ k) for i in range(8)]) for k in (1, 3, 4, 2, 5, 7, 6)]
+    terms = [
+        lax.ppermute(part, "head", [(i, ((i & 4) ^ (dx * 4)) + ((i + dy) & 3)) for i in range(8)])
+        for part, (dx, dy) in zip(parts[1:], HEADS[1:])
+    ]
     return pl.pallas_call(
         sum_kernel,
         out_shape=jax.ShapeDtypeStruct((16, width), BF),

time: 78.1 us -> 78.9 us (1.010)
  the two profiles are of different devices: /device:TPU:6 before, /device:TPU:2 now
where the time goes in v4:
time: 78.9 us; the launch traced here: 77.9 us
  starting transfers between devices  32.6 us (41%)
  waiting for transfers between devices  25.9 us (33%)
  Pallas kernels  13.7 us (17%)
  matrix products  3.34 us (4%)
  local copies, waits for them, and re-layouts  1.11 us (1%)
  other arithmetic  1.04 us (1%)
    ppermute x7, starting transfers between devices, on_device(): lax.ppermute(part, 'head', [(i, (i & 4 ^ dx * 4) + (i + dy & 3)) for i in...  12 us
    ppermute x7, waiting for transfers between devices, on_device(): lax.ppermute(part, 'head', [(i, (i & 4 ^ dx * 4) + (i + dy & 3)) for i in...  9.98 us
    pallas_call x1, Pallas kernels, near_call(): pl.pallas_call(near_kernel, out_shape=[jax.ShapeDtypeStruct((SESS * QROWS...  7.49 us
    ppermute x3, waiting for transfers between devices, on_device(): lax.ppermute(p, 'rep', group_perm(r))  7.45 us
    ppermute x1, waiting for transfers between devices, on_device(): up1 = lax.ppermute(kv, 'rep', z_perm(1))  6.22 us
    ppermute x1, starting transfers between devices, on_device(): dn1 = lax.ppermute(kv, 'rep', z_perm(-1))  4.03 us
    ppermute x3, starting transfers between devices, on_device(): sents = [lax.ppermute(sent, 'rep', group_perm(r)) for r in (1, 2, 3)]  3.46 us
    ppermute x3, starting transfers between devices, on_device(): lax.ppermute(p, 'rep', group_perm(r))  3.45 us
  transfers between devices with their start and end apart: 20, of which 9 were waited for; matrix products, arithmetic and copies ran while one was open for 0% of the time, Pallas kernels for 13%

profile of v4, /device:TPU:2, one launch (start us, length us, event | category | flops | bytes accessed | tf_op | source)
XLA Modules:
  0.0 77.9 jit_solution(4279335792158794140)
XLA Ops:
  1.0 2.0 %collective-permute-start.3 = (bf16[1024,128]{1,0:T(8,128)(2,1)S(1)}, bf16[1024,128]{1,0:T(8,128)(2,1)S(1)}, u32[]{:S(2)}, u32[]{:S(2)}) collective-permute-start(bf16[1024,128]{1,0:T(8,128)(2,1)S(1)} %bitcast.10), channel_id=1, source_target_pairs={{0,16},{8,24},{16,32},{24,40},{32,48},{40,56},{48,64},{56,72},{64,... | collective-permute-start | bytes 786440 | tf_op jit(solution)/shard_map/ppermute | solution.py:344
  3.0 4.0 %collective-permute-start.4 = (bf16[1024,128]{1,0:T(8,128)(2,1)S(1)}, bf16[1024,128]{1,0:T(8,128)(2,1)S(1)}, u32[]{:S(2)}, u32[]{:S(2)}) collective-permute-start(bf16[1024,128]{1,0:T(8,128)(2,1)S(1)} %bitcast.11), channel_id=1, source_target_pairs={{0,112},{8,120},{16,0},{24,8},{32,16},{40,24},{48,32},{56,40},{64,... | collective-permute-start | bytes 786440 | tf_op jit(solution)/shard_map/ppermute | solution.py:345
  7.0 6.2 %collective-permute-done.3.up1 = bf16[1024,128]{1,0:T(8,128)(2,1)S(1)} collective-permute-done((bf16[1024,128]{1,0:T(8,128)(2,1)S(1)}, bf16[1024,128]{1,0:T(8,128)(2,1)S(1)}, u32[]{:S(2)}, u32[]{:S(2)}) %collective-permute-start.3) | collective-permute-done | bytes 262176 | tf_op jit(solution)/shard_map/ppermute | solution.py:344
  13.3 3.2 %collective-permute-start.6 = (bf16[1024,128]{1,0:T(8,128)(2,1)S(1)}, bf16[1024,128]{1,0:T(8,128)(2,1)S(1)}, u32[]{:S(2)}, u32[]{:S(2)}) collective-permute-start(bf16[1024,128]{1,0:T(8,128)(2,1)S(1)} %collective-permute-done.4.dn1), channel_id=1, source_target_pairs={{0,112},{8,120},{16,0},{24,8},{32,16},{40,24},{48,32},{56,40},{64,... | collective-permute-start | bytes 786440 | tf_op jit(solution)/shard_map/ppermute | solution.py:347
  16.5 2.7 %pack.1 = (bf16[528,128]{1,0:T(8,128)(2,1)}, bf16[1808,128]{1,0:T(8,128)(2,1)}) custom-call(bf16[512,128]{1,0:T(8,128)(2,1)} %bitcast.15, bf16[128,128]{1,0:T(8,128)(2,1)} %bitcast.16, bf16[128,128]{1,0:T(8,128)(2,1)} %bitcast.17, bf16[512,128]{1,0:T(8,128)(2,1)} %bitcast.13, bf16[512,128]{1,0:T(8,128)(2,1)} %bitcast.14, s32[2,16]{1,0:T(2,128)} %table.1, ...), custom_call_target="tpu_custom_call" | custom-call | tf_op jit(solution)/shard_map/pack/pallas_call | solution.py:348
  19.3 2.2 %collective-permute-start.1 = (bf16[528,128]{1,0:T(8,128)(2,1)}, bf16[528,128]{1,0:T(8,128)(2,1)S(1)}, u32[]{:S(2)}, u32[]{:S(2)}) collective-permute-start(bf16[528,128]{1,0:T(8,128)(2,1)} %get-tuple-element.17), channel_id=1, source_target_pairs={{0,128},{8,136},{16,144},{24,152},{32,160},{40,168},{48,176},{56,1... | collective-permute-start | bytes 405512 | tf_op jit(solution)/shard_map/ppermute | solution.py:364
  23.9 3.0 %collective-permute-start.7 = (bf16[1024,128]{1,0:T(8,128)(2,1)S(1)}, bf16[1024,128]{1,0:T(8,128)(2,1)S(1)}, u32[]{:S(2)}, u32[]{:S(2)}) collective-permute-start(bf16[1024,128]{1,0:T(8,128)(2,1)S(1)} %collective-permute-done.5.up2), channel_id=1, source_target_pairs={{0,16},{8,24},{16,32},{24,40},{32,48},{40,56},{48,64},{56,72},{64,... | collective-permute-start | bytes 786440 | tf_op jit(solution)/shard_map/ppermute | solution.py:365
  27.5 1.9 %collective-permute-done.2.s3 = bf16[528,128]{1,0:T(8,128)(2,1)S(1)} collective-permute-done((bf16[528,128]{1,0:T(8,128)(2,1)}, bf16[528,128]{1,0:T(8,128)(2,1)S(1)}, u32[]{:S(2)}, u32[]{:S(2)}) %collective-permute-start.2) | collective-permute-done | bytes 135200 | tf_op jit(solution)/shard_map/ppermute | solution.py:364
  30.5 7.5 %near_pages.1 = (bf16[2048,128]{1,0:T(8,128)(2,1)S(1)}, s32[160]{0:T(256)S(1)}, f32[8,1,256]{2,1,0:T(1,128)S(1)}, f32[8,1,256]{2,1,0:T(1,128)S(1)}, f32[8,128,256]{2,1,0:T(8,128)S(1)}) custom-call(s32[32]{0:T(128)S(1)} %and_select_fusion.7.maps, bf16[1808,128]{1,0:T(8,128)(2,1)S(1)} %copy-done, bf16[528,128]{1,0:T(8,128)(2,1)S(1)} %collective-permute-done.s1, ...), custom_call_target="tpu_custom_call" | custom-call | flops 4000000000 | bytes 4194304 | tf_op jit(solution)/shard_map/near_pages/pallas_call | solution.py:298
  38.0 2.5 %far_pages.1 = (f32[136,512]{1,0:T(8,128)S(1)}, bf16[144,512]{1,0:T(8,128)(2,1)S(1)}, bf16[144,512]{1,0:T(8,128)(2,1)S(1)}, bf16[144,512]{1,0:T(8,128)(2,1)S(1)}) custom-call(s32[160]{0:T(256)S(1)} %get-tuple-element.18.refs_0_, bf16[2048,128]{1,0:T(8,128)(2,1)S(1)} %get-tuple-element.19.refs_1_, bf16[1024,128]{1,0:T(8,128)(2,1)S(1)} %collective-permute-done.7.refs_2_, ...), custom_call_target="tpu_custom_call" | custom-call | flops 1000000000 | bytes 4194304 | tf_op jit(solution)/shard_map/far_pages/pallas_call | solution.py:322
  40.5 2.4 %collective-permute-start.10 = (bf16[144,512]{1,0:T(8,128)(2,1)S(1)}, bf16[144,512]{1,0:T(8,128)(2,1)S(1)}, u32[]{:S(2)}, u32[]{:S(2)}) collective-permute-start(bf16[144,512]{1,0:T(8,128)(2,1)S(1)} %get-tuple-element.24), channel_id=1, source_target_pairs={{0,136},{8,128},{16,152},{24,144},{32,168},{40,160},{48,184},{56,1... | collective-permute-start | bytes 442376 | tf_op jit(solution)/shard_map/ppermute | solution.py:381
  43.9 4.0 %collective-permute-done.10.p1 = bf16[144,512]{1,0:T(8,128)(2,1)S(1)} collective-permute-done((bf16[144,512]{1,0:T(8,128)(2,1)S(1)}, bf16[144,512]{1,0:T(8,128)(2,1)S(1)}, u32[]{:S(2)}, u32[]{:S(2)}) %collective-permute-start.10) | collective-permute-done | bytes 147488 | tf_op jit(solution)/shard_map/ppermute | solution.py:381
  47.9 3.5 %collective-permute-done.11.p2 = bf16[144,512]{1,0:T(8,128)(2,1)S(1)} collective-permute-done((bf16[144,512]{1,0:T(8,128)(2,1)S(1)}, bf16[144,512]{1,0:T(8,128)(2,1)S(1)}, u32[]{:S(2)}, u32[]{:S(2)}) %collective-permute-start.11) | collective-permute-done | bytes 147488 | tf_op jit(solution)/shard_map/ppermute | solution.py:381
  51.6 3.3 %convolution_convert_fusion = bf16[128,5120]{1,0:T(8,128)(2,1)S(1)} fusion(bf16[128,512]{1,0:T(8,128)(2,1)S(1)} %combine.1, bf16[512,5120]{1,0:T(8,128)(2,1)} %param.15), kind=kOutput, calls=%fused_computation | convolution fusion | flops 671744000 | bytes 6684672 | tf_op jit(solution)/shard_map/dot_general | solution.py:393
  55.1 1.7 %collective-permute-start.13 = (bf16[16,5120]{1,0:T(8,128)(2,1)S(1)}, bf16[16,5120]{1,0:T(8,128)(2,1)S(1)}, u32[]{:S(2)}, u32[]{:S(2)}) collective-permute-start(bf16[16,5120]{1,0:T(8,128)(2,1)S(1)} %get-tuple-element.33), channel_id=1, source_target_pairs={{0,1},{1,2},{2,3},{3,0},{4,5},{5,6},{6,7},{7,4},{8,9},{9,10},{10,1... | collective-permute-start | bytes 491528 | tf_op jit(solution)/shard_map/ppermute | solution.py:396
  56.7 1.7 %collective-permute-start.14 = (bf16[16,5120]{1,0:T(8,128)(2,1)S(1)}, bf16[16,5120]{1,0:T(8,128)(2,1)S(1)}, u32[]{:S(2)}, u32[]{:S(2)}) collective-permute-start(bf16[16,5120]{1,0:T(8,128)(2,1)S(1)} %get-tuple-element.32), channel_id=1, source_target_pairs={{0,3},{1,0},{2,1},{3,2},{4,7},{5,4},{6,5},{7,6},{8,11},{9,8},{10,9... | collective-permute-start | bytes 491528 | tf_op jit(solution)/shard_map/ppermute | solution.py:396
  58.4 2.0 %collective-permute-start.15 = (bf16[16,5120]{1,0:T(8,128)(2,1)S(1)}, bf16[16,5120]{1,0:T(8,128)(2,1)S(1)}, u32[]{:S(2)}, u32[]{:S(2)}) collective-permute-start(bf16[16,5120]{1,0:T(8,128)(2,1)S(1)} %get-tuple-element.31), channel_id=1, source_target_pairs={{0,2},{1,3},{2,0},{3,1},{4,6},{5,7},{6,4},{7,5},{8,10},{9,11},{10,... | collective-permute-start | bytes 491528 | tf_op jit(solution)/shard_map/ppermute | solution.py:396
  61.3 1.2 %collective-permute-start.17 = (bf16[16,5120]{1,0:T(8,128)(2,1)S(1)}, bf16[16,5120]{1,0:T(8,128)(2,1)S(1)}, u32[]{:S(2)}, u32[]{:S(2)}) collective-permute-start(bf16[16,5120]{1,0:T(8,128)(2,1)S(1)} %get-tuple-element.29), channel_id=1, source_target_pairs={{0,5},{1,6},{2,7},{3,4},{4,1},{5,2},{6,3},{7,0},{8,13},{9,14},{10,... | collective-permute-start | bytes 491528 | tf_op jit(solution)/shard_map/ppermute | solution.py:396
  62.5 3.1 %collective-permute-start.18 = (bf16[16,5120]{1,0:T(8,128)(2,1)S(1)}, bf16[16,5120]{1,0:T(8,128)(2,1)S(1)}, u32[]{:S(2)}, u32[]{:S(2)}) collective-permute-start(bf16[16,5120]{1,0:T(8,128)(2,1)S(1)} %get-tuple-element.28), channel_id=1, source_target_pairs={{0,7},{1,4},{2,5},{3,6},{4,3},{5,0},{6,1},{7,2},{8,15},{9,12},{10,... | collective-permute-start | bytes 491528 | tf_op jit(solution)/shard_map/ppermute | solution.py:396
  65.6 1.5 %collective-permute-start.19 = (bf16[16,5120]{1,0:T(8,128)(2,1)S(1)}, bf16[16,5120]{1,0:T(8,128)(2,1)S(1)}, u32[]{:S(2)}, u32[]{:S(2)}) collective-permute-start(bf16[16,5120]{1,0:T(8,128)(2,1)S(1)} %get-tuple-element.27), channel_id=1, source_target_pairs={{0,6},{1,7},{2,4},{3,5},{4,2},{5,3},{6,0},{7,1},{8,14},{9,15},{10,... | collective-permute-start | bytes 491528 | tf_op jit(solution)/shard_map/ppermute | solution.py:396
  67.1 2.4 %collective-permute-done.15.refs_3_ = bf16[16,5120]{1,0:T(8,128)(2,1)S(1)} collective-permute-done((bf16[16,5120]{1,0:T(8,128)(2,1)S(1)}, bf16[16,5120]{1,0:T(8,128)(2,1)S(1)}, u32[]{:S(2)}, u32[]{:S(2)}) %collective-permute-start.15) | collective-permute-done | bytes 163872 | tf_op jit(solution)/shard_map/ppermute | solution.py:396
  69.5 1.7 %collective-permute-done.17.refs_5_ = bf16[16,5120]{1,0:T(8,128)(2,1)S(1)} collective-permute-done((bf16[16,5120]{1,0:T(8,128)(2,1)S(1)}, bf16[16,5120]{1,0:T(8,128)(2,1)S(1)}, u32[]{:S(2)}, u32[]{:S(2)}) %collective-permute-start.17) | collective-permute-done | bytes 163872 | tf_op jit(solution)/shard_map/ppermute | solution.py:396
  71.2 3.1 %collective-permute-done.18.refs_6_ = bf16[16,5120]{1,0:T(8,128)(2,1)S(1)} collective-permute-done((bf16[16,5120]{1,0:T(8,128)(2,1)S(1)}, bf16[16,5120]{1,0:T(8,128)(2,1)S(1)}, u32[]{:S(2)}, u32[]{:S(2)}) %collective-permute-start.18) | collective-permute-done | bytes 163872 | tf_op jit(solution)/shard_map/ppermute | solution.py:396
  74.3 2.8 %collective-permute-done.19.refs_7_ = bf16[16,5120]{1,0:T(8,128)(2,1)S(1)} collective-permute-done((bf16[16,5120]{1,0:T(8,128)(2,1)S(1)}, bf16[16,5120]{1,0:T(8,128)(2,1)S(1)}, u32[]{:S(2)}, u32[]{:S(2)}) %collective-permute-start.19) | collective-permute-done | bytes 163872 | tf_op jit(solution)/shard_map/ppermute | solution.py:396
  (30 shorter events, 8.2 us)
Async XLA Ops:
  1.0 15.5 %copy-start.1 = (bf16[8,1,128,128]{3,2,1,0:T(8,128)(2,1)}, bf16[8,1,128,128]{3,2,1,0:T(8,128)(2,1)S(1)}, u32[]{:S(2)}) copy-start(bf16[8,1,128,128]{3,2,1,0:T(8,128)(2,1)S(1)} %pad_maximum_fusion) | copy-start | bytes 786436
  1.0 12.2 %collective-permute-start.3 = (bf16[1024,128]{1,0:T(8,128)(2,1)S(1)}, bf16[1024,128]{1,0:T(8,128)(2,1)S(1)}, u32[]{:S(2)}, u32[]{:S(2)}) collective-permute-start(bf16[1024,128]{1,0:T(8,128)(2,1)S(1)} %bitcast.10), channel_id=1, source_target_pairs={{0,16},{8,24},{16,32},{24,40},{32,48},{40,56},{48,64},{56,72},{64,... | collective-permute-start | bytes 786440 | tf_op jit(solution)/shard_map/ppermute | solution.py:344
  3.0 10.2 %collective-permute-start.4 = (bf16[1024,128]{1,0:T(8,128)(2,1)S(1)}, bf16[1024,128]{1,0:T(8,128)(2,1)S(1)}, u32[]{:S(2)}, u32[]{:S(2)}) collective-permute-start(bf16[1024,128]{1,0:T(8,128)(2,1)S(1)} %bitcast.11), channel_id=1, source_target_pairs={{0,112},{8,120},{16,0},{24,8},{32,16},{40,24},{48,32},{56,40},{64,... | collective-permute-start | bytes 786440 | tf_op jit(solution)/shard_map/ppermute | solution.py:345
  13.2 9.4 %collective-permute-start.5 = (bf16[1024,128]{1,0:T(8,128)(2,1)S(1)}, bf16[1024,128]{1,0:T(8,128)(2,1)S(1)}, u32[]{:S(2)}, u32[]{:S(2)}) collective-permute-start(bf16[1024,128]{1,0:T(8,128)(2,1)S(1)} %collective-permute-done.3.up1), channel_id=1, source_target_pairs={{0,16},{8,24},{16,32},{24,40},{32,48},{40,56},{48,64},{56,72},{64,... | collective-permute-start | bytes 786440 | tf_op jit(solution)/shard_map/ppermute | solution.py:346
  13.3 9.4 %collective-permute-start.6 = (bf16[1024,128]{1,0:T(8,128)(2,1)S(1)}, bf16[1024,128]{1,0:T(8,128)(2,1)S(1)}, u32[]{:S(2)}, u32[]{:S(2)}) collective-permute-start(bf16[1024,128]{1,0:T(8,128)(2,1)S(1)} %collective-permute-done.4.dn1), channel_id=1, source_target_pairs={{0,112},{8,120},{16,0},{24,8},{32,16},{40,24},{48,32},{56,40},{64,... | collective-permute-start | bytes 786440 | tf_op jit(solution)/shard_map/ppermute | solution.py:347
  19.2 7.7 %collective-permute-start = (bf16[528,128]{1,0:T(8,128)(2,1)}, bf16[528,128]{1,0:T(8,128)(2,1)S(1)}, u32[]{:S(2)}, u32[]{:S(2)}) collective-permute-start(bf16[528,128]{1,0:T(8,128)(2,1)} %get-tuple-element.17), channel_id=1, source_target_pairs={{0,8},{8,0},{16,24},{24,16},{32,40},{40,32},{48,56},{56,48},{64,72... | collective-permute-start | bytes 405512 | tf_op jit(solution)/shard_map/ppermute | solution.py:364
  19.3 8.2 %collective-permute-start.1 = (bf16[528,128]{1,0:T(8,128)(2,1)}, bf16[528,128]{1,0:T(8,128)(2,1)S(1)}, u32[]{:S(2)}, u32[]{:S(2)}) collective-permute-start(bf16[528,128]{1,0:T(8,128)(2,1)} %get-tuple-element.17), channel_id=1, source_target_pairs={{0,128},{8,136},{16,144},{24,152},{32,160},{40,168},{48,176},{56,1... | collective-permute-start | bytes 405512 | tf_op jit(solution)/shard_map/ppermute | solution.py:364
  21.5 7.9 %collective-permute-start.2 = (bf16[528,128]{1,0:T(8,128)(2,1)}, bf16[528,128]{1,0:T(8,128)(2,1)S(1)}, u32[]{:S(2)}, u32[]{:S(2)}) collective-permute-start(bf16[528,128]{1,0:T(8,128)(2,1)} %get-tuple-element.17), channel_id=1, source_target_pairs={{0,136},{8,128},{16,152},{24,144},{32,168},{40,160},{48,184},{56,1... | collective-permute-start | bytes 405512 | tf_op jit(solution)/shard_map/ppermute | solution.py:364
  22.7 15.2 %collective-permute-start.9 = (bf16[1024,128]{1,0:T(8,128)(2,1)S(1)}, bf16[1024,128]{1,0:T(8,128)(2,1)S(1)}, u32[]{:S(2)}, u32[]{:S(2)}) collective-permute-start(bf16[1024,128]{1,0:T(8,128)(2,1)S(1)} %broadcast_select_fusion), channel_id=1, source_target_pairs={{0,32},{8,104},{16,48},{24,120},{32,64},{40,8},{48,80},{56,24},{64... | collective-permute-start | bytes 786440 | tf_op jit(solution)/shard_map/ppermute | solution.py:368
  23.9 14.0 %collective-permute-start.7 = (bf16[1024,128]{1,0:T(8,128)(2,1)S(1)}, bf16[1024,128]{1,0:T(8,128)(2,1)S(1)}, u32[]{:S(2)}, u32[]{:S(2)}) collective-permute-start(bf16[1024,128]{1,0:T(8,128)(2,1)S(1)} %collective-permute-done.5.up2), channel_id=1, source_target_pairs={{0,16},{8,24},{16,32},{24,40},{32,48},{40,56},{48,64},{56,72},{64,... | collective-permute-start | bytes 786440 | tf_op jit(solution)/shard_map/ppermute | solution.py:365
  26.9 11.1 %collective-permute-start.8 = (bf16[1024,128]{1,0:T(8,128)(2,1)S(1)}, bf16[1024,128]{1,0:T(8,128)(2,1)S(1)}, u32[]{:S(2)}, u32[]{:S(2)}) collective-permute-start(bf16[1024,128]{1,0:T(8,128)(2,1)S(1)} %collective-permute-done.6.dn2), channel_id=1, source_target_pairs={{0,112},{8,120},{16,0},{24,8},{32,16},{40,24},{48,32},{56,40},{64,... | collective-permute-start | bytes 786440 | tf_op jit(solution)/shard_map/ppermute | solution.py:366
  29.4 1.0 %copy-start = (bf16[1808,128]{1,0:T(8,128)(2,1)S(1)}, bf16[1808,128]{1,0:T(8,128)(2,1)}, u32[]{:S(2)}) copy-start(bf16[1808,128]{1,0:T(8,128)(2,1)} %get-tuple-element.16.local) | copy-start | bytes 1388548
  40.5 7.4 %collective-permute-start.10 = (bf16[144,512]{1,0:T(8,128)(2,1)S(1)}, bf16[144,512]{1,0:T(8,128)(2,1)S(1)}, u32[]{:S(2)}, u32[]{:S(2)}) collective-permute-start(bf16[144,512]{1,0:T(8,128)(2,1)S(1)} %get-tuple-element.24), channel_id=1, source_target_pairs={{0,136},{8,128},{16,152},{24,144},{32,168},{40,160},{48,184},{56,1... | collective-permute-start | bytes 442376 | tf_op jit(solution)/shard_map/ppermute | solution.py:381
  42.9 8.5 %collective-permute-start.11 = (bf16[144,512]{1,0:T(8,128)(2,1)S(1)}, bf16[144,512]{1,0:T(8,128)(2,1)S(1)}, u32[]{:S(2)}, u32[]{:S(2)}) collective-permute-start(bf16[144,512]{1,0:T(8,128)(2,1)S(1)} %get-tuple-element.25), channel_id=1, source_target_pairs={{0,128},{8,136},{16,144},{24,152},{32,160},{40,168},{48,176},{56,1... | collective-permute-start | bytes 442376 | tf_op jit(solution)/shard_map/ppermute | solution.py:381
  43.9 7.5 %collective-permute-start.12 = (bf16[144,512]{1,0:T(8,128)(2,1)S(1)}, bf16[144,512]{1,0:T(8,128)(2,1)S(1)}, u32[]{:S(2)}, u32[]{:S(2)}) collective-permute-start(bf16[144,512]{1,0:T(8,128)(2,1)S(1)} %get-tuple-element.26), channel_id=1, source_target_pairs={{0,8},{8,0},{16,24},{24,16},{32,40},{40,32},{48,56},{56,48},{64,72... | collective-permute-start | bytes 442376 | tf_op jit(solution)/shard_map/ppermute | solution.py:381
  55.1 7.4 %collective-permute-start.13 = (bf16[16,5120]{1,0:T(8,128)(2,1)S(1)}, bf16[16,5120]{1,0:T(8,128)(2,1)S(1)}, u32[]{:S(2)}, u32[]{:S(2)}) collective-permute-start(bf16[16,5120]{1,0:T(8,128)(2,1)S(1)} %get-tuple-element.33), channel_id=1, source_target_pairs={{0,1},{1,2},{2,3},{3,0},{4,5},{5,6},{6,7},{7,4},{8,9},{9,10},{10,1... | collective-permute-start | bytes 491528 | tf_op jit(solution)/shard_map/ppermute | solution.py:396
  56.7 8.9 %collective-permute-start.14 = (bf16[16,5120]{1,0:T(8,128)(2,1)S(1)}, bf16[16,5120]{1,0:T(8,128)(2,1)S(1)}, u32[]{:S(2)}, u32[]{:S(2)}) collective-permute-start(bf16[16,5120]{1,0:T(8,128)(2,1)S(1)} %get-tuple-element.32), channel_id=1, source_target_pairs={{0,3},{1,0},{2,1},{3,2},{4,7},{5,4},{6,5},{7,6},{8,11},{9,8},{10,9... | collective-permute-start | bytes 491528 | tf_op jit(solution)/shard_map/ppermute | solution.py:396
  58.4 11.1 %collective-permute-start.15 = (bf16[16,5120]{1,0:T(8,128)(2,1)S(1)}, bf16[16,5120]{1,0:T(8,128)(2,1)S(1)}, u32[]{:S(2)}, u32[]{:S(2)}) collective-permute-start(bf16[16,5120]{1,0:T(8,128)(2,1)S(1)} %get-tuple-element.31), channel_id=1, source_target_pairs={{0,2},{1,3},{2,0},{3,1},{4,6},{5,7},{6,4},{7,5},{8,10},{9,11},{10,... | collective-permute-start | bytes 491528 | tf_op jit(solution)/shard_map/ppermute | solution.py:396
  60.4 9.1 %collective-permute-start.16 = (bf16[16,5120]{1,0:T(8,128)(2,1)S(1)}, bf16[16,5120]{1,0:T(8,128)(2,1)S(1)}, u32[]{:S(2)}, u32[]{:S(2)}) collective-permute-start(bf16[16,5120]{1,0:T(8,128)(2,1)S(1)} %get-tuple-element.30), channel_id=1, source_target_pairs={{0,4},{1,5},{2,6},{3,7},{4,0},{5,1},{6,2},{7,3},{8,12},{9,13},{10,... | collective-permute-start | bytes 491528 | tf_op jit(solution)/shard_map/ppermute | solution.py:396
  61.3 9.9 %collective-permute-start.17 = (bf16[16,5120]{1,0:T(8,128)(2,1)S(1)}, bf16[16,5120]{1,0:T(8,128)(2,1)S(1)}, u32[]{:S(2)}, u32[]{:S(2)}) collective-permute-start(bf16[16,5120]{1,0:T(8,128)(2,1)S(1)} %get-tuple-element.29), channel_id=1, source_target_pairs={{0,5},{1,6},{2,7},{3,4},{4,1},{5,2},{6,3},{7,0},{8,13},{9,14},{10,... | collective-permute-start | bytes 491528 | tf_op jit(solution)/shard_map/ppermute | solution.py:396
  62.5 11.8 %collective-permute-start.18 = (bf16[16,5120]{1,0:T(8,128)(2,1)S(1)}, bf16[16,5120]{1,0:T(8,128)(2,1)S(1)}, u32[]{:S(2)}, u32[]{:S(2)}) collective-permute-start(bf16[16,5120]{1,0:T(8,128)(2,1)S(1)} %get-tuple-element.28), channel_id=1, source_target_pairs={{0,7},{1,4},{2,5},{3,6},{4,3},{5,0},{6,1},{7,2},{8,15},{9,12},{10,... | collective-permute-start | bytes 491528 | tf_op jit(solution)/shard_map/ppermute | solution.py:396
  65.6 11.5 %collective-permute-start.19 = (bf16[16,5120]{1,0:T(8,128)(2,1)S(1)}, bf16[16,5120]{1,0:T(8,128)(2,1)S(1)}, u32[]{:S(2)}, u32[]{:S(2)}) collective-permute-start(bf16[16,5120]{1,0:T(8,128)(2,1)S(1)} %get-tuple-element.27), channel_id=1, source_target_pairs={{0,6},{1,7},{2,4},{3,5},{4,2},{5,3},{6,0},{7,1},{8,14},{9,15},{10,... | collective-permute-start | bytes 491528 | tf_op jit(solution)/shard_map/ppermute | solution.py:396

commit v5 on v4

--- a/solution.py
+++ b/solution.py
@@ -343,8 +343,6 @@
     kv = jnp.concatenate([prefix_keys, prefix_values], axis=0).reshape(BLOCK, HD)
     up1 = lax.ppermute(kv, "rep", z_perm(1))
     dn1 = lax.ppermute(kv, "rep", z_perm(-1))
-    up2 = lax.ppermute(up1, "rep", z_perm(1))
-    dn2 = lax.ppermute(dn1, "rep", z_perm(-1))
     sent, local = pl.pallas_call(
         pack_kernel,
         out_shape=[
@@ -361,6 +359,9 @@
         prefix_keys.reshape(-1, HD), prefix_values.reshape(-1, HD), page_table, tree_parent.reshape(1, -1),
         kv,
     )
+    up1, dn1, sent = lax.optimization_barrier((up1, dn1, sent))
+    up2 = lax.ppermute(up1, "rep", z_perm(1))
+    dn2 = lax.ppermute(dn1, "rep", z_perm(-1))
     sents = [lax.ppermute(sent, "rep", group_perm(r)) for r in (1, 2, 3)]
     up3 = lax.ppermute(up2, "rep", z_perm(1))
     dn3 = lax.ppermute(dn2, "rep", z_perm(-1))

time: 78.9 us -> 77.3 us (0.980); the launches traced: 77.9 us -> 77.3 us
  starting transfers between devices: 32.6 us -> 37.7 us
  waiting for transfers between devices: 25.9 us -> 21 us
    ppermute x7, starting transfers between devices: 12 us -> 15.2 us  [on_device(): lax.ppermute(part, 'head', [(i, (i & 4 ^ dx * 4) + (i + dy & 3)) for i in...]
    ppermute x7, waiting for transfers between devices: 9.98 us -> 7.18 us  [on_device(): lax.ppermute(part, 'head', [(i, (i & 4 ^ dx * 4) + (i + dy & 3)) for i in...]
    ppermute x1, waiting for transfers between devices: 6.22 us -> 3.51 us  [on_device(): up1 = lax.ppermute(kv, 'rep', z_perm(1))]
    ppermute x3, waiting for transfers between devices: 2.27 us -> 0.01 us  [on_device(): sents = [lax.ppermute(sent, 'rep', group_perm(r)) for r in (1, 2, 3)]]
    ppermute x1, waiting for transfers between devices: 0.01 us -> 1.98 us  [on_device(): up2 = lax.ppermute(up1, 'rep', z_perm(1))]
    ppermute x1, starting transfers between devices: 1.18 us -> 3.07 us  [on_device(): lax.ppermute(held, 'rep', [(rep_of(a, z, c), rep_of(a, z + 2 - 4 * c, c))...]
    ppermute x1, waiting for transfers between devices: 0.01 us -> 1.5 us  [on_device(): up3 = lax.ppermute(up2, 'rep', z_perm(1))]
    ppermute x1, starting transfers between devices: 2.95 us -> 1.81 us  [on_device(): up3 = lax.ppermute(up2, 'rep', z_perm(1))]
  transfers between devices with their start and end apart: 20 -> 20, of which waited for: 9 -> 9; matrix products, arithmetic and copies ran while one was open for 0% -> 0% of each run, Pallas kernels for 13% -> 12%
where the time goes in v5:
time: 77.3 us
  starting transfers between devices  37.7 us (49%)
  waiting for transfers between devices  21 us (27%)
  Pallas kernels  13.1 us (17%)
  matrix products  3.34 us (4%)
  local copies, waits for them, and re-layouts  1.11 us (1%)
  other arithmetic  1.03 us (1%)
    ppermute x7, starting transfers between devices, on_device(): lax.ppermute(part, 'head', [(i, (i & 4 ^ dx * 4) + (i + dy & 3)) for i in...  15.2 us
    ppermute x7, waiting for transfers between devices, on_device(): lax.ppermute(part, 'head', [(i, (i & 4 ^ dx * 4) + (i + dy & 3)) for i in...  7.18 us
    ppermute x3, waiting for transfers between devices, on_device(): lax.ppermute(p, 'rep', group_perm(r))  6.79 us
    pallas_call x1, Pallas kernels, near_call(): pl.pallas_call(near_kernel, out_shape=[jax.ShapeDtypeStruct((SESS * QROWS...  6.42 us
    ppermute x1, starting transfers between devices, on_device(): dn1 = lax.ppermute(kv, 'rep', z_perm(-1))  4.03 us
    ppermute x1, waiting for transfers between devices, on_device(): up1 = lax.ppermute(kv, 'rep', z_perm(1))  3.51 us
    ppermute x3, starting transfers between devices, on_device(): sents = [lax.ppermute(sent, 'rep', group_perm(r)) for r in (1, 2, 3)]  3.46 us
    ppermute x3, starting transfers between devices, on_device(): lax.ppermute(p, 'rep', group_perm(r))  3.45 us
  transfers between devices with their start and end apart: 20, of which 9 were waited for; matrix products, arithmetic and copies ran while one was open for 0% of the time, Pallas kernels for 12%

profile of v5, /device:TPU:2, one launch (start us, length us, event | category | flops | bytes accessed | tf_op | source)
XLA Modules:
  0.0 77.3 jit_solution(14302176635454170246)
XLA Ops:
  1.0 2.0 %collective-permute-start = (bf16[1024,128]{1,0:T(8,128)(2,1)S(1)}, bf16[1024,128]{1,0:T(8,128)(2,1)S(1)}, u32[]{:S(2)}, u32[]{:S(2)}) collective-permute-start(bf16[1024,128]{1,0:T(8,128)(2,1)S(1)} %bitcast.10), channel_id=1, source_target_pairs={{0,16},{8,24},{16,32},{24,40},{32,48},{40,56},{48,64},{56,72},{64,... | collective-permute-start | bytes 786440 | tf_op jit(solution)/shard_map/ppermute | solution.py:344
  3.0 4.0 %collective-permute-start.1 = (bf16[1024,128]{1,0:T(8,128)(2,1)S(1)}, bf16[1024,128]{1,0:T(8,128)(2,1)S(1)}, u32[]{:S(2)}, u32[]{:S(2)}) collective-permute-start(bf16[1024,128]{1,0:T(8,128)(2,1)S(1)} %bitcast.11), channel_id=1, source_target_pairs={{0,112},{8,120},{16,0},{24,8},{32,16},{40,24},{48,32},{56,40},{64,... | collective-permute-start | bytes 786440 | tf_op jit(solution)/shard_map/ppermute | solution.py:345
  7.0 2.7 %pack.1 = (bf16[528,128]{1,0:T(8,128)(2,1)}, bf16[1808,128]{1,0:T(8,128)(2,1)}) custom-call(bf16[512,128]{1,0:T(8,128)(2,1)} %bitcast.15, bf16[128,128]{1,0:T(8,128)(2,1)} %bitcast.16, bf16[128,128]{1,0:T(8,128)(2,1)} %bitcast.17, bf16[512,128]{1,0:T(8,128)(2,1)} %bitcast.13, bf16[512,128]{1,0:T(8,128)(2,1)} %bitcast.14, s32[2,16]{1,0:T(2,128)} %table.1, ...), custom_call_target="tpu_custom_call" | custom-call | tf_op jit(solution)/shard_map/pack/pallas_call | solution.py:346
  9.7 3.5 %collective-permute-done.up1 = bf16[1024,128]{1,0:T(8,128)(2,1)S(1)} collective-permute-done((bf16[1024,128]{1,0:T(8,128)(2,1)S(1)}, bf16[1024,128]{1,0:T(8,128)(2,1)S(1)}, u32[]{:S(2)}, u32[]{:S(2)}) %collective-permute-start) | collective-permute-done | bytes 262176 | tf_op jit(solution)/shard_map/ppermute | solution.py:344
  13.3 3.2 %collective-permute-start.6 = (bf16[1024,128]{1,0:T(8,128)(2,1)S(1)}, bf16[1024,128]{1,0:T(8,128)(2,1)S(1)}, u32[]{:S(2)}, u32[]{:S(2)}) collective-permute-start(bf16[1024,128]{1,0:T(8,128)(2,1)S(1)} %collective-permute-done.1.dn1), channel_id=1, source_target_pairs={{0,112},{8,120},{16,0},{24,8},{32,16},{40,24},{48,32},{56,40},{64,... | collective-permute-start | bytes 786440 | tf_op jit(solution)/shard_map/ppermute | solution.py:364
  16.6 2.2 %collective-permute-start.3 = (bf16[528,128]{1,0:T(8,128)(2,1)}, bf16[528,128]{1,0:T(8,128)(2,1)S(1)}, u32[]{:S(2)}, u32[]{:S(2)}) collective-permute-start(bf16[528,128]{1,0:T(8,128)(2,1)} %get-tuple-element.21), channel_id=1, source_target_pairs={{0,128},{8,136},{16,144},{24,152},{32,160},{40,168},{48,176},{56,1... | collective-permute-start | bytes 405512 | tf_op jit(solution)/shard_map/ppermute | solution.py:365
  20.0 2.0 %collective-permute-done.5.up2 = bf16[1024,128]{1,0:T(8,128)(2,1)S(1)} collective-permute-done((bf16[1024,128]{1,0:T(8,128)(2,1)S(1)}, bf16[1024,128]{1,0:T(8,128)(2,1)S(1)}, u32[]{:S(2)}, u32[]{:S(2)}) %collective-permute-start.5) | collective-permute-done | bytes 262176 | tf_op jit(solution)/shard_map/ppermute | solution.py:363
  22.0 3.1 %collective-permute-start.9 = (bf16[1024,128]{1,0:T(8,128)(2,1)S(1)}, bf16[1024,128]{1,0:T(8,128)(2,1)S(1)}, u32[]{:S(2)}, u32[]{:S(2)}) collective-permute-start(bf16[1024,128]{1,0:T(8,128)(2,1)S(1)} %broadcast_select_fusion), channel_id=1, source_target_pairs={{0,32},{8,104},{16,48},{24,120},{32,64},{40,8},{48,80},{56,24},{64... | collective-permute-start | bytes 786440 | tf_op jit(solution)/shard_map/ppermute | solution.py:369
  25.1 1.8 %collective-permute-start.7 = (bf16[1024,128]{1,0:T(8,128)(2,1)S(1)}, bf16[1024,128]{1,0:T(8,128)(2,1)S(1)}, u32[]{:S(2)}, u32[]{:S(2)}) collective-permute-start(bf16[1024,128]{1,0:T(8,128)(2,1)S(1)} %collective-permute-done.5.up2), channel_id=1, source_target_pairs={{0,16},{8,24},{16,32},{24,40},{32,48},{40,56},{48,64},{56,72},{64,... | collective-permute-start | bytes 786440 | tf_op jit(solution)/shard_map/ppermute | solution.py:366
  26.9 1.4 %collective-permute-start.8 = (bf16[1024,128]{1,0:T(8,128)(2,1)S(1)}, bf16[1024,128]{1,0:T(8,128)(2,1)S(1)}, u32[]{:S(2)}, u32[]{:S(2)}) collective-permute-start(bf16[1024,128]{1,0:T(8,128)(2,1)S(1)} %collective-permute-done.6.dn2), channel_id=1, source_target_pairs={{0,112},{8,120},{16,0},{24,8},{32,16},{40,24},{48,32},{56,40},{64,... | collective-permute-start | bytes 786440 | tf_op jit(solution)/shard_map/ppermute | solution.py:367
  29.3 6.4 %near_pages.1 = (bf16[2048,128]{1,0:T(8,128)(2,1)S(1)}, s32[160]{0:T(256)S(1)}, f32[8,1,256]{2,1,0:T(1,128)S(1)}, f32[8,1,256]{2,1,0:T(1,128)S(1)}, f32[8,128,256]{2,1,0:T(8,128)S(1)}) custom-call(s32[32]{0:T(128)S(1)} %and_select_fusion.7.maps, bf16[1808,128]{1,0:T(8,128)(2,1)S(1)} %copy-done, bf16[528,128]{1,0:T(8,128)(2,1)S(1)} %collective-permute-done.2.s1, ...), custom_call_target="tpu_custom_call" | custom-call | flops 4000000000 | bytes 4194304 | tf_op jit(solution)/shard_map/near_pages/pallas_call | solution.py:298
  35.8 1.5 %collective-permute-done.7.refs_2_ = bf16[1024,128]{1,0:T(8,128)(2,1)S(1)} collective-permute-done((bf16[1024,128]{1,0:T(8,128)(2,1)S(1)}, bf16[1024,128]{1,0:T(8,128)(2,1)S(1)}, u32[]{:S(2)}, u32[]{:S(2)}) %collective-permute-start.7) | collective-permute-done | bytes 262176 | tf_op jit(solution)/shard_map/ppermute | solution.py:366
  37.3 2.9 %far_pages.1 = (f32[136,512]{1,0:T(8,128)S(1)}, bf16[144,512]{1,0:T(8,128)(2,1)S(1)}, bf16[144,512]{1,0:T(8,128)(2,1)S(1)}, bf16[144,512]{1,0:T(8,128)(2,1)S(1)}) custom-call(s32[160]{0:T(256)S(1)} %get-tuple-element.24.refs_0_, bf16[2048,128]{1,0:T(8,128)(2,1)S(1)} %get-tuple-element.25.refs_1_, bf16[1024,128]{1,0:T(8,128)(2,1)S(1)} %collective-permute-done.7.refs_2_, ...), custom_call_target="tpu_custom_call" | custom-call | flops 1000000000 | bytes 4194304 | tf_op jit(solution)/shard_map/far_pages/pallas_call | solution.py:322
  40.3 2.7 %collective-permute-start.11 = (bf16[144,512]{1,0:T(8,128)(2,1)S(1)}, bf16[144,512]{1,0:T(8,128)(2,1)S(1)}, u32[]{:S(2)}, u32[]{:S(2)}) collective-permute-start(bf16[144,512]{1,0:T(8,128)(2,1)S(1)} %get-tuple-element.31), channel_id=1, source_target_pairs={{0,128},{8,136},{16,144},{24,152},{32,160},{40,168},{48,176},{56,1... | collective-permute-start | bytes 442376 | tf_op jit(solution)/shard_map/ppermute | solution.py:382
  43.7 4.3 %collective-permute-done.10.p1 = bf16[144,512]{1,0:T(8,128)(2,1)S(1)} collective-permute-done((bf16[144,512]{1,0:T(8,128)(2,1)S(1)}, bf16[144,512]{1,0:T(8,128)(2,1)S(1)}, u32[]{:S(2)}, u32[]{:S(2)}) %collective-permute-start.10) | collective-permute-done | bytes 147488 | tf_op jit(solution)/shard_map/ppermute | solution.py:382
  47.9 2.5 %collective-permute-done.11.p2 = bf16[144,512]{1,0:T(8,128)(2,1)S(1)} collective-permute-done((bf16[144,512]{1,0:T(8,128)(2,1)S(1)}, bf16[144,512]{1,0:T(8,128)(2,1)S(1)}, u32[]{:S(2)}, u32[]{:S(2)}) %collective-permute-start.11) | collective-permute-done | bytes 147488 | tf_op jit(solution)/shard_map/ppermute | solution.py:382
  50.7 3.3 %convolution_convert_fusion = bf16[128,5120]{1,0:T(8,128)(2,1)S(1)} fusion(bf16[128,512]{1,0:T(8,128)(2,1)S(1)} %combine.1, bf16[512,5120]{1,0:T(8,128)(2,1)} %param.15), kind=kOutput, calls=%fused_computation | convolution fusion | flops 671744000 | bytes 6684672 | tf_op jit(solution)/shard_map/dot_general | solution.py:394
  54.1 1.7 %collective-permute-start.13 = (bf16[16,5120]{1,0:T(8,128)(2,1)S(1)}, bf16[16,5120]{1,0:T(8,128)(2,1)S(1)}, u32[]{:S(2)}, u32[]{:S(2)}) collective-permute-start(bf16[16,5120]{1,0:T(8,128)(2,1)S(1)} %get-tuple-element.39), channel_id=1, source_target_pairs={{0,1},{1,2},{2,3},{3,0},{4,5},{5,6},{6,7},{7,4},{8,9},{9,10},{10,1... | collective-permute-start | bytes 491528 | tf_op jit(solution)/shard_map/ppermute | solution.py:397
  55.8 1.7 %collective-permute-start.14 = (bf16[16,5120]{1,0:T(8,128)(2,1)S(1)}, bf16[16,5120]{1,0:T(8,128)(2,1)S(1)}, u32[]{:S(2)}, u32[]{:S(2)}) collective-permute-start(bf16[16,5120]{1,0:T(8,128)(2,1)S(1)} %get-tuple-element.38), channel_id=1, source_target_pairs={{0,3},{1,0},{2,1},{3,2},{4,7},{5,4},{6,5},{7,6},{8,11},{9,8},{10,9... | collective-permute-start | bytes 491528 | tf_op jit(solution)/shard_map/ppermute | solution.py:397
  57.4 2.0 %collective-permute-start.15 = (bf16[16,5120]{1,0:T(8,128)(2,1)S(1)}, bf16[16,5120]{1,0:T(8,128)(2,1)S(1)}, u32[]{:S(2)}, u32[]{:S(2)}) collective-permute-start(bf16[16,5120]{1,0:T(8,128)(2,1)S(1)} %get-tuple-element.37), channel_id=1, source_target_pairs={{0,2},{1,3},{2,0},{3,1},{4,6},{5,7},{6,4},{7,5},{8,10},{9,11},{10,... | collective-permute-start | bytes 491528 | tf_op jit(solution)/shard_map/ppermute | solution.py:397
  61.7 3.0 %collective-permute-start.18 = (bf16[16,5120]{1,0:T(8,128)(2,1)S(1)}, bf16[16,5120]{1,0:T(8,128)(2,1)S(1)}, u32[]{:S(2)}, u32[]{:S(2)}) collective-permute-start(bf16[16,5120]{1,0:T(8,128)(2,1)S(1)} %get-tuple-element.34), channel_id=1, source_target_pairs={{0,7},{1,4},{2,5},{3,6},{4,3},{5,0},{6,1},{7,2},{8,15},{9,12},{10,... | collective-permute-start | bytes 491528 | tf_op jit(solution)/shard_map/ppermute | solution.py:397
  64.8 4.7 %collective-permute-start.19 = (bf16[16,5120]{1,0:T(8,128)(2,1)S(1)}, bf16[16,5120]{1,0:T(8,128)(2,1)S(1)}, u32[]{:S(2)}, u32[]{:S(2)}) collective-permute-start(bf16[16,5120]{1,0:T(8,128)(2,1)S(1)} %get-tuple-element.33), channel_id=1, source_target_pairs={{0,6},{1,7},{2,4},{3,5},{4,2},{5,3},{6,0},{7,1},{8,14},{9,15},{10,... | collective-permute-start | bytes 491528 | tf_op jit(solution)/shard_map/ppermute | solution.py:397
  70.2 3.5 %collective-permute-done.18.refs_6_ = bf16[16,5120]{1,0:T(8,128)(2,1)S(1)} collective-permute-done((bf16[16,5120]{1,0:T(8,128)(2,1)S(1)}, bf16[16,5120]{1,0:T(8,128)(2,1)S(1)}, u32[]{:S(2)}, u32[]{:S(2)}) %collective-permute-start.18) | collective-permute-done | bytes 163872 | tf_op jit(solution)/shard_map/ppermute | solution.py:397
  73.7 2.8 %collective-permute-done.19.refs_7_ = bf16[16,5120]{1,0:T(8,128)(2,1)S(1)} collective-permute-done((bf16[16,5120]{1,0:T(8,128)(2,1)S(1)}, bf16[16,5120]{1,0:T(8,128)(2,1)S(1)}, u32[]{:S(2)}, u32[]{:S(2)}) %collective-permute-start.19) | collective-permute-done | bytes 163872 | tf_op jit(solution)/shard_map/ppermute | solution.py:397
  (30 shorter events, 8.3 us)
Async XLA Ops:
  1.0 6.0 %copy-start.1 = (bf16[8,1,128,128]{3,2,1,0:T(8,128)(2,1)}, bf16[8,1,128,128]{3,2,1,0:T(8,128)(2,1)S(1)}, u32[]{:S(2)}) copy-start(bf16[8,1,128,128]{3,2,1,0:T(8,128)(2,1)S(1)} %pad_maximum_fusion) | copy-start | bytes 786436
  1.0 12.2 %collective-permute-start = (bf16[1024,128]{1,0:T(8,128)(2,1)S(1)}, bf16[1024,128]{1,0:T(8,128)(2,1)S(1)}, u32[]{:S(2)}, u32[]{:S(2)}) collective-permute-start(bf16[1024,128]{1,0:T(8,128)(2,1)S(1)} %bitcast.10), channel_id=1, source_target_pairs={{0,16},{8,24},{16,32},{24,40},{32,48},{40,56},{48,64},{56,72},{64,... | collective-permute-start | bytes 786440 | tf_op jit(solution)/shard_map/ppermute | solution.py:344
  3.0 10.2 %collective-permute-start.1 = (bf16[1024,128]{1,0:T(8,128)(2,1)S(1)}, bf16[1024,128]{1,0:T(8,128)(2,1)S(1)}, u32[]{:S(2)}, u32[]{:S(2)}) collective-permute-start(bf16[1024,128]{1,0:T(8,128)(2,1)S(1)} %bitcast.11), channel_id=1, source_target_pairs={{0,112},{8,120},{16,0},{24,8},{32,16},{40,24},{48,32},{56,40},{64,... | collective-permute-start | bytes 786440 | tf_op jit(solution)/shard_map/ppermute | solution.py:345
  13.2 8.7 %collective-permute-start.5 = (bf16[1024,128]{1,0:T(8,128)(2,1)S(1)}, bf16[1024,128]{1,0:T(8,128)(2,1)S(1)}, u32[]{:S(2)}, u32[]{:S(2)}) collective-permute-start(bf16[1024,128]{1,0:T(8,128)(2,1)S(1)} %collective-permute-done.up1), channel_id=1, source_target_pairs={{0,16},{8,24},{16,32},{24,40},{32,48},{40,56},{48,64},{56,72},{64,... | collective-permute-start | bytes 786440 | tf_op jit(solution)/shard_map/ppermute | solution.py:363
  13.3 8.7 %collective-permute-start.6 = (bf16[1024,128]{1,0:T(8,128)(2,1)S(1)}, bf16[1024,128]{1,0:T(8,128)(2,1)S(1)}, u32[]{:S(2)}, u32[]{:S(2)}) collective-permute-start(bf16[1024,128]{1,0:T(8,128)(2,1)S(1)} %collective-permute-done.1.dn1), channel_id=1, source_target_pairs={{0,112},{8,120},{16,0},{24,8},{32,16},{40,24},{48,32},{56,40},{64,... | collective-permute-start | bytes 786440 | tf_op jit(solution)/shard_map/ppermute | solution.py:364
  16.5 10.4 %collective-permute-start.2 = (bf16[528,128]{1,0:T(8,128)(2,1)}, bf16[528,128]{1,0:T(8,128)(2,1)S(1)}, u32[]{:S(2)}, u32[]{:S(2)}) collective-permute-start(bf16[528,128]{1,0:T(8,128)(2,1)} %get-tuple-element.21), channel_id=1, source_target_pairs={{0,8},{8,0},{16,24},{24,16},{32,40},{40,32},{48,56},{56,48},{64,72... | collective-permute-start | bytes 405512 | tf_op jit(solution)/shard_map/ppermute | solution.py:365
  16.6 11.7 %collective-permute-start.3 = (bf16[528,128]{1,0:T(8,128)(2,1)}, bf16[528,128]{1,0:T(8,128)(2,1)S(1)}, u32[]{:S(2)}, u32[]{:S(2)}) collective-permute-start(bf16[528,128]{1,0:T(8,128)(2,1)} %get-tuple-element.21), channel_id=1, source_target_pairs={{0,128},{8,136},{16,144},{24,152},{32,160},{40,168},{48,176},{56,1... | collective-permute-start | bytes 405512 | tf_op jit(solution)/shard_map/ppermute | solution.py:365
  18.8 9.5 %collective-permute-start.4 = (bf16[528,128]{1,0:T(8,128)(2,1)}, bf16[528,128]{1,0:T(8,128)(2,1)S(1)}, u32[]{:S(2)}, u32[]{:S(2)}) collective-permute-start(bf16[528,128]{1,0:T(8,128)(2,1)} %get-tuple-element.21), channel_id=1, source_target_pairs={{0,136},{8,128},{16,152},{24,144},{32,168},{40,160},{48,184},{56,1... | collective-permute-start | bytes 405512 | tf_op jit(solution)/shard_map/ppermute | solution.py:365
  22.0 13.8 %collective-permute-start.9 = (bf16[1024,128]{1,0:T(8,128)(2,1)S(1)}, bf16[1024,128]{1,0:T(8,128)(2,1)S(1)}, u32[]{:S(2)}, u32[]{:S(2)}) collective-permute-start(bf16[1024,128]{1,0:T(8,128)(2,1)S(1)} %broadcast_select_fusion), channel_id=1, source_target_pairs={{0,32},{8,104},{16,48},{24,120},{32,64},{40,8},{48,80},{56,24},{64... | collective-permute-start | bytes 786440 | tf_op jit(solution)/shard_map/ppermute | solution.py:369
  25.1 12.2 %collective-permute-start.7 = (bf16[1024,128]{1,0:T(8,128)(2,1)S(1)}, bf16[1024,128]{1,0:T(8,128)(2,1)S(1)}, u32[]{:S(2)}, u32[]{:S(2)}) collective-permute-start(bf16[1024,128]{1,0:T(8,128)(2,1)S(1)} %collective-permute-done.5.up2), channel_id=1, source_target_pairs={{0,16},{8,24},{16,32},{24,40},{32,48},{40,56},{48,64},{56,72},{64,... | collective-permute-start | bytes 786440 | tf_op jit(solution)/shard_map/ppermute | solution.py:366
  26.9 10.4 %collective-permute-start.8 = (bf16[1024,128]{1,0:T(8,128)(2,1)S(1)}, bf16[1024,128]{1,0:T(8,128)(2,1)S(1)}, u32[]{:S(2)}, u32[]{:S(2)}) collective-permute-start(bf16[1024,128]{1,0:T(8,128)(2,1)S(1)} %collective-permute-done.6.dn2), channel_id=1, source_target_pairs={{0,112},{8,120},{16,0},{24,8},{32,16},{40,24},{48,32},{56,40},{64,... | collective-permute-start | bytes 786440 | tf_op jit(solution)/shard_map/ppermute | solution.py:367
  28.3 1.0 %copy-start = (bf16[1808,128]{1,0:T(8,128)(2,1)S(1)}, bf16[1808,128]{1,0:T(8,128)(2,1)}, u32[]{:S(2)}) copy-start(bf16[1808,128]{1,0:T(8,128)(2,1)} %get-tuple-element.19.local) | copy-start | bytes 1388548
  40.2 7.7 %collective-permute-start.10 = (bf16[144,512]{1,0:T(8,128)(2,1)S(1)}, bf16[144,512]{1,0:T(8,128)(2,1)S(1)}, u32[]{:S(2)}, u32[]{:S(2)}) collective-permute-start(bf16[144,512]{1,0:T(8,128)(2,1)S(1)} %get-tuple-element.30), channel_id=1, source_target_pairs={{0,136},{8,128},{16,152},{24,144},{32,168},{40,160},{48,184},{56,1... | collective-permute-start | bytes 442376 | tf_op jit(solution)/shard_map/ppermute | solution.py:382
  40.3 10.1 %collective-permute-start.11 = (bf16[144,512]{1,0:T(8,128)(2,1)S(1)}, bf16[144,512]{1,0:T(8,128)(2,1)S(1)}, u32[]{:S(2)}, u32[]{:S(2)}) collective-permute-start(bf16[144,512]{1,0:T(8,128)(2,1)S(1)} %get-tuple-element.31), channel_id=1, source_target_pairs={{0,128},{8,136},{16,144},{24,152},{32,160},{40,168},{48,176},{56,1... | collective-permute-start | bytes 442376 | tf_op jit(solution)/shard_map/ppermute | solution.py:382
  43.0 7.4 %collective-permute-start.12 = (bf16[144,512]{1,0:T(8,128)(2,1)S(1)}, bf16[144,512]{1,0:T(8,128)(2,1)S(1)}, u32[]{:S(2)}, u32[]{:S(2)}) collective-permute-start(bf16[144,512]{1,0:T(8,128)(2,1)S(1)} %get-tuple-element.32), channel_id=1, source_target_pairs={{0,8},{8,0},{16,24},{24,16},{32,40},{40,32},{48,56},{56,48},{64,72... | collective-permute-start | bytes 442376 | tf_op jit(solution)/shard_map/ppermute | solution.py:382
  54.1 7.6 %collective-permute-start.13 = (bf16[16,5120]{1,0:T(8,128)(2,1)S(1)}, bf16[16,5120]{1,0:T(8,128)(2,1)S(1)}, u32[]{:S(2)}, u32[]{:S(2)}) collective-permute-start(bf16[16,5120]{1,0:T(8,128)(2,1)S(1)} %get-tuple-element.39), channel_id=1, source_target_pairs={{0,1},{1,2},{2,3},{3,0},{4,5},{5,6},{6,7},{7,4},{8,9},{9,10},{10,1... | collective-permute-start | bytes 491528 | tf_op jit(solution)/shard_map/ppermute | solution.py:397
  55.8 9.0 %collective-permute-start.14 = (bf16[16,5120]{1,0:T(8,128)(2,1)S(1)}, bf16[16,5120]{1,0:T(8,128)(2,1)S(1)}, u32[]{:S(2)}, u32[]{:S(2)}) collective-permute-start(bf16[16,5120]{1,0:T(8,128)(2,1)S(1)} %get-tuple-element.38), channel_id=1, source_target_pairs={{0,3},{1,0},{2,1},{3,2},{4,7},{5,4},{6,5},{7,6},{8,11},{9,8},{10,9... | collective-permute-start | bytes 491528 | tf_op jit(solution)/shard_map/ppermute | solution.py:397
  57.4 12.1 %collective-permute-start.15 = (bf16[16,5120]{1,0:T(8,128)(2,1)S(1)}, bf16[16,5120]{1,0:T(8,128)(2,1)S(1)}, u32[]{:S(2)}, u32[]{:S(2)}) collective-permute-start(bf16[16,5120]{1,0:T(8,128)(2,1)S(1)} %get-tuple-element.37), channel_id=1, source_target_pairs={{0,2},{1,3},{2,0},{3,1},{4,6},{5,7},{6,4},{7,5},{8,10},{9,11},{10,... | collective-permute-start | bytes 491528 | tf_op jit(solution)/shard_map/ppermute | solution.py:397
  59.4 10.1 %collective-permute-start.16 = (bf16[16,5120]{1,0:T(8,128)(2,1)S(1)}, bf16[16,5120]{1,0:T(8,128)(2,1)S(1)}, u32[]{:S(2)}, u32[]{:S(2)}) collective-permute-start(bf16[16,5120]{1,0:T(8,128)(2,1)S(1)} %get-tuple-element.36), channel_id=1, source_target_pairs={{0,4},{1,5},{2,6},{3,7},{4,0},{5,1},{6,2},{7,3},{8,12},{9,13},{10,... | collective-permute-start | bytes 491528 | tf_op jit(solution)/shard_map/ppermute | solution.py:397
  60.5 9.7 %collective-permute-start.17 = (bf16[16,5120]{1,0:T(8,128)(2,1)S(1)}, bf16[16,5120]{1,0:T(8,128)(2,1)S(1)}, u32[]{:S(2)}, u32[]{:S(2)}) collective-permute-start(bf16[16,5120]{1,0:T(8,128)(2,1)S(1)} %get-tuple-element.35), channel_id=1, source_target_pairs={{0,5},{1,6},{2,7},{3,4},{4,1},{5,2},{6,3},{7,0},{8,13},{9,14},{10,... | collective-permute-start | bytes 491528 | tf_op jit(solution)/shard_map/ppermute | solution.py:397
  61.7 12.0 %collective-permute-start.18 = (bf16[16,5120]{1,0:T(8,128)(2,1)S(1)}, bf16[16,5120]{1,0:T(8,128)(2,1)S(1)}, u32[]{:S(2)}, u32[]{:S(2)}) collective-permute-start(bf16[16,5120]{1,0:T(8,128)(2,1)S(1)} %get-tuple-element.34), channel_id=1, source_target_pairs={{0,7},{1,4},{2,5},{3,6},{4,3},{5,0},{6,1},{7,2},{8,15},{9,12},{10,... | collective-permute-start | bytes 491528 | tf_op jit(solution)/shard_map/ppermute | solution.py:397
  64.8 11.8 %collective-permute-start.19 = (bf16[16,5120]{1,0:T(8,128)(2,1)S(1)}, bf16[16,5120]{1,0:T(8,128)(2,1)S(1)}, u32[]{:S(2)}, u32[]{:S(2)}) collective-permute-start(bf16[16,5120]{1,0:T(8,128)(2,1)S(1)} %get-tuple-element.33), channel_id=1, source_target_pairs={{0,6},{1,7},{2,4},{3,5},{4,2},{5,3},{6,0},{7,1},{8,14},{9,15},{10,... | collective-permute-start | bytes 491528 | tf_op jit(solution)/shard_map/ppermute | solution.py:397

commit v6 on v5

--- a/solution.py
+++ b/solution.py
@@ -28,7 +28,7 @@
 GROUPS = ((0, -1, 1, -2, 2), (-3, 3, 4))
 
 
-HEADS = ((0, 0), (0, 1), (0, 3), (0, 2), (1, 0), (1, 1), (1, 3), (1, 2))
+HEADS = ((0, 0), (1, 0), (0, 2), (1, 2), (0, 1), (1, 1), (0, 3), (1, 3))
 
 
 def rep_of(xh, z, c):
@@ -268,9 +268,14 @@
             attn[pl.ds(k * 16, 16), pl.ds(h * HD, HD)] = block.astype(BF)
 
 
-def sum_kernel(*refs):
-    out = refs[-1]
-    out[...] = functools.reduce(jnp.add, [r[...].astype(F32) for r in refs[:-1]]).astype(BF)
+def sum_y_kernel(p0, p1, p2, p3, mine, other):
+    total = functools.reduce(jnp.add, [r[...].astype(F32) for r in (p0, p1, p2, p3)])
+    mine[...] = total[:16]
+    other[...] = total[16:].astype(BF)
+
+
+def sum_x_kernel(mine, got, out):
+    out[...] = (mine[...] + got[...].astype(F32)).astype(BF)
 
 
 VMEM = pl.BlockSpec(memory_space=pltpu.VMEM)
@@ -392,19 +397,28 @@
         name="combine",
     )(head.reshape(1).astype(jnp.int32), own, *back)
     rows = jnp.dot(attn, out_weight, preferred_element_type=F32).astype(BF)
-    parts = [rows[k * 16:(k + 1) * 16] for k in range(8)]
+    parts = [rows[k * 32:(k + 1) * 32] for k in range(4)]
     terms = [
-        lax.ppermute(part, "head", [(i, ((i & 4) ^ (dx * 4)) + ((i + dy) & 3)) for i in range(8)])
-        for part, (dx, dy) in zip(parts[1:], HEADS[1:])
-    ]
+        lax.ppermute(part, "head", [(i, (i & 4) + ((i + dy) & 3)) for i in range(8)])
+        for part, (_, dy) in zip(parts[1:], HEADS[2::2])
+    ]
+    mine, other = pl.pallas_call(
+        sum_y_kernel,
+        out_shape=[jax.ShapeDtypeStruct((16, width), F32), jax.ShapeDtypeStruct((16, width), BF)],
+        in_specs=[VMEM] * 4,
+        out_specs=[VMEM] * 2,
+        compiler_params=pltpu.CompilerParams(vmem_limit_bytes=16 << 20),
+        name="sum_along_y",
+    )(parts[0], *terms)
+    got = lax.ppermute(other, "head", [(i, i ^ 4) for i in range(8)])
     return pl.pallas_call(
-        sum_kernel,
+        sum_x_kernel,
         out_shape=jax.ShapeDtypeStruct((16, width), BF),
-        in_specs=[VMEM] * 8,
+        in_specs=[VMEM] * 2,
         out_specs=VMEM,
-        compiler_params=pltpu.CompilerParams(vmem_limit_bytes=24 << 20),
-        name="sum_heads",
-    )(parts[0], *terms)
+        compiler_params=pltpu.CompilerParams(vmem_limit_bytes=16 << 20),
+        name="sum_along_x",
+    )(mine, got)
 
 
 def solution(mesh):

time: 77.3 us -> 80 us (1.035)
  waiting for transfers between devices: 21 us -> 29 us
  starting transfers between devices: 37.7 us -> 30.6 us
  Pallas kernels: 13.1 us -> 14.2 us
    ppermute x7 -> x4, waiting for transfers between devices: 7.18 us -> 17.6 us  [the longest x3 13 us: on_device(): lax.ppermute(part, 'head', [(i, (i & 4) + (i + dy & 3)) for i in range(8)])]
    ppermute x7 -> x4, starting transfers between devices: 15.2 us -> 8.17 us  [the longest x3 6.51 us: on_device(): lax.ppermute(part, 'head', [(i, (i & 4) + (i + dy & 3)) for i in range(8)])]
    ppermute x3, waiting for transfers between devices: 6.79 us -> 4.91 us  [on_device(): lax.ppermute(p, 'rep', group_perm(r))]
  transfers between devices with their start and end apart: 20 -> 17, of which waited for: 9 -> 9; matrix products, arithmetic and copies ran while one was open for 0% -> 0% of each run, Pallas kernels for 12% -> 12%
where the time goes in v6:
time: 80 us; the launch traced here: 79.4 us
  starting transfers between devices  30.6 us (38%)
  waiting for transfers between devices  29 us (36%)
  Pallas kernels  14.2 us (18%)
  matrix products  3.34 us (4%)
  local copies, waits for them, and re-layouts  1.11 us (1%)
  other arithmetic  1.03 us (1%)
    ppermute x3, waiting for transfers between devices, on_device(): lax.ppermute(part, 'head', [(i, (i & 4) + (i + dy & 3)) for i in range(8)])  13 us
    pallas_call x1, Pallas kernels, near_call(): pl.pallas_call(near_kernel, out_shape=[jax.ShapeDtypeStruct((SESS * QROWS...  7.02 us
    ppermute x3, starting transfers between devices, on_device(): lax.ppermute(part, 'head', [(i, (i & 4) + (i + dy & 3)) for i in range(8)])  6.51 us
    ppermute x3, waiting for transfers between devices, on_device(): lax.ppermute(p, 'rep', group_perm(r))  4.91 us
    ppermute x1, waiting for transfers between devices, on_device(): got = lax.ppermute(other, 'head', [(i, i ^ 4) for i in range(8)])  4.65 us
    ppermute x1, starting transfers between devices, on_device(): dn1 = lax.ppermute(kv, 'rep', z_perm(-1))  4.03 us
    ppermute x1, waiting for transfers between devices, on_device(): up1 = lax.ppermute(kv, 'rep', z_perm(1))  3.53 us
    ppermute x3, starting transfers between devices, on_device(): sents = [lax.ppermute(sent, 'rep', group_perm(r)) for r in (1, 2, 3)]  3.46 us
  transfers between devices with their start and end apart: 17, of which 9 were waited for; matrix products, arithmetic and copies ran while one was open for 0% of the time, Pallas kernels for 12%

profile of v6, /device:TPU:2, one launch (start us, length us, event | category | flops | bytes accessed | tf_op | source)
XLA Modules:
  0.0 79.4 jit_solution(2919656887159634640)
XLA Ops:
  1.0 2.0 %collective-permute-start = (bf16[1024,128]{1,0:T(8,128)(2,1)S(1)}, bf16[1024,128]{1,0:T(8,128)(2,1)S(1)}, u32[]{:S(2)}, u32[]{:S(2)}) collective-permute-start(bf16[1024,128]{1,0:T(8,128)(2,1)S(1)} %bitcast.10), channel_id=1, source_target_pairs={{0,16},{8,24},{16,32},{24,40},{32,48},{40,56},{48,64},{56,72},{64,... | collective-permute-start | bytes 786440 | tf_op jit(solution)/shard_map/ppermute | solution.py:349
  3.0 4.0 %collective-permute-start.1 = (bf16[1024,128]{1,0:T(8,128)(2,1)S(1)}, bf16[1024,128]{1,0:T(8,128)(2,1)S(1)}, u32[]{:S(2)}, u32[]{:S(2)}) collective-permute-start(bf16[1024,128]{1,0:T(8,128)(2,1)S(1)} %bitcast.11), channel_id=1, source_target_pairs={{0,112},{8,120},{16,0},{24,8},{32,16},{40,24},{48,32},{56,40},{64,... | collective-permute-start | bytes 786440 | tf_op jit(solution)/shard_map/ppermute | solution.py:350
  7.0 2.7 %pack.1 = (bf16[528,128]{1,0:T(8,128)(2,1)}, bf16[1808,128]{1,0:T(8,128)(2,1)}) custom-call(bf16[512,128]{1,0:T(8,128)(2,1)} %bitcast.15, bf16[128,128]{1,0:T(8,128)(2,1)} %bitcast.16, bf16[128,128]{1,0:T(8,128)(2,1)} %bitcast.17, bf16[512,128]{1,0:T(8,128)(2,1)} %bitcast.13, bf16[512,128]{1,0:T(8,128)(2,1)} %bitcast.14, s32[2,16]{1,0:T(2,128)} %table.1, ...), custom_call_target="tpu_custom_call" | custom-call | tf_op jit(solution)/shard_map/pack/pallas_call | solution.py:351
  9.7 3.5 %collective-permute-done.up1 = bf16[1024,128]{1,0:T(8,128)(2,1)S(1)} collective-permute-done((bf16[1024,128]{1,0:T(8,128)(2,1)S(1)}, bf16[1024,128]{1,0:T(8,128)(2,1)S(1)}, u32[]{:S(2)}, u32[]{:S(2)}) %collective-permute-start) | collective-permute-done | bytes 262176 | tf_op jit(solution)/shard_map/ppermute | solution.py:349
  13.3 3.2 %collective-permute-start.6 = (bf16[1024,128]{1,0:T(8,128)(2,1)S(1)}, bf16[1024,128]{1,0:T(8,128)(2,1)S(1)}, u32[]{:S(2)}, u32[]{:S(2)}) collective-permute-start(bf16[1024,128]{1,0:T(8,128)(2,1)S(1)} %collective-permute-done.1.dn1), channel_id=1, source_target_pairs={{0,112},{8,120},{16,0},{24,8},{32,16},{40,24},{48,32},{56,40},{64,... | collective-permute-start | bytes 786440 | tf_op jit(solution)/shard_map/ppermute | solution.py:369
  16.6 2.2 %collective-permute-start.3 = (bf16[528,128]{1,0:T(8,128)(2,1)}, bf16[528,128]{1,0:T(8,128)(2,1)S(1)}, u32[]{:S(2)}, u32[]{:S(2)}) collective-permute-start(bf16[528,128]{1,0:T(8,128)(2,1)} %get-tuple-element.23), channel_id=1, source_target_pairs={{0,128},{8,136},{16,144},{24,152},{32,160},{40,168},{48,176},{56,1... | collective-permute-start | bytes 405512 | tf_op jit(solution)/shard_map/ppermute | solution.py:370
  18.8 1.2 %collective-permute-start.4 = (bf16[528,128]{1,0:T(8,128)(2,1)}, bf16[528,128]{1,0:T(8,128)(2,1)S(1)}, u32[]{:S(2)}, u32[]{:S(2)}) collective-permute-start(bf16[528,128]{1,0:T(8,128)(2,1)} %get-tuple-element.23), channel_id=1, source_target_pairs={{0,136},{8,128},{16,152},{24,144},{32,168},{40,160},{48,184},{56,1... | collective-permute-start | bytes 405512 | tf_op jit(solution)/shard_map/ppermute | solution.py:370
  20.0 2.0 %collective-permute-done.5.up2 = bf16[1024,128]{1,0:T(8,128)(2,1)S(1)} collective-permute-done((bf16[1024,128]{1,0:T(8,128)(2,1)S(1)}, bf16[1024,128]{1,0:T(8,128)(2,1)S(1)}, u32[]{:S(2)}, u32[]{:S(2)}) %collective-permute-start.5) | collective-permute-done | bytes 262176 | tf_op jit(solution)/shard_map/ppermute | solution.py:368
  22.0 3.1 %collective-permute-start.9 = (bf16[1024,128]{1,0:T(8,128)(2,1)S(1)}, bf16[1024,128]{1,0:T(8,128)(2,1)S(1)}, u32[]{:S(2)}, u32[]{:S(2)}) collective-permute-start(bf16[1024,128]{1,0:T(8,128)(2,1)S(1)} %broadcast_select_fusion), channel_id=1, source_target_pairs={{0,32},{8,104},{16,48},{24,120},{32,64},{40,8},{48,80},{56,24},{64... | collective-permute-start | bytes 786440 | tf_op jit(solution)/shard_map/ppermute | solution.py:374
  25.1 1.8 %collective-permute-start.7 = (bf16[1024,128]{1,0:T(8,128)(2,1)S(1)}, bf16[1024,128]{1,0:T(8,128)(2,1)S(1)}, u32[]{:S(2)}, u32[]{:S(2)}) collective-permute-start(bf16[1024,128]{1,0:T(8,128)(2,1)S(1)} %collective-permute-done.5.up2), channel_id=1, source_target_pairs={{0,16},{8,24},{16,32},{24,40},{32,48},{40,56},{48,64},{56,72},{64,... | collective-permute-start | bytes 786440 | tf_op jit(solution)/shard_map/ppermute | solution.py:371
  26.9 1.4 %collective-permute-start.8 = (bf16[1024,128]{1,0:T(8,128)(2,1)S(1)}, bf16[1024,128]{1,0:T(8,128)(2,1)S(1)}, u32[]{:S(2)}, u32[]{:S(2)}) collective-permute-start(bf16[1024,128]{1,0:T(8,128)(2,1)S(1)} %collective-permute-done.6.dn2), channel_id=1, source_target_pairs={{0,112},{8,120},{16,0},{24,8},{32,16},{40,24},{48,32},{56,40},{64,... | collective-permute-start | bytes 786440 | tf_op jit(solution)/shard_map/ppermute | solution.py:372
  28.3 1.0 %copy-done = bf16[1808,128]{1,0:T(8,128)(2,1)S(1)} copy-done((bf16[1808,128]{1,0:T(8,128)(2,1)S(1)}, bf16[1808,128]{1,0:T(8,128)(2,1)}, u32[]{:S(2)}) %copy-start) | copy-done | bytes 462872
  29.3 7.0 %near_pages.1 = (bf16[2048,128]{1,0:T(8,128)(2,1)S(1)}, s32[160]{0:T(256)S(1)}, f32[8,1,256]{2,1,0:T(1,128)S(1)}, f32[8,1,256]{2,1,0:T(1,128)S(1)}, f32[8,128,256]{2,1,0:T(8,128)S(1)}) custom-call(s32[32]{0:T(128)S(1)} %and_select_fusion.7.maps, bf16[1808,128]{1,0:T(8,128)(2,1)S(1)} %copy-done, bf16[528,128]{1,0:T(8,128)(2,1)S(1)} %collective-permute-done.2.s1, ...), custom_call_target="tpu_custom_call" | custom-call | flops 4000000000 | bytes 4194304 | tf_op jit(solution)/shard_map/near_pages/pallas_call | solution.py:303
  37.3 3.4 %far_pages.1 = (f32[136,512]{1,0:T(8,128)S(1)}, bf16[144,512]{1,0:T(8,128)(2,1)S(1)}, bf16[144,512]{1,0:T(8,128)(2,1)S(1)}, bf16[144,512]{1,0:T(8,128)(2,1)S(1)}) custom-call(s32[160]{0:T(256)S(1)} %get-tuple-element.26.refs_0_, bf16[2048,128]{1,0:T(8,128)(2,1)S(1)} %get-tuple-element.27.refs_1_, bf16[1024,128]{1,0:T(8,128)(2,1)S(1)} %collective-permute-done.7.refs_2_, ...), custom_call_target="tpu_custom_call" | custom-call | flops 1000000000 | bytes 4194304 | tf_op jit(solution)/shard_map/far_pages/pallas_call | solution.py:327
  40.8 1.7 %collective-permute-start.11 = (bf16[144,512]{1,0:T(8,128)(2,1)S(1)}, bf16[144,512]{1,0:T(8,128)(2,1)S(1)}, u32[]{:S(2)}, u32[]{:S(2)}) collective-permute-start(bf16[144,512]{1,0:T(8,128)(2,1)S(1)} %get-tuple-element.33), channel_id=1, source_target_pairs={{0,128},{8,136},{16,144},{24,152},{32,160},{40,168},{48,176},{56,1... | collective-permute-start | bytes 442376 | tf_op jit(solution)/shard_map/ppermute | solution.py:387
  42.5 1.6 %collective-permute-start.12 = (bf16[144,512]{1,0:T(8,128)(2,1)S(1)}, bf16[144,512]{1,0:T(8,128)(2,1)S(1)}, u32[]{:S(2)}, u32[]{:S(2)}) collective-permute-start(bf16[144,512]{1,0:T(8,128)(2,1)S(1)} %get-tuple-element.34), channel_id=1, source_target_pairs={{0,8},{8,0},{16,24},{24,16},{32,40},{40,32},{48,56},{56,48},{64,72... | collective-permute-start | bytes 442376 | tf_op jit(solution)/shard_map/ppermute | solution.py:387
  44.2 4.2 %collective-permute-done.10.p1 = bf16[144,512]{1,0:T(8,128)(2,1)S(1)} collective-permute-done((bf16[144,512]{1,0:T(8,128)(2,1)S(1)}, bf16[144,512]{1,0:T(8,128)(2,1)S(1)}, u32[]{:S(2)}, u32[]{:S(2)}) %collective-permute-start.10) | collective-permute-done | bytes 147488 | tf_op jit(solution)/shard_map/ppermute | solution.py:387
  49.3 3.3 %convolution_convert_fusion = bf16[128,5120]{1,0:T(8,128)(2,1)S(1)} fusion(bf16[128,512]{1,0:T(8,128)(2,1)S(1)} %combine.1, bf16[512,5120]{1,0:T(8,128)(2,1)} %param.15), kind=kOutput, calls=%fused_computation | convolution fusion | flops 671744000 | bytes 6684672 | tf_op jit(solution)/shard_map/dot_general | solution.py:399
  52.7 3.3 %collective-permute-start.13 = (bf16[32,5120]{1,0:T(8,128)(2,1)S(1)}, bf16[32,5120]{1,0:T(8,128)(2,1)S(1)}, u32[]{:S(2)}, u32[]{:S(2)}) collective-permute-start(bf16[32,5120]{1,0:T(8,128)(2,1)S(1)} %get-tuple-element.39), channel_id=1, source_target_pairs={{0,2},{1,3},{2,0},{3,1},{4,6},{5,7},{6,4},{7,5},{8,10},{9,11},{10,... | collective-permute-start | bytes 983048 | tf_op jit(solution)/shard_map/ppermute | solution.py:402
  56.7 2.6 %collective-permute-start.15 = (bf16[32,5120]{1,0:T(8,128)(2,1)S(1)}, bf16[32,5120]{1,0:T(8,128)(2,1)S(1)}, u32[]{:S(2)}, u32[]{:S(2)}) collective-permute-start(bf16[32,5120]{1,0:T(8,128)(2,1)S(1)} %get-tuple-element.37), channel_id=1, source_target_pairs={{0,3},{1,0},{2,1},{3,2},{4,7},{5,4},{6,5},{7,6},{8,11},{9,8},{10,9... | collective-permute-start | bytes 983048 | tf_op jit(solution)/shard_map/ppermute | solution.py:402
  59.3 5.7 %collective-permute-done.13.p1 = bf16[32,5120]{1,0:T(8,128)(2,1)S(1)} collective-permute-done((bf16[32,5120]{1,0:T(8,128)(2,1)S(1)}, bf16[32,5120]{1,0:T(8,128)(2,1)S(1)}, u32[]{:S(2)}, u32[]{:S(2)}) %collective-permute-start.13) | collective-permute-done | bytes 327712 | tf_op jit(solution)/shard_map/ppermute | solution.py:402
  65.0 7.0 %collective-permute-done.14.p2 = bf16[32,5120]{1,0:T(8,128)(2,1)S(1)} collective-permute-done((bf16[32,5120]{1,0:T(8,128)(2,1)S(1)}, bf16[32,5120]{1,0:T(8,128)(2,1)S(1)}, u32[]{:S(2)}, u32[]{:S(2)}) %collective-permute-start.14) | collective-permute-done | bytes 327712 | tf_op jit(solution)/shard_map/ppermute | solution.py:402
  72.4 1.7 %collective-permute-start.16 = (bf16[16,5120]{1,0:T(8,128)(2,1)S(1)}, bf16[16,5120]{1,0:T(8,128)(2,1)S(1)}, u32[]{:S(2)}, u32[]{:S(2)}) collective-permute-start(bf16[16,5120]{1,0:T(8,128)(2,1)S(1)} %get-tuple-element.36), channel_id=1, source_target_pairs={{0,4},{1,5},{2,6},{3,7},{4,0},{5,1},{6,2},{7,3},{8,12},{9,13},{10,... | collective-permute-start | bytes 491528 | tf_op jit(solution)/shard_map/ppermute | solution.py:413
  74.1 4.6 %collective-permute-done.16.got = bf16[16,5120]{1,0:T(8,128)(2,1)S(1)} collective-permute-done((bf16[16,5120]{1,0:T(8,128)(2,1)S(1)}, bf16[16,5120]{1,0:T(8,128)(2,1)S(1)}, u32[]{:S(2)}, u32[]{:S(2)}) %collective-permute-start.16) | collective-permute-done | bytes 163872 | tf_op jit(solution)/shard_map/ppermute | solution.py:413
  (25 shorter events, 5.0 us)
Async XLA Ops:
  1.0 6.0 %copy-start.1 = (bf16[8,1,128,128]{3,2,1,0:T(8,128)(2,1)}, bf16[8,1,128,128]{3,2,1,0:T(8,128)(2,1)S(1)}, u32[]{:S(2)}) copy-start(bf16[8,1,128,128]{3,2,1,0:T(8,128)(2,1)S(1)} %pad_maximum_fusion) | copy-start | bytes 786436
  1.0 12.2 %collective-permute-start = (bf16[1024,128]{1,0:T(8,128)(2,1)S(1)}, bf16[1024,128]{1,0:T(8,128)(2,1)S(1)}, u32[]{:S(2)}, u32[]{:S(2)}) collective-permute-start(bf16[1024,128]{1,0:T(8,128)(2,1)S(1)} %bitcast.10), channel_id=1, source_target_pairs={{0,16},{8,24},{16,32},{24,40},{32,48},{40,56},{48,64},{56,72},{64,... | collective-permute-start | bytes 786440 | tf_op jit(solution)/shard_map/ppermute | solution.py:349
  3.0 10.2 %collective-permute-start.1 = (bf16[1024,128]{1,0:T(8,128)(2,1)S(1)}, bf16[1024,128]{1,0:T(8,128)(2,1)S(1)}, u32[]{:S(2)}, u32[]{:S(2)}) collective-permute-start(bf16[1024,128]{1,0:T(8,128)(2,1)S(1)} %bitcast.11), channel_id=1, source_target_pairs={{0,112},{8,120},{16,0},{24,8},{32,16},{40,24},{48,32},{56,40},{64,... | collective-permute-start | bytes 786440 | tf_op jit(solution)/shard_map/ppermute | solution.py:350
  13.2 8.7 %collective-permute-start.5 = (bf16[1024,128]{1,0:T(8,128)(2,1)S(1)}, bf16[1024,128]{1,0:T(8,128)(2,1)S(1)}, u32[]{:S(2)}, u32[]{:S(2)}) collective-permute-start(bf16[1024,128]{1,0:T(8,128)(2,1)S(1)} %collective-permute-done.up1), channel_id=1, source_target_pairs={{0,16},{8,24},{16,32},{24,40},{32,48},{40,56},{48,64},{56,72},{64,... | collective-permute-start | bytes 786440 | tf_op jit(solution)/shard_map/ppermute | solution.py:368
  13.3 8.7 %collective-permute-start.6 = (bf16[1024,128]{1,0:T(8,128)(2,1)S(1)}, bf16[1024,128]{1,0:T(8,128)(2,1)S(1)}, u32[]{:S(2)}, u32[]{:S(2)}) collective-permute-start(bf16[1024,128]{1,0:T(8,128)(2,1)S(1)} %collective-permute-done.1.dn1), channel_id=1, source_target_pairs={{0,112},{8,120},{16,0},{24,8},{32,16},{40,24},{48,32},{56,40},{64,... | collective-permute-start | bytes 786440 | tf_op jit(solution)/shard_map/ppermute | solution.py:369
  16.5 10.4 %collective-permute-start.2 = (bf16[528,128]{1,0:T(8,128)(2,1)}, bf16[528,128]{1,0:T(8,128)(2,1)S(1)}, u32[]{:S(2)}, u32[]{:S(2)}) collective-permute-start(bf16[528,128]{1,0:T(8,128)(2,1)} %get-tuple-element.23), channel_id=1, source_target_pairs={{0,8},{8,0},{16,24},{24,16},{32,40},{40,32},{48,56},{56,48},{64,72... | collective-permute-start | bytes 405512 | tf_op jit(solution)/shard_map/ppermute | solution.py:370
  16.6 11.7 %collective-permute-start.3 = (bf16[528,128]{1,0:T(8,128)(2,1)}, bf16[528,128]{1,0:T(8,128)(2,1)S(1)}, u32[]{:S(2)}, u32[]{:S(2)}) collective-permute-start(bf16[528,128]{1,0:T(8,128)(2,1)} %get-tuple-element.23), channel_id=1, source_target_pairs={{0,128},{8,136},{16,144},{24,152},{32,160},{40,168},{48,176},{56,1... | collective-permute-start | bytes 405512 | tf_op jit(solution)/shard_map/ppermute | solution.py:370
  18.8 9.5 %collective-permute-start.4 = (bf16[528,128]{1,0:T(8,128)(2,1)}, bf16[528,128]{1,0:T(8,128)(2,1)S(1)}, u32[]{:S(2)}, u32[]{:S(2)}) collective-permute-start(bf16[528,128]{1,0:T(8,128)(2,1)} %get-tuple-element.23), channel_id=1, source_target_pairs={{0,136},{8,128},{16,152},{24,144},{32,168},{40,160},{48,184},{56,1... | collective-permute-start | bytes 405512 | tf_op jit(solution)/shard_map/ppermute | solution.py:370
  22.0 14.4 %collective-permute-start.9 = (bf16[1024,128]{1,0:T(8,128)(2,1)S(1)}, bf16[1024,128]{1,0:T(8,128)(2,1)S(1)}, u32[]{:S(2)}, u32[]{:S(2)}) collective-permute-start(bf16[1024,128]{1,0:T(8,128)(2,1)S(1)} %broadcast_select_fusion), channel_id=1, source_target_pairs={{0,32},{8,104},{16,48},{24,120},{32,64},{40,8},{48,80},{56,24},{64... | collective-permute-start | bytes 786440 | tf_op jit(solution)/shard_map/ppermute | solution.py:374
  25.1 12.2 %collective-permute-start.7 = (bf16[1024,128]{1,0:T(8,128)(2,1)S(1)}, bf16[1024,128]{1,0:T(8,128)(2,1)S(1)}, u32[]{:S(2)}, u32[]{:S(2)}) collective-permute-start(bf16[1024,128]{1,0:T(8,128)(2,1)S(1)} %collective-permute-done.5.up2), channel_id=1, source_target_pairs={{0,16},{8,24},{16,32},{24,40},{32,48},{40,56},{48,64},{56,72},{64,... | collective-permute-start | bytes 786440 | tf_op jit(solution)/shard_map/ppermute | solution.py:371
  26.9 10.4 %collective-permute-start.8 = (bf16[1024,128]{1,0:T(8,128)(2,1)S(1)}, bf16[1024,128]{1,0:T(8,128)(2,1)S(1)}, u32[]{:S(2)}, u32[]{:S(2)}) collective-permute-start(bf16[1024,128]{1,0:T(8,128)(2,1)S(1)} %collective-permute-done.6.dn2), channel_id=1, source_target_pairs={{0,112},{8,120},{16,0},{24,8},{32,16},{40,24},{48,32},{56,40},{64,... | collective-permute-start | bytes 786440 | tf_op jit(solution)/shard_map/ppermute | solution.py:372
  28.3 1.0 %copy-start = (bf16[1808,128]{1,0:T(8,128)(2,1)S(1)}, bf16[1808,128]{1,0:T(8,128)(2,1)}, u32[]{:S(2)}) copy-start(bf16[1808,128]{1,0:T(8,128)(2,1)} %get-tuple-element.21.local) | copy-start | bytes 1388548
  40.7 7.6 %collective-permute-start.10 = (bf16[144,512]{1,0:T(8,128)(2,1)S(1)}, bf16[144,512]{1,0:T(8,128)(2,1)S(1)}, u32[]{:S(2)}, u32[]{:S(2)}) collective-permute-start(bf16[144,512]{1,0:T(8,128)(2,1)S(1)} %get-tuple-element.32), channel_id=1, source_target_pairs={{0,136},{8,128},{16,152},{24,144},{32,168},{40,160},{48,184},{56,1... | collective-permute-start | bytes 442376 | tf_op jit(solution)/shard_map/ppermute | solution.py:387
  40.8 8.3 %collective-permute-start.11 = (bf16[144,512]{1,0:T(8,128)(2,1)S(1)}, bf16[144,512]{1,0:T(8,128)(2,1)S(1)}, u32[]{:S(2)}, u32[]{:S(2)}) collective-permute-start(bf16[144,512]{1,0:T(8,128)(2,1)S(1)} %get-tuple-element.33), channel_id=1, source_target_pairs={{0,128},{8,136},{16,144},{24,152},{32,160},{40,168},{48,176},{56,1... | collective-permute-start | bytes 442376 | tf_op jit(solution)/shard_map/ppermute | solution.py:387
  42.5 6.5 %collective-permute-start.12 = (bf16[144,512]{1,0:T(8,128)(2,1)S(1)}, bf16[144,512]{1,0:T(8,128)(2,1)S(1)}, u32[]{:S(2)}, u32[]{:S(2)}) collective-permute-start(bf16[144,512]{1,0:T(8,128)(2,1)S(1)} %get-tuple-element.34), channel_id=1, source_target_pairs={{0,8},{8,0},{16,24},{24,16},{32,40},{40,32},{48,56},{56,48},{64,72... | collective-permute-start | bytes 442376 | tf_op jit(solution)/shard_map/ppermute | solution.py:387
  52.7 12.2 %collective-permute-start.13 = (bf16[32,5120]{1,0:T(8,128)(2,1)S(1)}, bf16[32,5120]{1,0:T(8,128)(2,1)S(1)}, u32[]{:S(2)}, u32[]{:S(2)}) collective-permute-start(bf16[32,5120]{1,0:T(8,128)(2,1)S(1)} %get-tuple-element.39), channel_id=1, source_target_pairs={{0,2},{1,3},{2,0},{3,1},{4,6},{5,7},{6,4},{7,5},{8,10},{9,11},{10,... | collective-permute-start | bytes 983048 | tf_op jit(solution)/shard_map/ppermute | solution.py:402
  56.0 15.9 %collective-permute-start.14 = (bf16[32,5120]{1,0:T(8,128)(2,1)S(1)}, bf16[32,5120]{1,0:T(8,128)(2,1)S(1)}, u32[]{:S(2)}, u32[]{:S(2)}) collective-permute-start(bf16[32,5120]{1,0:T(8,128)(2,1)S(1)} %get-tuple-element.38), channel_id=1, source_target_pairs={{0,1},{1,2},{2,3},{3,0},{4,5},{5,6},{6,7},{7,4},{8,9},{9,10},{10,1... | collective-permute-start | bytes 983048 | tf_op jit(solution)/shard_map/ppermute | solution.py:402
  56.7 15.6 %collective-permute-start.15 = (bf16[32,5120]{1,0:T(8,128)(2,1)S(1)}, bf16[32,5120]{1,0:T(8,128)(2,1)S(1)}, u32[]{:S(2)}, u32[]{:S(2)}) collective-permute-start(bf16[32,5120]{1,0:T(8,128)(2,1)S(1)} %get-tuple-element.37), channel_id=1, source_target_pairs={{0,3},{1,0},{2,1},{3,2},{4,7},{5,4},{6,5},{7,6},{8,11},{9,8},{10,9... | collective-permute-start | bytes 983048 | tf_op jit(solution)/shard_map/ppermute | solution.py:402
  72.4 6.3 %collective-permute-start.16 = (bf16[16,5120]{1,0:T(8,128)(2,1)S(1)}, bf16[16,5120]{1,0:T(8,128)(2,1)S(1)}, u32[]{:S(2)}, u32[]{:S(2)}) collective-permute-start(bf16[16,5120]{1,0:T(8,128)(2,1)S(1)} %get-tuple-element.36), channel_id=1, source_target_pairs={{0,4},{1,5},{2,6},{3,7},{4,0},{5,1},{6,2},{7,3},{8,12},{9,13},{10,... | collective-permute-start | bytes 491528 | tf_op jit(solution)/shard_map/ppermute | solution.py:413

commit v7 on v5

--- a/solution.py
+++ b/solution.py
@@ -63,10 +63,10 @@
         )
         for (_, k), p in zip(at, probs)
     ]
-    for (s, _), n, p, fix, part, (m_ref, l_ref, a_ref) in zip(at, news, probs, fixes, parts, streams):
+    for (s, _), o, n, p, fix, part, (m_ref, l_ref, a_ref) in zip(at, olds, news, probs, fixes, parts, streams):
         m_ref[s] = n
         l_ref[s] = l_ref[s] * fix + jnp.sum(p, axis=0, keepdims=True)
-        a_ref[s] = a_ref[s] * fix + part
+        a_ref[s] = jnp.where(o > NEG, a_ref[s] * fix, 0.0) + part
 
 
 def all_pairs(entries, q_ref, kv, streams):
@@ -82,17 +82,16 @@
 
 
 def clear(streams):
-    for m_ref, l_ref, a_ref in streams:
+    for m_ref, l_ref, _ in streams:
         m_ref[...] = jnp.full(m_ref.shape, NEG, F32)
         l_ref[...] = jnp.zeros(l_ref.shape, F32)
-        a_ref[...] = jnp.zeros(a_ref.shape, F32)
 
 
 def merge(states):
     top = functools.reduce(jnp.maximum, [m for m, _, _ in states])
     ws = [jnp.exp2((m - top) * C2) for m, _, _ in states]
     total = sum(w * l for w, (_, l, _) in zip(ws, states))
-    acc = sum(w * a for w, (_, _, a) in zip(ws, states))
+    acc = sum(jnp.where(m > NEG, w * a, 0.0) for w, (m, _, a) in zip(ws, states))
     return top, total, acc
 
 
@@ -122,9 +121,9 @@
         cp.wait()
 
 
-def near_kernel(maps, local, s1, s2, s3, up1, dn1, up2, dn2, q_out, list_far, *refs):
+def near_kernel(maps, local, s1, s2, s3, up1, dn1, up2, dn2, q_out, list_far, list_far_x, *refs):
     m_out, l_out, a_out, tails, ids, tbl, list_near, found, kv = refs[:9]
-    lists = (list_near, list_far)
+    lists = (list_near, list_far, list_far_x)
     streams = streams_of(refs[9:-1])
     sems = refs[-1]
     sents = (local, s1, s2, s3)
@@ -187,14 +186,15 @@
     def sort(i, counts):
         entry = found[i]
         kind = entry >> 16
+        kind = kind + (kind & (entry >> 10))
         out = []
-        for k in range(2):
+        for k in range(3):
             lists[k][counts[k] + 1] = entry & 65535
             out.append(counts[k] + (kind == k).astype(jnp.int32))
         return tuple(out)
 
-    counts = lax.fori_loop(0, total, sort, (jnp.int32(0),) * 2)
-    for k in range(2):
+    counts = lax.fori_loop(0, total, sort, (jnp.int32(0),) * 3)
+    for k in range(3):
         lists[k][0] = counts[k]
         for r in range(STREAMS - 1):
             lists[k][counts[k] + 1 + r] = jnp.int32(SESS * 256)
@@ -215,20 +215,19 @@
     return copies
 
 
-def far_kernel(nb, *refs):
+def far_kernel(nb, first, *refs):
     list_far, q_ref = refs[:2]
     blocks = refs[2:2 + nb]
     before = refs[2 + nb:5 + nb]
-    own = refs[5 + nb]
-    outs = refs[6 + nb:9 + nb]
-    kv = refs[9 + nb]
-    streams = streams_of(refs[10 + nb:-1])
+    outs = refs[5 + nb:7 + nb]
+    kv = refs[7 + nb]
+    streams = streams_of(refs[8 + nb:-1])
     copies = load_blocks(blocks, kv, [refs[-1].at[i] for i in range(nb)])
     clear(streams)
     for cp in copies:
         cp.wait()
     all_pairs(list_far, q_ref, kv, streams)
-    for s in range(SESS):
+    for s in range(first, first + SESS // 2):
         top, total, acc = merge([(m[s], l[s], a[s]) for m, l, a in [before] + streams])
         some = total > 0.0
         safe = jnp.where(some, total, 1.0)
@@ -236,10 +235,10 @@
         lse = jnp.where(some, top * C2 + jnp.log2(safe), NEG)
         lanes = pl.ds((s % 2) * QROWS, QROWS)
         if s < 2:
-            own[pl.ds(0, HD), lanes] = acc
-            own[pl.ds(HD, 8), lanes] = jnp.broadcast_to(lse, (8, QROWS))
+            outs[0][pl.ds(0, HD), lanes] = acc
+            outs[0][pl.ds(HD, 8), lanes] = jnp.broadcast_to(lse, (8, QROWS))
         else:
-            out = outs[s // 2 - 1]
+            out = outs[(s - first) // 2]
             out[pl.ds(0, HD), lanes] = acc.astype(BF)
             hi = lse.astype(BF).astype(F32)
             mid = (lse - hi).astype(BF).astype(F32)
@@ -298,9 +297,10 @@
     return pl.pallas_call(
         near_kernel,
         out_shape=[jax.ShapeDtypeStruct((SESS * QROWS, HD), BF), jax.ShapeDtypeStruct((160,), jnp.int32)]
+        + [jax.ShapeDtypeStruct((160,), jnp.int32)]
         + state_shapes(SESS),
         in_specs=[SMEM] + [VMEM] * 4 + [ANY] * 4,
-        out_specs=[VMEM, SMEM] + [VMEM] * 3,
+        out_specs=[VMEM, SMEM, SMEM] + [VMEM] * 3,
         scratch_shapes=[
             pltpu.VMEM((64, 128), BF),
             pltpu.VMEM((64, 128), jnp.int32),
@@ -317,20 +317,21 @@
     )(*args)
 
 
-def far_call(pages, q_all, blocks, state):
+def far_call(pages, q_all, blocks, state, first, name):
     nb = len(blocks)
+    part = jax.ShapeDtypeStruct((HD + 16, 2 * QROWS), BF)
+    own = jax.ShapeDtypeStruct((HD + 8, 2 * QROWS), F32)
     return pl.pallas_call(
-        functools.partial(far_kernel, nb),
-        out_shape=[jax.ShapeDtypeStruct((HD + 8, 2 * QROWS), F32)]
-        + [jax.ShapeDtypeStruct((HD + 16, 2 * QROWS), BF)] * 3,
+        functools.partial(far_kernel, nb, first),
+        out_shape=[part if first else own, part],
         in_specs=[SMEM, VMEM] + [ANY] * nb + [VMEM] * 3,
-        out_specs=[VMEM] * 4,
+        out_specs=[VMEM] * 2,
         scratch_shapes=[pltpu.VMEM((nb * BLOCK, HD), BF)]
         + stream_scratch() * STREAMS
         + [pltpu.SemaphoreType.DMA((nb,))],
         compiler_params=pltpu.CompilerParams(vmem_limit_bytes=24 << 20),
         cost_estimate=pl.CostEstimate(flops=10**9, bytes_accessed=4 << 20, transcendentals=1 << 20),
-        name="far_pages",
+        name=name,
     )(pages, q_all, *blocks, *state)
 
 
@@ -377,9 +378,13 @@
     for k, offsets in enumerate(GROUPS):
         for i, o in enumerate(offsets):
             maps = jnp.where(same & (step == o % Z), k * 65536 + i * 8, maps)
-    q_all, list_far, *state = near_call(maps, local, *sents, up1, dn1, up2, dn2)
-    own, p1, p2, p3 = far_call(list_far, q_all, (up3, dn3, opposite), state)
-    back = [lax.ppermute(p, "rep", group_perm(r)) for r, p in ((3, p3), (2, p2), (1, p1))]
+    q_all, list_far, list_far_x, *state = near_call(maps, local, *sents, up1, dn1, up2, dn2)
+    blocks = (up3, dn3, opposite)
+    p2, p3 = far_call(list_far_x, q_all, blocks, state, SESS // 2, "far_pages_x")
+    p3 = lax.ppermute(p3, "rep", group_perm(3))
+    p2 = lax.ppermute(p2, "rep", group_perm(2))
+    own, p1 = far_call(list_far, q_all, blocks, state, 0, "far_pages_own")
+    back = [p3, p2, lax.ppermute(p1, "rep", group_perm(1))]
     width = out_weight.shape[1]
     attn = pl.pallas_call(
         combine_kernel,

time: 77.3 us -> 77.2 us (level); the launches traced: 77.3 us -> 76 us
  waiting for transfers between devices: 21 us -> 15.2 us
  Pallas kernels: 13.1 us -> 15.7 us
  starting transfers between devices: 37.7 us -> 39.5 us
    ppermute x3, waiting for transfers between devices: 6.79 us -> 2.14 us  [the longest x1 1.4 us: on_device(): p3 = lax.ppermute(p3, 'rep', group_perm(3))]
    pallas_call x1 -> x2, Pallas kernels: 2.92 us -> 4.5 us  [far_call(): pl.pallas_call(functools.partial(far_kernel, nb, first), out_shape=[part...]
    ppermute x7, starting transfers between devices: 15.2 us -> 16.2 us  [on_device(): lax.ppermute(part, 'head', [(i, (i & 4 ^ dx * 4) + (i + dy & 3)) for i in...]
    pallas_call x1, Pallas kernels: 6.42 us -> 7.43 us  [near_call(): pl.pallas_call(near_kernel, out_shape=[jax.ShapeDtypeStruct((SESS * QROWS...]
    ppermute x1, waiting for transfers between devices: 1.5 us -> 0.49 us  [on_device(): up3 = lax.ppermute(up2, 'rep', z_perm(1))]
  transfers between devices with their start and end apart: 20 -> 20, of which waited for: 9 -> 8; matrix products, arithmetic and copies ran while one was open for 0% -> 0% of each run, Pallas kernels for 12% -> 16%
where the time goes in v7:
time: 77.2 us; the launch traced here: 76 us
  starting transfers between devices  39.5 us (51%)
  Pallas kernels  15.7 us (20%)
  waiting for transfers between devices  15.2 us (20%)
  matrix products  3.34 us (4%)
  local copies, waits for them, and re-layouts  1.11 us (1%)
  other arithmetic  1.03 us (1%)
    ppermute x7, starting transfers between devices, on_device(): lax.ppermute(part, 'head', [(i, (i & 4 ^ dx * 4) + (i + dy & 3)) for i in...  16.2 us
    pallas_call x1, Pallas kernels, near_call(): pl.pallas_call(near_kernel, out_shape=[jax.ShapeDtypeStruct((SESS * QROWS...  7.43 us
    ppermute x7, waiting for transfers between devices, on_device(): lax.ppermute(part, 'head', [(i, (i & 4 ^ dx * 4) + (i + dy & 3)) for i in...  7.1 us
    pallas_call x2, Pallas kernels, far_call(): pl.pallas_call(functools.partial(far_kernel, nb, first), out_shape=[part...  4.5 us
    ppermute x1, starting transfers between devices, on_device(): dn1 = lax.ppermute(kv, 'rep', z_perm(-1))  4.03 us
    ppermute x1, waiting for transfers between devices, on_device(): up1 = lax.ppermute(kv, 'rep', z_perm(1))  3.51 us
    ppermute x3, starting transfers between devices, on_device(): sents = [lax.ppermute(sent, 'rep', group_perm(r)) for r in (1, 2, 3)]  3.46 us
    dot_general x1, matrix products, on_device(): rows = jnp.dot(attn, out_weight, preferred_element_type=F32).astype(BF)  3.34 us
  transfers between devices with their start and end apart: 20, of which 8 were waited for; matrix products, arithmetic and copies ran while one was open for 0% of the time, Pallas kernels for 16%

profile of v7, /device:TPU:2, one launch (start us, length us, event | category | flops | bytes accessed | tf_op | source)
XLA Modules:
  0.0 76.0 jit_solution(8792326267577467785)
XLA Ops:
  1.0 2.0 %collective-permute-start = (bf16[1024,128]{1,0:T(8,128)(2,1)S(1)}, bf16[1024,128]{1,0:T(8,128)(2,1)S(1)}, u32[]{:S(2)}, u32[]{:S(2)}) collective-permute-start(bf16[1024,128]{1,0:T(8,128)(2,1)S(1)} %bitcast.10), channel_id=1, source_target_pairs={{0,16},{8,24},{16,32},{24,40},{32,48},{40,56},{48,64},{56,72},{64,... | collective-permute-start | bytes 786440 | tf_op jit(solution)/shard_map/ppermute | solution.py:345
  3.0 4.0 %collective-permute-start.1 = (bf16[1024,128]{1,0:T(8,128)(2,1)S(1)}, bf16[1024,128]{1,0:T(8,128)(2,1)S(1)}, u32[]{:S(2)}, u32[]{:S(2)}) collective-permute-start(bf16[1024,128]{1,0:T(8,128)(2,1)S(1)} %bitcast.11), channel_id=1, source_target_pairs={{0,112},{8,120},{16,0},{24,8},{32,16},{40,24},{48,32},{56,40},{64,... | collective-permute-start | bytes 786440 | tf_op jit(solution)/shard_map/ppermute | solution.py:346
  7.0 2.7 %pack.1 = (bf16[528,128]{1,0:T(8,128)(2,1)}, bf16[1808,128]{1,0:T(8,128)(2,1)}) custom-call(bf16[512,128]{1,0:T(8,128)(2,1)} %bitcast.15, bf16[128,128]{1,0:T(8,128)(2,1)} %bitcast.16, bf16[128,128]{1,0:T(8,128)(2,1)} %bitcast.17, bf16[512,128]{1,0:T(8,128)(2,1)} %bitcast.13, bf16[512,128]{1,0:T(8,128)(2,1)} %bitcast.14, s32[2,16]{1,0:T(2,128)} %table.1, ...), custom_call_target="tpu_custom_call" | custom-call | tf_op jit(solution)/shard_map/pack/pallas_call | solution.py:347
  9.7 3.5 %collective-permute-done.up1 = bf16[1024,128]{1,0:T(8,128)(2,1)S(1)} collective-permute-done((bf16[1024,128]{1,0:T(8,128)(2,1)S(1)}, bf16[1024,128]{1,0:T(8,128)(2,1)S(1)}, u32[]{:S(2)}, u32[]{:S(2)}) %collective-permute-start) | collective-permute-done | bytes 262176 | tf_op jit(solution)/shard_map/ppermute | solution.py:345
  13.3 3.2 %collective-permute-start.6 = (bf16[1024,128]{1,0:T(8,128)(2,1)S(1)}, bf16[1024,128]{1,0:T(8,128)(2,1)S(1)}, u32[]{:S(2)}, u32[]{:S(2)}) collective-permute-start(bf16[1024,128]{1,0:T(8,128)(2,1)S(1)} %collective-permute-done.1.dn1), channel_id=1, source_target_pairs={{0,112},{8,120},{16,0},{24,8},{32,16},{40,24},{48,32},{56,40},{64,... | collective-permute-start | bytes 786440 | tf_op jit(solution)/shard_map/ppermute | solution.py:365
  16.6 2.2 %collective-permute-start.3 = (bf16[528,128]{1,0:T(8,128)(2,1)}, bf16[528,128]{1,0:T(8,128)(2,1)S(1)}, u32[]{:S(2)}, u32[]{:S(2)}) collective-permute-start(bf16[528,128]{1,0:T(8,128)(2,1)} %get-tuple-element.22), channel_id=1, source_target_pairs={{0,128},{8,136},{16,144},{24,152},{32,160},{40,168},{48,176},{56,1... | collective-permute-start | bytes 405512 | tf_op jit(solution)/shard_map/ppermute | solution.py:366
  20.0 2.0 %collective-permute-done.5.up2 = bf16[1024,128]{1,0:T(8,128)(2,1)S(1)} collective-permute-done((bf16[1024,128]{1,0:T(8,128)(2,1)S(1)}, bf16[1024,128]{1,0:T(8,128)(2,1)S(1)}, u32[]{:S(2)}, u32[]{:S(2)}) %collective-permute-start.5) | collective-permute-done | bytes 262176 | tf_op jit(solution)/shard_map/ppermute | solution.py:364
  22.0 3.1 %collective-permute-start.9 = (bf16[1024,128]{1,0:T(8,128)(2,1)S(1)}, bf16[1024,128]{1,0:T(8,128)(2,1)S(1)}, u32[]{:S(2)}, u32[]{:S(2)}) collective-permute-start(bf16[1024,128]{1,0:T(8,128)(2,1)S(1)} %broadcast_select_fusion), channel_id=1, source_target_pairs={{0,32},{8,104},{16,48},{24,120},{32,64},{40,8},{48,80},{56,24},{64... | collective-permute-start | bytes 786440 | tf_op jit(solution)/shard_map/ppermute | solution.py:370
  25.1 1.8 %collective-permute-start.7 = (bf16[1024,128]{1,0:T(8,128)(2,1)S(1)}, bf16[1024,128]{1,0:T(8,128)(2,1)S(1)}, u32[]{:S(2)}, u32[]{:S(2)}) collective-permute-start(bf16[1024,128]{1,0:T(8,128)(2,1)S(1)} %collective-permute-done.5.up2), channel_id=1, source_target_pairs={{0,16},{8,24},{16,32},{24,40},{32,48},{40,56},{48,64},{56,72},{64,... | collective-permute-start | bytes 786440 | tf_op jit(solution)/shard_map/ppermute | solution.py:367
  26.9 1.4 %collective-permute-start.8 = (bf16[1024,128]{1,0:T(8,128)(2,1)S(1)}, bf16[1024,128]{1,0:T(8,128)(2,1)S(1)}, u32[]{:S(2)}, u32[]{:S(2)}) collective-permute-start(bf16[1024,128]{1,0:T(8,128)(2,1)S(1)} %collective-permute-done.6.dn2), channel_id=1, source_target_pairs={{0,112},{8,120},{16,0},{24,8},{32,16},{40,24},{48,32},{56,40},{64,... | collective-permute-start | bytes 786440 | tf_op jit(solution)/shard_map/ppermute | solution.py:368
  29.3 7.4 %near_pages.1 = (bf16[2048,128]{1,0:T(8,128)(2,1)S(1)}, s32[160]{0:T(256)S(1)}, s32[160]{0:T(256)S(1)}, f32[8,1,256]{2,1,0:T(1,128)S(1)}, f32[8,1,256]{2,1,0:T(1,128)S(1)}, /*index=5*/f32[8,128,256]{2,1,0:T(8,128)S(1)}) custom-call(s32[32]{0:T(128)S(1)} %and_select_fusion.7.maps, bf16[1808,128]{1,0:T(8,128)(2,1)S(1)} %copy-done, ...), custom_call_target="tpu_custom_call" | custom-call | flops 4000000000 | bytes 4194304 | tf_op jit(solution)/shard_map/near_pages/pallas_call | solution.py:297
  37.3 2.5 %far_pages_x.1 = (bf16[144,512]{1,0:T(8,128)(2,1)S(1)}, bf16[144,512]{1,0:T(8,128)(2,1)S(1)}) custom-call(s32[160]{0:T(256)S(1)} %get-tuple-element.31.refs_0_, bf16[2048,128]{1,0:T(8,128)(2,1)S(1)} %get-tuple-element.26.refs_1_, bf16[1024,128]{1,0:T(8,128)(2,1)S(1)} %collective-permute-done.7.refs_2_, bf16[1024,128]{1,0:T(8,128)(2,1)S(1)} %collective-permute-done.8.refs_3_, ...), custom_call_target="tpu_custom_call" | custom-call | flops 1000000000 | bytes 4194304 | tf_op jit(solution)/shard_map/far_pages_x/pallas_call | solution.py:324
  39.9 1.7 %collective-permute-start.11 = (bf16[144,512]{1,0:T(8,128)(2,1)S(1)}, bf16[144,512]{1,0:T(8,128)(2,1)S(1)}, u32[]{:S(2)}, u32[]{:S(2)}) collective-permute-start(bf16[144,512]{1,0:T(8,128)(2,1)S(1)} %get-tuple-element.33), channel_id=1, source_target_pairs={{0,128},{8,136},{16,144},{24,152},{32,160},{40,168},{48,176},{56,1... | collective-permute-start | bytes 442376 | tf_op jit(solution)/shard_map/ppermute | solution.py:385
  41.6 2.0 %far_pages_own.1 = (f32[136,512]{1,0:T(8,128)S(1)}, bf16[144,512]{1,0:T(8,128)(2,1)S(1)}) custom-call(s32[160]{0:T(256)S(1)} %get-tuple-element.25.refs_0_, bf16[2048,128]{1,0:T(8,128)(2,1)S(1)} %get-tuple-element.26.refs_1_, bf16[1024,128]{1,0:T(8,128)(2,1)S(1)} %collective-permute-done.7.refs_2_, bf16[1024,128]{1,0:T(8,128)(2,1)S(1)} %collective-permute-done.8.refs_3_, ...), custom_call_target="tpu_custom_call" | custom-call | flops 1000000000 | bytes 4194304 | tf_op jit(solution)/shard_map/far_pages_own/pallas_call | solution.py:324
  43.6 2.4 %collective-permute-start.12 = (bf16[144,512]{1,0:T(8,128)(2,1)S(1)}, bf16[144,512]{1,0:T(8,128)(2,1)S(1)}, u32[]{:S(2)}, u32[]{:S(2)}) collective-permute-start(bf16[144,512]{1,0:T(8,128)(2,1)S(1)} %get-tuple-element.34), channel_id=1, source_target_pairs={{0,8},{8,0},{16,24},{24,16},{32,40},{40,32},{48,56},{56,48},{64,72... | collective-permute-start | bytes 442376 | tf_op jit(solution)/shard_map/ppermute | solution.py:387
  48.4 3.3 %convolution_convert_fusion = bf16[128,5120]{1,0:T(8,128)(2,1)S(1)} fusion(bf16[128,512]{1,0:T(8,128)(2,1)S(1)} %combine.1, bf16[512,5120]{1,0:T(8,128)(2,1)} %param.15), kind=kOutput, calls=%fused_computation | convolution fusion | flops 671744000 | bytes 6684672 | tf_op jit(solution)/shard_map/dot_general | solution.py:399
  51.8 1.7 %collective-permute-start.13 = (bf16[16,5120]{1,0:T(8,128)(2,1)S(1)}, bf16[16,5120]{1,0:T(8,128)(2,1)S(1)}, u32[]{:S(2)}, u32[]{:S(2)}) collective-permute-start(bf16[16,5120]{1,0:T(8,128)(2,1)S(1)} %get-tuple-element.41), channel_id=1, source_target_pairs={{0,1},{1,2},{2,3},{3,0},{4,5},{5,6},{6,7},{7,4},{8,9},{9,10},{10,1... | collective-permute-start | bytes 491528 | tf_op jit(solution)/shard_map/ppermute | solution.py:402
  53.5 1.7 %collective-permute-start.14 = (bf16[16,5120]{1,0:T(8,128)(2,1)S(1)}, bf16[16,5120]{1,0:T(8,128)(2,1)S(1)}, u32[]{:S(2)}, u32[]{:S(2)}) collective-permute-start(bf16[16,5120]{1,0:T(8,128)(2,1)S(1)} %get-tuple-element.40), channel_id=1, source_target_pairs={{0,3},{1,0},{2,1},{3,2},{4,7},{5,4},{6,5},{7,6},{8,11},{9,8},{10,9... | collective-permute-start | bytes 491528 | tf_op jit(solution)/shard_map/ppermute | solution.py:402
  55.2 2.0 %collective-permute-start.15 = (bf16[16,5120]{1,0:T(8,128)(2,1)S(1)}, bf16[16,5120]{1,0:T(8,128)(2,1)S(1)}, u32[]{:S(2)}, u32[]{:S(2)}) collective-permute-start(bf16[16,5120]{1,0:T(8,128)(2,1)S(1)} %get-tuple-element.39), channel_id=1, source_target_pairs={{0,2},{1,3},{2,0},{3,1},{4,6},{5,7},{6,4},{7,5},{8,10},{9,11},{10,... | collective-permute-start | bytes 491528 | tf_op jit(solution)/shard_map/ppermute | solution.py:402
  57.1 2.3 %collective-permute-start.16 = (bf16[16,5120]{1,0:T(8,128)(2,1)S(1)}, bf16[16,5120]{1,0:T(8,128)(2,1)S(1)}, u32[]{:S(2)}, u32[]{:S(2)}) collective-permute-start(bf16[16,5120]{1,0:T(8,128)(2,1)S(1)} %get-tuple-element.38), channel_id=1, source_target_pairs={{0,4},{1,5},{2,6},{3,7},{4,0},{5,1},{6,2},{7,3},{8,12},{9,13},{10,... | collective-permute-start | bytes 491528 | tf_op jit(solution)/shard_map/ppermute | solution.py:402
  60.1 3.7 %collective-permute-start.18 = (bf16[16,5120]{1,0:T(8,128)(2,1)S(1)}, bf16[16,5120]{1,0:T(8,128)(2,1)S(1)}, u32[]{:S(2)}, u32[]{:S(2)}) collective-permute-start(bf16[16,5120]{1,0:T(8,128)(2,1)S(1)} %get-tuple-element.36), channel_id=1, source_target_pairs={{0,7},{1,4},{2,5},{3,6},{4,3},{5,0},{6,1},{7,2},{8,15},{9,12},{10,... | collective-permute-start | bytes 491528 | tf_op jit(solution)/shard_map/ppermute | solution.py:402
  63.7 4.8 %collective-permute-start.19 = (bf16[16,5120]{1,0:T(8,128)(2,1)S(1)}, bf16[16,5120]{1,0:T(8,128)(2,1)S(1)}, u32[]{:S(2)}, u32[]{:S(2)}) collective-permute-start(bf16[16,5120]{1,0:T(8,128)(2,1)S(1)} %get-tuple-element.35), channel_id=1, source_target_pairs={{0,6},{1,7},{2,4},{3,5},{4,2},{5,3},{6,0},{7,1},{8,14},{9,15},{10,... | collective-permute-start | bytes 491528 | tf_op jit(solution)/shard_map/ppermute | solution.py:402
  68.6 3.1 %collective-permute-done.18.refs_6_ = bf16[16,5120]{1,0:T(8,128)(2,1)S(1)} collective-permute-done((bf16[16,5120]{1,0:T(8,128)(2,1)S(1)}, bf16[16,5120]{1,0:T(8,128)(2,1)S(1)}, u32[]{:S(2)}, u32[]{:S(2)}) %collective-permute-start.18) | collective-permute-done | bytes 163872 | tf_op jit(solution)/shard_map/ppermute | solution.py:402
  71.7 3.5 %collective-permute-done.19.refs_7_ = bf16[16,5120]{1,0:T(8,128)(2,1)S(1)} collective-permute-done((bf16[16,5120]{1,0:T(8,128)(2,1)S(1)}, bf16[16,5120]{1,0:T(8,128)(2,1)S(1)}, u32[]{:S(2)}, u32[]{:S(2)}) %collective-permute-start.19) | collective-permute-done | bytes 163872 | tf_op jit(solution)/shard_map/ppermute | solution.py:402
  (31 shorter events, 7.8 us)
Async XLA Ops:
  1.0 6.0 %copy-start.1 = (bf16[8,1,128,128]{3,2,1,0:T(8,128)(2,1)}, bf16[8,1,128,128]{3,2,1,0:T(8,128)(2,1)S(1)}, u32[]{:S(2)}) copy-start(bf16[8,1,128,128]{3,2,1,0:T(8,128)(2,1)S(1)} %pad_maximum_fusion) | copy-start | bytes 786436
  1.0 12.2 %collective-permute-start = (bf16[1024,128]{1,0:T(8,128)(2,1)S(1)}, bf16[1024,128]{1,0:T(8,128)(2,1)S(1)}, u32[]{:S(2)}, u32[]{:S(2)}) collective-permute-start(bf16[1024,128]{1,0:T(8,128)(2,1)S(1)} %bitcast.10), channel_id=1, source_target_pairs={{0,16},{8,24},{16,32},{24,40},{32,48},{40,56},{48,64},{56,72},{64,... | collective-permute-start | bytes 786440 | tf_op jit(solution)/shard_map/ppermute | solution.py:345
  3.0 10.2 %collective-permute-start.1 = (bf16[1024,128]{1,0:T(8,128)(2,1)S(1)}, bf16[1024,128]{1,0:T(8,128)(2,1)S(1)}, u32[]{:S(2)}, u32[]{:S(2)}) collective-permute-start(bf16[1024,128]{1,0:T(8,128)(2,1)S(1)} %bitcast.11), channel_id=1, source_target_pairs={{0,112},{8,120},{16,0},{24,8},{32,16},{40,24},{48,32},{56,40},{64,... | collective-permute-start | bytes 786440 | tf_op jit(solution)/shard_map/ppermute | solution.py:346
  13.2 8.7 %collective-permute-start.5 = (bf16[1024,128]{1,0:T(8,128)(2,1)S(1)}, bf16[1024,128]{1,0:T(8,128)(2,1)S(1)}, u32[]{:S(2)}, u32[]{:S(2)}) collective-permute-start(bf16[1024,128]{1,0:T(8,128)(2,1)S(1)} %collective-permute-done.up1), channel_id=1, source_target_pairs={{0,16},{8,24},{16,32},{24,40},{32,48},{40,56},{48,64},{56,72},{64,... | collective-permute-start | bytes 786440 | tf_op jit(solution)/shard_map/ppermute | solution.py:364
  13.3 8.7 %collective-permute-start.6 = (bf16[1024,128]{1,0:T(8,128)(2,1)S(1)}, bf16[1024,128]{1,0:T(8,128)(2,1)S(1)}, u32[]{:S(2)}, u32[]{:S(2)}) collective-permute-start(bf16[1024,128]{1,0:T(8,128)(2,1)S(1)} %collective-permute-done.1.dn1), channel_id=1, source_target_pairs={{0,112},{8,120},{16,0},{24,8},{32,16},{40,24},{48,32},{56,40},{64,... | collective-permute-start | bytes 786440 | tf_op jit(solution)/shard_map/ppermute | solution.py:365
  16.5 10.4 %collective-permute-start.2 = (bf16[528,128]{1,0:T(8,128)(2,1)}, bf16[528,128]{1,0:T(8,128)(2,1)S(1)}, u32[]{:S(2)}, u32[]{:S(2)}) collective-permute-start(bf16[528,128]{1,0:T(8,128)(2,1)} %get-tuple-element.22), channel_id=1, source_target_pairs={{0,8},{8,0},{16,24},{24,16},{32,40},{40,32},{48,56},{56,48},{64,72... | collective-permute-start | bytes 405512 | tf_op jit(solution)/shard_map/ppermute | solution.py:366
  16.6 11.7 %collective-permute-start.3 = (bf16[528,128]{1,0:T(8,128)(2,1)}, bf16[528,128]{1,0:T(8,128)(2,1)S(1)}, u32[]{:S(2)}, u32[]{:S(2)}) collective-permute-start(bf16[528,128]{1,0:T(8,128)(2,1)} %get-tuple-element.22), channel_id=1, source_target_pairs={{0,128},{8,136},{16,144},{24,152},{32,160},{40,168},{48,176},{56,1... | collective-permute-start | bytes 405512 | tf_op jit(solution)/shard_map/ppermute | solution.py:366
  18.8 9.5 %collective-permute-start.4 = (bf16[528,128]{1,0:T(8,128)(2,1)}, bf16[528,128]{1,0:T(8,128)(2,1)S(1)}, u32[]{:S(2)}, u32[]{:S(2)}) collective-permute-start(bf16[528,128]{1,0:T(8,128)(2,1)} %get-tuple-element.22), channel_id=1, source_target_pairs={{0,136},{8,128},{16,152},{24,144},{32,168},{40,160},{48,184},{56,1... | collective-permute-start | bytes 405512 | tf_op jit(solution)/shard_map/ppermute | solution.py:366
  22.0 14.8 %collective-permute-start.9 = (bf16[1024,128]{1,0:T(8,128)(2,1)S(1)}, bf16[1024,128]{1,0:T(8,128)(2,1)S(1)}, u32[]{:S(2)}, u32[]{:S(2)}) collective-permute-start(bf16[1024,128]{1,0:T(8,128)(2,1)S(1)} %broadcast_select_fusion), channel_id=1, source_target_pairs={{0,32},{8,104},{16,48},{24,120},{32,64},{40,8},{48,80},{56,24},{64... | collective-permute-start | bytes 786440 | tf_op jit(solution)/shard_map/ppermute | solution.py:370
  25.1 12.2 %collective-permute-start.7 = (bf16[1024,128]{1,0:T(8,128)(2,1)S(1)}, bf16[1024,128]{1,0:T(8,128)(2,1)S(1)}, u32[]{:S(2)}, u32[]{:S(2)}) collective-permute-start(bf16[1024,128]{1,0:T(8,128)(2,1)S(1)} %collective-permute-done.5.up2), channel_id=1, source_target_pairs={{0,16},{8,24},{16,32},{24,40},{32,48},{40,56},{48,64},{56,72},{64,... | collective-permute-start | bytes 786440 | tf_op jit(solution)/shard_map/ppermute | solution.py:367
  26.9 10.4 %collective-permute-start.8 = (bf16[1024,128]{1,0:T(8,128)(2,1)S(1)}, bf16[1024,128]{1,0:T(8,128)(2,1)S(1)}, u32[]{:S(2)}, u32[]{:S(2)}) collective-permute-start(bf16[1024,128]{1,0:T(8,128)(2,1)S(1)} %collective-permute-done.6.dn2), channel_id=1, source_target_pairs={{0,112},{8,120},{16,0},{24,8},{32,16},{40,24},{48,32},{56,40},{64,... | collective-permute-start | bytes 786440 | tf_op jit(solution)/shard_map/ppermute | solution.py:368
  28.3 1.0 %copy-start = (bf16[1808,128]{1,0:T(8,128)(2,1)S(1)}, bf16[1808,128]{1,0:T(8,128)(2,1)}, u32[]{:S(2)}) copy-start(bf16[1808,128]{1,0:T(8,128)(2,1)} %get-tuple-element.20.local) | copy-start | bytes 1388548
  39.8 7.6 %collective-permute-start.10 = (bf16[144,512]{1,0:T(8,128)(2,1)S(1)}, bf16[144,512]{1,0:T(8,128)(2,1)S(1)}, u32[]{:S(2)}, u32[]{:S(2)}) collective-permute-start(bf16[144,512]{1,0:T(8,128)(2,1)S(1)} %get-tuple-element.32), channel_id=1, source_target_pairs={{0,136},{8,128},{16,152},{24,144},{32,168},{40,160},{48,184},{56,1... | collective-permute-start | bytes 442376 | tf_op jit(solution)/shard_map/ppermute | solution.py:384
  39.9 8.3 %collective-permute-start.11 = (bf16[144,512]{1,0:T(8,128)(2,1)S(1)}, bf16[144,512]{1,0:T(8,128)(2,1)S(1)}, u32[]{:S(2)}, u32[]{:S(2)}) collective-permute-start(bf16[144,512]{1,0:T(8,128)(2,1)S(1)} %get-tuple-element.33), channel_id=1, source_target_pairs={{0,128},{8,136},{16,144},{24,152},{32,160},{40,168},{48,176},{56,1... | collective-permute-start | bytes 442376 | tf_op jit(solution)/shard_map/ppermute | solution.py:385
  43.6 4.6 %collective-permute-start.12 = (bf16[144,512]{1,0:T(8,128)(2,1)S(1)}, bf16[144,512]{1,0:T(8,128)(2,1)S(1)}, u32[]{:S(2)}, u32[]{:S(2)}) collective-permute-start(bf16[144,512]{1,0:T(8,128)(2,1)S(1)} %get-tuple-element.34), channel_id=1, source_target_pairs={{0,8},{8,0},{16,24},{24,16},{32,40},{40,32},{48,56},{56,48},{64,72... | collective-permute-start | bytes 442376 | tf_op jit(solution)/shard_map/ppermute | solution.py:387
  51.8 8.2 %collective-permute-start.13 = (bf16[16,5120]{1,0:T(8,128)(2,1)S(1)}, bf16[16,5120]{1,0:T(8,128)(2,1)S(1)}, u32[]{:S(2)}, u32[]{:S(2)}) collective-permute-start(bf16[16,5120]{1,0:T(8,128)(2,1)S(1)} %get-tuple-element.41), channel_id=1, source_target_pairs={{0,1},{1,2},{2,3},{3,0},{4,5},{5,6},{6,7},{7,4},{8,9},{9,10},{10,1... | collective-permute-start | bytes 491528 | tf_op jit(solution)/shard_map/ppermute | solution.py:402
  53.5 10.2 %collective-permute-start.14 = (bf16[16,5120]{1,0:T(8,128)(2,1)S(1)}, bf16[16,5120]{1,0:T(8,128)(2,1)S(1)}, u32[]{:S(2)}, u32[]{:S(2)}) collective-permute-start(bf16[16,5120]{1,0:T(8,128)(2,1)S(1)} %get-tuple-element.40), channel_id=1, source_target_pairs={{0,3},{1,0},{2,1},{3,2},{4,7},{5,4},{6,5},{7,6},{8,11},{9,8},{10,9... | collective-permute-start | bytes 491528 | tf_op jit(solution)/shard_map/ppermute | solution.py:402
  55.2 13.4 %collective-permute-start.15 = (bf16[16,5120]{1,0:T(8,128)(2,1)S(1)}, bf16[16,5120]{1,0:T(8,128)(2,1)S(1)}, u32[]{:S(2)}, u32[]{:S(2)}) collective-permute-start(bf16[16,5120]{1,0:T(8,128)(2,1)S(1)} %get-tuple-element.39), channel_id=1, source_target_pairs={{0,2},{1,3},{2,0},{3,1},{4,6},{5,7},{6,4},{7,5},{8,10},{9,11},{10,... | collective-permute-start | bytes 491528 | tf_op jit(solution)/shard_map/ppermute | solution.py:402
  57.1 11.4 %collective-permute-start.16 = (bf16[16,5120]{1,0:T(8,128)(2,1)S(1)}, bf16[16,5120]{1,0:T(8,128)(2,1)S(1)}, u32[]{:S(2)}, u32[]{:S(2)}) collective-permute-start(bf16[16,5120]{1,0:T(8,128)(2,1)S(1)} %get-tuple-element.38), channel_id=1, source_target_pairs={{0,4},{1,5},{2,6},{3,7},{4,0},{5,1},{6,2},{7,3},{8,12},{9,13},{10,... | collective-permute-start | bytes 491528 | tf_op jit(solution)/shard_map/ppermute | solution.py:402
  59.5 9.1 %collective-permute-start.17 = (bf16[16,5120]{1,0:T(8,128)(2,1)S(1)}, bf16[16,5120]{1,0:T(8,128)(2,1)S(1)}, u32[]{:S(2)}, u32[]{:S(2)}) collective-permute-start(bf16[16,5120]{1,0:T(8,128)(2,1)S(1)} %get-tuple-element.37), channel_id=1, source_target_pairs={{0,5},{1,6},{2,7},{3,4},{4,1},{5,2},{6,3},{7,0},{8,13},{9,14},{10,... | collective-permute-start | bytes 491528 | tf_op jit(solution)/shard_map/ppermute | solution.py:402
  60.1 11.6 %collective-permute-start.18 = (bf16[16,5120]{1,0:T(8,128)(2,1)S(1)}, bf16[16,5120]{1,0:T(8,128)(2,1)S(1)}, u32[]{:S(2)}, u32[]{:S(2)}) collective-permute-start(bf16[16,5120]{1,0:T(8,128)(2,1)S(1)} %get-tuple-element.36), channel_id=1, source_target_pairs={{0,7},{1,4},{2,5},{3,6},{4,3},{5,0},{6,1},{7,2},{8,15},{9,12},{10,... | collective-permute-start | bytes 491528 | tf_op jit(solution)/shard_map/ppermute | solution.py:402
  63.7 11.4 %collective-permute-start.19 = (bf16[16,5120]{1,0:T(8,128)(2,1)S(1)}, bf16[16,5120]{1,0:T(8,128)(2,1)S(1)}, u32[]{:S(2)}, u32[]{:S(2)}) collective-permute-start(bf16[16,5120]{1,0:T(8,128)(2,1)S(1)} %get-tuple-element.35), channel_id=1, source_target_pairs={{0,6},{1,7},{2,4},{3,5},{4,2},{5,3},{6,0},{7,1},{8,14},{9,15},{10,... | collective-permute-start | bytes 491528 | tf_op jit(solution)/shard_map/ppermute | solution.py:402

commit v8 on v7

--- a/solution.py
+++ b/solution.py
@@ -360,10 +360,11 @@
         prefix_keys.reshape(-1, HD), prefix_values.reshape(-1, HD), page_table, tree_parent.reshape(1, -1),
         kv,
     )
-    up1, dn1, sent = lax.optimization_barrier((up1, dn1, sent))
-    up2 = lax.ppermute(up1, "rep", z_perm(1))
-    dn2 = lax.ppermute(dn1, "rep", z_perm(-1))
-    sents = [lax.ppermute(sent, "rep", group_perm(r)) for r in (1, 2, 3)]
+    up2 = lax.ppermute(kv, "rep", z_perm(2))
+    dn2 = lax.ppermute(kv, "rep", z_perm(-2))
+    q_x = lax.ppermute(sent, "rep", group_perm(2))
+    q_x, sent = lax.optimization_barrier((q_x, sent))
+    sents = [lax.ppermute(sent, "rep", group_perm(1)), q_x, lax.ppermute(q_x, "rep", group_perm(1))]
     up3 = lax.ppermute(up2, "rep", z_perm(1))
     dn3 = lax.ppermute(dn2, "rep", z_perm(-1))
     held = jnp.where((rep & 1) == 0, up2, dn2)

time: 77.2 us -> 76.8 us (level)
  waiting for transfers between devices: 15.2 us -> 19.1 us
  Pallas kernels: 15.7 us -> 13 us
  starting transfers between devices: 39.5 us -> 38.5 us
    ppermute x1, waiting for transfers between devices: 3.51 us -> 0.01 us  [on_device(): up1 = lax.ppermute(kv, 'rep', z_perm(1))]
    ppermute x1, waiting for transfers between devices: 0.74 us -> 3.8 us  [on_device(): p2 = lax.ppermute(p2, 'rep', group_perm(2))]
    ppermute x5, waiting for transfers between devices: 1.99 us -> 4.94 us  [the longest x1 3.55 us: on_device(): dn2 = lax.ppermute(kv, 'rep', z_perm(-2))]
    ppermute x5, starting transfers between devices: 6.7 us -> 9.19 us  [the longest x1 3.35 us: on_device(): up2 = lax.ppermute(kv, 'rep', z_perm(2))]
    ppermute x1, starting transfers between devices: 0.09 us -> 2.53 us  [on_device(): p3 = lax.ppermute(p3, 'rep', group_perm(3))]
    ppermute x1, starting transfers between devices: 4.03 us -> 2.22 us  [on_device(): dn1 = lax.ppermute(kv, 'rep', z_perm(-1))]
    ppermute x1, starting transfers between devices: 2.41 us -> 0.61 us  [on_device(): back = [p3, p2, lax.ppermute(p1, 'rep', group_perm(1))]]
    pallas_call x2, Pallas kernels: 4.5 us -> 3.02 us  [far_call(): pl.pallas_call(functools.partial(far_kernel, nb, first), out_shape=[part...]
  transfers between devices with their start and end apart: 20 -> 20, of which waited for: 8 -> 11; matrix products, arithmetic and copies ran while one was open for 0% -> 0% of each run, Pallas kernels for 16% -> 14%
where the time goes in v8:
time: 76.8 us; the launch traced here: 76.2 us
  starting transfers between devices  38.5 us (50%)
  waiting for transfers between devices  19.1 us (25%)
  Pallas kernels  13 us (17%)
  matrix products  3.34 us (4%)
  local copies, waits for them, and re-layouts  1.11 us (1%)
  other arithmetic  1.03 us (1%)
    ppermute x7, starting transfers between devices, on_device(): lax.ppermute(part, 'head', [(i, (i & 4 ^ dx * 4) + (i + dy & 3)) for i in...  15.1 us
    ppermute x7, waiting for transfers between devices, on_device(): lax.ppermute(part, 'head', [(i, (i & 4 ^ dx * 4) + (i + dy & 3)) for i in...  7.25 us
    pallas_call x1, Pallas kernels, near_call(): pl.pallas_call(near_kernel, out_shape=[jax.ShapeDtypeStruct((SESS * QROWS...  6.23 us
    ppermute x1, starting transfers between devices, on_device(): lax.ppermute(held, 'rep', [(rep_of(a, z, c), rep_of(a, z + 2 - 4 * c, c))...  4.22 us
    ppermute x1, waiting for transfers between devices, on_device(): p2 = lax.ppermute(p2, 'rep', group_perm(2))  3.8 us
    ppermute x1, waiting for transfers between devices, on_device(): dn2 = lax.ppermute(kv, 'rep', z_perm(-2))  3.55 us
    ppermute x1, starting transfers between devices, on_device(): up2 = lax.ppermute(kv, 'rep', z_perm(2))  3.35 us
    dot_general x1, matrix products, on_device(): rows = jnp.dot(attn, out_weight, preferred_element_type=F32).astype(BF)  3.34 us
  transfers between devices with their start and end apart: 20, of which 11 were waited for; matrix products, arithmetic and copies ran while one was open for 0% of the time, Pallas kernels for 14%

profile of v8, /device:TPU:2, one launch (start us, length us, event | category | flops | bytes accessed | tf_op | source)
XLA Modules:
  0.0 76.2 jit_solution(12540475269273633336)
XLA Ops:
  1.0 3.3 %collective-permute-start.5 = (bf16[1024,128]{1,0:T(8,128)(2,1)S(1)}, bf16[1024,128]{1,0:T(8,128)(2,1)S(1)}, u32[]{:S(2)}, u32[]{:S(2)}) collective-permute-start(bf16[1024,128]{1,0:T(8,128)(2,1)S(1)} %bitcast.10), channel_id=1, source_target_pairs={{0,32},{8,40},{16,48},{24,56},{32,64},{40,72},{48,80},{56,88},{64,... | collective-permute-start | bytes 786440 | tf_op jit(solution)/shard_map/ppermute | solution.py:363
  4.4 3.1 %collective-permute-start.6 = (bf16[1024,128]{1,0:T(8,128)(2,1)S(1)}, bf16[1024,128]{1,0:T(8,128)(2,1)S(1)}, u32[]{:S(2)}, u32[]{:S(2)}) collective-permute-start(bf16[1024,128]{1,0:T(8,128)(2,1)S(1)} %bitcast.11), channel_id=1, source_target_pairs={{0,96},{8,104},{16,112},{24,120},{32,0},{40,8},{48,16},{56,24},{64... | collective-permute-start | bytes 786440 | tf_op jit(solution)/shard_map/ppermute | solution.py:364
  7.5 2.7 %pack.1 = (bf16[528,128]{1,0:T(8,128)(2,1)}, bf16[1808,128]{1,0:T(8,128)(2,1)}) custom-call(bf16[512,128]{1,0:T(8,128)(2,1)} %bitcast.17, bf16[128,128]{1,0:T(8,128)(2,1)} %bitcast.18, bf16[128,128]{1,0:T(8,128)(2,1)} %bitcast.19, bf16[512,128]{1,0:T(8,128)(2,1)} %bitcast.15, bf16[512,128]{1,0:T(8,128)(2,1)} %bitcast.16, s32[2,16]{1,0:T(2,128)} %table.1, ...), custom_call_target="tpu_custom_call" | custom-call | tf_op jit(solution)/shard_map/pack/pallas_call | solution.py:347
  10.2 2.2 %collective-permute-start = (bf16[528,128]{1,0:T(8,128)(2,1)}, bf16[528,128]{1,0:T(8,128)(2,1)S(1)}, u32[]{:S(2)}, u32[]{:S(2)}) collective-permute-start(bf16[528,128]{1,0:T(8,128)(2,1)} %get-tuple-element.21), channel_id=1, source_target_pairs={{0,128},{8,136},{16,144},{24,152},{32,160},{40,168},{48,176},{56,1... | collective-permute-start | bytes 405512 | tf_op jit(solution)/shard_map/ppermute | solution.py:365
  13.4 2.2 %collective-permute-start.4 = (bf16[1024,128]{1,0:T(8,128)(2,1)}, bf16[1024,128]{1,0:T(8,128)(2,1)S(1)}, u32[]{:S(2)}, u32[]{:S(2)}) collective-permute-start(bf16[1024,128]{1,0:T(8,128)(2,1)} %bitcast.14), channel_id=1, source_target_pairs={{0,112},{8,120},{16,0},{24,8},{32,16},{40,24},{48,32},{56,40},{64,... | collective-permute-start | bytes 786440 | tf_op jit(solution)/shard_map/ppermute | solution.py:346
  15.6 1.4 %collective-permute-done.s2 = bf16[528,128]{1,0:T(8,128)(2,1)S(1)} collective-permute-done((bf16[528,128]{1,0:T(8,128)(2,1)}, bf16[528,128]{1,0:T(8,128)(2,1)S(1)}, u32[]{:S(2)}, u32[]{:S(2)}) %collective-permute-start) | collective-permute-done | bytes 135200 | tf_op jit(solution)/shard_map/ppermute | solution.py:365
  17.5 3.6 %collective-permute-done.6.dn2 = bf16[1024,128]{1,0:T(8,128)(2,1)S(1)} collective-permute-done((bf16[1024,128]{1,0:T(8,128)(2,1)S(1)}, bf16[1024,128]{1,0:T(8,128)(2,1)S(1)}, u32[]{:S(2)}, u32[]{:S(2)}) %collective-permute-start.6) | collective-permute-done | bytes 262176 | tf_op jit(solution)/shard_map/ppermute | solution.py:364
  21.1 4.2 %collective-permute-start.9 = (bf16[1024,128]{1,0:T(8,128)(2,1)S(1)}, bf16[1024,128]{1,0:T(8,128)(2,1)S(1)}, u32[]{:S(2)}, u32[]{:S(2)}) collective-permute-start(bf16[1024,128]{1,0:T(8,128)(2,1)S(1)} %broadcast_select_fusion), channel_id=1, source_target_pairs={{0,32},{8,104},{16,48},{24,120},{32,64},{40,8},{48,80},{56,24},{64... | collective-permute-start | bytes 786440 | tf_op jit(solution)/shard_map/ppermute | solution.py:371
  25.8 1.3 %collective-permute-done.4.dn1 = bf16[1024,128]{1,0:T(8,128)(2,1)S(1)} collective-permute-done((bf16[1024,128]{1,0:T(8,128)(2,1)}, bf16[1024,128]{1,0:T(8,128)(2,1)S(1)}, u32[]{:S(2)}, u32[]{:S(2)}) %collective-permute-start.4) | collective-permute-done | bytes 262176 | tf_op jit(solution)/shard_map/ppermute | solution.py:346
  27.0 2.0 %collective-permute-start.8 = (bf16[1024,128]{1,0:T(8,128)(2,1)S(1)}, bf16[1024,128]{1,0:T(8,128)(2,1)S(1)}, u32[]{:S(2)}, u32[]{:S(2)}) collective-permute-start(bf16[1024,128]{1,0:T(8,128)(2,1)S(1)} %collective-permute-done.6.dn2), channel_id=1, source_target_pairs={{0,112},{8,120},{16,0},{24,8},{32,16},{40,24},{48,32},{56,40},{64,... | collective-permute-start | bytes 786440 | tf_op jit(solution)/shard_map/ppermute | solution.py:369
  30.1 6.2 %near_pages.1 = (bf16[2048,128]{1,0:T(8,128)(2,1)S(1)}, s32[160]{0:T(256)S(1)}, s32[160]{0:T(256)S(1)}, f32[8,1,256]{2,1,0:T(1,128)S(1)}, f32[8,1,256]{2,1,0:T(1,128)S(1)}, /*index=5*/f32[8,128,256]{2,1,0:T(8,128)S(1)}) custom-call(s32[32]{0:T(128)S(1)} %and_select_fusion.7.maps, bf16[1808,128]{1,0:T(8,128)(2,1)S(1)} %copy-done, ...), custom_call_target="tpu_custom_call" | custom-call | flops 4000000000 | bytes 4194304 | tf_op jit(solution)/shard_map/near_pages/pallas_call | solution.py:297
  37.0 1.5 %far_pages_x.1 = (bf16[144,512]{1,0:T(8,128)(2,1)S(1)}, bf16[144,512]{1,0:T(8,128)(2,1)S(1)}) custom-call(s32[160]{0:T(256)S(1)} %get-tuple-element.29.refs_0_, bf16[2048,128]{1,0:T(8,128)(2,1)S(1)} %get-tuple-element.24.refs_1_, bf16[1024,128]{1,0:T(8,128)(2,1)S(1)} %collective-permute-done.7.refs_2_, bf16[1024,128]{1,0:T(8,128)(2,1)S(1)} %collective-permute-done.8.refs_3_, ...), custom_call_target="tpu_custom_call" | custom-call | flops 1000000000 | bytes 4194304 | tf_op jit(solution)/shard_map/far_pages_x/pallas_call | solution.py:324
  38.5 2.5 %collective-permute-start.10 = (bf16[144,512]{1,0:T(8,128)(2,1)S(1)}, bf16[144,512]{1,0:T(8,128)(2,1)S(1)}, u32[]{:S(2)}, u32[]{:S(2)}) collective-permute-start(bf16[144,512]{1,0:T(8,128)(2,1)S(1)} %get-tuple-element.30), channel_id=1, source_target_pairs={{0,136},{8,128},{16,152},{24,144},{32,168},{40,160},{48,184},{56,1... | collective-permute-start | bytes 442376 | tf_op jit(solution)/shard_map/ppermute | solution.py:385
  42.3 1.5 %far_pages_own.1 = (f32[136,512]{1,0:T(8,128)S(1)}, bf16[144,512]{1,0:T(8,128)(2,1)S(1)}) custom-call(s32[160]{0:T(256)S(1)} %get-tuple-element.23.refs_0_, bf16[2048,128]{1,0:T(8,128)(2,1)S(1)} %get-tuple-element.24.refs_1_, bf16[1024,128]{1,0:T(8,128)(2,1)S(1)} %collective-permute-done.7.refs_2_, bf16[1024,128]{1,0:T(8,128)(2,1)S(1)} %collective-permute-done.8.refs_3_, ...), custom_call_target="tpu_custom_call" | custom-call | flops 1000000000 | bytes 4194304 | tf_op jit(solution)/shard_map/far_pages_own/pallas_call | solution.py:324
  45.6 3.8 %collective-permute-done.11.p2 = bf16[144,512]{1,0:T(8,128)(2,1)S(1)} collective-permute-done((bf16[144,512]{1,0:T(8,128)(2,1)S(1)}, bf16[144,512]{1,0:T(8,128)(2,1)S(1)}, u32[]{:S(2)}, u32[]{:S(2)}) %collective-permute-start.11) | collective-permute-done | bytes 147488 | tf_op jit(solution)/shard_map/ppermute | solution.py:386
  49.6 3.3 %convolution_convert_fusion = bf16[128,5120]{1,0:T(8,128)(2,1)S(1)} fusion(bf16[128,512]{1,0:T(8,128)(2,1)S(1)} %combine.1, bf16[512,5120]{1,0:T(8,128)(2,1)} %param.15), kind=kOutput, calls=%fused_computation | convolution fusion | flops 671744000 | bytes 6684672 | tf_op jit(solution)/shard_map/dot_general | solution.py:400
  53.1 1.7 %collective-permute-start.13 = (bf16[16,5120]{1,0:T(8,128)(2,1)S(1)}, bf16[16,5120]{1,0:T(8,128)(2,1)S(1)}, u32[]{:S(2)}, u32[]{:S(2)}) collective-permute-start(bf16[16,5120]{1,0:T(8,128)(2,1)S(1)} %get-tuple-element.39), channel_id=1, source_target_pairs={{0,1},{1,2},{2,3},{3,0},{4,5},{5,6},{6,7},{7,4},{8,9},{9,10},{10,1... | collective-permute-start | bytes 491528 | tf_op jit(solution)/shard_map/ppermute | solution.py:403
  54.7 1.6 %collective-permute-start.14 = (bf16[16,5120]{1,0:T(8,128)(2,1)S(1)}, bf16[16,5120]{1,0:T(8,128)(2,1)S(1)}, u32[]{:S(2)}, u32[]{:S(2)}) collective-permute-start(bf16[16,5120]{1,0:T(8,128)(2,1)S(1)} %get-tuple-element.38), channel_id=1, source_target_pairs={{0,3},{1,0},{2,1},{3,2},{4,7},{5,4},{6,5},{7,6},{8,11},{9,8},{10,9... | collective-permute-start | bytes 491528 | tf_op jit(solution)/shard_map/ppermute | solution.py:403
  56.4 2.0 %collective-permute-start.15 = (bf16[16,5120]{1,0:T(8,128)(2,1)S(1)}, bf16[16,5120]{1,0:T(8,128)(2,1)S(1)}, u32[]{:S(2)}, u32[]{:S(2)}) collective-permute-start(bf16[16,5120]{1,0:T(8,128)(2,1)S(1)} %get-tuple-element.37), channel_id=1, source_target_pairs={{0,2},{1,3},{2,0},{3,1},{4,6},{5,7},{6,4},{7,5},{8,10},{9,11},{10,... | collective-permute-start | bytes 491528 | tf_op jit(solution)/shard_map/ppermute | solution.py:403
  59.3 1.2 %collective-permute-start.17 = (bf16[16,5120]{1,0:T(8,128)(2,1)S(1)}, bf16[16,5120]{1,0:T(8,128)(2,1)S(1)}, u32[]{:S(2)}, u32[]{:S(2)}) collective-permute-start(bf16[16,5120]{1,0:T(8,128)(2,1)S(1)} %get-tuple-element.35), channel_id=1, source_target_pairs={{0,5},{1,6},{2,7},{3,4},{4,1},{5,2},{6,3},{7,0},{8,13},{9,14},{10,... | collective-permute-start | bytes 491528 | tf_op jit(solution)/shard_map/ppermute | solution.py:403
  60.6 2.9 %collective-permute-start.18 = (bf16[16,5120]{1,0:T(8,128)(2,1)S(1)}, bf16[16,5120]{1,0:T(8,128)(2,1)S(1)}, u32[]{:S(2)}, u32[]{:S(2)}) collective-permute-start(bf16[16,5120]{1,0:T(8,128)(2,1)S(1)} %get-tuple-element.34), channel_id=1, source_target_pairs={{0,7},{1,4},{2,5},{3,6},{4,3},{5,0},{6,1},{7,2},{8,15},{9,12},{10,... | collective-permute-start | bytes 491528 | tf_op jit(solution)/shard_map/ppermute | solution.py:403
  63.5 4.7 %collective-permute-start.19 = (bf16[16,5120]{1,0:T(8,128)(2,1)S(1)}, bf16[16,5120]{1,0:T(8,128)(2,1)S(1)}, u32[]{:S(2)}, u32[]{:S(2)}) collective-permute-start(bf16[16,5120]{1,0:T(8,128)(2,1)S(1)} %get-tuple-element.33), channel_id=1, source_target_pairs={{0,6},{1,7},{2,4},{3,5},{4,2},{5,3},{6,0},{7,1},{8,14},{9,15},{10,... | collective-permute-start | bytes 491528 | tf_op jit(solution)/shard_map/ppermute | solution.py:403
  69.1 3.5 %collective-permute-done.18.refs_6_ = bf16[16,5120]{1,0:T(8,128)(2,1)S(1)} collective-permute-done((bf16[16,5120]{1,0:T(8,128)(2,1)S(1)}, bf16[16,5120]{1,0:T(8,128)(2,1)S(1)}, u32[]{:S(2)}, u32[]{:S(2)}) %collective-permute-start.18) | collective-permute-done | bytes 163872 | tf_op jit(solution)/shard_map/ppermute | solution.py:403
  72.6 2.8 %collective-permute-done.19.refs_7_ = bf16[16,5120]{1,0:T(8,128)(2,1)S(1)} collective-permute-done((bf16[16,5120]{1,0:T(8,128)(2,1)S(1)}, bf16[16,5120]{1,0:T(8,128)(2,1)S(1)}, u32[]{:S(2)}, u32[]{:S(2)}) %collective-permute-start.19) | collective-permute-done | bytes 163872 | tf_op jit(solution)/shard_map/ppermute | solution.py:403
  (31 shorter events, 10.7 us)
Async XLA Ops:
  1.0 6.5 %copy-start.1 = (bf16[8,1,128,128]{3,2,1,0:T(8,128)(2,1)}, bf16[8,1,128,128]{3,2,1,0:T(8,128)(2,1)S(1)}, u32[]{:S(2)}) copy-start(bf16[8,1,128,128]{3,2,1,0:T(8,128)(2,1)S(1)} %pad_maximum_fusion) | copy-start | bytes 786436
  1.0 16.0 %collective-permute-start.5 = (bf16[1024,128]{1,0:T(8,128)(2,1)S(1)}, bf16[1024,128]{1,0:T(8,128)(2,1)S(1)}, u32[]{:S(2)}, u32[]{:S(2)}) collective-permute-start(bf16[1024,128]{1,0:T(8,128)(2,1)S(1)} %bitcast.10), channel_id=1, source_target_pairs={{0,32},{8,40},{16,48},{24,56},{32,64},{40,72},{48,80},{56,88},{64,... | collective-permute-start | bytes 786440 | tf_op jit(solution)/shard_map/ppermute | solution.py:363
  4.4 16.7 %collective-permute-start.6 = (bf16[1024,128]{1,0:T(8,128)(2,1)S(1)}, bf16[1024,128]{1,0:T(8,128)(2,1)S(1)}, u32[]{:S(2)}, u32[]{:S(2)}) collective-permute-start(bf16[1024,128]{1,0:T(8,128)(2,1)S(1)} %bitcast.11), channel_id=1, source_target_pairs={{0,96},{8,104},{16,112},{24,120},{32,0},{40,8},{48,16},{56,24},{64... | collective-permute-start | bytes 786440 | tf_op jit(solution)/shard_map/ppermute | solution.py:364
  10.2 6.8 %collective-permute-start = (bf16[528,128]{1,0:T(8,128)(2,1)}, bf16[528,128]{1,0:T(8,128)(2,1)S(1)}, u32[]{:S(2)}, u32[]{:S(2)}) collective-permute-start(bf16[528,128]{1,0:T(8,128)(2,1)} %get-tuple-element.21), channel_id=1, source_target_pairs={{0,128},{8,136},{16,144},{24,152},{32,160},{40,168},{48,176},{56,1... | collective-permute-start | bytes 405512 | tf_op jit(solution)/shard_map/ppermute | solution.py:365
  12.4 13.0 %collective-permute-start.3 = (bf16[1024,128]{1,0:T(8,128)(2,1)}, bf16[1024,128]{1,0:T(8,128)(2,1)S(1)}, u32[]{:S(2)}, u32[]{:S(2)}) collective-permute-start(bf16[1024,128]{1,0:T(8,128)(2,1)} %bitcast.13), channel_id=1, source_target_pairs={{0,16},{8,24},{16,32},{24,40},{32,48},{40,56},{48,64},{56,72},{64,... | collective-permute-start | bytes 786440 | tf_op jit(solution)/shard_map/ppermute | solution.py:345
  13.4 13.6 %collective-permute-start.4 = (bf16[1024,128]{1,0:T(8,128)(2,1)}, bf16[1024,128]{1,0:T(8,128)(2,1)S(1)}, u32[]{:S(2)}, u32[]{:S(2)}) collective-permute-start(bf16[1024,128]{1,0:T(8,128)(2,1)} %bitcast.14), channel_id=1, source_target_pairs={{0,112},{8,120},{16,0},{24,8},{32,16},{40,24},{48,32},{56,40},{64,... | collective-permute-start | bytes 786440 | tf_op jit(solution)/shard_map/ppermute | solution.py:346
  17.0 12.1 %collective-permute-start.2 = (bf16[528,128]{1,0:T(8,128)(2,1)S(1)}, bf16[528,128]{1,0:T(8,128)(2,1)S(1)}, u32[]{:S(2)}, u32[]{:S(2)}) collective-permute-start(bf16[528,128]{1,0:T(8,128)(2,1)S(1)} %collective-permute-done.s2), channel_id=1, source_target_pairs={{0,8},{8,0},{16,24},{24,16},{32,40},{40,32},{48,56},{56,48},{64,72... | collective-permute-start | bytes 405512 | tf_op jit(solution)/shard_map/ppermute | solution.py:367
  17.0 12.1 %collective-permute-start.1 = (bf16[528,128]{1,0:T(8,128)(2,1)}, bf16[528,128]{1,0:T(8,128)(2,1)S(1)}, u32[]{:S(2)}, u32[]{:S(2)}) collective-permute-start(bf16[528,128]{1,0:T(8,128)(2,1)} %get-tuple-element.21), channel_id=1, source_target_pairs={{0,8},{8,0},{16,24},{24,16},{32,40},{40,32},{48,56},{56,48},{64,72... | collective-permute-start | bytes 405512 | tf_op jit(solution)/shard_map/ppermute | solution.py:367
  21.1 15.2 %collective-permute-start.9 = (bf16[1024,128]{1,0:T(8,128)(2,1)S(1)}, bf16[1024,128]{1,0:T(8,128)(2,1)S(1)}, u32[]{:S(2)}, u32[]{:S(2)}) collective-permute-start(bf16[1024,128]{1,0:T(8,128)(2,1)S(1)} %broadcast_select_fusion), channel_id=1, source_target_pairs={{0,32},{8,104},{16,48},{24,120},{32,64},{40,8},{48,80},{56,24},{64... | collective-permute-start | bytes 786440 | tf_op jit(solution)/shard_map/ppermute | solution.py:371
  25.3 11.1 %collective-permute-start.7 = (bf16[1024,128]{1,0:T(8,128)(2,1)S(1)}, bf16[1024,128]{1,0:T(8,128)(2,1)S(1)}, u32[]{:S(2)}, u32[]{:S(2)}) collective-permute-start(bf16[1024,128]{1,0:T(8,128)(2,1)S(1)} %collective-permute-done.5.up2), channel_id=1, source_target_pairs={{0,16},{8,24},{16,32},{24,40},{32,48},{40,56},{48,64},{56,72},{64,... | collective-permute-start | bytes 786440 | tf_op jit(solution)/shard_map/ppermute | solution.py:368
  27.0 9.9 %collective-permute-start.8 = (bf16[1024,128]{1,0:T(8,128)(2,1)S(1)}, bf16[1024,128]{1,0:T(8,128)(2,1)S(1)}, u32[]{:S(2)}, u32[]{:S(2)}) collective-permute-start(bf16[1024,128]{1,0:T(8,128)(2,1)S(1)} %collective-permute-done.6.dn2), channel_id=1, source_target_pairs={{0,112},{8,120},{16,0},{24,8},{32,16},{40,24},{48,32},{56,40},{64,... | collective-permute-start | bytes 786440 | tf_op jit(solution)/shard_map/ppermute | solution.py:369
  29.1 1.0 %copy-start = (bf16[1808,128]{1,0:T(8,128)(2,1)S(1)}, bf16[1808,128]{1,0:T(8,128)(2,1)}, u32[]{:S(2)}) copy-start(bf16[1808,128]{1,0:T(8,128)(2,1)} %get-tuple-element.19.local) | copy-start | bytes 1388548
  38.5 7.1 %collective-permute-start.10 = (bf16[144,512]{1,0:T(8,128)(2,1)S(1)}, bf16[144,512]{1,0:T(8,128)(2,1)S(1)}, u32[]{:S(2)}, u32[]{:S(2)}) collective-permute-start(bf16[144,512]{1,0:T(8,128)(2,1)S(1)} %get-tuple-element.30), channel_id=1, source_target_pairs={{0,136},{8,128},{16,152},{24,144},{32,168},{40,160},{48,184},{56,1... | collective-permute-start | bytes 442376 | tf_op jit(solution)/shard_map/ppermute | solution.py:385
  41.0 8.3 %collective-permute-start.11 = (bf16[144,512]{1,0:T(8,128)(2,1)S(1)}, bf16[144,512]{1,0:T(8,128)(2,1)S(1)}, u32[]{:S(2)}, u32[]{:S(2)}) collective-permute-start(bf16[144,512]{1,0:T(8,128)(2,1)S(1)} %get-tuple-element.31), channel_id=1, source_target_pairs={{0,128},{8,136},{16,144},{24,152},{32,160},{40,168},{48,176},{56,1... | collective-permute-start | bytes 442376 | tf_op jit(solution)/shard_map/ppermute | solution.py:386
  43.8 5.6 %collective-permute-start.12 = (bf16[144,512]{1,0:T(8,128)(2,1)S(1)}, bf16[144,512]{1,0:T(8,128)(2,1)S(1)}, u32[]{:S(2)}, u32[]{:S(2)}) collective-permute-start(bf16[144,512]{1,0:T(8,128)(2,1)S(1)} %get-tuple-element.32), channel_id=1, source_target_pairs={{0,8},{8,0},{16,24},{24,16},{32,40},{40,32},{48,56},{56,48},{64,72... | collective-permute-start | bytes 442376 | tf_op jit(solution)/shard_map/ppermute | solution.py:388
  53.1 7.6 %collective-permute-start.13 = (bf16[16,5120]{1,0:T(8,128)(2,1)S(1)}, bf16[16,5120]{1,0:T(8,128)(2,1)S(1)}, u32[]{:S(2)}, u32[]{:S(2)}) collective-permute-start(bf16[16,5120]{1,0:T(8,128)(2,1)S(1)} %get-tuple-element.39), channel_id=1, source_target_pairs={{0,1},{1,2},{2,3},{3,0},{4,5},{5,6},{6,7},{7,4},{8,9},{9,10},{10,1... | collective-permute-start | bytes 491528 | tf_op jit(solution)/shard_map/ppermute | solution.py:403
  54.7 8.8 %collective-permute-start.14 = (bf16[16,5120]{1,0:T(8,128)(2,1)S(1)}, bf16[16,5120]{1,0:T(8,128)(2,1)S(1)}, u32[]{:S(2)}, u32[]{:S(2)}) collective-permute-start(bf16[16,5120]{1,0:T(8,128)(2,1)S(1)} %get-tuple-element.38), channel_id=1, source_target_pairs={{0,3},{1,0},{2,1},{3,2},{4,7},{5,4},{6,5},{7,6},{8,11},{9,8},{10,9... | collective-permute-start | bytes 491528 | tf_op jit(solution)/shard_map/ppermute | solution.py:403
  56.4 11.9 %collective-permute-start.15 = (bf16[16,5120]{1,0:T(8,128)(2,1)S(1)}, bf16[16,5120]{1,0:T(8,128)(2,1)S(1)}, u32[]{:S(2)}, u32[]{:S(2)}) collective-permute-start(bf16[16,5120]{1,0:T(8,128)(2,1)S(1)} %get-tuple-element.37), channel_id=1, source_target_pairs={{0,2},{1,3},{2,0},{3,1},{4,6},{5,7},{6,4},{7,5},{8,10},{9,11},{10,... | collective-permute-start | bytes 491528 | tf_op jit(solution)/shard_map/ppermute | solution.py:403
  58.4 9.9 %collective-permute-start.16 = (bf16[16,5120]{1,0:T(8,128)(2,1)S(1)}, bf16[16,5120]{1,0:T(8,128)(2,1)S(1)}, u32[]{:S(2)}, u32[]{:S(2)}) collective-permute-start(bf16[16,5120]{1,0:T(8,128)(2,1)S(1)} %get-tuple-element.36), channel_id=1, source_target_pairs={{0,4},{1,5},{2,6},{3,7},{4,0},{5,1},{6,2},{7,3},{8,12},{9,13},{10,... | collective-permute-start | bytes 491528 | tf_op jit(solution)/shard_map/ppermute | solution.py:403
  59.3 9.9 %collective-permute-start.17 = (bf16[16,5120]{1,0:T(8,128)(2,1)S(1)}, bf16[16,5120]{1,0:T(8,128)(2,1)S(1)}, u32[]{:S(2)}, u32[]{:S(2)}) collective-permute-start(bf16[16,5120]{1,0:T(8,128)(2,1)S(1)} %get-tuple-element.35), channel_id=1, source_target_pairs={{0,5},{1,6},{2,7},{3,4},{4,1},{5,2},{6,3},{7,0},{8,13},{9,14},{10,... | collective-permute-start | bytes 491528 | tf_op jit(solution)/shard_map/ppermute | solution.py:403
  60.6 12.0 %collective-permute-start.18 = (bf16[16,5120]{1,0:T(8,128)(2,1)S(1)}, bf16[16,5120]{1,0:T(8,128)(2,1)S(1)}, u32[]{:S(2)}, u32[]{:S(2)}) collective-permute-start(bf16[16,5120]{1,0:T(8,128)(2,1)S(1)} %get-tuple-element.34), channel_id=1, source_target_pairs={{0,7},{1,4},{2,5},{3,6},{4,3},{5,0},{6,1},{7,2},{8,15},{9,12},{10,... | collective-permute-start | bytes 491528 | tf_op jit(solution)/shard_map/ppermute | solution.py:403
  63.5 11.9 %collective-permute-start.19 = (bf16[16,5120]{1,0:T(8,128)(2,1)S(1)}, bf16[16,5120]{1,0:T(8,128)(2,1)S(1)}, u32[]{:S(2)}, u32[]{:S(2)}) collective-permute-start(bf16[16,5120]{1,0:T(8,128)(2,1)S(1)} %get-tuple-element.33), channel_id=1, source_target_pairs={{0,6},{1,7},{2,4},{3,5},{4,2},{5,3},{6,0},{7,1},{8,14},{9,15},{10,... | collective-permute-start | bytes 491528 | tf_op jit(solution)/shard_map/ppermute | solution.py:403

commit v9 on v7

--- a/solution.py
+++ b/solution.py
@@ -28,7 +28,7 @@
 GROUPS = ((0, -1, 1, -2, 2), (-3, 3, 4))
 
 
-HEADS = ((0, 0), (0, 1), (0, 3), (0, 2), (1, 0), (1, 1), (1, 3), (1, 2))
+HEADS = (0, 1, 5, 3, 7, 2, 6, 4)
 
 
 def rep_of(xh, z, c):
@@ -260,8 +260,8 @@
     inv = 1.0 / sum(ws)
     mixed = sum(v * (w * inv) for v, w in zip(vals, ws))
     rows_f32[...] = mixed.T
-    for k, (dx, dy) in enumerate(HEADS):
-        first = ((head_ref[0] & 4) ^ (dx * 4)) * 64 + ((head_ref[0] + dy) & 3) * 64
+    for k, flip in enumerate(HEADS):
+        first = (head_ref[0] ^ flip) * 64
         for h in range(4):
             block = rows_f32[pl.ds(first + h, 16, stride=4), :]
             attn[pl.ds(k * 16, 16), pl.ds(h * HD, HD)] = block.astype(BF)
@@ -399,8 +399,8 @@
     rows = jnp.dot(attn, out_weight, preferred_element_type=F32).astype(BF)
     parts = [rows[k * 16:(k + 1) * 16] for k in range(8)]
     terms = [
-        lax.ppermute(part, "head", [(i, ((i & 4) ^ (dx * 4)) + ((i + dy) & 3)) for i in range(8)])
-        for part, (dx, dy) in zip(parts[1:], HEADS[1:])
+        lax.ppermute(part, "head", [(i, i ^ flip) for i in range(8)])
+        for part, flip in zip(parts[1:], HEADS[1:])
     ]
     return pl.pallas_call(
         sum_kernel,

time: 77.2 us -> 75.4 us (0.977); the launches traced: 76 us -> 75.3 us
  waiting for transfers between devices: 15.2 us -> 20 us
  starting transfers between devices: 39.5 us -> 36.2 us
  Pallas kernels: 15.7 us -> 13.5 us
    ppermute x7, starting transfers between devices: 16.2 us -> 13 us  [on_device(): lax.ppermute(part, 'head', [(i, i ^ flip) for i in range(8)])]
    ppermute x7, waiting for transfers between devices: 7.1 us -> 9.62 us  [on_device(): lax.ppermute(part, 'head', [(i, i ^ flip) for i in range(8)])]
    ppermute x1, waiting for transfers between devices: 0.49 us -> 2.2 us  [on_device(): up3 = lax.ppermute(up2, 'rep', z_perm(1))]
    pallas_call x1, Pallas kernels: 7.43 us -> 5.72 us  [near_call(): pl.pallas_call(near_kernel, out_shape=[jax.ShapeDtypeStruct((SESS * QROWS...]
  transfers between devices with their start and end apart: 20 -> 20, of which waited for: 8 -> 9; matrix products, arithmetic and copies ran while one was open for 0% -> 0% of each run, Pallas kernels for 16% -> 13%
where the time goes in v9:
time: 75.4 us; the launch traced here: 75.3 us
  starting transfers between devices  36.2 us (48%)
  waiting for transfers between devices  20 us (27%)
  Pallas kernels  13.5 us (18%)
  matrix products  3.34 us (4%)
  local copies, waits for them, and re-layouts  1.11 us (1%)
  other arithmetic  1.03 us (1%)
    ppermute x7, starting transfers between devices, on_device(): lax.ppermute(part, 'head', [(i, i ^ flip) for i in range(8)])  13 us
    ppermute x7, waiting for transfers between devices, on_device(): lax.ppermute(part, 'head', [(i, i ^ flip) for i in range(8)])  9.62 us
    pallas_call x1, Pallas kernels, near_call(): pl.pallas_call(near_kernel, out_shape=[jax.ShapeDtypeStruct((SESS * QROWS...  5.72 us
    ppermute x1, starting transfers between devices, on_device(): dn1 = lax.ppermute(kv, 'rep', z_perm(-1))  4.03 us
    pallas_call x2, Pallas kernels, far_call(): pl.pallas_call(functools.partial(far_kernel, nb, first), out_shape=[part...  4 us
    ppermute x1, waiting for transfers between devices, on_device(): up1 = lax.ppermute(kv, 'rep', z_perm(1))  3.51 us
    ppermute x3, starting transfers between devices, on_device(): sents = [lax.ppermute(sent, 'rep', group_perm(r)) for r in (1, 2, 3)]  3.46 us
    dot_general x1, matrix products, on_device(): rows = jnp.dot(attn, out_weight, preferred_element_type=F32).astype(BF)  3.34 us
  transfers between devices with their start and end apart: 20, of which 9 were waited for; matrix products, arithmetic and copies ran while one was open for 0% of the time, Pallas kernels for 13%

profile of v9, /device:TPU:2, one launch (start us, length us, event | category | flops | bytes accessed | tf_op | source)
XLA Modules:
  0.0 75.3 jit_solution(859369029532753130)
XLA Ops:
  1.0 2.0 %collective-permute-start = (bf16[1024,128]{1,0:T(8,128)(2,1)S(1)}, bf16[1024,128]{1,0:T(8,128)(2,1)S(1)}, u32[]{:S(2)}, u32[]{:S(2)}) collective-permute-start(bf16[1024,128]{1,0:T(8,128)(2,1)S(1)} %bitcast.10), channel_id=1, source_target_pairs={{0,16},{8,24},{16,32},{24,40},{32,48},{40,56},{48,64},{56,72},{64,... | collective-permute-start | bytes 786440 | tf_op jit(solution)/shard_map/ppermute | solution.py:345
  3.0 4.0 %collective-permute-start.1 = (bf16[1024,128]{1,0:T(8,128)(2,1)S(1)}, bf16[1024,128]{1,0:T(8,128)(2,1)S(1)}, u32[]{:S(2)}, u32[]{:S(2)}) collective-permute-start(bf16[1024,128]{1,0:T(8,128)(2,1)S(1)} %bitcast.11), channel_id=1, source_target_pairs={{0,112},{8,120},{16,0},{24,8},{32,16},{40,24},{48,32},{56,40},{64,... | collective-permute-start | bytes 786440 | tf_op jit(solution)/shard_map/ppermute | solution.py:346
  7.0 2.7 %pack.1 = (bf16[528,128]{1,0:T(8,128)(2,1)}, bf16[1808,128]{1,0:T(8,128)(2,1)}) custom-call(bf16[512,128]{1,0:T(8,128)(2,1)} %bitcast.15, bf16[128,128]{1,0:T(8,128)(2,1)} %bitcast.16, bf16[128,128]{1,0:T(8,128)(2,1)} %bitcast.17, bf16[512,128]{1,0:T(8,128)(2,1)} %bitcast.13, bf16[512,128]{1,0:T(8,128)(2,1)} %bitcast.14, s32[2,16]{1,0:T(2,128)} %table.1, ...), custom_call_target="tpu_custom_call" | custom-call | tf_op jit(solution)/shard_map/pack/pallas_call | solution.py:347
  9.7 3.5 %collective-permute-done.up1 = bf16[1024,128]{1,0:T(8,128)(2,1)S(1)} collective-permute-done((bf16[1024,128]{1,0:T(8,128)(2,1)S(1)}, bf16[1024,128]{1,0:T(8,128)(2,1)S(1)}, u32[]{:S(2)}, u32[]{:S(2)}) %collective-permute-start) | collective-permute-done | bytes 262176 | tf_op jit(solution)/shard_map/ppermute | solution.py:345
  13.3 3.2 %collective-permute-start.6 = (bf16[1024,128]{1,0:T(8,128)(2,1)S(1)}, bf16[1024,128]{1,0:T(8,128)(2,1)S(1)}, u32[]{:S(2)}, u32[]{:S(2)}) collective-permute-start(bf16[1024,128]{1,0:T(8,128)(2,1)S(1)} %collective-permute-done.1.dn1), channel_id=1, source_target_pairs={{0,112},{8,120},{16,0},{24,8},{32,16},{40,24},{48,32},{56,40},{64,... | collective-permute-start | bytes 786440 | tf_op jit(solution)/shard_map/ppermute | solution.py:365
  16.6 2.2 %collective-permute-start.3 = (bf16[528,128]{1,0:T(8,128)(2,1)}, bf16[528,128]{1,0:T(8,128)(2,1)S(1)}, u32[]{:S(2)}, u32[]{:S(2)}) collective-permute-start(bf16[528,128]{1,0:T(8,128)(2,1)} %get-tuple-element.22), channel_id=1, source_target_pairs={{0,128},{8,136},{16,144},{24,152},{32,160},{40,168},{48,176},{56,1... | collective-permute-start | bytes 405512 | tf_op jit(solution)/shard_map/ppermute | solution.py:366
  20.0 2.0 %collective-permute-done.5.up2 = bf16[1024,128]{1,0:T(8,128)(2,1)S(1)} collective-permute-done((bf16[1024,128]{1,0:T(8,128)(2,1)S(1)}, bf16[1024,128]{1,0:T(8,128)(2,1)S(1)}, u32[]{:S(2)}, u32[]{:S(2)}) %collective-permute-start.5) | collective-permute-done | bytes 262176 | tf_op jit(solution)/shard_map/ppermute | solution.py:364
  22.0 3.1 %collective-permute-start.9 = (bf16[1024,128]{1,0:T(8,128)(2,1)S(1)}, bf16[1024,128]{1,0:T(8,128)(2,1)S(1)}, u32[]{:S(2)}, u32[]{:S(2)}) collective-permute-start(bf16[1024,128]{1,0:T(8,128)(2,1)S(1)} %broadcast_select_fusion), channel_id=1, source_target_pairs={{0,32},{8,104},{16,48},{24,120},{32,64},{40,8},{48,80},{56,24},{64... | collective-permute-start | bytes 786440 | tf_op jit(solution)/shard_map/ppermute | solution.py:370
  25.1 1.8 %collective-permute-start.7 = (bf16[1024,128]{1,0:T(8,128)(2,1)S(1)}, bf16[1024,128]{1,0:T(8,128)(2,1)S(1)}, u32[]{:S(2)}, u32[]{:S(2)}) collective-permute-start(bf16[1024,128]{1,0:T(8,128)(2,1)S(1)} %collective-permute-done.5.up2), channel_id=1, source_target_pairs={{0,16},{8,24},{16,32},{24,40},{32,48},{40,56},{48,64},{56,72},{64,... | collective-permute-start | bytes 786440 | tf_op jit(solution)/shard_map/ppermute | solution.py:367
  26.9 1.4 %collective-permute-start.8 = (bf16[1024,128]{1,0:T(8,128)(2,1)S(1)}, bf16[1024,128]{1,0:T(8,128)(2,1)S(1)}, u32[]{:S(2)}, u32[]{:S(2)}) collective-permute-start(bf16[1024,128]{1,0:T(8,128)(2,1)S(1)} %collective-permute-done.6.dn2), channel_id=1, source_target_pairs={{0,112},{8,120},{16,0},{24,8},{32,16},{40,24},{48,32},{56,40},{64,... | collective-permute-start | bytes 786440 | tf_op jit(solution)/shard_map/ppermute | solution.py:368
  29.3 5.7 %near_pages.1 = (bf16[2048,128]{1,0:T(8,128)(2,1)S(1)}, s32[160]{0:T(256)S(1)}, s32[160]{0:T(256)S(1)}, f32[8,1,256]{2,1,0:T(1,128)S(1)}, f32[8,1,256]{2,1,0:T(1,128)S(1)}, /*index=5*/f32[8,128,256]{2,1,0:T(8,128)S(1)}) custom-call(s32[32]{0:T(128)S(1)} %and_select_fusion.7.maps, bf16[1808,128]{1,0:T(8,128)(2,1)S(1)} %copy-done, ...), custom_call_target="tpu_custom_call" | custom-call | flops 4000000000 | bytes 4194304 | tf_op jit(solution)/shard_map/near_pages/pallas_call | solution.py:297
  35.1 2.2 %collective-permute-done.7.refs_2_ = bf16[1024,128]{1,0:T(8,128)(2,1)S(1)} collective-permute-done((bf16[1024,128]{1,0:T(8,128)(2,1)S(1)}, bf16[1024,128]{1,0:T(8,128)(2,1)S(1)}, u32[]{:S(2)}, u32[]{:S(2)}) %collective-permute-start.7) | collective-permute-done | bytes 262176 | tf_op jit(solution)/shard_map/ppermute | solution.py:367
  37.3 2.5 %far_pages_x.1 = (bf16[144,512]{1,0:T(8,128)(2,1)S(1)}, bf16[144,512]{1,0:T(8,128)(2,1)S(1)}) custom-call(s32[160]{0:T(256)S(1)} %get-tuple-element.31.refs_0_, bf16[2048,128]{1,0:T(8,128)(2,1)S(1)} %get-tuple-element.26.refs_1_, bf16[1024,128]{1,0:T(8,128)(2,1)S(1)} %collective-permute-done.7.refs_2_, bf16[1024,128]{1,0:T(8,128)(2,1)S(1)} %collective-permute-done.8.refs_3_, ...), custom_call_target="tpu_custom_call" | custom-call | flops 1000000000 | bytes 4194304 | tf_op jit(solution)/shard_map/far_pages_x/pallas_call | solution.py:324
  41.1 1.5 %far_pages_own.1 = (f32[136,512]{1,0:T(8,128)S(1)}, bf16[144,512]{1,0:T(8,128)(2,1)S(1)}) custom-call(s32[160]{0:T(256)S(1)} %get-tuple-element.25.refs_0_, bf16[2048,128]{1,0:T(8,128)(2,1)S(1)} %get-tuple-element.26.refs_1_, bf16[1024,128]{1,0:T(8,128)(2,1)S(1)} %collective-permute-done.7.refs_2_, bf16[1024,128]{1,0:T(8,128)(2,1)S(1)} %collective-permute-done.8.refs_3_, ...), custom_call_target="tpu_custom_call" | custom-call | flops 1000000000 | bytes 4194304 | tf_op jit(solution)/shard_map/far_pages_own/pallas_call | solution.py:324
  42.6 2.9 %collective-permute-start.12 = (bf16[144,512]{1,0:T(8,128)(2,1)S(1)}, bf16[144,512]{1,0:T(8,128)(2,1)S(1)}, u32[]{:S(2)}, u32[]{:S(2)}) collective-permute-start(bf16[144,512]{1,0:T(8,128)(2,1)S(1)} %get-tuple-element.34), channel_id=1, source_target_pairs={{0,8},{8,0},{16,24},{24,16},{32,40},{40,32},{48,56},{56,48},{64,72... | collective-permute-start | bytes 442376 | tf_op jit(solution)/shard_map/ppermute | solution.py:387
  45.5 1.4 %collective-permute-done.10.p1 = bf16[144,512]{1,0:T(8,128)(2,1)S(1)} collective-permute-done((bf16[144,512]{1,0:T(8,128)(2,1)S(1)}, bf16[144,512]{1,0:T(8,128)(2,1)S(1)}, u32[]{:S(2)}, u32[]{:S(2)}) %collective-permute-start.10) | collective-permute-done | bytes 147488 | tf_op jit(solution)/shard_map/ppermute | solution.py:384
  48.4 3.3 %convolution_convert_fusion = bf16[128,5120]{1,0:T(8,128)(2,1)S(1)} fusion(bf16[128,512]{1,0:T(8,128)(2,1)S(1)} %combine.1, bf16[512,5120]{1,0:T(8,128)(2,1)} %param.15), kind=kOutput, calls=%fused_computation | convolution fusion | flops 671744000 | bytes 6684672 | tf_op jit(solution)/shard_map/dot_general | solution.py:399
  51.8 1.7 %collective-permute-start.13 = (bf16[16,5120]{1,0:T(8,128)(2,1)S(1)}, bf16[16,5120]{1,0:T(8,128)(2,1)S(1)}, u32[]{:S(2)}, u32[]{:S(2)}) collective-permute-start(bf16[16,5120]{1,0:T(8,128)(2,1)S(1)} %get-tuple-element.41), channel_id=1, source_target_pairs={{0,1},{1,0},{2,3},{3,2},{4,5},{5,4},{6,7},{7,6},{8,9},{9,8},{10,11... | collective-permute-start | bytes 491528 | tf_op jit(solution)/shard_map/ppermute | solution.py:402
  54.8 3.1 %collective-permute-start.15 = (bf16[16,5120]{1,0:T(8,128)(2,1)S(1)}, bf16[16,5120]{1,0:T(8,128)(2,1)S(1)}, u32[]{:S(2)}, u32[]{:S(2)}) collective-permute-start(bf16[16,5120]{1,0:T(8,128)(2,1)S(1)} %get-tuple-element.39), channel_id=1, source_target_pairs={{0,3},{1,2},{2,1},{3,0},{4,7},{5,6},{6,5},{7,4},{8,11},{9,10},{10,... | collective-permute-start | bytes 491528 | tf_op jit(solution)/shard_map/ppermute | solution.py:402
  58.1 2.0 %collective-permute-start.17 = (bf16[16,5120]{1,0:T(8,128)(2,1)S(1)}, bf16[16,5120]{1,0:T(8,128)(2,1)S(1)}, u32[]{:S(2)}, u32[]{:S(2)}) collective-permute-start(bf16[16,5120]{1,0:T(8,128)(2,1)S(1)} %get-tuple-element.37), channel_id=1, source_target_pairs={{0,2},{1,3},{2,0},{3,1},{4,6},{5,7},{6,4},{7,5},{8,10},{9,11},{10,... | collective-permute-start | bytes 491528 | tf_op jit(solution)/shard_map/ppermute | solution.py:402
  60.1 2.3 %collective-permute-done.13.refs_1_ = bf16[16,5120]{1,0:T(8,128)(2,1)S(1)} collective-permute-done((bf16[16,5120]{1,0:T(8,128)(2,1)S(1)}, bf16[16,5120]{1,0:T(8,128)(2,1)S(1)}, u32[]{:S(2)}, u32[]{:S(2)}) %collective-permute-start.13) | collective-permute-done | bytes 163872 | tf_op jit(solution)/shard_map/ppermute | solution.py:402
  62.4 4.1 %collective-permute-start.18 = (bf16[16,5120]{1,0:T(8,128)(2,1)S(1)}, bf16[16,5120]{1,0:T(8,128)(2,1)S(1)}, u32[]{:S(2)}, u32[]{:S(2)}) collective-permute-start(bf16[16,5120]{1,0:T(8,128)(2,1)S(1)} %get-tuple-element.36), channel_id=1, source_target_pairs={{0,6},{1,7},{2,4},{3,5},{4,2},{5,3},{6,0},{7,1},{8,14},{9,15},{10,... | collective-permute-start | bytes 491528 | tf_op jit(solution)/shard_map/ppermute | solution.py:402
  67.2 4.8 %collective-permute-done.15.refs_3_ = bf16[16,5120]{1,0:T(8,128)(2,1)S(1)} collective-permute-done((bf16[16,5120]{1,0:T(8,128)(2,1)S(1)}, bf16[16,5120]{1,0:T(8,128)(2,1)S(1)}, u32[]{:S(2)}, u32[]{:S(2)}) %collective-permute-start.15) | collective-permute-done | bytes 163872 | tf_op jit(solution)/shard_map/ppermute | solution.py:402
  73.0 1.4 %collective-permute-done.19.refs_7_ = bf16[16,5120]{1,0:T(8,128)(2,1)S(1)} collective-permute-done((bf16[16,5120]{1,0:T(8,128)(2,1)S(1)}, bf16[16,5120]{1,0:T(8,128)(2,1)S(1)}, u32[]{:S(2)}, u32[]{:S(2)}) %collective-permute-start.19) | collective-permute-done | bytes 163872 | tf_op jit(solution)/shard_map/ppermute | solution.py:402
  (31 shorter events, 10.3 us)
Async XLA Ops:
  1.0 6.0 %copy-start.1 = (bf16[8,1,128,128]{3,2,1,0:T(8,128)(2,1)}, bf16[8,1,128,128]{3,2,1,0:T(8,128)(2,1)S(1)}, u32[]{:S(2)}) copy-start(bf16[8,1,128,128]{3,2,1,0:T(8,128)(2,1)S(1)} %pad_maximum_fusion) | copy-start | bytes 786436
  1.0 12.2 %collective-permute-start = (bf16[1024,128]{1,0:T(8,128)(2,1)S(1)}, bf16[1024,128]{1,0:T(8,128)(2,1)S(1)}, u32[]{:S(2)}, u32[]{:S(2)}) collective-permute-start(bf16[1024,128]{1,0:T(8,128)(2,1)S(1)} %bitcast.10), channel_id=1, source_target_pairs={{0,16},{8,24},{16,32},{24,40},{32,48},{40,56},{48,64},{56,72},{64,... | collective-permute-start | bytes 786440 | tf_op jit(solution)/shard_map/ppermute | solution.py:345
  3.0 10.2 %collective-permute-start.1 = (bf16[1024,128]{1,0:T(8,128)(2,1)S(1)}, bf16[1024,128]{1,0:T(8,128)(2,1)S(1)}, u32[]{:S(2)}, u32[]{:S(2)}) collective-permute-start(bf16[1024,128]{1,0:T(8,128)(2,1)S(1)} %bitcast.11), channel_id=1, source_target_pairs={{0,112},{8,120},{16,0},{24,8},{32,16},{40,24},{48,32},{56,40},{64,... | collective-permute-start | bytes 786440 | tf_op jit(solution)/shard_map/ppermute | solution.py:346
  13.2 8.7 %collective-permute-start.5 = (bf16[1024,128]{1,0:T(8,128)(2,1)S(1)}, bf16[1024,128]{1,0:T(8,128)(2,1)S(1)}, u32[]{:S(2)}, u32[]{:S(2)}) collective-permute-start(bf16[1024,128]{1,0:T(8,128)(2,1)S(1)} %collective-permute-done.up1), channel_id=1, source_target_pairs={{0,16},{8,24},{16,32},{24,40},{32,48},{40,56},{48,64},{56,72},{64,... | collective-permute-start | bytes 786440 | tf_op jit(solution)/shard_map/ppermute | solution.py:364
  13.3 8.7 %collective-permute-start.6 = (bf16[1024,128]{1,0:T(8,128)(2,1)S(1)}, bf16[1024,128]{1,0:T(8,128)(2,1)S(1)}, u32[]{:S(2)}, u32[]{:S(2)}) collective-permute-start(bf16[1024,128]{1,0:T(8,128)(2,1)S(1)} %collective-permute-done.1.dn1), channel_id=1, source_target_pairs={{0,112},{8,120},{16,0},{24,8},{32,16},{40,24},{48,32},{56,40},{64,... | collective-permute-start | bytes 786440 | tf_op jit(solution)/shard_map/ppermute | solution.py:365
  16.5 10.4 %collective-permute-start.2 = (bf16[528,128]{1,0:T(8,128)(2,1)}, bf16[528,128]{1,0:T(8,128)(2,1)S(1)}, u32[]{:S(2)}, u32[]{:S(2)}) collective-permute-start(bf16[528,128]{1,0:T(8,128)(2,1)} %get-tuple-element.22), channel_id=1, source_target_pairs={{0,8},{8,0},{16,24},{24,16},{32,40},{40,32},{48,56},{56,48},{64,72... | collective-permute-start | bytes 405512 | tf_op jit(solution)/shard_map/ppermute | solution.py:366
  16.6 11.7 %collective-permute-start.3 = (bf16[528,128]{1,0:T(8,128)(2,1)}, bf16[528,128]{1,0:T(8,128)(2,1)S(1)}, u32[]{:S(2)}, u32[]{:S(2)}) collective-permute-start(bf16[528,128]{1,0:T(8,128)(2,1)} %get-tuple-element.22), channel_id=1, source_target_pairs={{0,128},{8,136},{16,144},{24,152},{32,160},{40,168},{48,176},{56,1... | collective-permute-start | bytes 405512 | tf_op jit(solution)/shard_map/ppermute | solution.py:366
  18.8 9.5 %collective-permute-start.4 = (bf16[528,128]{1,0:T(8,128)(2,1)}, bf16[528,128]{1,0:T(8,128)(2,1)S(1)}, u32[]{:S(2)}, u32[]{:S(2)}) collective-permute-start(bf16[528,128]{1,0:T(8,128)(2,1)} %get-tuple-element.22), channel_id=1, source_target_pairs={{0,136},{8,128},{16,152},{24,144},{32,168},{40,160},{48,184},{56,1... | collective-permute-start | bytes 405512 | tf_op jit(solution)/shard_map/ppermute | solution.py:366
  22.0 13.1 %collective-permute-start.9 = (bf16[1024,128]{1,0:T(8,128)(2,1)S(1)}, bf16[1024,128]{1,0:T(8,128)(2,1)S(1)}, u32[]{:S(2)}, u32[]{:S(2)}) collective-permute-start(bf16[1024,128]{1,0:T(8,128)(2,1)S(1)} %broadcast_select_fusion), channel_id=1, source_target_pairs={{0,32},{8,104},{16,48},{24,120},{32,64},{40,8},{48,80},{56,24},{64... | collective-permute-start | bytes 786440 | tf_op jit(solution)/shard_map/ppermute | solution.py:370
  25.1 12.2 %collective-permute-start.7 = (bf16[1024,128]{1,0:T(8,128)(2,1)S(1)}, bf16[1024,128]{1,0:T(8,128)(2,1)S(1)}, u32[]{:S(2)}, u32[]{:S(2)}) collective-permute-start(bf16[1024,128]{1,0:T(8,128)(2,1)S(1)} %collective-permute-done.5.up2), channel_id=1, source_target_pairs={{0,16},{8,24},{16,32},{24,40},{32,48},{40,56},{48,64},{56,72},{64,... | collective-permute-start | bytes 786440 | tf_op jit(solution)/shard_map/ppermute | solution.py:367
  26.9 10.4 %collective-permute-start.8 = (bf16[1024,128]{1,0:T(8,128)(2,1)S(1)}, bf16[1024,128]{1,0:T(8,128)(2,1)S(1)}, u32[]{:S(2)}, u32[]{:S(2)}) collective-permute-start(bf16[1024,128]{1,0:T(8,128)(2,1)S(1)} %collective-permute-done.6.dn2), channel_id=1, source_target_pairs={{0,112},{8,120},{16,0},{24,8},{32,16},{40,24},{48,32},{56,40},{64,... | collective-permute-start | bytes 786440 | tf_op jit(solution)/shard_map/ppermute | solution.py:368
  28.3 1.0 %copy-start = (bf16[1808,128]{1,0:T(8,128)(2,1)S(1)}, bf16[1808,128]{1,0:T(8,128)(2,1)}, u32[]{:S(2)}) copy-start(bf16[1808,128]{1,0:T(8,128)(2,1)} %get-tuple-element.20.local) | copy-start | bytes 1388548
  39.8 7.1 %collective-permute-start.10 = (bf16[144,512]{1,0:T(8,128)(2,1)S(1)}, bf16[144,512]{1,0:T(8,128)(2,1)S(1)}, u32[]{:S(2)}, u32[]{:S(2)}) collective-permute-start(bf16[144,512]{1,0:T(8,128)(2,1)S(1)} %get-tuple-element.32), channel_id=1, source_target_pairs={{0,136},{8,128},{16,152},{24,144},{32,168},{40,160},{48,184},{56,1... | collective-permute-start | bytes 442376 | tf_op jit(solution)/shard_map/ppermute | solution.py:384
  39.9 8.3 %collective-permute-start.11 = (bf16[144,512]{1,0:T(8,128)(2,1)S(1)}, bf16[144,512]{1,0:T(8,128)(2,1)S(1)}, u32[]{:S(2)}, u32[]{:S(2)}) collective-permute-start(bf16[144,512]{1,0:T(8,128)(2,1)S(1)} %get-tuple-element.33), channel_id=1, source_target_pairs={{0,128},{8,136},{16,144},{24,152},{32,160},{40,168},{48,176},{56,1... | collective-permute-start | bytes 442376 | tf_op jit(solution)/shard_map/ppermute | solution.py:385
  42.6 5.6 %collective-permute-start.12 = (bf16[144,512]{1,0:T(8,128)(2,1)S(1)}, bf16[144,512]{1,0:T(8,128)(2,1)S(1)}, u32[]{:S(2)}, u32[]{:S(2)}) collective-permute-start(bf16[144,512]{1,0:T(8,128)(2,1)S(1)} %get-tuple-element.34), channel_id=1, source_target_pairs={{0,8},{8,0},{16,24},{24,16},{32,40},{40,32},{48,56},{56,48},{64,72... | collective-permute-start | bytes 442376 | tf_op jit(solution)/shard_map/ppermute | solution.py:387
  51.8 10.5 %collective-permute-start.13 = (bf16[16,5120]{1,0:T(8,128)(2,1)S(1)}, bf16[16,5120]{1,0:T(8,128)(2,1)S(1)}, u32[]{:S(2)}, u32[]{:S(2)}) collective-permute-start(bf16[16,5120]{1,0:T(8,128)(2,1)S(1)} %get-tuple-element.41), channel_id=1, source_target_pairs={{0,1},{1,0},{2,3},{3,2},{4,5},{5,4},{6,7},{7,6},{8,9},{9,8},{10,11... | collective-permute-start | bytes 491528 | tf_op jit(solution)/shard_map/ppermute | solution.py:402
  53.5 13.0 %collective-permute-start.14 = (bf16[16,5120]{1,0:T(8,128)(2,1)S(1)}, bf16[16,5120]{1,0:T(8,128)(2,1)S(1)}, u32[]{:S(2)}, u32[]{:S(2)}) collective-permute-start(bf16[16,5120]{1,0:T(8,128)(2,1)S(1)} %get-tuple-element.40), channel_id=1, source_target_pairs={{0,5},{1,4},{2,7},{3,6},{4,1},{5,0},{6,3},{7,2},{8,13},{9,12},{10,... | collective-permute-start | bytes 491528 | tf_op jit(solution)/shard_map/ppermute | solution.py:402
  54.8 17.2 %collective-permute-start.15 = (bf16[16,5120]{1,0:T(8,128)(2,1)S(1)}, bf16[16,5120]{1,0:T(8,128)(2,1)S(1)}, u32[]{:S(2)}, u32[]{:S(2)}) collective-permute-start(bf16[16,5120]{1,0:T(8,128)(2,1)S(1)} %get-tuple-element.39), channel_id=1, source_target_pairs={{0,3},{1,2},{2,1},{3,0},{4,7},{5,6},{6,5},{7,4},{8,11},{9,10},{10,... | collective-permute-start | bytes 491528 | tf_op jit(solution)/shard_map/ppermute | solution.py:402
  57.8 14.2 %collective-permute-start.16 = (bf16[16,5120]{1,0:T(8,128)(2,1)S(1)}, bf16[16,5120]{1,0:T(8,128)(2,1)S(1)}, u32[]{:S(2)}, u32[]{:S(2)}) collective-permute-start(bf16[16,5120]{1,0:T(8,128)(2,1)S(1)} %get-tuple-element.38), channel_id=1, source_target_pairs={{0,7},{1,6},{2,5},{3,4},{4,3},{5,2},{6,1},{7,0},{8,15},{9,14},{10,... | collective-permute-start | bytes 491528 | tf_op jit(solution)/shard_map/ppermute | solution.py:402
  58.1 14.9 %collective-permute-start.17 = (bf16[16,5120]{1,0:T(8,128)(2,1)S(1)}, bf16[16,5120]{1,0:T(8,128)(2,1)S(1)}, u32[]{:S(2)}, u32[]{:S(2)}) collective-permute-start(bf16[16,5120]{1,0:T(8,128)(2,1)S(1)} %get-tuple-element.37), channel_id=1, source_target_pairs={{0,2},{1,3},{2,0},{3,1},{4,6},{5,7},{6,4},{7,5},{8,10},{9,11},{10,... | collective-permute-start | bytes 491528 | tf_op jit(solution)/shard_map/ppermute | solution.py:402
  62.4 10.6 %collective-permute-start.18 = (bf16[16,5120]{1,0:T(8,128)(2,1)S(1)}, bf16[16,5120]{1,0:T(8,128)(2,1)S(1)}, u32[]{:S(2)}, u32[]{:S(2)}) collective-permute-start(bf16[16,5120]{1,0:T(8,128)(2,1)S(1)} %get-tuple-element.36), channel_id=1, source_target_pairs={{0,6},{1,7},{2,4},{3,5},{4,2},{5,3},{6,0},{7,1},{8,14},{9,15},{10,... | collective-permute-start | bytes 491528 | tf_op jit(solution)/shard_map/ppermute | solution.py:402
  66.5 8.0 %collective-permute-start.19 = (bf16[16,5120]{1,0:T(8,128)(2,1)S(1)}, bf16[16,5120]{1,0:T(8,128)(2,1)S(1)}, u32[]{:S(2)}, u32[]{:S(2)}) collective-permute-start(bf16[16,5120]{1,0:T(8,128)(2,1)S(1)} %get-tuple-element.35), channel_id=1, source_target_pairs={{0,4},{1,5},{2,6},{3,7},{4,0},{5,1},{6,2},{7,3},{8,12},{9,13},{10,... | collective-permute-start | bytes 491528 | tf_op jit(solution)/shard_map/ppermute | solution.py:402

commit v10 on v9

--- a/solution.py
+++ b/solution.py
@@ -25,6 +25,7 @@
 F32 = jnp.float32
 
 STREAMS = 4
+NEAR_STREAMS = 8
 GROUPS = ((0, -1, 1, -2, 2), (-3, 3, 4))
 
 
@@ -78,7 +79,7 @@
 
 
 def streams_of(refs):
-    return [tuple(refs[3 * r:3 * r + 3]) for r in range(STREAMS)]
+    return [tuple(refs[3 * r:3 * r + 3]) for r in range(len(refs) // 3)]
 
 
 def clear(streams):
@@ -196,7 +197,7 @@
     counts = lax.fori_loop(0, total, sort, (jnp.int32(0),) * 3)
     for k in range(3):
         lists[k][0] = counts[k]
-        for r in range(STREAMS - 1):
+        for r in range(NEAR_STREAMS - 1):
             lists[k][counts[k] + 1 + r] = jnp.int32(SESS * 256)
     for cp in copies:
         cp.wait()
@@ -309,7 +310,7 @@
             pltpu.SMEM((160,), jnp.int32),
             pltpu.VMEM((5 * BLOCK, HD), BF),
         ]
-        + stream_scratch() * STREAMS
+        + stream_scratch() * NEAR_STREAMS
         + [pltpu.SemaphoreType.DMA((6,))],
         compiler_params=pltpu.CompilerParams(vmem_limit_bytes=24 << 20),
         cost_estimate=pl.CostEstimate(flops=4 * 10**9, bytes_accessed=4 << 20, transcendentals=1 << 20),

time: 75.4 us -> 75.5 us (level)
  Pallas kernels: 13.5 us -> 12.2 us
    ppermute x7, waiting for transfers between devices: 9.62 us -> 7.84 us  [on_device(): lax.ppermute(part, 'head', [(i, i ^ flip) for i in range(8)])]
    ppermute x1, starting transfers between devices: 2.91 us -> 1.24 us  [on_device(): back = [p3, p2, lax.ppermute(p1, 'rep', group_perm(1))]]
    ppermute x1, starting transfers between devices: 1.21 us -> 2.7 us  [on_device(): p2 = lax.ppermute(p2, 'rep', group_perm(2))]
    ppermute x1, waiting for transfers between devices: 1.26 us -> 2.48 us  [on_device(): p2 = lax.ppermute(p2, 'rep', group_perm(2))]
    pallas_call x2, Pallas kernels: 4 us -> 3.19 us  [far_call(): pl.pallas_call(functools.partial(far_kernel, nb, first), out_shape=[part...]
where the time goes in v10:
time: 75.5 us; the launch traced here: 75 us
  starting transfers between devices  36.7 us (49%)
  waiting for transfers between devices  20.5 us (27%)
  Pallas kernels  12.2 us (16%)
  matrix products  3.34 us (4%)
  local copies, waits for them, and re-layouts  1.11 us (1%)
  other arithmetic  1.03 us (1%)
    ppermute x7, starting transfers between devices, on_device(): lax.ppermute(part, 'head', [(i, i ^ flip) for i in range(8)])  13.6 us
    ppermute x7, waiting for transfers between devices, on_device(): lax.ppermute(part, 'head', [(i, i ^ flip) for i in range(8)])  7.84 us
    pallas_call x1, Pallas kernels, near_call(): pl.pallas_call(near_kernel, out_shape=[jax.ShapeDtypeStruct((SESS * QROWS...  5.29 us
    ppermute x1, starting transfers between devices, on_device(): dn1 = lax.ppermute(kv, 'rep', z_perm(-1))  4.03 us
    ppermute x1, waiting for transfers between devices, on_device(): up1 = lax.ppermute(kv, 'rep', z_perm(1))  3.51 us
    ppermute x3, starting transfers between devices, on_device(): sents = [lax.ppermute(sent, 'rep', group_perm(r)) for r in (1, 2, 3)]  3.46 us
    dot_general x1, matrix products, on_device(): rows = jnp.dot(attn, out_weight, preferred_element_type=F32).astype(BF)  3.34 us
    ppermute x1, starting transfers between devices, on_device(): dn2 = lax.ppermute(dn1, 'rep', z_perm(-1))  3.23 us
  transfers between devices with their start and end apart: 20, of which 9 were waited for; matrix products, arithmetic and copies ran while one was open for 0% of the time, Pallas kernels for 13%

profile of v10, /device:TPU:2, one launch (start us, length us, event | category | flops | bytes accessed | tf_op | source)
XLA Modules:
  0.0 75.0 jit_solution(16572227023607456943)
XLA Ops:
  1.0 2.0 %collective-permute-start = (bf16[1024,128]{1,0:T(8,128)(2,1)S(1)}, bf16[1024,128]{1,0:T(8,128)(2,1)S(1)}, u32[]{:S(2)}, u32[]{:S(2)}) collective-permute-start(bf16[1024,128]{1,0:T(8,128)(2,1)S(1)} %bitcast.10), channel_id=1, source_target_pairs={{0,16},{8,24},{16,32},{24,40},{32,48},{40,56},{48,64},{56,72},{64,... | collective-permute-start | bytes 786440 | tf_op jit(solution)/shard_map/ppermute | solution.py:346
  3.0 4.0 %collective-permute-start.1 = (bf16[1024,128]{1,0:T(8,128)(2,1)S(1)}, bf16[1024,128]{1,0:T(8,128)(2,1)S(1)}, u32[]{:S(2)}, u32[]{:S(2)}) collective-permute-start(bf16[1024,128]{1,0:T(8,128)(2,1)S(1)} %bitcast.11), channel_id=1, source_target_pairs={{0,112},{8,120},{16,0},{24,8},{32,16},{40,24},{48,32},{56,40},{64,... | collective-permute-start | bytes 786440 | tf_op jit(solution)/shard_map/ppermute | solution.py:347
  7.0 2.7 %pack.1 = (bf16[528,128]{1,0:T(8,128)(2,1)}, bf16[1808,128]{1,0:T(8,128)(2,1)}) custom-call(bf16[512,128]{1,0:T(8,128)(2,1)} %bitcast.15, bf16[128,128]{1,0:T(8,128)(2,1)} %bitcast.16, bf16[128,128]{1,0:T(8,128)(2,1)} %bitcast.17, bf16[512,128]{1,0:T(8,128)(2,1)} %bitcast.13, bf16[512,128]{1,0:T(8,128)(2,1)} %bitcast.14, s32[2,16]{1,0:T(2,128)} %table.1, ...), custom_call_target="tpu_custom_call" | custom-call | tf_op jit(solution)/shard_map/pack/pallas_call | solution.py:348
  9.7 3.5 %collective-permute-done.up1 = bf16[1024,128]{1,0:T(8,128)(2,1)S(1)} collective-permute-done((bf16[1024,128]{1,0:T(8,128)(2,1)S(1)}, bf16[1024,128]{1,0:T(8,128)(2,1)S(1)}, u32[]{:S(2)}, u32[]{:S(2)}) %collective-permute-start) | collective-permute-done | bytes 262176 | tf_op jit(solution)/shard_map/ppermute | solution.py:346
  13.3 3.2 %collective-permute-start.6 = (bf16[1024,128]{1,0:T(8,128)(2,1)S(1)}, bf16[1024,128]{1,0:T(8,128)(2,1)S(1)}, u32[]{:S(2)}, u32[]{:S(2)}) collective-permute-start(bf16[1024,128]{1,0:T(8,128)(2,1)S(1)} %collective-permute-done.1.dn1), channel_id=1, source_target_pairs={{0,112},{8,120},{16,0},{24,8},{32,16},{40,24},{48,32},{56,40},{64,... | collective-permute-start | bytes 786440 | tf_op jit(solution)/shard_map/ppermute | solution.py:366
  16.6 2.2 %collective-permute-start.3 = (bf16[528,128]{1,0:T(8,128)(2,1)}, bf16[528,128]{1,0:T(8,128)(2,1)S(1)}, u32[]{:S(2)}, u32[]{:S(2)}) collective-permute-start(bf16[528,128]{1,0:T(8,128)(2,1)} %get-tuple-element.22), channel_id=1, source_target_pairs={{0,128},{8,136},{16,144},{24,152},{32,160},{40,168},{48,176},{56,1... | collective-permute-start | bytes 405512 | tf_op jit(solution)/shard_map/ppermute | solution.py:367
  20.0 2.0 %collective-permute-done.5.up2 = bf16[1024,128]{1,0:T(8,128)(2,1)S(1)} collective-permute-done((bf16[1024,128]{1,0:T(8,128)(2,1)S(1)}, bf16[1024,128]{1,0:T(8,128)(2,1)S(1)}, u32[]{:S(2)}, u32[]{:S(2)}) %collective-permute-start.5) | collective-permute-done | bytes 262176 | tf_op jit(solution)/shard_map/ppermute | solution.py:365
  22.0 3.1 %collective-permute-start.9 = (bf16[1024,128]{1,0:T(8,128)(2,1)S(1)}, bf16[1024,128]{1,0:T(8,128)(2,1)S(1)}, u32[]{:S(2)}, u32[]{:S(2)}) collective-permute-start(bf16[1024,128]{1,0:T(8,128)(2,1)S(1)} %broadcast_select_fusion), channel_id=1, source_target_pairs={{0,32},{8,104},{16,48},{24,120},{32,64},{40,8},{48,80},{56,24},{64... | collective-permute-start | bytes 786440 | tf_op jit(solution)/shard_map/ppermute | solution.py:371
  25.1 1.8 %collective-permute-start.7 = (bf16[1024,128]{1,0:T(8,128)(2,1)S(1)}, bf16[1024,128]{1,0:T(8,128)(2,1)S(1)}, u32[]{:S(2)}, u32[]{:S(2)}) collective-permute-start(bf16[1024,128]{1,0:T(8,128)(2,1)S(1)} %collective-permute-done.5.up2), channel_id=1, source_target_pairs={{0,16},{8,24},{16,32},{24,40},{32,48},{40,56},{48,64},{56,72},{64,... | collective-permute-start | bytes 786440 | tf_op jit(solution)/shard_map/ppermute | solution.py:368
  26.9 1.4 %collective-permute-start.8 = (bf16[1024,128]{1,0:T(8,128)(2,1)S(1)}, bf16[1024,128]{1,0:T(8,128)(2,1)S(1)}, u32[]{:S(2)}, u32[]{:S(2)}) collective-permute-start(bf16[1024,128]{1,0:T(8,128)(2,1)S(1)} %collective-permute-done.6.dn2), channel_id=1, source_target_pairs={{0,112},{8,120},{16,0},{24,8},{32,16},{40,24},{48,32},{56,40},{64,... | collective-permute-start | bytes 786440 | tf_op jit(solution)/shard_map/ppermute | solution.py:369
  29.3 5.3 %near_pages.1 = (bf16[2048,128]{1,0:T(8,128)(2,1)S(1)}, s32[160]{0:T(256)S(1)}, s32[160]{0:T(256)S(1)}, f32[8,1,256]{2,1,0:T(1,128)S(1)}, f32[8,1,256]{2,1,0:T(1,128)S(1)}, /*index=5*/f32[8,128,256]{2,1,0:T(8,128)S(1)}) custom-call(s32[32]{0:T(128)S(1)} %and_select_fusion.7.maps, bf16[1808,128]{1,0:T(8,128)(2,1)S(1)} %copy-done, ...), custom_call_target="tpu_custom_call" | custom-call | flops 4000000000 | bytes 4194304 | tf_op jit(solution)/shard_map/near_pages/pallas_call | solution.py:298
  34.6 2.6 %collective-permute-done.7.refs_2_ = bf16[1024,128]{1,0:T(8,128)(2,1)S(1)} collective-permute-done((bf16[1024,128]{1,0:T(8,128)(2,1)S(1)}, bf16[1024,128]{1,0:T(8,128)(2,1)S(1)}, u32[]{:S(2)}, u32[]{:S(2)}) %collective-permute-start.7) | collective-permute-done | bytes 262176 | tf_op jit(solution)/shard_map/ppermute | solution.py:368
  37.3 1.5 %far_pages_x.1 = (bf16[144,512]{1,0:T(8,128)(2,1)S(1)}, bf16[144,512]{1,0:T(8,128)(2,1)S(1)}) custom-call(s32[160]{0:T(256)S(1)} %get-tuple-element.31.refs_0_, bf16[2048,128]{1,0:T(8,128)(2,1)S(1)} %get-tuple-element.26.refs_1_, bf16[1024,128]{1,0:T(8,128)(2,1)S(1)} %collective-permute-done.7.refs_2_, bf16[1024,128]{1,0:T(8,128)(2,1)S(1)} %collective-permute-done.8.refs_3_, ...), custom_call_target="tpu_custom_call" | custom-call | flops 1000000000 | bytes 4194304 | tf_op jit(solution)/shard_map/far_pages_x/pallas_call | solution.py:325
  38.9 2.7 %collective-permute-start.11 = (bf16[144,512]{1,0:T(8,128)(2,1)S(1)}, bf16[144,512]{1,0:T(8,128)(2,1)S(1)}, u32[]{:S(2)}, u32[]{:S(2)}) collective-permute-start(bf16[144,512]{1,0:T(8,128)(2,1)S(1)} %get-tuple-element.33), channel_id=1, source_target_pairs={{0,128},{8,136},{16,144},{24,152},{32,160},{40,168},{48,176},{56,1... | collective-permute-start | bytes 442376 | tf_op jit(solution)/shard_map/ppermute | solution.py:386
  41.6 1.7 %far_pages_own.1 = (f32[136,512]{1,0:T(8,128)S(1)}, bf16[144,512]{1,0:T(8,128)(2,1)S(1)}) custom-call(s32[160]{0:T(256)S(1)} %get-tuple-element.25.refs_0_, bf16[2048,128]{1,0:T(8,128)(2,1)S(1)} %get-tuple-element.26.refs_1_, bf16[1024,128]{1,0:T(8,128)(2,1)S(1)} %collective-permute-done.7.refs_2_, bf16[1024,128]{1,0:T(8,128)(2,1)S(1)} %collective-permute-done.8.refs_3_, ...), custom_call_target="tpu_custom_call" | custom-call | flops 1000000000 | bytes 4194304 | tf_op jit(solution)/shard_map/far_pages_own/pallas_call | solution.py:325
  44.5 2.0 %collective-permute-done.10.p1 = bf16[144,512]{1,0:T(8,128)(2,1)S(1)} collective-permute-done((bf16[144,512]{1,0:T(8,128)(2,1)S(1)}, bf16[144,512]{1,0:T(8,128)(2,1)S(1)}, u32[]{:S(2)}, u32[]{:S(2)}) %collective-permute-start.10) | collective-permute-done | bytes 147488 | tf_op jit(solution)/shard_map/ppermute | solution.py:385
  46.5 2.5 %collective-permute-done.11.p2 = bf16[144,512]{1,0:T(8,128)(2,1)S(1)} collective-permute-done((bf16[144,512]{1,0:T(8,128)(2,1)S(1)}, bf16[144,512]{1,0:T(8,128)(2,1)S(1)}, u32[]{:S(2)}, u32[]{:S(2)}) %collective-permute-start.11) | collective-permute-done | bytes 147488 | tf_op jit(solution)/shard_map/ppermute | solution.py:386
  49.3 3.3 %convolution_convert_fusion = bf16[128,5120]{1,0:T(8,128)(2,1)S(1)} fusion(bf16[128,512]{1,0:T(8,128)(2,1)S(1)} %combine.1, bf16[512,5120]{1,0:T(8,128)(2,1)} %param.15), kind=kOutput, calls=%fused_computation | convolution fusion | flops 671744000 | bytes 6684672 | tf_op jit(solution)/shard_map/dot_general | solution.py:400
  52.7 1.7 %collective-permute-start.13 = (bf16[16,5120]{1,0:T(8,128)(2,1)S(1)}, bf16[16,5120]{1,0:T(8,128)(2,1)S(1)}, u32[]{:S(2)}, u32[]{:S(2)}) collective-permute-start(bf16[16,5120]{1,0:T(8,128)(2,1)S(1)} %get-tuple-element.41), channel_id=1, source_target_pairs={{0,1},{1,0},{2,3},{3,2},{4,5},{5,4},{6,7},{7,6},{8,9},{9,8},{10,11... | collective-permute-start | bytes 491528 | tf_op jit(solution)/shard_map/ppermute | solution.py:403
  55.3 3.0 %collective-permute-start.15 = (bf16[16,5120]{1,0:T(8,128)(2,1)S(1)}, bf16[16,5120]{1,0:T(8,128)(2,1)S(1)}, u32[]{:S(2)}, u32[]{:S(2)}) collective-permute-start(bf16[16,5120]{1,0:T(8,128)(2,1)S(1)} %get-tuple-element.39), channel_id=1, source_target_pairs={{0,3},{1,2},{2,1},{3,0},{4,7},{5,6},{6,5},{7,4},{8,11},{9,10},{10,... | collective-permute-start | bytes 491528 | tf_op jit(solution)/shard_map/ppermute | solution.py:403
  59.0 2.0 %collective-permute-start.17 = (bf16[16,5120]{1,0:T(8,128)(2,1)S(1)}, bf16[16,5120]{1,0:T(8,128)(2,1)S(1)}, u32[]{:S(2)}, u32[]{:S(2)}) collective-permute-start(bf16[16,5120]{1,0:T(8,128)(2,1)S(1)} %get-tuple-element.37), channel_id=1, source_target_pairs={{0,2},{1,3},{2,0},{3,1},{4,6},{5,7},{6,4},{7,5},{8,10},{9,11},{10,... | collective-permute-start | bytes 491528 | tf_op jit(solution)/shard_map/ppermute | solution.py:403
  61.0 1.7 %collective-permute-done.13.refs_1_ = bf16[16,5120]{1,0:T(8,128)(2,1)S(1)} collective-permute-done((bf16[16,5120]{1,0:T(8,128)(2,1)S(1)}, bf16[16,5120]{1,0:T(8,128)(2,1)S(1)}, u32[]{:S(2)}, u32[]{:S(2)}) %collective-permute-start.13) | collective-permute-done | bytes 163872 | tf_op jit(solution)/shard_map/ppermute | solution.py:403
  62.6 4.4 %collective-permute-start.18 = (bf16[16,5120]{1,0:T(8,128)(2,1)S(1)}, bf16[16,5120]{1,0:T(8,128)(2,1)S(1)}, u32[]{:S(2)}, u32[]{:S(2)}) collective-permute-start(bf16[16,5120]{1,0:T(8,128)(2,1)S(1)} %get-tuple-element.36), channel_id=1, source_target_pairs={{0,6},{1,7},{2,4},{3,5},{4,2},{5,3},{6,0},{7,1},{8,14},{9,15},{10,... | collective-permute-start | bytes 491528 | tf_op jit(solution)/shard_map/ppermute | solution.py:403
  68.0 4.0 %collective-permute-done.15.refs_3_ = bf16[16,5120]{1,0:T(8,128)(2,1)S(1)} collective-permute-done((bf16[16,5120]{1,0:T(8,128)(2,1)S(1)}, bf16[16,5120]{1,0:T(8,128)(2,1)S(1)}, u32[]{:S(2)}, u32[]{:S(2)}) %collective-permute-start.15) | collective-permute-done | bytes 163872 | tf_op jit(solution)/shard_map/ppermute | solution.py:403
  (31 shorter events, 10.5 us)
Async XLA Ops:
  1.0 6.0 %copy-start.1 = (bf16[8,1,128,128]{3,2,1,0:T(8,128)(2,1)}, bf16[8,1,128,128]{3,2,1,0:T(8,128)(2,1)S(1)}, u32[]{:S(2)}) copy-start(bf16[8,1,128,128]{3,2,1,0:T(8,128)(2,1)S(1)} %pad_maximum_fusion) | copy-start | bytes 786436
  1.0 12.2 %collective-permute-start = (bf16[1024,128]{1,0:T(8,128)(2,1)S(1)}, bf16[1024,128]{1,0:T(8,128)(2,1)S(1)}, u32[]{:S(2)}, u32[]{:S(2)}) collective-permute-start(bf16[1024,128]{1,0:T(8,128)(2,1)S(1)} %bitcast.10), channel_id=1, source_target_pairs={{0,16},{8,24},{16,32},{24,40},{32,48},{40,56},{48,64},{56,72},{64,... | collective-permute-start | bytes 786440 | tf_op jit(solution)/shard_map/ppermute | solution.py:346
  3.0 10.2 %collective-permute-start.1 = (bf16[1024,128]{1,0:T(8,128)(2,1)S(1)}, bf16[1024,128]{1,0:T(8,128)(2,1)S(1)}, u32[]{:S(2)}, u32[]{:S(2)}) collective-permute-start(bf16[1024,128]{1,0:T(8,128)(2,1)S(1)} %bitcast.11), channel_id=1, source_target_pairs={{0,112},{8,120},{16,0},{24,8},{32,16},{40,24},{48,32},{56,40},{64,... | collective-permute-start | bytes 786440 | tf_op jit(solution)/shard_map/ppermute | solution.py:347
  13.2 8.7 %collective-permute-start.5 = (bf16[1024,128]{1,0:T(8,128)(2,1)S(1)}, bf16[1024,128]{1,0:T(8,128)(2,1)S(1)}, u32[]{:S(2)}, u32[]{:S(2)}) collective-permute-start(bf16[1024,128]{1,0:T(8,128)(2,1)S(1)} %collective-permute-done.up1), channel_id=1, source_target_pairs={{0,16},{8,24},{16,32},{24,40},{32,48},{40,56},{48,64},{56,72},{64,... | collective-permute-start | bytes 786440 | tf_op jit(solution)/shard_map/ppermute | solution.py:365
  13.3 8.7 %collective-permute-start.6 = (bf16[1024,128]{1,0:T(8,128)(2,1)S(1)}, bf16[1024,128]{1,0:T(8,128)(2,1)S(1)}, u32[]{:S(2)}, u32[]{:S(2)}) collective-permute-start(bf16[1024,128]{1,0:T(8,128)(2,1)S(1)} %collective-permute-done.1.dn1), channel_id=1, source_target_pairs={{0,112},{8,120},{16,0},{24,8},{32,16},{40,24},{48,32},{56,40},{64,... | collective-permute-start | bytes 786440 | tf_op jit(solution)/shard_map/ppermute | solution.py:366
  16.5 10.4 %collective-permute-start.2 = (bf16[528,128]{1,0:T(8,128)(2,1)}, bf16[528,128]{1,0:T(8,128)(2,1)S(1)}, u32[]{:S(2)}, u32[]{:S(2)}) collective-permute-start(bf16[528,128]{1,0:T(8,128)(2,1)} %get-tuple-element.22), channel_id=1, source_target_pairs={{0,8},{8,0},{16,24},{24,16},{32,40},{40,32},{48,56},{56,48},{64,72... | collective-permute-start | bytes 405512 | tf_op jit(solution)/shard_map/ppermute | solution.py:367
  16.6 11.7 %collective-permute-start.3 = (bf16[528,128]{1,0:T(8,128)(2,1)}, bf16[528,128]{1,0:T(8,128)(2,1)S(1)}, u32[]{:S(2)}, u32[]{:S(2)}) collective-permute-start(bf16[528,128]{1,0:T(8,128)(2,1)} %get-tuple-element.22), channel_id=1, source_target_pairs={{0,128},{8,136},{16,144},{24,152},{32,160},{40,168},{48,176},{56,1... | collective-permute-start | bytes 405512 | tf_op jit(solution)/shard_map/ppermute | solution.py:367
  18.8 9.5 %collective-permute-start.4 = (bf16[528,128]{1,0:T(8,128)(2,1)}, bf16[528,128]{1,0:T(8,128)(2,1)S(1)}, u32[]{:S(2)}, u32[]{:S(2)}) collective-permute-start(bf16[528,128]{1,0:T(8,128)(2,1)} %get-tuple-element.22), channel_id=1, source_target_pairs={{0,136},{8,128},{16,152},{24,144},{32,168},{40,160},{48,184},{56,1... | collective-permute-start | bytes 405512 | tf_op jit(solution)/shard_map/ppermute | solution.py:367
  22.0 12.6 %collective-permute-start.9 = (bf16[1024,128]{1,0:T(8,128)(2,1)S(1)}, bf16[1024,128]{1,0:T(8,128)(2,1)S(1)}, u32[]{:S(2)}, u32[]{:S(2)}) collective-permute-start(bf16[1024,128]{1,0:T(8,128)(2,1)S(1)} %broadcast_select_fusion), channel_id=1, source_target_pairs={{0,32},{8,104},{16,48},{24,120},{32,64},{40,8},{48,80},{56,24},{64... | collective-permute-start | bytes 786440 | tf_op jit(solution)/shard_map/ppermute | solution.py:371
  25.1 12.2 %collective-permute-start.7 = (bf16[1024,128]{1,0:T(8,128)(2,1)S(1)}, bf16[1024,128]{1,0:T(8,128)(2,1)S(1)}, u32[]{:S(2)}, u32[]{:S(2)}) collective-permute-start(bf16[1024,128]{1,0:T(8,128)(2,1)S(1)} %collective-permute-done.5.up2), channel_id=1, source_target_pairs={{0,16},{8,24},{16,32},{24,40},{32,48},{40,56},{48,64},{56,72},{64,... | collective-permute-start | bytes 786440 | tf_op jit(solution)/shard_map/ppermute | solution.py:368
  26.9 10.4 %collective-permute-start.8 = (bf16[1024,128]{1,0:T(8,128)(2,1)S(1)}, bf16[1024,128]{1,0:T(8,128)(2,1)S(1)}, u32[]{:S(2)}, u32[]{:S(2)}) collective-permute-start(bf16[1024,128]{1,0:T(8,128)(2,1)S(1)} %collective-permute-done.6.dn2), channel_id=1, source_target_pairs={{0,112},{8,120},{16,0},{24,8},{32,16},{40,24},{48,32},{56,40},{64,... | collective-permute-start | bytes 786440 | tf_op jit(solution)/shard_map/ppermute | solution.py:369
  28.3 1.0 %copy-start = (bf16[1808,128]{1,0:T(8,128)(2,1)S(1)}, bf16[1808,128]{1,0:T(8,128)(2,1)}, u32[]{:S(2)}) copy-start(bf16[1808,128]{1,0:T(8,128)(2,1)} %get-tuple-element.20.local) | copy-start | bytes 1388548
  38.8 7.7 %collective-permute-start.10 = (bf16[144,512]{1,0:T(8,128)(2,1)S(1)}, bf16[144,512]{1,0:T(8,128)(2,1)S(1)}, u32[]{:S(2)}, u32[]{:S(2)}) collective-permute-start(bf16[144,512]{1,0:T(8,128)(2,1)S(1)} %get-tuple-element.32), channel_id=1, source_target_pairs={{0,136},{8,128},{16,152},{24,144},{32,168},{40,160},{48,184},{56,1... | collective-permute-start | bytes 442376 | tf_op jit(solution)/shard_map/ppermute | solution.py:385
  38.9 10.1 %collective-permute-start.11 = (bf16[144,512]{1,0:T(8,128)(2,1)S(1)}, bf16[144,512]{1,0:T(8,128)(2,1)S(1)}, u32[]{:S(2)}, u32[]{:S(2)}) collective-permute-start(bf16[144,512]{1,0:T(8,128)(2,1)S(1)} %get-tuple-element.33), channel_id=1, source_target_pairs={{0,128},{8,136},{16,144},{24,152},{32,160},{40,168},{48,176},{56,1... | collective-permute-start | bytes 442376 | tf_op jit(solution)/shard_map/ppermute | solution.py:386
  43.3 5.7 %collective-permute-start.12 = (bf16[144,512]{1,0:T(8,128)(2,1)S(1)}, bf16[144,512]{1,0:T(8,128)(2,1)S(1)}, u32[]{:S(2)}, u32[]{:S(2)}) collective-permute-start(bf16[144,512]{1,0:T(8,128)(2,1)S(1)} %get-tuple-element.34), channel_id=1, source_target_pairs={{0,8},{8,0},{16,24},{24,16},{32,40},{40,32},{48,56},{56,48},{64,72... | collective-permute-start | bytes 442376 | tf_op jit(solution)/shard_map/ppermute | solution.py:388
  52.7 9.9 %collective-permute-start.13 = (bf16[16,5120]{1,0:T(8,128)(2,1)S(1)}, bf16[16,5120]{1,0:T(8,128)(2,1)S(1)}, u32[]{:S(2)}, u32[]{:S(2)}) collective-permute-start(bf16[16,5120]{1,0:T(8,128)(2,1)S(1)} %get-tuple-element.41), channel_id=1, source_target_pairs={{0,1},{1,0},{2,3},{3,2},{4,5},{5,4},{6,7},{7,6},{8,9},{9,8},{10,11... | collective-permute-start | bytes 491528 | tf_op jit(solution)/shard_map/ppermute | solution.py:403
  54.4 12.7 %collective-permute-start.14 = (bf16[16,5120]{1,0:T(8,128)(2,1)S(1)}, bf16[16,5120]{1,0:T(8,128)(2,1)S(1)}, u32[]{:S(2)}, u32[]{:S(2)}) collective-permute-start(bf16[16,5120]{1,0:T(8,128)(2,1)S(1)} %get-tuple-element.40), channel_id=1, source_target_pairs={{0,5},{1,4},{2,7},{3,6},{4,1},{5,0},{6,3},{7,2},{8,13},{9,12},{10,... | collective-permute-start | bytes 491528 | tf_op jit(solution)/shard_map/ppermute | solution.py:403
  55.3 16.8 %collective-permute-start.15 = (bf16[16,5120]{1,0:T(8,128)(2,1)S(1)}, bf16[16,5120]{1,0:T(8,128)(2,1)S(1)}, u32[]{:S(2)}, u32[]{:S(2)}) collective-permute-start(bf16[16,5120]{1,0:T(8,128)(2,1)S(1)} %get-tuple-element.39), channel_id=1, source_target_pairs={{0,3},{1,2},{2,1},{3,0},{4,7},{5,6},{6,5},{7,4},{8,11},{9,10},{10,... | collective-permute-start | bytes 491528 | tf_op jit(solution)/shard_map/ppermute | solution.py:403
  58.3 13.7 %collective-permute-start.16 = (bf16[16,5120]{1,0:T(8,128)(2,1)S(1)}, bf16[16,5120]{1,0:T(8,128)(2,1)S(1)}, u32[]{:S(2)}, u32[]{:S(2)}) collective-permute-start(bf16[16,5120]{1,0:T(8,128)(2,1)S(1)} %get-tuple-element.38), channel_id=1, source_target_pairs={{0,7},{1,6},{2,5},{3,4},{4,3},{5,2},{6,1},{7,0},{8,15},{9,14},{10,... | collective-permute-start | bytes 491528 | tf_op jit(solution)/shard_map/ppermute | solution.py:403
  59.0 14.3 %collective-permute-start.17 = (bf16[16,5120]{1,0:T(8,128)(2,1)S(1)}, bf16[16,5120]{1,0:T(8,128)(2,1)S(1)}, u32[]{:S(2)}, u32[]{:S(2)}) collective-permute-start(bf16[16,5120]{1,0:T(8,128)(2,1)S(1)} %get-tuple-element.37), channel_id=1, source_target_pairs={{0,2},{1,3},{2,0},{3,1},{4,6},{5,7},{6,4},{7,5},{8,10},{9,11},{10,... | collective-permute-start | bytes 491528 | tf_op jit(solution)/shard_map/ppermute | solution.py:403
  62.6 10.6 %collective-permute-start.18 = (bf16[16,5120]{1,0:T(8,128)(2,1)S(1)}, bf16[16,5120]{1,0:T(8,128)(2,1)S(1)}, u32[]{:S(2)}, u32[]{:S(2)}) collective-permute-start(bf16[16,5120]{1,0:T(8,128)(2,1)S(1)} %get-tuple-element.36), channel_id=1, source_target_pairs={{0,6},{1,7},{2,4},{3,5},{4,2},{5,3},{6,0},{7,1},{8,14},{9,15},{10,... | collective-permute-start | bytes 491528 | tf_op jit(solution)/shard_map/ppermute | solution.py:403
  67.0 7.1 %collective-permute-start.19 = (bf16[16,5120]{1,0:T(8,128)(2,1)S(1)}, bf16[16,5120]{1,0:T(8,128)(2,1)S(1)}, u32[]{:S(2)}, u32[]{:S(2)}) collective-permute-start(bf16[16,5120]{1,0:T(8,128)(2,1)S(1)} %get-tuple-element.35), channel_id=1, source_target_pairs={{0,4},{1,5},{2,6},{3,7},{4,0},{5,1},{6,2},{7,3},{8,12},{9,13},{10,... | collective-permute-start | bytes 491528 | tf_op jit(solution)/shard_map/ppermute | solution.py:403

commit v11 on v9

--- a/solution.py
+++ b/solution.py
@@ -28,7 +28,7 @@
 GROUPS = ((0, -1, 1, -2, 2), (-3, 3, 4))
 
 
-HEADS = (0, 1, 5, 3, 7, 2, 6, 4)
+HEADS = (0, 5, 1, 7, 3, 2, 6, 4)
 
 
 def rep_of(xh, z, c):

time: 75.4 us -> 77.5 us (1.028); the launches traced: 75.3 us -> 76.3 us
  starting transfers between devices: 36.2 us -> 34.8 us
  waiting for transfers between devices: 20 us -> 21.3 us
  Pallas kernels: 13.5 us -> 14.6 us
    ppermute x1, starting transfers between devices: 2.91 us -> 0.27 us  [on_device(): back = [p3, p2, lax.ppermute(p1, 'rep', group_perm(1))]]
    ppermute x1, starting transfers between devices: 1.21 us -> 2.7 us  [on_device(): p2 = lax.ppermute(p2, 'rep', group_perm(2))]
    ppermute x1, waiting for transfers between devices: 1.26 us -> 2.48 us  [on_device(): p2 = lax.ppermute(p2, 'rep', group_perm(2))]
    ppermute x1, waiting for transfers between devices: 2.2 us -> 1.13 us  [on_device(): up3 = lax.ppermute(up2, 'rep', z_perm(1))]
    pallas_call x1, Pallas kernels: 5.72 us -> 6.8 us  [near_call(): pl.pallas_call(near_kernel, out_shape=[jax.ShapeDtypeStruct((SESS * QROWS...]
  transfers between devices with their start and end apart: 20 -> 20, of which waited for: 9 -> 6; matrix products, arithmetic and copies ran while one was open for 0% -> 0% of each run, Pallas kernels for 13% -> 16%
where the time goes in v11:
time: 77.5 us; the launch traced here: 76.3 us
  starting transfers between devices  34.8 us (45%)
  waiting for transfers between devices  21.3 us (27%)
  Pallas kernels  14.6 us (19%)
  matrix products  3.34 us (4%)
  local copies, waits for them, and re-layouts  1.11 us (1%)
  other arithmetic  1.03 us (1%)
    ppermute x7, starting transfers between devices, on_device(): lax.ppermute(part, 'head', [(i, i ^ flip) for i in range(8)])  12.7 us
    ppermute x7, waiting for transfers between devices, on_device(): lax.ppermute(part, 'head', [(i, i ^ flip) for i in range(8)])  10 us
    pallas_call x1, Pallas kernels, near_call(): pl.pallas_call(near_kernel, out_shape=[jax.ShapeDtypeStruct((SESS * QROWS...  6.8 us
    ppermute x1, starting transfers between devices, on_device(): dn1 = lax.ppermute(kv, 'rep', z_perm(-1))  4.03 us
    pallas_call x2, Pallas kernels, far_call(): pl.pallas_call(functools.partial(far_kernel, nb, first), out_shape=[part...  4.01 us
    ppermute x1, waiting for transfers between devices, on_device(): up1 = lax.ppermute(kv, 'rep', z_perm(1))  3.51 us
    ppermute x3, starting transfers between devices, on_device(): sents = [lax.ppermute(sent, 'rep', group_perm(r)) for r in (1, 2, 3)]  3.46 us
    dot_general x1, matrix products, on_device(): rows = jnp.dot(attn, out_weight, preferred_element_type=F32).astype(BF)  3.34 us
  transfers between devices with their start and end apart: 20, of which 6 were waited for; matrix products, arithmetic and copies ran while one was open for 0% of the time, Pallas kernels for 16%

profile of v11, /device:TPU:2, one launch (start us, length us, event | category | flops | bytes accessed | tf_op | source)
XLA Modules:
  0.0 76.3 jit_solution(44400935663899498)
XLA Ops:
  1.0 2.0 %collective-permute-start = (bf16[1024,128]{1,0:T(8,128)(2,1)S(1)}, bf16[1024,128]{1,0:T(8,128)(2,1)S(1)}, u32[]{:S(2)}, u32[]{:S(2)}) collective-permute-start(bf16[1024,128]{1,0:T(8,128)(2,1)S(1)} %bitcast.10), channel_id=1, source_target_pairs={{0,16},{8,24},{16,32},{24,40},{32,48},{40,56},{48,64},{56,72},{64,... | collective-permute-start | bytes 786440 | tf_op jit(solution)/shard_map/ppermute | solution.py:345
  3.0 4.0 %collective-permute-start.1 = (bf16[1024,128]{1,0:T(8,128)(2,1)S(1)}, bf16[1024,128]{1,0:T(8,128)(2,1)S(1)}, u32[]{:S(2)}, u32[]{:S(2)}) collective-permute-start(bf16[1024,128]{1,0:T(8,128)(2,1)S(1)} %bitcast.11), channel_id=1, source_target_pairs={{0,112},{8,120},{16,0},{24,8},{32,16},{40,24},{48,32},{56,40},{64,... | collective-permute-start | bytes 786440 | tf_op jit(solution)/shard_map/ppermute | solution.py:346
  7.0 2.7 %pack.1 = (bf16[528,128]{1,0:T(8,128)(2,1)}, bf16[1808,128]{1,0:T(8,128)(2,1)}) custom-call(bf16[512,128]{1,0:T(8,128)(2,1)} %bitcast.15, bf16[128,128]{1,0:T(8,128)(2,1)} %bitcast.16, bf16[128,128]{1,0:T(8,128)(2,1)} %bitcast.17, bf16[512,128]{1,0:T(8,128)(2,1)} %bitcast.13, bf16[512,128]{1,0:T(8,128)(2,1)} %bitcast.14, s32[2,16]{1,0:T(2,128)} %table.1, ...), custom_call_target="tpu_custom_call" | custom-call | tf_op jit(solution)/shard_map/pack/pallas_call | solution.py:347
  9.7 3.5 %collective-permute-done.up1 = bf16[1024,128]{1,0:T(8,128)(2,1)S(1)} collective-permute-done((bf16[1024,128]{1,0:T(8,128)(2,1)S(1)}, bf16[1024,128]{1,0:T(8,128)(2,1)S(1)}, u32[]{:S(2)}, u32[]{:S(2)}) %collective-permute-start) | collective-permute-done | bytes 262176 | tf_op jit(solution)/shard_map/ppermute | solution.py:345
  13.3 3.2 %collective-permute-start.6 = (bf16[1024,128]{1,0:T(8,128)(2,1)S(1)}, bf16[1024,128]{1,0:T(8,128)(2,1)S(1)}, u32[]{:S(2)}, u32[]{:S(2)}) collective-permute-start(bf16[1024,128]{1,0:T(8,128)(2,1)S(1)} %collective-permute-done.1.dn1), channel_id=1, source_target_pairs={{0,112},{8,120},{16,0},{24,8},{32,16},{40,24},{48,32},{56,40},{64,... | collective-permute-start | bytes 786440 | tf_op jit(solution)/shard_map/ppermute | solution.py:365
  16.6 2.2 %collective-permute-start.3 = (bf16[528,128]{1,0:T(8,128)(2,1)}, bf16[528,128]{1,0:T(8,128)(2,1)S(1)}, u32[]{:S(2)}, u32[]{:S(2)}) collective-permute-start(bf16[528,128]{1,0:T(8,128)(2,1)} %get-tuple-element.22), channel_id=1, source_target_pairs={{0,128},{8,136},{16,144},{24,152},{32,160},{40,168},{48,176},{56,1... | collective-permute-start | bytes 405512 | tf_op jit(solution)/shard_map/ppermute | solution.py:366
  18.8 1.2 %collective-permute-start.4 = (bf16[528,128]{1,0:T(8,128)(2,1)}, bf16[528,128]{1,0:T(8,128)(2,1)S(1)}, u32[]{:S(2)}, u32[]{:S(2)}) collective-permute-start(bf16[528,128]{1,0:T(8,128)(2,1)} %get-tuple-element.22), channel_id=1, source_target_pairs={{0,136},{8,128},{16,152},{24,144},{32,168},{40,160},{48,184},{56,1... | collective-permute-start | bytes 405512 | tf_op jit(solution)/shard_map/ppermute | solution.py:366
  20.0 2.0 %collective-permute-done.5.up2 = bf16[1024,128]{1,0:T(8,128)(2,1)S(1)} collective-permute-done((bf16[1024,128]{1,0:T(8,128)(2,1)S(1)}, bf16[1024,128]{1,0:T(8,128)(2,1)S(1)}, u32[]{:S(2)}, u32[]{:S(2)}) %collective-permute-start.5) | collective-permute-done | bytes 262176 | tf_op jit(solution)/shard_map/ppermute | solution.py:364
  22.0 3.1 %collective-permute-start.9 = (bf16[1024,128]{1,0:T(8,128)(2,1)S(1)}, bf16[1024,128]{1,0:T(8,128)(2,1)S(1)}, u32[]{:S(2)}, u32[]{:S(2)}) collective-permute-start(bf16[1024,128]{1,0:T(8,128)(2,1)S(1)} %broadcast_select_fusion), channel_id=1, source_target_pairs={{0,32},{8,104},{16,48},{24,120},{32,64},{40,8},{48,80},{56,24},{64... | collective-permute-start | bytes 786440 | tf_op jit(solution)/shard_map/ppermute | solution.py:370
  25.1 1.8 %collective-permute-start.7 = (bf16[1024,128]{1,0:T(8,128)(2,1)S(1)}, bf16[1024,128]{1,0:T(8,128)(2,1)S(1)}, u32[]{:S(2)}, u32[]{:S(2)}) collective-permute-start(bf16[1024,128]{1,0:T(8,128)(2,1)S(1)} %collective-permute-done.5.up2), channel_id=1, source_target_pairs={{0,16},{8,24},{16,32},{24,40},{32,48},{40,56},{48,64},{56,72},{64,... | collective-permute-start | bytes 786440 | tf_op jit(solution)/shard_map/ppermute | solution.py:367
  26.9 1.4 %collective-permute-start.8 = (bf16[1024,128]{1,0:T(8,128)(2,1)S(1)}, bf16[1024,128]{1,0:T(8,128)(2,1)S(1)}, u32[]{:S(2)}, u32[]{:S(2)}) collective-permute-start(bf16[1024,128]{1,0:T(8,128)(2,1)S(1)} %collective-permute-done.6.dn2), channel_id=1, source_target_pairs={{0,112},{8,120},{16,0},{24,8},{32,16},{40,24},{48,32},{56,40},{64,... | collective-permute-start | bytes 786440 | tf_op jit(solution)/shard_map/ppermute | solution.py:368
  29.3 6.8 %near_pages.1 = (bf16[2048,128]{1,0:T(8,128)(2,1)S(1)}, s32[160]{0:T(256)S(1)}, s32[160]{0:T(256)S(1)}, f32[8,1,256]{2,1,0:T(1,128)S(1)}, f32[8,1,256]{2,1,0:T(1,128)S(1)}, /*index=5*/f32[8,128,256]{2,1,0:T(8,128)S(1)}) custom-call(s32[32]{0:T(128)S(1)} %and_select_fusion.7.maps, bf16[1808,128]{1,0:T(8,128)(2,1)S(1)} %copy-done, ...), custom_call_target="tpu_custom_call" | custom-call | flops 4000000000 | bytes 4194304 | tf_op jit(solution)/shard_map/near_pages/pallas_call | solution.py:297
  36.1 1.1 %collective-permute-done.7.refs_2_ = bf16[1024,128]{1,0:T(8,128)(2,1)S(1)} collective-permute-done((bf16[1024,128]{1,0:T(8,128)(2,1)S(1)}, bf16[1024,128]{1,0:T(8,128)(2,1)S(1)}, u32[]{:S(2)}, u32[]{:S(2)}) %collective-permute-start.7) | collective-permute-done | bytes 262176 | tf_op jit(solution)/shard_map/ppermute | solution.py:367
  37.3 1.5 %far_pages_x.1 = (bf16[144,512]{1,0:T(8,128)(2,1)S(1)}, bf16[144,512]{1,0:T(8,128)(2,1)S(1)}) custom-call(s32[160]{0:T(256)S(1)} %get-tuple-element.31.refs_0_, bf16[2048,128]{1,0:T(8,128)(2,1)S(1)} %get-tuple-element.26.refs_1_, bf16[1024,128]{1,0:T(8,128)(2,1)S(1)} %collective-permute-done.7.refs_2_, bf16[1024,128]{1,0:T(8,128)(2,1)S(1)} %collective-permute-done.8.refs_3_, ...), custom_call_target="tpu_custom_call" | custom-call | flops 1000000000 | bytes 4194304 | tf_op jit(solution)/shard_map/far_pages_x/pallas_call | solution.py:324
  38.9 2.7 %collective-permute-start.11 = (bf16[144,512]{1,0:T(8,128)(2,1)S(1)}, bf16[144,512]{1,0:T(8,128)(2,1)S(1)}, u32[]{:S(2)}, u32[]{:S(2)}) collective-permute-start(bf16[144,512]{1,0:T(8,128)(2,1)S(1)} %get-tuple-element.33), channel_id=1, source_target_pairs={{0,128},{8,136},{16,144},{24,152},{32,160},{40,168},{48,176},{56,1... | collective-permute-start | bytes 442376 | tf_op jit(solution)/shard_map/ppermute | solution.py:385
  41.6 2.5 %far_pages_own.1 = (f32[136,512]{1,0:T(8,128)S(1)}, bf16[144,512]{1,0:T(8,128)(2,1)S(1)}) custom-call(s32[160]{0:T(256)S(1)} %get-tuple-element.25.refs_0_, bf16[2048,128]{1,0:T(8,128)(2,1)S(1)} %get-tuple-element.26.refs_1_, bf16[1024,128]{1,0:T(8,128)(2,1)S(1)} %collective-permute-done.7.refs_2_, bf16[1024,128]{1,0:T(8,128)(2,1)S(1)} %collective-permute-done.8.refs_3_, ...), custom_call_target="tpu_custom_call" | custom-call | flops 1000000000 | bytes 4194304 | tf_op jit(solution)/shard_map/far_pages_own/pallas_call | solution.py:324
  44.4 2.2 %collective-permute-done.10.p1 = bf16[144,512]{1,0:T(8,128)(2,1)S(1)} collective-permute-done((bf16[144,512]{1,0:T(8,128)(2,1)S(1)}, bf16[144,512]{1,0:T(8,128)(2,1)S(1)}, u32[]{:S(2)}, u32[]{:S(2)}) %collective-permute-start.10) | collective-permute-done | bytes 147488 | tf_op jit(solution)/shard_map/ppermute | solution.py:384
  46.5 2.5 %collective-permute-done.11.p2 = bf16[144,512]{1,0:T(8,128)(2,1)S(1)} collective-permute-done((bf16[144,512]{1,0:T(8,128)(2,1)S(1)}, bf16[144,512]{1,0:T(8,128)(2,1)S(1)}, u32[]{:S(2)}, u32[]{:S(2)}) %collective-permute-start.11) | collective-permute-done | bytes 147488 | tf_op jit(solution)/shard_map/ppermute | solution.py:385
  49.3 3.3 %convolution_convert_fusion = bf16[128,5120]{1,0:T(8,128)(2,1)S(1)} fusion(bf16[128,512]{1,0:T(8,128)(2,1)S(1)} %combine.1, bf16[512,5120]{1,0:T(8,128)(2,1)} %param.15), kind=kOutput, calls=%fused_computation | convolution fusion | flops 671744000 | bytes 6684672 | tf_op jit(solution)/shard_map/dot_general | solution.py:399
  52.7 2.1 %collective-permute-start.13 = (bf16[16,5120]{1,0:T(8,128)(2,1)S(1)}, bf16[16,5120]{1,0:T(8,128)(2,1)S(1)}, u32[]{:S(2)}, u32[]{:S(2)}) collective-permute-start(bf16[16,5120]{1,0:T(8,128)(2,1)S(1)} %get-tuple-element.41), channel_id=1, source_target_pairs={{0,5},{1,4},{2,7},{3,6},{4,1},{5,0},{6,3},{7,2},{8,13},{9,12},{10,... | collective-permute-start | bytes 491528 | tf_op jit(solution)/shard_map/ppermute | solution.py:402
  55.3 3.4 %collective-permute-start.15 = (bf16[16,5120]{1,0:T(8,128)(2,1)S(1)}, bf16[16,5120]{1,0:T(8,128)(2,1)S(1)}, u32[]{:S(2)}, u32[]{:S(2)}) collective-permute-start(bf16[16,5120]{1,0:T(8,128)(2,1)S(1)} %get-tuple-element.39), channel_id=1, source_target_pairs={{0,7},{1,6},{2,5},{3,4},{4,3},{5,2},{6,1},{7,0},{8,15},{9,14},{10,... | collective-permute-start | bytes 491528 | tf_op jit(solution)/shard_map/ppermute | solution.py:402
  59.0 2.0 %collective-permute-start.17 = (bf16[16,5120]{1,0:T(8,128)(2,1)S(1)}, bf16[16,5120]{1,0:T(8,128)(2,1)S(1)}, u32[]{:S(2)}, u32[]{:S(2)}) collective-permute-start(bf16[16,5120]{1,0:T(8,128)(2,1)S(1)} %get-tuple-element.37), channel_id=1, source_target_pairs={{0,2},{1,3},{2,0},{3,1},{4,6},{5,7},{6,4},{7,5},{8,10},{9,11},{10,... | collective-permute-start | bytes 491528 | tf_op jit(solution)/shard_map/ppermute | solution.py:402
  61.0 3.5 %collective-permute-start.18 = (bf16[16,5120]{1,0:T(8,128)(2,1)S(1)}, bf16[16,5120]{1,0:T(8,128)(2,1)S(1)}, u32[]{:S(2)}, u32[]{:S(2)}) collective-permute-start(bf16[16,5120]{1,0:T(8,128)(2,1)S(1)} %get-tuple-element.36), channel_id=1, source_target_pairs={{0,6},{1,7},{2,4},{3,5},{4,2},{5,3},{6,0},{7,1},{8,14},{9,15},{10,... | collective-permute-start | bytes 491528 | tf_op jit(solution)/shard_map/ppermute | solution.py:402
  65.5 10.0 %collective-permute-done.16.refs_4_ = bf16[16,5120]{1,0:T(8,128)(2,1)S(1)} collective-permute-done((bf16[16,5120]{1,0:T(8,128)(2,1)S(1)}, bf16[16,5120]{1,0:T(8,128)(2,1)S(1)}, u32[]{:S(2)}, u32[]{:S(2)}) %collective-permute-start.16) | collective-permute-done | bytes 163872 | tf_op jit(solution)/shard_map/ppermute | solution.py:402
  (31 shorter events, 5.4 us)
Async XLA Ops:
  1.0 6.0 %copy-start.1 = (bf16[8,1,128,128]{3,2,1,0:T(8,128)(2,1)}, bf16[8,1,128,128]{3,2,1,0:T(8,128)(2,1)S(1)}, u32[]{:S(2)}) copy-start(bf16[8,1,128,128]{3,2,1,0:T(8,128)(2,1)S(1)} %pad_maximum_fusion) | copy-start | bytes 786436
  1.0 12.2 %collective-permute-start = (bf16[1024,128]{1,0:T(8,128)(2,1)S(1)}, bf16[1024,128]{1,0:T(8,128)(2,1)S(1)}, u32[]{:S(2)}, u32[]{:S(2)}) collective-permute-start(bf16[1024,128]{1,0:T(8,128)(2,1)S(1)} %bitcast.10), channel_id=1, source_target_pairs={{0,16},{8,24},{16,32},{24,40},{32,48},{40,56},{48,64},{56,72},{64,... | collective-permute-start | bytes 786440 | tf_op jit(solution)/shard_map/ppermute | solution.py:345
  3.0 10.2 %collective-permute-start.1 = (bf16[1024,128]{1,0:T(8,128)(2,1)S(1)}, bf16[1024,128]{1,0:T(8,128)(2,1)S(1)}, u32[]{:S(2)}, u32[]{:S(2)}) collective-permute-start(bf16[1024,128]{1,0:T(8,128)(2,1)S(1)} %bitcast.11), channel_id=1, source_target_pairs={{0,112},{8,120},{16,0},{24,8},{32,16},{40,24},{48,32},{56,40},{64,... | collective-permute-start | bytes 786440 | tf_op jit(solution)/shard_map/ppermute | solution.py:346
  13.2 8.7 %collective-permute-start.5 = (bf16[1024,128]{1,0:T(8,128)(2,1)S(1)}, bf16[1024,128]{1,0:T(8,128)(2,1)S(1)}, u32[]{:S(2)}, u32[]{:S(2)}) collective-permute-start(bf16[1024,128]{1,0:T(8,128)(2,1)S(1)} %collective-permute-done.up1), channel_id=1, source_target_pairs={{0,16},{8,24},{16,32},{24,40},{32,48},{40,56},{48,64},{56,72},{64,... | collective-permute-start | bytes 786440 | tf_op jit(solution)/shard_map/ppermute | solution.py:364
  13.3 8.7 %collective-permute-start.6 = (bf16[1024,128]{1,0:T(8,128)(2,1)S(1)}, bf16[1024,128]{1,0:T(8,128)(2,1)S(1)}, u32[]{:S(2)}, u32[]{:S(2)}) collective-permute-start(bf16[1024,128]{1,0:T(8,128)(2,1)S(1)} %collective-permute-done.1.dn1), channel_id=1, source_target_pairs={{0,112},{8,120},{16,0},{24,8},{32,16},{40,24},{48,32},{56,40},{64,... | collective-permute-start | bytes 786440 | tf_op jit(solution)/shard_map/ppermute | solution.py:365
  16.5 10.4 %collective-permute-start.2 = (bf16[528,128]{1,0:T(8,128)(2,1)}, bf16[528,128]{1,0:T(8,128)(2,1)S(1)}, u32[]{:S(2)}, u32[]{:S(2)}) collective-permute-start(bf16[528,128]{1,0:T(8,128)(2,1)} %get-tuple-element.22), channel_id=1, source_target_pairs={{0,8},{8,0},{16,24},{24,16},{32,40},{40,32},{48,56},{56,48},{64,72... | collective-permute-start | bytes 405512 | tf_op jit(solution)/shard_map/ppermute | solution.py:366
  16.6 11.7 %collective-permute-start.3 = (bf16[528,128]{1,0:T(8,128)(2,1)}, bf16[528,128]{1,0:T(8,128)(2,1)S(1)}, u32[]{:S(2)}, u32[]{:S(2)}) collective-permute-start(bf16[528,128]{1,0:T(8,128)(2,1)} %get-tuple-element.22), channel_id=1, source_target_pairs={{0,128},{8,136},{16,144},{24,152},{32,160},{40,168},{48,176},{56,1... | collective-permute-start | bytes 405512 | tf_op jit(solution)/shard_map/ppermute | solution.py:366
  18.8 9.5 %collective-permute-start.4 = (bf16[528,128]{1,0:T(8,128)(2,1)}, bf16[528,128]{1,0:T(8,128)(2,1)S(1)}, u32[]{:S(2)}, u32[]{:S(2)}) collective-permute-start(bf16[528,128]{1,0:T(8,128)(2,1)} %get-tuple-element.22), channel_id=1, source_target_pairs={{0,136},{8,128},{16,152},{24,144},{32,168},{40,160},{48,184},{56,1... | collective-permute-start | bytes 405512 | tf_op jit(solution)/shard_map/ppermute | solution.py:366
  22.0 14.2 %collective-permute-start.9 = (bf16[1024,128]{1,0:T(8,128)(2,1)S(1)}, bf16[1024,128]{1,0:T(8,128)(2,1)S(1)}, u32[]{:S(2)}, u32[]{:S(2)}) collective-permute-start(bf16[1024,128]{1,0:T(8,128)(2,1)S(1)} %broadcast_select_fusion), channel_id=1, source_target_pairs={{0,32},{8,104},{16,48},{24,120},{32,64},{40,8},{48,80},{56,24},{64... | collective-permute-start | bytes 786440 | tf_op jit(solution)/shard_map/ppermute | solution.py:370
  25.1 12.2 %collective-permute-start.7 = (bf16[1024,128]{1,0:T(8,128)(2,1)S(1)}, bf16[1024,128]{1,0:T(8,128)(2,1)S(1)}, u32[]{:S(2)}, u32[]{:S(2)}) collective-permute-start(bf16[1024,128]{1,0:T(8,128)(2,1)S(1)} %collective-permute-done.5.up2), channel_id=1, source_target_pairs={{0,16},{8,24},{16,32},{24,40},{32,48},{40,56},{48,64},{56,72},{64,... | collective-permute-start | bytes 786440 | tf_op jit(solution)/shard_map/ppermute | solution.py:367
  26.9 10.4 %collective-permute-start.8 = (bf16[1024,128]{1,0:T(8,128)(2,1)S(1)}, bf16[1024,128]{1,0:T(8,128)(2,1)S(1)}, u32[]{:S(2)}, u32[]{:S(2)}) collective-permute-start(bf16[1024,128]{1,0:T(8,128)(2,1)S(1)} %collective-permute-done.6.dn2), channel_id=1, source_target_pairs={{0,112},{8,120},{16,0},{24,8},{32,16},{40,24},{48,32},{56,40},{64,... | collective-permute-start | bytes 786440 | tf_op jit(solution)/shard_map/ppermute | solution.py:368
  28.3 1.0 %copy-start = (bf16[1808,128]{1,0:T(8,128)(2,1)S(1)}, bf16[1808,128]{1,0:T(8,128)(2,1)}, u32[]{:S(2)}) copy-start(bf16[1808,128]{1,0:T(8,128)(2,1)} %get-tuple-element.20.local) | copy-start | bytes 1388548
  38.8 7.7 %collective-permute-start.10 = (bf16[144,512]{1,0:T(8,128)(2,1)S(1)}, bf16[144,512]{1,0:T(8,128)(2,1)S(1)}, u32[]{:S(2)}, u32[]{:S(2)}) collective-permute-start(bf16[144,512]{1,0:T(8,128)(2,1)S(1)} %get-tuple-element.32), channel_id=1, source_target_pairs={{0,136},{8,128},{16,152},{24,144},{32,168},{40,160},{48,184},{56,1... | collective-permute-start | bytes 442376 | tf_op jit(solution)/shard_map/ppermute | solution.py:384
  38.9 10.1 %collective-permute-start.11 = (bf16[144,512]{1,0:T(8,128)(2,1)S(1)}, bf16[144,512]{1,0:T(8,128)(2,1)S(1)}, u32[]{:S(2)}, u32[]{:S(2)}) collective-permute-start(bf16[144,512]{1,0:T(8,128)(2,1)S(1)} %get-tuple-element.33), channel_id=1, source_target_pairs={{0,128},{8,136},{16,144},{24,152},{32,160},{40,168},{48,176},{56,1... | collective-permute-start | bytes 442376 | tf_op jit(solution)/shard_map/ppermute | solution.py:385
  44.1 4.9 %collective-permute-start.12 = (bf16[144,512]{1,0:T(8,128)(2,1)S(1)}, bf16[144,512]{1,0:T(8,128)(2,1)S(1)}, u32[]{:S(2)}, u32[]{:S(2)}) collective-permute-start(bf16[144,512]{1,0:T(8,128)(2,1)S(1)} %get-tuple-element.34), channel_id=1, source_target_pairs={{0,8},{8,0},{16,24},{24,16},{32,40},{40,32},{48,56},{56,48},{64,72... | collective-permute-start | bytes 442376 | tf_op jit(solution)/shard_map/ppermute | solution.py:387
  52.7 8.3 %collective-permute-start.13 = (bf16[16,5120]{1,0:T(8,128)(2,1)S(1)}, bf16[16,5120]{1,0:T(8,128)(2,1)S(1)}, u32[]{:S(2)}, u32[]{:S(2)}) collective-permute-start(bf16[16,5120]{1,0:T(8,128)(2,1)S(1)} %get-tuple-element.41), channel_id=1, source_target_pairs={{0,5},{1,4},{2,7},{3,6},{4,1},{5,0},{6,3},{7,2},{8,13},{9,12},{10,... | collective-permute-start | bytes 491528 | tf_op jit(solution)/shard_map/ppermute | solution.py:402
  54.9 9.6 %collective-permute-start.14 = (bf16[16,5120]{1,0:T(8,128)(2,1)S(1)}, bf16[16,5120]{1,0:T(8,128)(2,1)S(1)}, u32[]{:S(2)}, u32[]{:S(2)}) collective-permute-start(bf16[16,5120]{1,0:T(8,128)(2,1)S(1)} %get-tuple-element.40), channel_id=1, source_target_pairs={{0,1},{1,0},{2,3},{3,2},{4,5},{5,4},{6,7},{7,6},{8,9},{9,8},{10,11... | collective-permute-start | bytes 491528 | tf_op jit(solution)/shard_map/ppermute | solution.py:402
  55.3 10.2 %collective-permute-start.15 = (bf16[16,5120]{1,0:T(8,128)(2,1)S(1)}, bf16[16,5120]{1,0:T(8,128)(2,1)S(1)}, u32[]{:S(2)}, u32[]{:S(2)}) collective-permute-start(bf16[16,5120]{1,0:T(8,128)(2,1)S(1)} %get-tuple-element.39), channel_id=1, source_target_pairs={{0,7},{1,6},{2,5},{3,4},{4,3},{5,2},{6,1},{7,0},{8,15},{9,14},{10,... | collective-permute-start | bytes 491528 | tf_op jit(solution)/shard_map/ppermute | solution.py:402
  58.7 16.7 %collective-permute-start.16 = (bf16[16,5120]{1,0:T(8,128)(2,1)S(1)}, bf16[16,5120]{1,0:T(8,128)(2,1)S(1)}, u32[]{:S(2)}, u32[]{:S(2)}) collective-permute-start(bf16[16,5120]{1,0:T(8,128)(2,1)S(1)} %get-tuple-element.38), channel_id=1, source_target_pairs={{0,3},{1,2},{2,1},{3,0},{4,7},{5,6},{6,5},{7,4},{8,11},{9,10},{10,... | collective-permute-start | bytes 491528 | tf_op jit(solution)/shard_map/ppermute | solution.py:402
  59.0 16.5 %collective-permute-start.17 = (bf16[16,5120]{1,0:T(8,128)(2,1)S(1)}, bf16[16,5120]{1,0:T(8,128)(2,1)S(1)}, u32[]{:S(2)}, u32[]{:S(2)}) collective-permute-start(bf16[16,5120]{1,0:T(8,128)(2,1)S(1)} %get-tuple-element.37), channel_id=1, source_target_pairs={{0,2},{1,3},{2,0},{3,1},{4,6},{5,7},{6,4},{7,5},{8,10},{9,11},{10,... | collective-permute-start | bytes 491528 | tf_op jit(solution)/shard_map/ppermute | solution.py:402
  61.0 14.5 %collective-permute-start.18 = (bf16[16,5120]{1,0:T(8,128)(2,1)S(1)}, bf16[16,5120]{1,0:T(8,128)(2,1)S(1)}, u32[]{:S(2)}, u32[]{:S(2)}) collective-permute-start(bf16[16,5120]{1,0:T(8,128)(2,1)S(1)} %get-tuple-element.36), channel_id=1, source_target_pairs={{0,6},{1,7},{2,4},{3,5},{4,2},{5,3},{6,0},{7,1},{8,14},{9,15},{10,... | collective-permute-start | bytes 491528 | tf_op jit(solution)/shard_map/ppermute | solution.py:402
  64.5 11.0 %collective-permute-start.19 = (bf16[16,5120]{1,0:T(8,128)(2,1)S(1)}, bf16[16,5120]{1,0:T(8,128)(2,1)S(1)}, u32[]{:S(2)}, u32[]{:S(2)}) collective-permute-start(bf16[16,5120]{1,0:T(8,128)(2,1)S(1)} %get-tuple-element.35), channel_id=1, source_target_pairs={{0,4},{1,5},{2,6},{3,7},{4,0},{5,1},{6,2},{7,3},{8,12},{9,13},{10,... | collective-permute-start | bytes 491528 | tf_op jit(solution)/shard_map/ppermute | solution.py:402
